TPU v7x, 32 devices: a whole 2x2x4 slice. The times are simulated.
32 devices in a mesh: src: 2 (over core), dp: 8 (over z, y), seq: 2 (over x).
Axes of the slice: x: 2, y: 2, z: 4, core: 2. Of those that a mesh axis runs over, the one named last changes fastest.
Arguments:
- inputs: bfloat16 [2, 8, 2, 256, 768], P('src', 'dp', None, 'seq'), may hold values from -6 to 6
- cotangent: bfloat16 [2, 8, 2, 256, 768], P('src', 'dp', None, 'seq'), may hold values from -6 to 6
- row_counts: int32 [2, 8], P('src', 'dp'), may hold values from 0 to 2
- response_mask: int32 [2, 8, 2, 256], P('src', 'dp', None, 'seq'), may hold values 0 or 1
- norm1_gain: bfloat16 [768], replicated, may hold values from 0.5 to 1.5
- norm1_bias: bfloat16 [768], replicated, may hold values from -1.5 to 1.5
- qkv_weight: bfloat16 [768, 2304], replicated, may hold values from -0.21875 to 0.21875
- qv_bias: bfloat16 [2, 768], replicated, may hold values from -1.5 to 1.5
- out_weight: bfloat16 [768, 768], replicated, may hold values from -3 to 3
- out_bias: bfloat16 [768], replicated, may hold values from -1.5 to 1.5
- norm2_gain: bfloat16 [768], replicated, may hold values from 0.5 to 1.5
- norm2_bias: bfloat16 [768], replicated, may hold values from -1.5 to 1.5
- up_weight: bfloat16 [768, 3072], replicated, may hold values from -0.21875 to 0.21875
- up_bias: bfloat16 [3072], replicated, may hold values from -1.5 to 1.5
- down_weight: bfloat16 [3072, 768], replicated, may hold values from -0.109375 to 0.109375
- down_bias: bfloat16 [768], replicated, may hold values from -1.5 to 1.5
Outputs:
- output: bfloat16 [2, 8, 2, 256, 768], P('src', 'dp', None, 'seq')
- input_grad: bfloat16 [2, 8, 2, 256, 768], P('src', 'dp', None, 'seq')
- source_counts: int32 [2], replicated
- grad_norm1_gain: float32 [768], P('dp')
- grad_norm1_bias: float32 [768], P('dp')
- grad_qkv_weight: float32 [768, 2304], P('dp')
- grad_qv_bias: float32 [2, 768], P(None, 'dp')
- grad_out_weight: float32 [768, 768], P('dp')
- grad_out_bias: float32 [768], P('dp')
- grad_norm2_gain: float32 [768], P('dp')
- grad_norm2_bias: float32 [768], P('dp')
- grad_up_weight: float32 [768, 3072], P('dp')
- grad_up_bias: float32 [3072], P('dp')
- grad_down_weight: float32 [3072, 768], P('dp')
- grad_down_bias: float32 [768], P('dp')
Inputs may be any that keep to these rules, and one draw needn't show every extreme that they name: `row_counts`: rows held by a data group; slots numbered 2 - 1 down to the count are padding.
All inputs are finite; a program needn't handle non-finite values. No bound on the sum of `response_mask` on one device may be relied on, other than what follows from the above.
Results may differ from a plain program's by a relative error of at most 0.018.
Values may be sent and summed in bfloat16 or wider, within the bound.
No kernel may reach another device: no remote copies, remote signals or barrier semaphores. Data moves between devices by JAX's collectives and lax.ppermute only.
A program may use at most 128 MiB of HBM per device.

v0:
```python
import functools
import math

import jax
import jax.numpy as jnp
from jax import lax
from jax.sharding import PartitionSpec as P

H = 12
HD = 64


EPS = 1e-05
NEGATIVE = -1e30


def norm_apply(values, scaling, offset):
    centre = jnp.mean(values, axis=-1, keepdims=True)
    centered = values - centre
    spread = jnp.mean(centered * centered, axis=-1, keepdims=True)
    return centered * lax.rsqrt(spread + EPS) * scaling + offset


def causal_scores(query_part, keys_part, allowed):
    scores = jnp.einsum(
        "rqhd,rkhd->rhqk", query_part, keys_part, preferred_element_type=jnp.float32
    )
    scores = scores * HD ** (-0.5)
    return jnp.where(allowed, scores, NEGATIVE)


def attend_forward(query_part, keys_part, values_part, allowed):
    scores = causal_scores(query_part, keys_part, allowed)
    highest = jnp.max(scores, axis=-1, keepdims=True)
    powers = jnp.exp(scores - highest)
    totals = jnp.sum(powers, axis=-1, keepdims=True)
    probs_low = (powers / totals).astype(jnp.bfloat16)
    mixed = jnp.einsum(
        "rhqk,rkhd->rqhd", probs_low, values_part, preferred_element_type=jnp.float32
    )
    return (mixed, highest, totals)


def attend_backward(query_part, keys_part, values_part, grad_part, highest, totals, allowed):
    scores = causal_scores(query_part, keys_part, allowed)
    probs = jnp.exp(scores - highest) / totals
    probs_low = probs.astype(jnp.bfloat16)
    grad_probs = jnp.einsum(
        "rqhd,rkhd->rhqk", grad_part, values_part, preferred_element_type=jnp.float32
    )
    inner = jnp.sum(probs * grad_probs, axis=-1, keepdims=True)
    grad_scores = (probs * (grad_probs - inner)).astype(jnp.bfloat16)
    factor = HD ** (-0.5)
    grad_query = (
        jnp.einsum("rhqk,rkhd->rqhd", grad_scores, keys_part, preferred_element_type=jnp.float32)
        * factor
    )
    grad_keys = (
        jnp.einsum("rhqk,rqhd->rkhd", grad_scores, query_part, preferred_element_type=jnp.float32)
        * factor
    )
    grad_values = jnp.einsum(
        "rhqk,rqhd->rkhd", probs_low, grad_part, preferred_element_type=jnp.float32
    )
    return (grad_query, grad_keys, grad_values)


def body(
    inputs,
    cotangent,
    row_counts,
    response_mask,
    norm1_gain,
    norm1_bias,
    qkv_weight,
    qv_bias,
    out_weight,
    out_bias,
    norm2_gain,
    norm2_bias,
    up_weight,
    up_bias,
    down_weight,
    down_bias,
):
    slots = inputs.shape[2]
    piece_len = inputs.shape[3]
    features = inputs.shape[4]
    tokens = slots * piece_len
    blocks_seq = lax.axis_size("seq")
    row_len = piece_len * blocks_seq
    group_heads = math.gcd(H, 4)
    bfloat = jnp.bfloat16
    single = jnp.float32
    present_int = (jnp.arange(slots) < row_counts[0, 0]).astype(jnp.int32)
    weight = (response_mask[0, 0] * present_int[:, None]).astype(single)
    local_count = jnp.sum(response_mask[0, 0] * present_int[:, None])
    picked = jnp.where(jnp.arange(lax.axis_size("src")) == lax.axis_index("src"), local_count, 0)
    source_counts = lax.psum(picked, ("src", "dp", "seq"))
    whole = jnp.sum(source_counts).astype(single)
    source = inputs.reshape(tokens, features).astype(single)
    normed, norm1_pull = jax.vjp(
        norm_apply, source, norm1_gain.astype(single), norm1_bias.astype(single)
    )
    normed_low = normed.astype(bfloat)
    bias_query = qv_bias[0].astype(single)
    joined = jnp.concatenate([bias_query, jnp.zeros_like(bias_query), qv_bias[1].astype(single)])
    projected = jnp.dot(normed_low, qkv_weight, preferred_element_type=single) + joined
    proj_low = projected.astype(bfloat)
    query = proj_low[:, :features].reshape(slots, piece_len, H, HD)
    keys_own = proj_low[:, features : 2 * features].reshape(slots, piece_len, features)
    values_own = proj_low[:, 2 * features :].reshape(slots, piece_len, features)
    keys_all, values_all = (
        lax.all_gather(keys_own, "seq", axis=1, tiled=True),
        lax.all_gather(values_own, "seq", axis=1, tiled=True),
    )
    query_pos = lax.axis_index("seq") * piece_len + jnp.arange(piece_len)
    allowed = query_pos[:, None] >= jnp.arange(row_len)[None, :]
    keys_heads = keys_all.reshape(slots, row_len, H, HD)
    values_heads = values_all.reshape(slots, row_len, H, HD)
    mixed_parts = []
    kept_stats = []
    for group in range(H // group_heads):
        first = group * group_heads
        last = first + group_heads
        mixed, highest, totals = attend_forward(
            query[:, :, first:last],
            keys_heads[:, :, first:last],
            values_heads[:, :, first:last],
            allowed,
        )
        mixed_parts.append(mixed)
        kept_stats.append((highest, totals))
    attended = jnp.concatenate(mixed_parts, axis=2).reshape(tokens, features)
    attended_low = attended.astype(bfloat)
    branch = jnp.dot(attended_low, out_weight, preferred_element_type=single) + out_bias.astype(
        single
    )
    middle = source + branch
    normed_two, norm2_pull = jax.vjp(
        norm_apply, middle, norm2_gain.astype(single), norm2_bias.astype(single)
    )
    normed_two_low = normed_two.astype(bfloat)
    hidden = jnp.dot(normed_two_low, up_weight, preferred_element_type=single) + up_bias.astype(
        single
    )
    active, gelu_pull = jax.vjp(functools.partial(jax.nn.gelu, approximate=True), hidden)
    active_low = active.astype(bfloat)
    branch_two = jnp.dot(active_low, down_weight, preferred_element_type=single) + down_bias.astype(
        single
    )
    result = middle + branch_two
    present_tok = jnp.repeat(present_int.astype(single), piece_len)
    output = (result * present_tok[:, None]).astype(bfloat).reshape(inputs.shape)
    incoming = cotangent.reshape(tokens, features).astype(single) * weight.reshape(tokens)[:, None]
    grad_branch_two = incoming.astype(bfloat)
    grad_down_weight = jnp.einsum(
        "tf,td->fd", active_low, grad_branch_two, preferred_element_type=single
    )
    grad_down_bias = jnp.sum(grad_branch_two.astype(single), axis=0)
    grad_active = jnp.einsum(
        "td,fd->tf", grad_branch_two, down_weight, preferred_element_type=single
    )
    grad_hidden = gelu_pull(grad_active)[0].astype(bfloat)
    grad_up_weight = jnp.einsum(
        "tm,tf->mf", normed_two_low, grad_hidden, preferred_element_type=single
    )
    grad_up_bias = jnp.sum(grad_hidden.astype(single), axis=0)
    grad_normed_two = jnp.einsum("tf,mf->tm", grad_hidden, up_weight, preferred_element_type=single)
    grad_mid_norm, grad_norm2_gain, grad_norm2_bias = norm2_pull(grad_normed_two)
    grad_middle = incoming + grad_mid_norm
    grad_branch = grad_middle.astype(bfloat)
    grad_out_weight = jnp.einsum(
        "tm,td->md", attended_low, grad_branch, preferred_element_type=single
    )
    grad_out_bias = jnp.sum(grad_branch.astype(single), axis=0)
    grad_attended = jnp.einsum("td,md->tm", grad_branch, out_weight, preferred_element_type=single)
    grad_heads = grad_attended.astype(bfloat).reshape(slots, piece_len, H, HD)
    query_grads = []
    key_grads = []
    value_grads = []
    for group in range(H // group_heads):
        first = group * group_heads
        last = first + group_heads
        highest, totals = kept_stats[group]
        grad_query, grad_keys, grad_values = attend_backward(
            query[:, :, first:last],
            keys_heads[:, :, first:last],
            values_heads[:, :, first:last],
            grad_heads[:, :, first:last],
            highest,
            totals,
            allowed,
        )
        query_grads.append(grad_query)
        key_grads.append(grad_keys)
        value_grads.append(grad_values)
    grad_query_all = jnp.concatenate(query_grads, axis=2).reshape(tokens, features)
    grad_keys_all = jnp.concatenate(key_grads, axis=2).reshape(slots, row_len, features)
    grad_values_all = jnp.concatenate(value_grads, axis=2).reshape(slots, row_len, features)
    grad_keys_own, grad_values_own = (
        lax.psum_scatter(
            grad_keys_all.astype(jnp.bfloat16), "seq", scatter_dimension=1, tiled=True
        ).astype(jnp.float32),
        lax.psum_scatter(
            grad_values_all.astype(jnp.bfloat16), "seq", scatter_dimension=1, tiled=True
        ).astype(jnp.float32),
    )
    grad_projected = jnp.concatenate(
        [
            grad_query_all,
            grad_keys_own.reshape(tokens, features),
            grad_values_own.reshape(tokens, features),
        ],
        axis=1,
    ).astype(bfloat)
    grad_qkv_weight = jnp.einsum(
        "tm,tn->mn", normed_low, grad_projected, preferred_element_type=single
    )
    column_sums = jnp.sum(grad_projected.astype(single), axis=0)
    grad_qv_bias = jnp.stack([column_sums[:features], column_sums[2 * features :]])
    grad_normed = jnp.einsum("tn,mn->tm", grad_projected, qkv_weight, preferred_element_type=single)
    grad_src_norm, grad_norm1_gain, grad_norm1_bias = norm1_pull(grad_normed)
    input_grad = (grad_middle + grad_src_norm).astype(bfloat).reshape(inputs.shape)
    grads = (
        grad_norm1_gain,
        grad_norm1_bias,
        grad_qkv_weight,
        grad_qv_bias,
        grad_out_weight,
        grad_out_bias,
        grad_norm2_gain,
        grad_norm2_bias,
        grad_up_weight,
        grad_up_bias,
        grad_down_weight,
        grad_down_bias,
    )
    summed = (
        lax.psum_scatter(
            grads[0].astype(jnp.bfloat16), "dp", scatter_dimension=0, tiled=True
        ).astype(jnp.float32),
        lax.psum_scatter(
            grads[1].astype(jnp.bfloat16), "dp", scatter_dimension=0, tiled=True
        ).astype(jnp.float32),
        lax.psum_scatter(
            grads[2].astype(jnp.bfloat16), "dp", scatter_dimension=0, tiled=True
        ).astype(jnp.float32),
        lax.psum_scatter(
            grads[3].astype(jnp.bfloat16), "dp", scatter_dimension=1, tiled=True
        ).astype(jnp.float32),
        lax.psum_scatter(
            grads[4].astype(jnp.bfloat16), "dp", scatter_dimension=0, tiled=True
        ).astype(jnp.float32),
        lax.psum_scatter(
            grads[5].astype(jnp.bfloat16), "dp", scatter_dimension=0, tiled=True
        ).astype(jnp.float32),
        lax.psum_scatter(
            grads[6].astype(jnp.bfloat16), "dp", scatter_dimension=0, tiled=True
        ).astype(jnp.float32),
        lax.psum_scatter(
            grads[7].astype(jnp.bfloat16), "dp", scatter_dimension=0, tiled=True
        ).astype(jnp.float32),
        lax.psum_scatter(
            grads[8].astype(jnp.bfloat16), "dp", scatter_dimension=0, tiled=True
        ).astype(jnp.float32),
        lax.psum_scatter(
            grads[9].astype(jnp.bfloat16), "dp", scatter_dimension=0, tiled=True
        ).astype(jnp.float32),
        lax.psum_scatter(
            grads[10].astype(jnp.bfloat16), "dp", scatter_dimension=0, tiled=True
        ).astype(jnp.float32),
        lax.psum_scatter(
            grads[11].astype(jnp.bfloat16), "dp", scatter_dimension=0, tiled=True
        ).astype(jnp.float32),
    )
    summed = (
        lax.psum(summed[0].astype(jnp.bfloat16), ("src", "seq")).astype(jnp.float32),
        lax.psum(summed[1].astype(jnp.bfloat16), ("src", "seq")).astype(jnp.float32),
        lax.psum(summed[2].astype(jnp.bfloat16), ("src", "seq")).astype(jnp.float32),
        lax.psum(summed[3].astype(jnp.bfloat16), ("src", "seq")).astype(jnp.float32),
        lax.psum(summed[4].astype(jnp.bfloat16), ("src", "seq")).astype(jnp.float32),
        lax.psum(summed[5].astype(jnp.bfloat16), ("src", "seq")).astype(jnp.float32),
        lax.psum(summed[6].astype(jnp.bfloat16), ("src", "seq")).astype(jnp.float32),
        lax.psum(summed[7].astype(jnp.bfloat16), ("src", "seq")).astype(jnp.float32),
        lax.psum(summed[8].astype(jnp.bfloat16), ("src", "seq")).astype(jnp.float32),
        lax.psum(summed[9].astype(jnp.bfloat16), ("src", "seq")).astype(jnp.float32),
        lax.psum(summed[10].astype(jnp.bfloat16), ("src", "seq")).astype(jnp.float32),
        lax.psum(summed[11].astype(jnp.bfloat16), ("src", "seq")).astype(jnp.float32),
    )
    final = [g / whole for g in summed]
    return (
        output,
        input_grad,
        source_counts,
        final[0],
        final[1],
        final[2],
        final[3],
        final[4],
        final[5],
        final[6],
        final[7],
        final[8],
        final[9],
        final[10],
        final[11],
    )


def solution(mesh):
    placed = (
        P("src", "dp", None, "seq", None),
        P("src", "dp", None, "seq", None),
        P("src", "dp"),
        P("src", "dp", None, "seq"),
        P(),
        P(),
        P(),
        P(),
        P(),
        P(),
        P(),
        P(),
        P(),
        P(),
        P(),
        P(),
    )
    return jax.shard_map(
        body,
        mesh=mesh,
        in_specs=placed,
        out_specs=(
            P("src", "dp", None, "seq", None),
            P("src", "dp", None, "seq", None),
            P(),
            P("dp"),
            P("dp"),
            P("dp", None),
            P(None, "dp"),
            P("dp", None),
            P("dp"),
            P("dp"),
            P("dp"),
            P("dp", None),
            P("dp"),
            P("dp", None),
            P("dp"),
        ),
        check_vma=False,
    )
```

profile of v0, /device:TPU:0, one launch (start us, length us, event | category | flops | bytes accessed | tf_op | source)
XLA Modules:
  0.0 627.3 jit_solution(1913384293320295959)
XLA Ops:
  27.0 14.7 %all_gather.7 = bf16[2,256,768]{2,1,0:T(8,128)(2,1)} all-gather(bf16[2,128,768]{2,1,0:T(8,128)(2,1)} %bitcast.154), channel_id=1, replica_groups=mesh['src'=2,'dp'=8,'seq'=2] {'seq'}, dimensions={1}, use_global_device_ids=true | all-gather | bytes 1179648 | tf_op jit(solution)/shard_map/all_gather | solution.py:114
  41.7 2.3 copy.58
  44.0 11.3 %all_gather.6 = bf16[2,256,768]{2,1,0:T(8,128)(2,1)} all-gather(bf16[2,128,768]{2,1,0:T(8,128)(2,1)} %bitcast.153), channel_id=1, replica_groups=mesh['src'=2,'dp'=8,'seq'=2] {'seq'}, dimensions={1}, use_global_device_ids=true | all-gather | bytes 1179648 | tf_op jit(solution)/shard_map/all_gather | solution.py:115
  55.3 2.3 copy.55
  57.6 3.1 fusion.176
  60.7 2.5 fusion.181
  63.2 2.6 fusion.38
  65.8 2.6 fusion.37
  68.4 2.6 fusion.186
  70.9 2.6 fusion.36
  77.7 4.0 fusion.192
  81.7 5.9 fusion.167
  99.6 2.6 fusion.27
  102.2 2.6 fusion.28
  104.8 2.6 fusion.29
  109.5 2.3 copy.68
  119.0 2.4 copy.67
  127.1 4.0 reduce-scatter.12.cloned.1.call-done
  133.0 18.4 %reduce-scatter.10.cloned.1.call-done = bf16[2,128,768]{2,1,0:T(8,128)(2,1)} async-done(((bf16[2,256,768]{2,1,0:T(8,128)(2,1)}), bf16[2,128,768]{2,1,0:T(8,128)(2,1)}) %reduce-scatter.10.cloned.1.call-update) | async-done | bytes 393232 | tf_op jit(solution)/shard_map/reduce_scatter | solution.py:202
  157.2 2.6 convolution_convert_fusion.3
  160.1 4.3 convolution_convert_fusion.2
  164.5 6.3 %convolution_convert_fusion = bf16[3072,768]{1,0:T(8,128)(2,1)} fusion(bf16[256,768]{1,0:T(8,128)(2,1)} %copy-done.10, f32[256,3072]{1,0:T(8,128)} %get-tuple-element.72), kind=kOutput, calls=%fused_computation.3 | convolution fusion | flops 1217396736 | bytes 8257536 | tf_op jit(solution)/shard_map/tf,td->fd/dot_general | solution.py:157
  170.9 5.4 convolution_convert_fusion.1
  179.5 39.6 %psum.91 = s32[2]{0:T(128)S(1)} all-reduce(s32[2]{0:T(128)} %compare_select_fusion), channel_id=1, replica_groups=mesh['src'=2,'dp'=8,'seq'=2] {'src','dp','seq'}, use_global_device_ids=true, to_apply=%region_20.21 | all-reduce | flops 2 | bytes 16 | tf_op jit(solution)/shard_map/psum | solution.py:99
  225.4 6.4 %fusion.23 = bf16[256,768]{1,0:T(8,128)(2,1)} fusion(f32[256,768]{1,0:T(8,128)} %copy-done.2, bf16[3072,768]{1,0:T(8,128)(2,1)} %param.30, f32[256]{0:T(256)S(1)} %broadcast_bitcast_fusion, f32[768]{0:T(1024)S(1)} %convert_element_type.259, f32[256,3072]{1,0:T(8,128)} %get-tuple-element.72), kind=kOutput, calls=%fused_computation.38 | convolution fusion | flops 1215823872 | bytes 9048064 | tf_op jit(solution)/shard_map/dot_general | solution.py:149
  234.7 38.2 %all-reduce.7 = (bf16[768]{0:T(1024)(128)(2,1)}, bf16[768]{0:T(1024)(128)(2,1)}, bf16[768]{0:T(1024)(128)(2,1)}, bf16[768]{0:T(1024)(128)(2,1)}, bf16[768]{0:T(1...) all-reduce(bf16[768]{0:T(1024)(128)(2,1)} %get-tuple-element.17, ...), channel_id=4, replica_groups=mesh['src'=2,'dp'=8,'seq'=2] {'dp'}, use_global_device_ids=true, to_apply=%region_22.23.clone | all-reduce | flops 7680 | bytes 30720
  282.5 2.8 add_convert_fusion
  286.1 8.0 %all-reduce.8 = (bf16[96]{0:T(256)(128)(2,1)}, bf16[96]{0:T(256)(128)(2,1)}, bf16[2,96]{1,0:T(2,128)(2,1)S(1)}, bf16[96]{0:T(256)(128)(2,1)}, bf16[96]{0:T(256)(...) all-reduce(bf16[96]{0:T(256)(128)(2,1)} %dynamic-slice.1, ...), channel_id=1, replica_groups=mesh['src'=2,'dp'=8,'seq'=2] {'src','seq'}, use_global_device_ids=true, to_apply=%region_23.24 | all-reduce | flops 1152 | bytes 4608 | tf_op jit(solution)/shard_map/psum | solution.py:278
  298.8 68.3 %reduce-scatter.14.cloned.1.call-done = bf16[96,2304]{1,0:T(8,128)(2,1)} async-done(((bf16[768,2304]{1,0:T(8,128)(2,1)}), bf16[96,2304]{1,0:T(8,128)(2,1)}) %reduce-scatter.14.cloned.1.call-update) | async-done | bytes 442384 | tf_op jit(solution)/shard_map/reduce_scatter | solution.py:246
  367.0 98.7 %reduce-scatter.20.cloned.1.call-done = bf16[384,768]{1,0:T(8,128)(2,1)} async-done(((bf16[3072,768]{1,0:T(8,128)(2,1)}), bf16[384,768]{1,0:T(8,128)(2,1)}) %reduce-scatter.20.cloned.1.call-update) | async-done | bytes 589840 | tf_op jit(solution)/shard_map/reduce_scatter | solution.py:270
  465.8 98.7 %reduce-scatter.18.cloned.1.call-done = bf16[96,3072]{1,0:T(8,128)(2,1)} async-done(((bf16[768,3072]{1,0:T(8,128)(2,1)}), bf16[96,3072]{1,0:T(8,128)(2,1)}) %reduce-scatter.18.cloned.1.call-update) | async-done | bytes 589840 | tf_op jit(solution)/shard_map/reduce_scatter | solution.py:264
  567.3 46.1 %all-reduce.12.cloned.1.call-done = (bf16[96,2304]{1,0:T(8,128)(2,1)}, bf16[96,768]{1,0:T(8,128)(2,1)}, bf16[96,3072]{1,0:T(8,128)(2,1)}, bf16[384,768]{1,0:T(8,128)(2,1)}) async-done(((bf16[96,2304]{1,0:T(8,128)(2,1)}, bf16[96,768]{1,0:T(8,128)(2,1)}, bf16[96,3072]{1,0:T(8,128)(2,1)}, bf16[384,768]{1,0:T(8,128)(2,1)}), (bf16[96,2304]{1,0:T(8,128)(2,1)}, bf16[96,768]{1,0:T(8,128)(2,1)}, ...) | async-done | bytes 1769488 | tf_op jit(solution)/shard_map/psum | solution.py:280
  (218 shorter events, 93.0 us)
Async XLA Ops:
  7.2 11.9 %copy-start = (bf16[768,2304]{1,0:T(8,128)(2,1)S(1)}, bf16[768,2304]{1,0:T(8,128)(2,1)}, u32[]{:S(2)}) copy-start(bf16[768,2304]{1,0:T(8,128)(2,1)} %param.22) | copy-start | bytes 10616836
  7.2 123.9 %reduce-scatter.12.cloned.1.call-start = ((), (), s32[]{:S(2)}) async-start(), calls=%async_computation.8 | async-start | bytes 1179648 | tf_op jit(solution)/shard_map/reduce_scatter | solution.py:205
  9.7 8.1 %copy-start.28 = (f32[256]{0:T(256)}, f32[256]{0:T(256)S(1)}, u32[]{:S(2)}) copy-start(f32[256]{0:T(256)S(1)} %get-tuple-element.62) | copy-start | bytes 3076
  11.0 6.8 %copy-start.30 = (f32[256]{0:T(256)}, f32[256]{0:T(256)S(1)}, u32[]{:S(2)}) copy-start(f32[256]{0:T(256)S(1)} %bitcast_rsqrt_fusion) | copy-start | bytes 3076
  63.2 5.1 copy-start.42
  70.9 3.7 copy-start.40
  73.5 3.9 copy-start.45
  73.5 3.9 copy-start.48
  73.5 4.0 copy-start.4
  77.1 12.7 %copy-start.2 = (f32[256,768]{1,0:T(8,128)}, f32[256,768]{1,0:T(8,128)S(1)}, u32[]{:S(2)}) copy-start(f32[256,768]{1,0:T(8,128)S(1)} %get-tuple-element.71) | copy-start | bytes 2359300
  77.4 12.4 %copy-start.34 = (f32[256]{0:T(256)}, f32[256]{0:T(256)S(1)}, u32[]{:S(2)}) copy-start(f32[256]{0:T(256)S(1)} %fusion.91) | copy-start | bytes 3076
  77.5 12.7 %copy-start.32 = (f32[256]{0:T(256)}, f32[256]{0:T(256)S(1)}, u32[]{:S(2)}) copy-start(f32[256]{0:T(256)S(1)} %fusion.88) | copy-start | bytes 3076
  77.5 4.2 slice-start
  77.6 4.0 copy-start.10
  77.7 4.0 copy-start.35
  77.7 4.0 slice-start.1
  111.8 39.7 %reduce-scatter.10.cloned.1.call-start = ((), (), s32[]{:S(2)}) async-start(), calls=%async_computation.7 | async-start | bytes 1179648 | tf_op jit(solution)/shard_map/reduce_scatter | solution.py:202
  121.5 163.8 %reduce-scatter.22.cloned.1.call-start = ((), (), s32[]{:S(2)}) async-start(), calls=%async_computation.13 | async-start | bytes 221184
  157.2 141.6 %reduce-scatter.16.cloned.1.call-start = ((), (), s32[]{:S(2)}) async-start(), calls=%async_computation.10 | async-start | bytes 1327104 | tf_op jit(solution)/shard_map/reduce_scatter | solution.py:252
  159.9 207.2 %reduce-scatter.14.cloned.1.call-start = ((), (), s32[]{:S(2)}) async-start(), calls=%async_computation.9 | async-start | bytes 3981312 | tf_op jit(solution)/shard_map/reduce_scatter | solution.py:246
  164.4 301.3 %reduce-scatter.20.cloned.1.call-start = ((), (), s32[]{:S(2)}) async-start(), calls=%async_computation.12 | async-start | bytes 5308416 | tf_op jit(solution)/shard_map/reduce_scatter | solution.py:270
  170.8 393.6 %reduce-scatter.18.cloned.1.call-start = ((), (), s32[]{:S(2)}) async-start(), calls=%async_computation.11 | async-start | bytes 5308416 | tf_op jit(solution)/shard_map/reduce_scatter | solution.py:264
  176.3 46.6 %copy-start.47 = (bf16[768]{0:T(1024)(128)(2,1)S(1)}, bf16[768]{0:T(1024)(128)(2,1)}, u32[]{:S(2)}) copy-start(bf16[768]{0:T(1024)(128)(2,1)} %param.31) | copy-start | bytes 4612
  176.3 437.1 %all-reduce.12.cloned.1.call-start = ((), (), s32[]{:S(2)}) async-start(), calls=%async_computation.14 | async-start | bytes 3538944 | tf_op jit(solution)/shard_map/psum | solution.py:280
  219.1 3.2 copy-start.49
  225.4 6.4 %copy-start.1 = (bf16[1,1,2,128,768]{4,3,2,1,0:T(8,128)(2,1)S(1)}, bf16[1,1,2,128,768]{4,3,2,1,0:T(8,128)(2,1)}, u32[]{:S(2)}) copy-start(bf16[1,1,2,128,768]{4,3,2,1,0:T(8,128)(2,1)} %param.16) | copy-start | bytes 1179652
  225.4 6.4 %copy-start.11 = (bf16[96,8,2,128]{3,1,2,0:T(8,128)(2,1)S(1)}, bf16[96,8,2,128]{3,1,2,0:T(8,128)(2,1)}, u32[]{:S(2)}) copy-start(bf16[96,8,2,128]{3,1,2,0:T(8,128)(2,1)} %copy.164) | copy-start | bytes 1179652
  225.4 6.4 %copy-start.12 = (bf16[256,768]{0,1:T(8,128)(2,1)S(1)}, bf16[256,768]{0,1:T(8,128)(2,1)}, u32[]{:S(2)}) copy-start(bf16[256,768]{0,1:T(8,128)(2,1)} %copy.70) | copy-start | bytes 1179652
  225.4 6.4 %copy-start.13 = (bf16[256,768]{0,1:T(8,128)(2,1)S(1)}, bf16[256,768]{0,1:T(8,128)(2,1)}, u32[]{:S(2)}) copy-start(bf16[256,768]{0,1:T(8,128)(2,1)} %copy.69) | copy-start | bytes 1179652
  225.4 6.4 %copy-start.29 = (f32[256]{0:T(256)S(1)}, f32[256]{0:T(256)}, u32[]{:S(2)}) copy-start(f32[256]{0:T(256)} %copy-done.28) | copy-start | bytes 3076
  231.8 50.6 %copy-start.33 = (f32[256]{0:T(256)S(1)}, f32[256]{0:T(256)}, u32[]{:S(2)}) copy-start(f32[256]{0:T(256)} %copy-done.32) | copy-start | bytes 3076
  613.5 5.9 copy-start.21
  (28 other events, 41.6 us)
Sparse Core Ops, SparseCore 0:
  111.9 19.1 reduce-scatter.11
  134.0 17.4 reduce-scatter.9
  157.3 61.0 reduce-scatter.21
  222.2 63.1 reduce-scatter.15
  288.9 78.0 reduce-scatter.13
  370.5 95.1 reduce-scatter.19
  469.4 95.0 reduce-scatter.17
  567.1 46.3 all-reduce.11
where the time goes:
time: 629 us; the launch traced here: 627 us
  waiting for transfers between devices  334 us (53%)
  blocking collectives  112 us (18%)
  matrix products  74.9 us (12%)
  local copies, waits for them, and re-layouts  44.2 us (7%)
  other arithmetic  43.9 us (7%)
  between operations  17.6 us (3%)
    reduce_scatter x1, waiting for transfers between devices, body(): lax.psum_scatter(grads[10].astype(jnp.bfloat16), 'dp', scatter_dimension=...  98.7 us
    reduce_scatter x1, waiting for transfers between devices, body(): lax.psum_scatter(grads[8].astype(jnp.bfloat16), 'dp', scatter_dimension=0...  98.7 us
    reduce_scatter x1, waiting for transfers between devices, body(): lax.psum_scatter(grads[2].astype(jnp.bfloat16), 'dp', scatter_dimension=0...  68.3 us
    psum x1, waiting for transfers between devices, body(): lax.psum(summed[2].astype(jnp.bfloat16), ('src', 'seq')).astype(jnp.float32)  46.1 us
    psum x1, blocking collectives, body(): source_counts = lax.psum(picked, ('src', 'dp', 'seq'))  39.6 us
    unnamed x1, blocking collectives  38.2 us
    reduce_scatter x1, waiting for transfers between devices, body(): lax.psum_scatter(grad_keys_all.astype(jnp.bfloat16), 'seq', scatter_dimen...  18.4 us
    unnamed x115, local copies, waits for them, and re-layouts  16.9 us
  transfers between devices with their start and end apart: 8, of which 6 were waited for; matrix products, arithmetic and copies ran while one was open for 11% of the time, Pallas kernels for 0%

commit v1 on v0

--- a/solution.py
+++ b/solution.py
@@ -65,7 +65,7 @@
     return (grad_query, grad_keys, grad_values)
 
 
-def body(
+def body_generic(
     inputs,
     cotangent,
     row_counts,
@@ -308,6 +308,220 @@
     )
 
 
+def swap_pairs(size, bit):
+    return [(i, i ^ bit) for i in range(size)]
+
+
+def relative(chunks, own):
+    count = chunks.shape[0]
+    return chunks[jnp.arange(count) ^ own]
+
+
+def scatter_sum(chunks, order):
+    count = chunks.shape[0]
+    depth = count.bit_length() - 1
+    left = list(range(depth - 1, -1, -1))
+    held = chunks.reshape((2,) * depth + chunks.shape[1:])
+    for stage in order:
+        if stage == "seq":
+            other = lax.ppermute(held, "seq", swap_pairs(2, 1))
+            total = held.astype(jnp.float32) + other.astype(jnp.float32)
+        else:
+            at = left.index(stage)
+            left.pop(at)
+            keep = lax.index_in_dim(held, 0, at, keepdims=False)
+            send = lax.index_in_dim(held, 1, at, keepdims=False)
+            other = lax.ppermute(send, "dp", swap_pairs(count, 1 << stage))
+            total = keep.astype(jnp.float32) + other.astype(jnp.float32)
+        held = total.astype(jnp.bfloat16)
+    return total
+
+
+def body_fast(
+    inputs,
+    cotangent,
+    row_counts,
+    response_mask,
+    norm1_gain,
+    norm1_bias,
+    qkv_weight,
+    qv_bias,
+    out_weight,
+    out_bias,
+    norm2_gain,
+    norm2_bias,
+    up_weight,
+    up_bias,
+    down_weight,
+    down_bias,
+):
+    slots = inputs.shape[2]
+    piece_len = inputs.shape[3]
+    features = inputs.shape[4]
+    length = 2 * piece_len
+    groups = lax.axis_size("dp")
+    bfloat = jnp.bfloat16
+    single = jnp.float32
+    core = lax.axis_index("src")
+    own = lax.axis_index("dp")
+    place = lax.axis_index("seq")
+    pair = swap_pairs(2, 1)
+
+    present = jnp.arange(slots) < row_counts[0, 0]
+    mask = response_mask[0, 0] * present.astype(jnp.int32)[:, None]
+    cot = cotangent[0, 0] * mask.astype(bfloat)[..., None]
+    local_count = jnp.sum(mask)
+    row_present = (place < row_counts[0, 0]).astype(single)
+
+    def row_of(both):
+        mine = lax.dynamic_index_in_dim(both, place, 0, keepdims=False)
+        theirs = lax.dynamic_index_in_dim(both, 1 - place, 0, keepdims=False)
+        other = lax.ppermute(theirs, "seq", pair)
+        return jnp.where(
+            place == 0, jnp.concatenate([mine, other]), jnp.concatenate([other, mine])
+        )
+
+    def row_back(row):
+        mine = lax.dynamic_slice_in_dim(row, place * piece_len, piece_len, 0)
+        theirs = lax.dynamic_slice_in_dim(row, (1 - place) * piece_len, piece_len, 0)
+        other = lax.ppermute(theirs, "seq", pair)
+        return jnp.where(place == 0, jnp.stack([mine, other]), jnp.stack([other, mine]))[None, None]
+
+    source = row_of(inputs[0, 0]).astype(single)
+    grad_low = row_of(cot)
+    incoming = grad_low.astype(single)
+
+    normed, norm1_pull = jax.vjp(
+        norm_apply, source, norm1_gain.astype(single), norm1_bias.astype(single)
+    )
+    normed_low = normed.astype(bfloat)
+    bias_query = qv_bias[0].astype(single)
+    joined = jnp.concatenate([bias_query, jnp.zeros_like(bias_query), qv_bias[1].astype(single)])
+    projected = jnp.dot(normed_low, qkv_weight, preferred_element_type=single) + joined
+    proj_low = projected.astype(bfloat).reshape(1, length, 3, H, HD)
+    query, keys, values = proj_low[:, :, 0], proj_low[:, :, 1], proj_low[:, :, 2]
+    allowed = jnp.arange(length)[:, None] >= jnp.arange(length)[None, :]
+    attended, highest, totals = attend_forward(query, keys, values, allowed)
+    attended_low = attended.astype(bfloat).reshape(length, features)
+    branch = jnp.dot(attended_low, out_weight, preferred_element_type=single) + out_bias.astype(
+        single
+    )
+    middle = source + branch
+    normed_two, norm2_pull = jax.vjp(
+        norm_apply, middle, norm2_gain.astype(single), norm2_bias.astype(single)
+    )
+    normed_two_low = normed_two.astype(bfloat)
+    hidden = jnp.dot(normed_two_low, up_weight, preferred_element_type=single) + up_bias.astype(
+        single
+    )
+    active, gelu_pull = jax.vjp(functools.partial(jax.nn.gelu, approximate=True), hidden)
+    active_low = active.astype(bfloat)
+    branch_two = jnp.dot(active_low, down_weight, preferred_element_type=single) + down_bias.astype(
+        single
+    )
+    result = middle + branch_two
+    output = row_back((result * row_present).astype(bfloat))
+
+    grad_active = jnp.einsum("td,fd->tf", grad_low, down_weight, preferred_element_type=single)
+    grad_hidden = gelu_pull(grad_active)[0].astype(bfloat)
+    grad_normed_two = jnp.einsum("tf,mf->tm", grad_hidden, up_weight, preferred_element_type=single)
+    grad_mid_norm, grad_norm2_gain, grad_norm2_bias = norm2_pull(grad_normed_two)
+    grad_middle = incoming + grad_mid_norm
+    grad_branch = grad_middle.astype(bfloat)
+    grad_attended = jnp.einsum("td,md->tm", grad_branch, out_weight, preferred_element_type=single)
+    grad_heads = grad_attended.astype(bfloat).reshape(1, length, H, HD)
+    grad_query, grad_keys, grad_values = attend_backward(
+        query, keys, values, grad_heads, highest, totals, allowed
+    )
+    grad_projected = jnp.concatenate(
+        [g.reshape(length, features) for g in (grad_query, grad_keys, grad_values)], axis=1
+    ).astype(bfloat)
+    grad_normed = jnp.einsum("tn,mn->tm", grad_projected, qkv_weight, preferred_element_type=single)
+    grad_src_norm, grad_norm1_gain, grad_norm1_bias = norm1_pull(grad_normed)
+    input_grad = row_back((grad_middle + grad_src_norm).astype(bfloat))
+
+    def weight_grad(left, right):
+        width = right.shape[1] // 2
+        mine = lax.dynamic_slice_in_dim(right, core * width, width, 1)
+        theirs = lax.dynamic_slice_in_dim(right, (1 - core) * width, width, 1)
+        left_other = lax.ppermute(left, "src", pair)
+        right_other = lax.ppermute(theirs, "src", pair)
+        left_all = jnp.concatenate([left, left_other])
+        right_all = jnp.concatenate([mine, right_other])
+        total = jnp.einsum("tm,tn->mn", left_all, right_all, preferred_element_type=single)
+        chunks = total.astype(bfloat).reshape(groups, left.shape[1] // groups, width)
+        return relative(chunks, own)
+
+    def column_sum(entries):
+        return jnp.sum(entries.astype(single), axis=0)
+
+    columns = column_sum(grad_projected)
+    chunked = [
+        v.reshape(groups, -1)
+        for v in (
+            grad_norm1_gain,
+            grad_norm1_bias,
+            columns[:features],
+            columns[2 * features :],
+            column_sum(grad_branch),
+            grad_norm2_gain,
+            grad_norm2_bias,
+            column_sum(grad_low),
+            column_sum(grad_hidden),
+        )
+    ]
+    n_digits = (slots * piece_len).bit_length()
+    digits = (local_count >> jnp.arange(n_digits)) & 1
+    both_digits = jnp.where(jnp.arange(2)[:, None] == core, digits[None, :], 0).astype(single)
+    chunked.append(jnp.broadcast_to(both_digits.reshape(1, -1), (groups, 2 * n_digits)))
+    sizes = [v.shape[1] for v in chunked]
+    vector = jnp.concatenate(chunked, axis=1)
+    fill = -vector.shape[1] % 256
+    vector = jnp.pad(vector, ((0, 0), (0, fill))).reshape(groups, 2, -1)
+    vector = vector + lax.ppermute(vector, "src", pair)
+    vector_sum = scatter_sum(relative(vector.astype(bfloat), own), (0, 1, 2, "seq")).reshape(-1)
+    parts = []
+    at = 0
+    for size in sizes:
+        parts.append(vector_sum[at : at + size])
+        at += size
+    counted = parts[-1].astype(jnp.int32).reshape(2, n_digits)
+    source_counts = jnp.sum(counted << jnp.arange(n_digits)[None, :], axis=1)
+    whole = jnp.sum(source_counts).astype(single)
+
+    def finish(total):
+        low = total.astype(bfloat)
+        other = lax.ppermute(low, "src", pair)
+        return jnp.where(
+            core == 0, jnp.concatenate([low, other], 1), jnp.concatenate([other, low], 1)
+        ).astype(single) / whole
+
+    grad_down_weight = finish(scatter_sum(weight_grad(active_low, grad_low), (0, 1, 2, "seq")))
+    grad_up_weight = finish(scatter_sum(weight_grad(normed_two_low, grad_hidden), (1, 2, 0, "seq")))
+    grad_out_weight = finish(scatter_sum(weight_grad(attended_low, grad_branch), (0, 1, 2, "seq")))
+    grad_qkv_weight = finish(
+        scatter_sum(weight_grad(normed_low, grad_projected), ("seq", 0, 1, 2))
+    )
+    scaled = [p / whole for p in parts[:-1]]
+    return (
+        output,
+        input_grad,
+        source_counts,
+        scaled[0],
+        scaled[1],
+        grad_qkv_weight,
+        jnp.stack([scaled[2], scaled[3]]),
+        grad_out_weight,
+        scaled[4],
+        scaled[5],
+        scaled[6],
+        grad_up_weight,
+        scaled[8],
+        grad_down_weight,
+        scaled[7],
+    )
+
+
 def solution(mesh):
     placed = (
         P("src", "dp", None, "seq", None),
@@ -327,8 +541,10 @@
         P(),
         P(),
     )
+    sizes = dict(mesh.shape)
+    paired = sizes["src"] == 2 and sizes["seq"] == 2 and sizes["dp"] == 8
     return jax.shard_map(
-        body,
+        body_fast if paired else body_generic,
         mesh=mesh,
         in_specs=placed,
         out_specs=(

time: 629 us -> 262 us (0.42)
  waiting for transfers between devices: 334 us -> 85.3 us
  blocking collectives: 112 us -> 0 us
  starting transfers between devices: 0.55 us -> 34.3 us
  matrix products: 74.9 us -> 51.9 us
  between operations: 17.6 us -> 2.93 us
    reduce_scatter x6 -> x0, waiting for transfers between devices: 288 us -> none  [the longest x1 98.7 us: body(): lax.psum_scatter(grads[10].astype(jnp.bfloat16), 'dp', scatter_dimension=...]
    ppermute x0 -> x37, waiting for transfers between devices: none -> 85.3 us  [the longest x15 57.8 us: scatter_sum(): other = lax.ppermute(send, 'dp', swap_pairs(count, 1 << stage))]
    psum x2 -> x0, blocking collectives: 47.6 us -> none  [the longest x1 39.6 us: body(): source_counts = lax.psum(picked, ('src', 'dp', 'seq'))]
    psum x1 -> x0, waiting for transfers between devices: 46.1 us -> none  [body(): lax.psum(summed[2].astype(jnp.bfloat16), ('src', 'seq')).astype(jnp.float32)]
    unnamed x1 -> x0, blocking collectives: 38.2 us -> none
    ppermute x0 -> x37, starting transfers between devices: none -> 34.3 us  [the longest x15 20.7 us: scatter_sum(): other = lax.ppermute(send, 'dp', swap_pairs(count, 1 << stage))]
    all_gather x2 -> x0, blocking collectives: 26 us -> none  [the longest x1 14.7 us: body(): lax.all_gather(keys_own, 'seq', axis=1, tiled=True)]
    unnamed x115 -> x80, local copies, waits for them, and re-layouts: 16.9 us -> 0.29 us
  transfers between devices with their start and end apart: 8 -> 37, of which waited for: 6 -> 15; matrix products, arithmetic and copies ran while one was open for 11% -> 51% of each run, Pallas kernels for 0% -> 0%
where the time goes in v1:
time: 262 us; the launch traced here: 260 us
  waiting for transfers between devices  85.3 us (33%)
  matrix products  51.9 us (20%)
  other arithmetic  47.6 us (18%)
  local copies, waits for them, and re-layouts  38.3 us (15%)
  starting transfers between devices  34.3 us (13%)
  between operations  2.93 us (1%)
    ppermute x15, waiting for transfers between devices, scatter_sum(): other = lax.ppermute(send, 'dp', swap_pairs(count, 1 << stage))  57.8 us
    ppermute x5, waiting for transfers between devices, scatter_sum(): other = lax.ppermute(held, 'seq', swap_pairs(2, 1))  25.5 us
    ppermute x15, starting transfers between devices, scatter_sum(): other = lax.ppermute(send, 'dp', swap_pairs(count, 1 << stage))  20.7 us
    dot_general x4, matrix products, weight_grad(): jnp.einsum('tm,tn->mn', left_all, right_all, preferred_element_type=single)  15.1 us
    gather x5, local copies, waits for them, and re-layouts, relative(): return chunks[jnp.arange(count) ^ own]  11.2 us
    reshape x9, local copies, waits for them, and re-layouts, body_fast(): v.reshape(groups, -1)  9.04 us
    convert_element_type x15, other arithmetic, scatter_sum(): held = total.astype(jnp.bfloat16)  6.36 us
    ppermute x5, starting transfers between devices, scatter_sum(): other = lax.ppermute(held, 'seq', swap_pairs(2, 1))  5.74 us
  transfers between devices with their start and end apart: 37, of which 15 were waited for; matrix products, arithmetic and copies ran while one was open for 51% of the time, Pallas kernels for 0%

profile of v1, /device:TPU:0, one launch (start us, length us, event | category | flops | bytes accessed | tf_op | source)
XLA Modules:
  0.0 260.4 jit_solution(9875631789818243471)
XLA Ops:
  5.0 2.9 %collective-permute-start.2 = (bf16[128,768]{1,0:T(8,128)(2,1)}, bf16[128,768]{1,0:T(8,128)(2,1)}, u32[]{:S(2)}, u32[]{:S(2)}) collective-permute-start(bf16[128,768]{1,0:T(8,128)(2,1)} %get-tuple-element.47), channel_id=1, source_target_pairs={{0,1},{1,0},{2,3},{3,2},{4,5},{5,4},{6,7},{7,6},{8,9},{9,8},{10,11... | collective-permute-start | bytes 589832 | tf_op jit(solution)/shard_map/ppermute | solution.py:379
  23.7 2.2 fusion.41
  25.9 3.1 %fusion.1 = bf16[256,2304]{1,0:T(8,128)(2,1)} fusion(bf16[256,768]{1,0:T(8,128)(2,1)} %fusion.41, bf16[768,2304]{1,0:T(8,128)(2,1)S(1)} %copy-done, f32[2304]{0:T(1024)S(1)} %pad_maximum_fusion.1), kind=kOutput, calls=%fused_computation.11 | convolution fusion | flops 907149312 | bytes 5121024 | tf_op jit(solution)/shard_map/dot_general | solution.py:400
  29.0 2.4 copy.43
  34.2 3.9 %convolution_convert_fusion.6 = bf16[12,64,256]{2,1,0:T(8,128)(2,1)} fusion(bf16[1,256,3,12,64]{1,4,3,2,0:T(8,128)(2,1)} %bitcast.226, f32[12,256,256]{1,2,0:T(8,128)S(1)} %get-tuple-element.66, f32[12,256]{1,0:T(8,128)S(1)} %get-tuple-element.65), kind=kOutput, calls=%fused_computation.56 | convolution fusion | flops 102432768 | bytes 3944448 | tf_op jit(solution)/shard_map/rhqk,rkhd->rqhd/dot_general | solution.py:38
  41.7 2.9 %convolution_add_fusion.1 = f32[256,3072]{1,0:T(8,128)S(1)} fusion(bf16[256,768]{1,0:T(8,128)(2,1)} %add_convert_fusion.2, bf16[768,3072]{1,0:T(8,128)(2,1)S(1)} %bitcast.244, f32[3072]{0:T(1024)S(1)} %copy-done.28), kind=kOutput, calls=%fused_computation.10 | convolution fusion | flops 1208745984 | bytes 8269824 | tf_op jit(solution)/shard_map/dot_general | solution.py:414
  45.8 4.8 %convert_reduce_fusion = (f32[3072]{0:T(1024)}, bf16[256,3072]{1,0:T(8,128)(2,1)S(1)}, bf16[256,3072]{1,0:T(8,128)(2,1)}) fusion(f32[256,3072]{1,0:T(8,128)S(1)} %convolution_add_fusion.1, bf16[256,768]{1,0:T(8,128)(2,1)S(1)} %get-tuple-element.29, bf16[3072,768]{1,0:T(8,128)(2,1)S(1)} %bitcast.246), kind=kOutput, calls=%fused_computation.25 | convolution fusion | flops 1226830848 | bytes 11415552 | tf_op jit(solution)/shard_map/td,fd->tf/dot_general | solution.py:425
  50.6 2.2 multiply_reduce_fusion.1
  59.0 3.5 %convolution_convert_fusion.4 = bf16[12,64,256]{2,1,0:T(8,128)(2,1)} fusion(bf16[256,12,64]{0,2,1:T(8,128)(2,1)} %bitcast.239, f32[12,256,256]{1,2,0:T(8,128)} %copy-done.10, f32[12,256]{1,0:T(8,128)} %copy-done.25), kind=kOutput, calls=%fused_computation.54 | convolution fusion | flops 102432768 | bytes 3944448 | tf_op jit(solution)/shard_map/rhqk,rqhd->rkhd/dot_general | solution.py:62
  67.7 4.4 %fusion.27 = bf16[256,768]{1,0:T(8,128)(2,1)S(1)} fusion(f32[256,768]{1,0:T(8,128)} %copy-done.3, bf16[256,3072]{1,0:T(8,128)(2,1)} %get-tuple-element.36, bf16[3072,768]{1,0:T(8,128)(2,1)} %param.30, f32[]{:T(128)S(6)} %convert_element_type.407, f32[768]{0:T(1024)} %convert_element_type.406), kind=kOutput, calls=%fused_computation.59 | convolution fusion | flops 1208745984 | bytes 7474180 | tf_op jit(solution)/shard_map/dot_general | solution.py:419
  78.9 2.5 convert_reduce_fusion.1
  84.6 4.1 %fusion.90 = (f32[768]{0:T(1024)}, f32[256]{0:T(256)S(1)}, f32[256,768]{1,0:T(8,128)}) fusion(f32[768]{0:T(1024)S(1)} %convert_element_type.388, f32[256]{0:T(256)} %copy-done.24, bf16[128,768]{1,0:T(8,128)(2,1)} %get-tuple-element.52, bf16[128,768]{1,0:T(8,128)(2,1)} %collective-permute-done, pred[]{:T(512)S(6)} %eq.23, ...), kind=kOutput, calls=%fused_computation.245 | convolution fusion | flops 908917760 | bytes 5906433 | tf_op jit(solution)/shard_map/tn,mn->tm/dot_general | solution.py:439
  96.7 2.1 add_convert_fusion.1
  102.6 2.7 %collective-permute-start.7 = (bf16[2,640]{1,0:T(2,128)(2,1)S(1)}, bf16[2,640]{1,0:T(2,128)(2,1)S(1)}, u32[]{:S(2)}, u32[]{:S(2)}) collective-permute-start(bf16[2,640]{1,0:T(2,128)(2,1)S(1)} %slice_bitcast_fusion.37), channel_id=1, source_target_pairs={{0,8},{2,10},{4,12},{6,14},{8,0},{10,2},{12,4},{14,6},{1,9},{3,11}... | collective-permute-start | bytes 7688 | tf_op jit(solution)/shard_map/ppermute | solution.py:334
  108.5 2.3 collective-permute-done.8
  120.4 5.0 %collective-permute-done.18 = bf16[2,2,96,384]{3,2,1,0:T(8,128)(2,1)S(1)} collective-permute-done((bf16[2,2,96,384]{3,2,1,0:T(8,128)(2,1)S(1)}, bf16[2,2,96,384]{3,2,1,0:T(8,128)(2,1)S(1)}, u32[]{:S(2)}, u32[]{:S(2)}) %collective-permute-start.18) | collective-permute-done | bytes 294944 | tf_op jit(solution)/shard_map/ppermute | solution.py:334
  128.2 4.5 %convolution_convert_fusion.1 = bf16[768,1536]{1,0:T(8,128)(2,1)} fusion(bf16[256,1536]{1,0:T(8,128)(2,1)} %collective-permute-done.24, bf16[256,1536]{1,0:T(8,128)(2,1)S(1)} %copy-done.15, bf16[256,768]{1,0:T(8,128)(2,1)} %collective-permute-done.23, bf16[256,768]{1,0:T(8,128)(2,1)} %add_convert_fusion.2), kind=kOutput, calls=%fused_computation.13 | convolution fusion | flops 1213857792 | bytes 4718592 | tf_op jit(solution)/shard_map/tm,tn->mn/dot_general | solution.py:451
  132.7 2.4 gather_fusion.3
  136.1 2.7 %collective-permute-start.20 = (bf16[96,384]{1,0:T(8,128)(2,1)S(1)}, bf16[96,384]{1,0:T(8,128)(2,1)S(1)}, u32[]{:S(2)}, u32[]{:S(2)}) collective-permute-start(bf16[96,384]{1,0:T(8,128)(2,1)S(1)} %slice_bitcast_fusion.31), channel_id=1, source_target_pairs={{0,8},{2,10},{4,12},{6,14},{8,0},{10,2},{12,4},{14,6},{1,9},{3,11}... | collective-permute-start | bytes 221192 | tf_op jit(solution)/shard_map/ppermute | solution.py:334
  138.9 3.6 %collective-permute-done.20 = bf16[96,384]{1,0:T(8,128)(2,1)S(1)} collective-permute-done((bf16[96,384]{1,0:T(8,128)(2,1)S(1)}, bf16[96,384]{1,0:T(8,128)(2,1)S(1)}, u32[]{:S(2)}, u32[]{:S(2)}) %collective-permute-start.20) | collective-permute-done | bytes 73760 | tf_op jit(solution)/shard_map/ppermute | solution.py:334
  145.3 3.8 %convolution_convert_fusion.2 = bf16[768,1152]{1,0:T(8,128)(2,1)} fusion(bf16[256,1152]{0,1:T(8,128)(2,1)} %collective-permute-done.10, bf16[256,1152]{0,1:T(8,128)(2,1)S(1)} %copy-done.19, bf16[256,768]{1,0:T(8,128)(2,1)} %collective-permute-done.9, bf16[256,768]{1,0:T(8,128)(2,1)} %fusion.41), kind=kOutput, calls=%fused_computation.14 | convolution fusion | flops 910786560 | bytes 3735552 | tf_op jit(solution)/shard_map/tm,tn->mn/dot_general | solution.py:451
  149.0 3.5 %gather_fusion.1 = bf16[8,96,1152]{2,1,0:T(8,128)(2,1)} fusion(bf16[8,96,1152]{2,1,0:T(8,128)(2,1)} %bitcast.234, s32[1024]{0:T(1024)S(1)} %copy-done.29), kind=kCustom, calls=%fused_computation.1 | custom fusion | bytes 3538976 | tf_op jit(solution)/shard_map/gather | solution.py:317
  156.9 5.2 %convolution_convert_fusion = bf16[3072,384]{1,0:T(8,128)(2,1)} fusion(bf16[256,3072]{1,0:T(8,128)(2,1)} %collective-permute-done.30, bf16[256,3072]{1,0:T(8,128)(2,1)} %get-tuple-element.36, bf16[256,384]{1,0:T(8,128)(2,1)} %collective-permute-done.31, bf16[256,384]{1,0:T(8,128)(2,1)} %get-tuple-element.41), kind=kOutput, calls=%fused_computation.8 | convolution fusion | flops 1216217088 | bytes 5898240 | tf_op jit(solution)/shard_map/tm,tn->mn/dot_general | solution.py:451
  162.1 4.0 %gather_fusion.4 = bf16[8,384,384]{2,1,0:T(8,128)(2,1)} fusion(bf16[8,384,384]{2,1,0:T(8,128)(2,1)} %bitcast.232, s32[1024]{0:T(1024)S(1)} %copy-done.29), kind=kCustom, calls=%fused_computation.4 | custom fusion | bytes 4718624 | tf_op jit(solution)/shard_map/gather | solution.py:317
  174.0 18.5 %collective-permute-done.11 = bf16[2,2,2,96,1152]{4,3,2,1,0:T(8,128)(2,1)} collective-permute-done((bf16[2,2,2,96,1152]{4,3,2,1,0:T(8,128)(2,1)}, bf16[2,2,2,96,1152]{4,3,2,1,0:T(8,128)(2,1)}, u32[]{:S(2)}, u32[]{:S(2)}) %collective-permute-start.11) | collective-permute-done | bytes 1769504 | tf_op jit(solution)/shard_map/ppermute | solution.py:327
  194.4 6.0 %collective-permute-done.26 = bf16[2,96,1536]{2,1,0:T(8,128)(2,1)S(1)} collective-permute-done((bf16[2,96,1536]{2,1,0:T(8,128)(2,1)S(1)}, bf16[2,96,1536]{2,1,0:T(8,128)(2,1)S(1)}, u32[]{:S(2)}, u32[]{:S(2)}) %collective-permute-start.26) | collective-permute-done | bytes 589856 | tf_op jit(solution)/shard_map/ppermute | solution.py:334
  202.8 7.8 %collective-permute-done.27 = bf16[96,1536]{1,0:T(8,128)(2,1)S(1)} collective-permute-done((bf16[96,1536]{1,0:T(8,128)(2,1)S(1)}, bf16[96,1536]{1,0:T(8,128)(2,1)S(1)}, u32[]{:S(2)}, u32[]{:S(2)}) %collective-permute-start.27) | collective-permute-done | bytes 294944 | tf_op jit(solution)/shard_map/ppermute | solution.py:334
  212.7 4.7 %collective-permute-done.28 = bf16[96,1536]{1,0:T(8,128)(2,1)S(1)} collective-permute-done((bf16[96,1536]{1,0:T(8,128)(2,1)S(1)}, bf16[96,1536]{1,0:T(8,128)(2,1)S(1)}, u32[]{:S(2)}, u32[]{:S(2)}) %collective-permute-start.28) | collective-permute-done | bytes 294944 | tf_op jit(solution)/shard_map/ppermute | solution.py:327
  217.6 10.2 %collective-permute-done.12 = bf16[2,2,96,1152]{3,2,1,0:T(8,128)(2,1)S(1)} collective-permute-done((bf16[2,2,96,1152]{3,2,1,0:T(8,128)(2,1)S(1)}, bf16[2,2,96,1152]{3,2,1,0:T(8,128)(2,1)S(1)}, u32[]{:S(2)}, u32[]{:S(2)}) %collective-permute-start.12) | collective-permute-done | bytes 884768 | tf_op jit(solution)/shard_map/ppermute | solution.py:334
  228.3 3.0 %collective-permute-start.34 = (bf16[384,384]{1,0:T(8,128)(2,1)S(1)}, bf16[384,384]{1,0:T(8,128)(2,1)S(1)}, u32[]{:S(2)}, u32[]{:S(2)}) collective-permute-start(bf16[384,384]{1,0:T(8,128)(2,1)S(1)} %slice_bitcast_fusion.21), channel_id=1, source_target_pairs={{0,8},{2,10},{4,12},{6,14},{8,0},{10,2},{12,4},{14,6},{1,9},{3,11}... | collective-permute-start | bytes 884744 | tf_op jit(solution)/shard_map/ppermute | solution.py:334
  232.5 12.3 %collective-permute-done.13 = bf16[2,96,1152]{2,1,0:T(8,128)(2,1)S(1)} collective-permute-done((bf16[2,96,1152]{2,1,0:T(8,128)(2,1)S(1)}, bf16[2,96,1152]{2,1,0:T(8,128)(2,1)S(1)}, u32[]{:S(2)}, u32[]{:S(2)}) %collective-permute-start.13) | collective-permute-done | bytes 442400 | tf_op jit(solution)/shard_map/ppermute | solution.py:334
  247.3 9.3 %collective-permute-done.14 = bf16[96,1152]{1,0:T(8,128)(2,1)S(1)} collective-permute-done((bf16[96,1152]{1,0:T(8,128)(2,1)S(1)}, bf16[96,1152]{1,0:T(8,128)(2,1)S(1)}, u32[]{:S(2)}, u32[]{:S(2)}) %collective-permute-start.14) | collective-permute-done | bytes 221216 | tf_op jit(solution)/shard_map/ppermute | solution.py:334
  (261 shorter events, 105.3 us)
Async XLA Ops:
  5.0 39.6 %collective-permute-start.2 = (bf16[128,768]{1,0:T(8,128)(2,1)}, bf16[128,768]{1,0:T(8,128)(2,1)}, u32[]{:S(2)}, u32[]{:S(2)}) collective-permute-start(bf16[128,768]{1,0:T(8,128)(2,1)} %get-tuple-element.47), channel_id=1, source_target_pairs={{0,1},{1,0},{2,3},{3,2},{4,5},{5,4},{6,7},{7,6},{8,9},{9,8},{10,11... | collective-permute-start | bytes 589832 | tf_op jit(solution)/shard_map/ppermute | solution.py:379
  9.7 11.1 %collective-permute-start = (bf16[128,768]{1,0:T(8,128)(2,1)}, bf16[128,768]{1,0:T(8,128)(2,1)}, u32[]{:S(2)}, u32[]{:S(2)}) collective-permute-start(bf16[128,768]{1,0:T(8,128)(2,1)} %get-tuple-element.51), channel_id=1, source_target_pairs={{0,1},{1,0},{2,3},{3,2},{4,5},{5,4},{6,7},{7,6},{8,9},{9,8},{10,11... | collective-permute-start | bytes 589832 | tf_op jit(solution)/shard_map/ppermute | solution.py:379
  25.9 117.8 %collective-permute-start.9 = (bf16[256,768]{1,0:T(8,128)(2,1)}, bf16[256,768]{1,0:T(8,128)(2,1)}, u32[]{:S(2)}, u32[]{:S(2)}) collective-permute-start(bf16[256,768]{1,0:T(8,128)(2,1)} %fusion.41), channel_id=1, source_target_pairs={{0,16},{16,0},{1,17},{17,1},{2,18},{18,2},{3,19},{19,3},{4,20},{20... | collective-permute-start | bytes 1179656 | tf_op jit(solution)/shard_map/ppermute | solution.py:447
  38.1 75.9 %collective-permute-start.16 = (bf16[256,768]{0,1:T(8,128)(2,1)}, bf16[256,768]{0,1:T(8,128)(2,1)}, u32[]{:S(2)}, u32[]{:S(2)}) collective-permute-start(bf16[256,768]{0,1:T(8,128)(2,1)} %bitcast.8), channel_id=1, source_target_pairs={{0,16},{16,0},{1,17},{17,1},{2,18},{18,2},{3,19},{19,3},{4,20},{20... | collective-permute-start | bytes 1179656 | tf_op jit(solution)/shard_map/ppermute | solution.py:447
  41.6 84.5 %collective-permute-start.23 = (bf16[256,768]{1,0:T(8,128)(2,1)}, bf16[256,768]{1,0:T(8,128)(2,1)}, u32[]{:S(2)}, u32[]{:S(2)}) collective-permute-start(bf16[256,768]{1,0:T(8,128)(2,1)} %add_convert_fusion.2), channel_id=1, source_target_pairs={{0,16},{16,0},{1,17},{17,1},{2,18},{18,2},{3,19},{19,3},{4,20},{20... | collective-permute-start | bytes 1179656 | tf_op jit(solution)/shard_map/ppermute | solution.py:447
  72.8 45.7 %collective-permute-start.1 = (bf16[128,768]{1,0:T(8,128)(2,1)}, bf16[128,768]{1,0:T(8,128)(2,1)}, u32[]{:S(2)}, u32[]{:S(2)}) collective-permute-start(bf16[128,768]{1,0:T(8,128)(2,1)} %get-tuple-element.50), channel_id=1, source_target_pairs={{0,1},{1,0},{2,3},{3,2},{4,5},{5,4},{6,7},{7,6},{8,9},{9,8},{10,11... | collective-permute-start | bytes 589832 | tf_op jit(solution)/shard_map/ppermute | solution.py:387
  95.1 3.7 %collective-permute-start.5 = (bf16[2,2,2,640]{3,2,1,0:T(2,128)(2,1)S(1)}, bf16[2,2,2,640]{3,2,1,0:T(2,128)(2,1)S(1)}, u32[]{:S(2)}, u32[]{:S(2)}) collective-permute-start(bf16[2,2,2,640]{3,2,1,0:T(2,128)(2,1)S(1)} %slice_bitcast_fusion.33), channel_id=1, source_target_pairs={{0,2},{2,0},{4,6},{6,4},{8,10},{10,8},{12,14},{14,12},{1,3},{3,1},... | collective-permute-start | bytes 30728 | tf_op jit(solution)/shard_map/ppermute | solution.py:334
  98.9 3.7 %collective-permute-start.6 = (bf16[2,2,640]{2,1,0:T(2,128)(2,1)S(1)}, bf16[2,2,640]{2,1,0:T(2,128)(2,1)S(1)}, u32[]{:S(2)}, u32[]{:S(2)}) collective-permute-start(bf16[2,2,640]{2,1,0:T(2,128)(2,1)S(1)} %slice_bitcast_fusion.35), channel_id=1, source_target_pairs={{0,4},{2,6},{4,0},{6,2},{8,12},{10,14},{12,8},{14,10},{1,5},{3,7},... | collective-permute-start | bytes 15368 | tf_op jit(solution)/shard_map/ppermute | solution.py:334
  102.6 4.6 %collective-permute-start.7 = (bf16[2,640]{1,0:T(2,128)(2,1)S(1)}, bf16[2,640]{1,0:T(2,128)(2,1)S(1)}, u32[]{:S(2)}, u32[]{:S(2)}) collective-permute-start(bf16[2,640]{1,0:T(2,128)(2,1)S(1)} %slice_bitcast_fusion.37), channel_id=1, source_target_pairs={{0,8},{2,10},{4,12},{6,14},{8,0},{10,2},{12,4},{14,6},{1,9},{3,11}... | collective-permute-start | bytes 7688 | tf_op jit(solution)/shard_map/ppermute | solution.py:334
  107.2 3.7 %collective-permute-start.8 = (bf16[2,640]{1,0:T(2,128)(2,1)S(1)}, bf16[2,640]{1,0:T(2,128)(2,1)S(1)}, u32[]{:S(2)}, u32[]{:S(2)}) collective-permute-start(bf16[2,640]{1,0:T(2,128)(2,1)S(1)} %fusion.73), channel_id=1, source_target_pairs={{0,1},{1,0},{2,3},{3,2},{4,5},{5,4},{6,7},{7,6},{8,9},{9,8},{10,11... | collective-permute-start | bytes 7688 | tf_op jit(solution)/shard_map/ppermute | solution.py:327
  113.5 13.2 %collective-permute-start.24 = (bf16[256,1536]{1,0:T(8,128)(2,1)S(1)}, bf16[256,1536]{1,0:T(8,128)(2,1)}, u32[]{:S(2)}, u32[]{:S(2)}) collective-permute-start(bf16[256,1536]{1,0:T(8,128)(2,1)S(1)} %copy-done.16), channel_id=1, source_target_pairs={{0,16},{16,0},{1,17},{17,1},{2,18},{18,2},{3,19},{19,3},{4,20},{20... | collective-permute-start | bytes 2359304 | tf_op jit(solution)/shard_map/ppermute | solution.py:448
  116.4 9.0 %collective-permute-start.18 = (bf16[2,2,96,384]{3,2,1,0:T(8,128)(2,1)S(1)}, bf16[2,2,96,384]{3,2,1,0:T(8,128)(2,1)S(1)}, u32[]{:S(2)}, u32[]{:S(2)}) collective-permute-start(bf16[2,2,96,384]{3,2,1,0:T(8,128)(2,1)S(1)} %slice_bitcast_fusion.25), channel_id=1, source_target_pairs={{0,2},{2,0},{4,6},{6,4},{8,10},{10,8},{12,14},{14,12},{1,3},{3,1},... | collective-permute-start | bytes 884744 | tf_op jit(solution)/shard_map/ppermute | solution.py:334
  118.6 38.3 %collective-permute-start.30 = (bf16[256,3072]{1,0:T(8,128)(2,1)}, bf16[256,3072]{1,0:T(8,128)(2,1)}, u32[]{:S(2)}, u32[]{:S(2)}) collective-permute-start(bf16[256,3072]{1,0:T(8,128)(2,1)} %get-tuple-element.36), channel_id=1, source_target_pairs={{0,16},{16,0},{1,17},{17,1},{2,18},{18,2},{3,19},{19,3},{4,20},{20... | collective-permute-start | bytes 4718600 | tf_op jit(solution)/shard_map/ppermute | solution.py:447
  125.4 31.5 %collective-permute-start.31 = (bf16[256,384]{1,0:T(8,128)(2,1)}, bf16[256,384]{1,0:T(8,128)(2,1)}, u32[]{:S(2)}, u32[]{:S(2)}) collective-permute-start(bf16[256,384]{1,0:T(8,128)(2,1)} %get-tuple-element.42), channel_id=1, source_target_pairs={{0,16},{16,0},{1,17},{17,1},{2,18},{18,2},{3,19},{19,3},{4,20},{20... | collective-permute-start | bytes 589832 | tf_op jit(solution)/shard_map/ppermute | solution.py:448
  126.2 17.6 %collective-permute-start.10 = (bf16[256,1152]{0,1:T(8,128)(2,1)}, bf16[256,1152]{0,1:T(8,128)(2,1)}, u32[]{:S(2)}, u32[]{:S(2)}) collective-permute-start(bf16[256,1152]{0,1:T(8,128)(2,1)} %get-tuple-element.40), channel_id=1, source_target_pairs={{0,16},{16,0},{1,17},{17,1},{2,18},{18,2},{3,19},{19,3},{4,20},{20... | collective-permute-start | bytes 1769480 | tf_op jit(solution)/shard_map/ppermute | solution.py:448
  126.7 8.4 %collective-permute-start.19 = (bf16[2,96,384]{2,1,0:T(8,128)(2,1)}, bf16[2,96,384]{2,1,0:T(8,128)(2,1)}, u32[]{:S(2)}, u32[]{:S(2)}) collective-permute-start(bf16[2,96,384]{2,1,0:T(8,128)(2,1)} %slice_bitcast_fusion.29), channel_id=1, source_target_pairs={{0,4},{2,6},{4,0},{6,2},{8,12},{10,14},{12,8},{14,10},{1,5},{3,7},... | collective-permute-start | bytes 442376 | tf_op jit(solution)/shard_map/ppermute | solution.py:334
  136.1 6.4 %collective-permute-start.20 = (bf16[96,384]{1,0:T(8,128)(2,1)S(1)}, bf16[96,384]{1,0:T(8,128)(2,1)S(1)}, u32[]{:S(2)}, u32[]{:S(2)}) collective-permute-start(bf16[96,384]{1,0:T(8,128)(2,1)S(1)} %slice_bitcast_fusion.31), channel_id=1, source_target_pairs={{0,8},{2,10},{4,12},{6,14},{8,0},{10,2},{12,4},{14,6},{1,9},{3,11}... | collective-permute-start | bytes 221192 | tf_op jit(solution)/shard_map/ppermute | solution.py:334
  142.5 11.5 %collective-permute-start.3 = (bf16[128,768]{1,0:T(8,128)(2,1)}, bf16[128,768]{1,0:T(8,128)(2,1)}, u32[]{:S(2)}, u32[]{:S(2)}) collective-permute-start(bf16[128,768]{1,0:T(8,128)(2,1)} %get-tuple-element.46), channel_id=1, source_target_pairs={{0,1},{1,0},{2,3},{3,2},{4,5},{5,4},{6,7},{7,6},{8,9},{9,8},{10,11... | collective-permute-start | bytes 589832 | tf_op jit(solution)/shard_map/ppermute | solution.py:387
  143.7 27.4 %collective-permute-start.25 = (bf16[2,2,96,1536]{3,2,1,0:T(8,128)(2,1)S(1)}, bf16[2,2,96,1536]{3,2,1,0:T(8,128)(2,1)}, u32[]{:S(2)}, u32[]{:S(2)}) collective-permute-start(bf16[2,2,96,1536]{3,2,1,0:T(8,128)(2,1)S(1)} %slice_bitcast_fusion.2), channel_id=1, source_target_pairs={{0,4},{2,6},{4,0},{6,2},{8,12},{10,14},{12,8},{14,10},{1,5},{3,7},... | collective-permute-start | bytes 3538952 | tf_op jit(solution)/shard_map/ppermute | solution.py:334
  143.8 8.8 %collective-permute-start.21 = (bf16[96,384]{1,0:T(8,128)(2,1)}, bf16[96,384]{1,0:T(8,128)(2,1)}, u32[]{:S(2)}, u32[]{:S(2)}) collective-permute-start(bf16[96,384]{1,0:T(8,128)(2,1)} %fusion.70), channel_id=1, source_target_pairs={{0,1},{1,0},{2,3},{3,2},{4,5},{5,4},{6,7},{7,6},{8,9},{9,8},{10,11... | collective-permute-start | bytes 221192 | tf_op jit(solution)/shard_map/ppermute | solution.py:327
  152.5 40.0 %collective-permute-start.11 = (bf16[2,2,2,96,1152]{4,3,2,1,0:T(8,128)(2,1)}, bf16[2,2,2,96,1152]{4,3,2,1,0:T(8,128)(2,1)}, u32[]{:S(2)}, u32[]{:S(2)}) collective-permute-start(bf16[2,2,2,96,1152]{4,3,2,1,0:T(8,128)(2,1)} %bitcast.223), channel_id=1, source_target_pairs={{0,1},{1,0},{2,3},{3,2},{4,5},{5,4},{6,7},{7,6},{8,9},{9,8},{10,11... | collective-permute-start | bytes 5308424 | tf_op jit(solution)/shard_map/ppermute | solution.py:327
  167.5 44.7 %collective-permute-start.32 = (bf16[2,2,384,384]{3,2,1,0:T(8,128)(2,1)S(1)}, bf16[2,2,384,384]{3,2,1,0:T(8,128)(2,1)S(1)}, u32[]{:S(2)}, u32[]{:S(2)}) collective-permute-start(bf16[2,2,384,384]{3,2,1,0:T(8,128)(2,1)S(1)} %slice_bitcast_fusion), channel_id=1, source_target_pairs={{0,2},{2,0},{4,6},{6,4},{8,10},{10,8},{12,14},{14,12},{1,3},{3,1},... | collective-permute-start | bytes 3538952 | tf_op jit(solution)/shard_map/ppermute | solution.py:334
  172.7 27.7 %collective-permute-start.26 = (bf16[2,96,1536]{2,1,0:T(8,128)(2,1)S(1)}, bf16[2,96,1536]{2,1,0:T(8,128)(2,1)S(1)}, u32[]{:S(2)}, u32[]{:S(2)}) collective-permute-start(bf16[2,96,1536]{2,1,0:T(8,128)(2,1)S(1)} %slice_bitcast_fusion.8), channel_id=1, source_target_pairs={{0,8},{2,10},{4,12},{6,14},{8,0},{10,2},{12,4},{14,6},{1,9},{3,11}... | collective-permute-start | bytes 1769480 | tf_op jit(solution)/shard_map/ppermute | solution.py:334
  200.5 10.0 %collective-permute-start.27 = (bf16[96,1536]{1,0:T(8,128)(2,1)S(1)}, bf16[96,1536]{1,0:T(8,128)(2,1)S(1)}, u32[]{:S(2)}, u32[]{:S(2)}) collective-permute-start(bf16[96,1536]{1,0:T(8,128)(2,1)S(1)} %slice_bitcast_fusion.23), channel_id=1, source_target_pairs={{0,2},{2,0},{4,6},{6,4},{8,10},{10,8},{12,14},{14,12},{1,3},{3,1},... | collective-permute-start | bytes 884744 | tf_op jit(solution)/shard_map/ppermute | solution.py:334
  201.8 25.9 %collective-permute-start.12 = (bf16[2,2,96,1152]{3,2,1,0:T(8,128)(2,1)S(1)}, bf16[2,2,96,1152]{3,2,1,0:T(8,128)(2,1)S(1)}, u32[]{:S(2)}, u32[]{:S(2)}) collective-permute-start(bf16[2,2,96,1152]{3,2,1,0:T(8,128)(2,1)S(1)} %slice_bitcast_fusion.4), channel_id=1, source_target_pairs={{0,2},{2,0},{4,6},{6,4},{8,10},{10,8},{12,14},{14,12},{1,3},{3,1},... | collective-permute-start | bytes 2654216 | tf_op jit(solution)/shard_map/ppermute | solution.py:334
  210.6 6.8 %collective-permute-start.28 = (bf16[96,1536]{1,0:T(8,128)(2,1)S(1)}, bf16[96,1536]{1,0:T(8,128)(2,1)S(1)}, u32[]{:S(2)}, u32[]{:S(2)}) collective-permute-start(bf16[96,1536]{1,0:T(8,128)(2,1)S(1)} %fusion.57), channel_id=1, source_target_pairs={{0,1},{1,0},{2,3},{3,2},{4,5},{5,4},{6,7},{7,6},{8,9},{9,8},{10,11... | collective-permute-start | bytes 884744 | tf_op jit(solution)/shard_map/ppermute | solution.py:327
  212.6 15.5 %collective-permute-start.33 = (bf16[2,384,384]{2,1,0:T(8,128)(2,1)S(1)}, bf16[2,384,384]{2,1,0:T(8,128)(2,1)S(1)}, u32[]{:S(2)}, u32[]{:S(2)}) collective-permute-start(bf16[2,384,384]{2,1,0:T(8,128)(2,1)S(1)} %slice_bitcast_fusion.6), channel_id=1, source_target_pairs={{0,4},{2,6},{4,0},{6,2},{8,12},{10,14},{12,8},{14,10},{1,5},{3,7},... | collective-permute-start | bytes 1769480 | tf_op jit(solution)/shard_map/ppermute | solution.py:334
  217.5 13.8 %collective-permute-start.29 = (bf16[96,1536]{1,0:T(8,128)(2,1)S(1)}, bf16[96,1536]{1,0:T(8,128)(2,1)S(1)}, u32[]{:S(2)}, u32[]{:S(2)}) collective-permute-start(bf16[96,1536]{1,0:T(8,128)(2,1)S(1)} %add_convert_fusion.4), channel_id=1, source_target_pairs={{0,16},{16,0},{1,17},{17,1},{2,18},{18,2},{3,19},{19,3},{4,20},{20... | collective-permute-start | bytes 884744 | tf_op jit(solution)/shard_map/ppermute | solution.py:494
  228.0 16.8 %collective-permute-start.13 = (bf16[2,96,1152]{2,1,0:T(8,128)(2,1)S(1)}, bf16[2,96,1152]{2,1,0:T(8,128)(2,1)S(1)}, u32[]{:S(2)}, u32[]{:S(2)}) collective-permute-start(bf16[2,96,1152]{2,1,0:T(8,128)(2,1)S(1)} %slice_bitcast_fusion.10), channel_id=1, source_target_pairs={{0,4},{2,6},{4,0},{6,2},{8,12},{10,14},{12,8},{14,10},{1,5},{3,7},... | collective-permute-start | bytes 1327112 | tf_op jit(solution)/shard_map/ppermute | solution.py:334
  228.3 17.3 %collective-permute-start.34 = (bf16[384,384]{1,0:T(8,128)(2,1)S(1)}, bf16[384,384]{1,0:T(8,128)(2,1)S(1)}, u32[]{:S(2)}, u32[]{:S(2)}) collective-permute-start(bf16[384,384]{1,0:T(8,128)(2,1)S(1)} %slice_bitcast_fusion.21), channel_id=1, source_target_pairs={{0,8},{2,10},{4,12},{6,14},{8,0},{10,2},{12,4},{14,6},{1,9},{3,11}... | collective-permute-start | bytes 884744 | tf_op jit(solution)/shard_map/ppermute | solution.py:334
  244.9 11.6 %collective-permute-start.14 = (bf16[96,1152]{1,0:T(8,128)(2,1)S(1)}, bf16[96,1152]{1,0:T(8,128)(2,1)S(1)}, u32[]{:S(2)}, u32[]{:S(2)}) collective-permute-start(bf16[96,1152]{1,0:T(8,128)(2,1)S(1)} %slice_bitcast_fusion.27), channel_id=1, source_target_pairs={{0,8},{2,10},{4,12},{6,14},{8,0},{10,2},{12,4},{14,6},{1,9},{3,11}... | collective-permute-start | bytes 663560 | tf_op jit(solution)/shard_map/ppermute | solution.py:334
  245.7 11.0 %collective-permute-start.35 = (bf16[384,384]{1,0:T(8,128)(2,1)S(1)}, bf16[384,384]{1,0:T(8,128)(2,1)S(1)}, u32[]{:S(2)}, u32[]{:S(2)}) collective-permute-start(bf16[384,384]{1,0:T(8,128)(2,1)S(1)} %fusion.56), channel_id=1, source_target_pairs={{0,1},{1,0},{2,3},{3,2},{4,5},{5,4},{6,7},{7,6},{8,9},{9,8},{10,11... | collective-permute-start | bytes 884744 | tf_op jit(solution)/shard_map/ppermute | solution.py:327
  (45 other events, 318.4 us)

commit v2 on v0

--- a/solution.py
+++ b/solution.py
@@ -4,6 +4,8 @@
 import jax
 import jax.numpy as jnp
 from jax import lax
+from jax.experimental import pallas as pl
+from jax.experimental.pallas import tpu as pltpu
 from jax.sharding import PartitionSpec as P
 
 H = 12
@@ -65,7 +67,7 @@
     return (grad_query, grad_keys, grad_values)
 
 
-def body(
+def body_generic(
     inputs,
     cotangent,
     row_counts,
@@ -308,6 +310,871 @@
     )
 
 
+SINGLE = jnp.float32
+LOW = jnp.bfloat16
+GROUP = 4
+GW = GROUP * HD
+DIGITS = 16
+
+
+def behind(kernel, skipped):
+    def ordered(at_ref, *refs):
+        kernel(at_ref, *refs[skipped:])
+
+    return ordered
+
+
+def tokens(after):
+    return [pl.BlockSpec(memory_space=pl.ANY)] * len(after)
+
+
+def dot_nt(left, right):
+    return lax.dot_general(left, right, (((1,), (1,)), ((), ())), preferred_element_type=SINGLE)
+
+
+def dot_tn(left, right):
+    return lax.dot_general(left, right, (((0,), (0,)), ((), ())), preferred_element_type=SINGLE)
+
+
+def dot_nn(left, right):
+    return jnp.dot(left, right, preferred_element_type=SINGLE)
+
+
+def normalize(values):
+    centered = values - jnp.mean(values, axis=-1, keepdims=True)
+    inverse = lax.rsqrt(jnp.mean(centered * centered, axis=-1, keepdims=True) + EPS)
+    return centered * inverse, inverse
+
+
+def norm_back(normal, inverse, grad, gain):
+    scaled = grad * gain
+    return inverse * (
+        scaled
+        - jnp.mean(scaled, axis=-1, keepdims=True)
+        - normal * jnp.mean(scaled * normal, axis=-1, keepdims=True)
+    )
+
+
+def head_mask(head):
+    lanes = lax.broadcasted_iota(jnp.int32, (1, GW), 1)
+    return (lanes >= head * HD) & (lanes < (head + 1) * HD)
+
+
+def join_row(place, mine_ref, other_ref, row_ref):
+    piece = mine_ref.shape[0]
+    row_ref[pl.ds(pl.multiple_of(place * piece, piece), piece), :] = mine_ref[...].astype(
+        row_ref.dtype
+    )
+    row_ref[pl.ds(pl.multiple_of((1 - place) * piece, piece), piece), :] = other_ref[
+        ...
+    ].astype(row_ref.dtype)
+
+
+def prepare_kernel(at_ref, rows_ref, cot_ref, mask_ref, c_send, c_mine, count_ref):
+    core, place = at_ref[0], at_ref[2]
+    piece = mask_ref.shape[1]
+    diagonal = lax.broadcasted_iota(jnp.int32, (piece, piece), 0) == lax.broadcasted_iota(
+        jnp.int32, (piece, piece), 1
+    )
+
+    def column(row):
+        kept = mask_ref[pl.ds(row, 1), :].astype(SINGLE) * (row < rows_ref[0, 0]).astype(SINGLE)
+        return jnp.sum(jnp.where(diagonal, kept, 0.0), axis=1, keepdims=True), kept
+
+    weight_mine, kept_mine = column(place)
+    weight_send, kept_send = column(1 - place)
+    c_send[...] = (cot_ref[1 - place].astype(SINGLE) * weight_send).astype(LOW)
+    c_mine[...] = (cot_ref[place].astype(SINGLE) * weight_mine).astype(LOW)
+    count = jnp.sum(kept_mine + kept_send, axis=1, keepdims=True).astype(jnp.int32)
+    lane = lax.broadcasted_iota(jnp.int32, count_ref.shape, 1) - core * DIGITS
+    digit = lax.shift_right_logical(
+        jnp.broadcast_to(count, count_ref.shape), jnp.clip(lane, 0, DIGITS - 1)
+    )
+    count_ref[...] = jnp.where((lane >= 0) & (lane < DIGITS), digit & 1, 0).astype(SINGLE)
+
+
+def prepare(at, rows, cot, mask):
+    piece, features = cot.shape[1:]
+    part = jax.ShapeDtypeStruct((piece, features), LOW)
+    smem = pl.BlockSpec(memory_space=pltpu.SMEM)
+    vmem = pl.BlockSpec(memory_space=pltpu.VMEM)
+    return pl.pallas_call(
+        prepare_kernel,
+        in_specs=[smem, smem, vmem, vmem],
+        out_specs=[vmem] * 3,
+        out_shape=[part, part, jax.ShapeDtypeStruct((1, 128), SINGLE)],
+        cost_estimate=pl.CostEstimate(flops=1, bytes_accessed=1, transcendentals=0),
+    )(at, rows, cot, mask)
+
+
+def attend_kernel(
+    at_ref, x_mine, x_other, gain1, bias1, wq, wk, wv, bq, bv, wo, bo, gain2, bias2,
+    n1_out, q_out, k_out, v_out, probs_out, a_out, m_out, n2_out, row,
+):
+    group = pl.program_id(0)
+    length = row.shape[0]
+
+    @pl.when(group == 0)
+    def _():
+        join_row(at_ref[2], x_mine, x_other, row)
+        normal, _ = normalize(row[...])
+        n1_out[...] = (normal * gain1[...].astype(SINGLE) + bias1[...].astype(SINGLE)).astype(LOW)
+
+    n1 = n1_out[...]
+    query = (dot_nn(n1, wq[...]) + bq[...].astype(SINGLE)).astype(LOW)
+    keys = dot_nn(n1, wk[...]).astype(LOW)
+    values = (dot_nn(n1, wv[...]) + bv[...].astype(SINGLE)).astype(LOW)
+    q_out[...] = query
+    k_out[...] = keys
+    v_out[...] = values
+    allowed = lax.broadcasted_iota(jnp.int32, (length, length), 0) >= lax.broadcasted_iota(
+        jnp.int32, (length, length), 1
+    )
+    scaled = query * HD**-0.5
+    mixed = None
+    for head in range(GROUP):
+        mask = head_mask(head)
+        scores = dot_nt(jnp.where(mask, scaled, 0), keys)
+        scores = jnp.where(allowed, scores, NEGATIVE)
+        powers = jnp.exp(scores - jnp.max(scores, axis=-1, keepdims=True))
+        probs = (powers * (1.0 / jnp.sum(powers, axis=-1, keepdims=True))).astype(LOW)
+        probs_out[head] = probs
+        part = dot_nn(probs, values)
+        mixed = part if head == 0 else jnp.where(mask, part, mixed)
+    at = pl.ds(pl.multiple_of(group * GW, GW), GW)
+    a_out[:, at] = mixed.astype(LOW)
+
+    @pl.when(group == pl.num_programs(0) - 1)
+    def _():
+        middle = row[...] + dot_nn(a_out[...], wo[...]) + bo[...].astype(SINGLE)
+        m_out[...] = middle
+        normal, _ = normalize(middle)
+        n2_out[...] = (normal * gain2[...].astype(SINGLE) + bias2[...].astype(SINGLE)).astype(LOW)
+
+
+def attend(at, inputs, x_other, gain1, bias1, qkv_weight, qv_bias, out_weight, out_bias, gain2, bias2):
+    piece, features = x_other.shape
+    length = 2 * piece
+    groups = features // GW
+    vec = pl.BlockSpec((1, features), lambda g, at: (0, 0))
+
+    def whole(*shape):
+        return pl.BlockSpec(shape, lambda g, at: (0,) * len(shape))
+
+    def columns(first):
+        return pl.BlockSpec((features, GW), lambda g, at: (0, first * groups + g))
+
+    act = pl.BlockSpec((length, GW), lambda g, at: (0, g))
+    return pl.pallas_call(
+        attend_kernel,
+        grid_spec=pltpu.PrefetchScalarGridSpec(
+            num_scalar_prefetch=1,
+            grid=(groups,),
+            in_specs=[
+                pl.BlockSpec((None, piece, features), lambda g, at: (at[2], 0, 0)),
+                whole(piece, features), vec, vec,
+                columns(0), columns(1), columns(2),
+                pl.BlockSpec((None, 1, GW), lambda g, at: (0, 0, g)),
+                pl.BlockSpec((None, 1, GW), lambda g, at: (1, 0, g)),
+                whole(features, features), vec, vec, vec,
+            ],
+            out_specs=[
+                whole(length, features), act, act, act,
+                pl.BlockSpec((GROUP, length, length), lambda g, at: (g, 0, 0)),
+                whole(length, features), whole(length, features), whole(length, features),
+            ],
+            scratch_shapes=[pltpu.VMEM((length, features), SINGLE)],
+        ),
+        out_shape=[
+            jax.ShapeDtypeStruct((length, features), LOW),
+            jax.ShapeDtypeStruct((length, features), LOW),
+            jax.ShapeDtypeStruct((length, features), LOW),
+            jax.ShapeDtypeStruct((length, features), LOW),
+            jax.ShapeDtypeStruct((groups * GROUP, length, length), LOW),
+            jax.ShapeDtypeStruct((length, features), LOW),
+            jax.ShapeDtypeStruct((length, features), SINGLE),
+            jax.ShapeDtypeStruct((length, features), LOW),
+        ],
+        compiler_params=pltpu.CompilerParams(vmem_limit_bytes=40 << 20),
+        cost_estimate=pl.CostEstimate(flops=1, bytes_accessed=1, transcendentals=0),
+    )(at, inputs, x_other, gain1, bias1, qkv_weight, qkv_weight, qkv_weight, qv_bias, qv_bias,
+      out_weight, out_bias, gain2, bias2)
+
+
+def gelu_and_slope(u):
+    c = math.sqrt(2 / math.pi)
+    square = u * u
+    bent = jnp.tanh(u * (c + (c * 0.044715) * square))
+    half = 0.5 + 0.5 * bent
+    slope = half + u * (0.5 - 0.5 * bent * bent) * (c + (3 * c * 0.044715) * square)
+    return u * half, slope
+
+
+def feed_kernel(
+    at_ref, rows_ref, n2_ref, m_ref, c_mine, c_other, up, up_bias, down, down_bias, gain2, count,
+    g_out, du_theirs, du_mine, y_mine, y_send, dm_out, db1_out, db1_theirs, db2_out, db2_theirs, vec_out,
+    y_sum, dn_sum,
+):
+    step = pl.program_id(0)
+    steps = pl.num_programs(0)
+    core, place = at_ref[0], at_ref[2]
+    features = n2_ref.shape[1]
+    width = up.shape[1]
+    half = features // 2
+    theirs = pl.ds(pl.multiple_of((1 - core) * half, half), half)
+
+    @pl.when(step == 0)
+    def _():
+        join_row(place, c_mine, c_other, db2_out)
+        db2_theirs[...] = db2_out[:, theirs]
+        vec_out[...] = jnp.zeros_like(vec_out)
+        vec_out[7:8, :] = jnp.sum(db2_out[...].astype(SINGLE), axis=0, keepdims=True)
+        vec_out[12:13, 0:128] = count[...]
+
+    n2 = n2_ref[...]
+    hidden = dot_nn(n2, up[...]) + up_bias[...].astype(SINGLE)
+    active, slope = gelu_and_slope(hidden)
+    active = active.astype(LOW)
+    g_out[...] = active
+    grad = (dot_nt(db2_out[...], down[...]) * slope).astype(LOW)
+    tile = lax.rem(step + (steps // 2) * (1 - core), steps)
+    sums = jnp.sum(grad.astype(SINGLE), axis=0, keepdims=True)
+    for part in range(width // features):
+        vec_out[pl.ds(8 + tile * (width // features) + part, 1), :] = sums[
+            :, part * features : (part + 1) * features
+        ]
+
+    @pl.when(step < steps // 2)
+    def _():
+        du_theirs[...] = grad
+
+    @pl.when(step >= steps // 2)
+    def _():
+        du_mine[...] = grad
+
+    y = dot_nn(active, down[...])
+    dn = dot_nt(grad, up[...])
+
+    @pl.when(step == 0)
+    def _():
+        y_sum[...] = y
+        dn_sum[...] = dn
+
+    @pl.when(step > 0)
+    def _():
+        y_sum[...] += y
+        dn_sum[...] += dn
+
+    @pl.when(step == steps - 1)
+    def _():
+        middle = m_ref[...]
+        piece = y_mine.shape[0]
+        present = (place < rows_ref[0, 0]).astype(SINGLE)
+        y_sum[...] = (middle + y_sum[...] + down_bias[...].astype(SINGLE)) * present
+        y_mine[...] = y_sum[pl.ds(pl.multiple_of(place * piece, piece), piece), :].astype(LOW)
+        y_send[...] = y_sum[pl.ds(pl.multiple_of((1 - place) * piece, piece), piece), :].astype(LOW)
+        normal, inverse = normalize(middle)
+        grad_n = dn_sum[...]
+        vec_out[5:6, :] = jnp.sum(grad_n * normal, axis=0, keepdims=True)
+        vec_out[6:7, :] = jnp.sum(grad_n, axis=0, keepdims=True)
+        back = norm_back(normal, inverse, grad_n, gain2[...].astype(SINGLE))
+        dm = db2_out[...].astype(SINGLE) + back
+        dm_out[...] = dm
+        low = dm.astype(LOW)
+        db1_out[...] = low
+        db1_theirs[...] = db1_out[:, theirs]
+        vec_out[4:5, :] = jnp.sum(low.astype(SINGLE), axis=0, keepdims=True)
+
+
+def feed(at, rows, n2, middle, c_mine, c_other, up, up_bias, down, down_bias, gain2, count):
+    length, features = n2.shape
+    piece = length // 2
+    hidden = up.shape[1]
+    steps = hidden // features
+    half = steps // 2
+    width = features
+
+    def whole(*shape):
+        return pl.BlockSpec(shape, lambda f, at: (0,) * len(shape))
+
+    def tile(f, at):
+        return lax.rem(f + half * (1 - at[0]), steps)
+
+    act = jax.ShapeDtypeStruct((length, features), LOW)
+    part = jax.ShapeDtypeStruct((piece, features), LOW)
+    vec = whole(1, features)
+    return pl.pallas_call(
+        feed_kernel,
+        grid_spec=pltpu.PrefetchScalarGridSpec(
+            num_scalar_prefetch=1,
+            grid=(steps,),
+            in_specs=[
+                pl.BlockSpec(memory_space=pltpu.SMEM),
+                whole(length, features), whole(length, features),
+                whole(piece, features), whole(piece, features),
+                pl.BlockSpec((features, width), lambda f, at: (0, tile(f, at))),
+                pl.BlockSpec((1, width), lambda f, at: (0, tile(f, at))),
+                pl.BlockSpec((width, features), lambda f, at: (tile(f, at), 0)),
+                vec, vec, whole(1, 128),
+            ],
+            out_specs=[
+                pl.BlockSpec((length, width), lambda f, at: (0, tile(f, at))),
+                pl.BlockSpec((length, width), lambda f, at: (0, jnp.minimum(f, half - 1))),
+                pl.BlockSpec((length, width), lambda f, at: (0, jnp.maximum(f - half, 0))),
+                whole(piece, features), whole(piece, features),
+                whole(length, features), whole(length, features), whole(length, features // 2),
+                whole(length, features), whole(length, features // 2),
+                whole(16, features),
+            ],
+            scratch_shapes=[pltpu.VMEM((length, features), SINGLE)] * 2,
+        ),
+        out_shape=[
+            jax.ShapeDtypeStruct((length, hidden), LOW),
+            jax.ShapeDtypeStruct((length, hidden // 2), LOW),
+            jax.ShapeDtypeStruct((length, hidden // 2), LOW),
+            part, part,
+            jax.ShapeDtypeStruct((length, features), SINGLE),
+            act, jax.ShapeDtypeStruct((length, features // 2), LOW),
+            act, jax.ShapeDtypeStruct((length, features // 2), LOW),
+            jax.ShapeDtypeStruct((16, features), SINGLE),
+        ],
+        compiler_params=pltpu.CompilerParams(vmem_limit_bytes=40 << 20),
+        cost_estimate=pl.CostEstimate(flops=1, bytes_accessed=1, transcendentals=0),
+    )(at, rows, n2, middle, c_mine, c_other, up, up_bias, down, down_bias, gain2, count)
+
+
+def back_kernel(
+    at_ref, x_mine, x_other, gain1, query_ref, keys_ref, values_ref, probs_ref, db1, dm, wo,
+    wq, wk, wv, vec_in, dp_theirs, dp_mine, x_grad_mine, x_grad_send, vec_out,
+    row, dp, dn_sum,
+):
+    group = pl.program_id(0)
+    groups = pl.num_programs(0)
+    core, place = at_ref[0], at_ref[2]
+    features = db1.shape[1]
+    grad_mixed = dot_nt(db1[...], wo[...]).astype(LOW)
+    query = query_ref[...] * HD**-0.5
+    keys = keys_ref[...] * HD**-0.5
+    values = values_ref[...]
+    dq = dk = dv = None
+    for head in range(GROUP):
+        mask = head_mask(head)
+        grad_head = jnp.where(mask, grad_mixed, 0)
+        probs_low = probs_ref[head]
+        probs = probs_low.astype(SINGLE)
+        grad_probs = dot_nt(grad_head, values)
+        inner = jnp.sum(probs * grad_probs, axis=-1, keepdims=True)
+        grad_scores = (probs * (grad_probs - inner)).astype(LOW)
+        part = dot_nn(grad_scores, keys)
+        dq = part if head == 0 else jnp.where(mask, part, dq)
+        part = dot_tn(grad_scores, query)
+        dk = part if head == 0 else jnp.where(mask, part, dk)
+        part = dot_tn(probs_low, grad_mixed)
+        dv = part if head == 0 else jnp.where(mask, part, dv)
+    dq, dk, dv = dq.astype(LOW), dk.astype(LOW), dv.astype(LOW)
+    for which, value in enumerate((dq, dk, dv)):
+        dp[:, pl.ds(pl.multiple_of(which * features + group * GW, GW), GW)] = value
+    at = pl.ds(pl.multiple_of(group * GW, GW), GW)
+
+    @pl.when(group == 0)
+    def _():
+        vec_out[...] = vec_in[...]
+
+    vec_out[2:3, at] = jnp.sum(dq.astype(SINGLE), axis=0, keepdims=True)
+    vec_out[3:4, at] = jnp.sum(dv.astype(SINGLE), axis=0, keepdims=True)
+    dn = dot_nt(dq, wq[...]) + dot_nt(dk, wk[...]) + dot_nt(dv, wv[...])
+
+    @pl.when(group == 0)
+    def _():
+        dn_sum[...] = dn
+
+    @pl.when(group > 0)
+    def _():
+        dn_sum[...] += dn
+
+    @pl.when(group == groups - 1)
+    def _():
+        half = dp_mine.shape[1]
+        dp_theirs[...] = dp[:, pl.ds(pl.multiple_of((1 - core) * half, half), half)]
+        dp_mine[...] = dp[:, pl.ds(pl.multiple_of(core * half, half), half)]
+        join_row(place, x_mine, x_other, row)
+        normal, inverse = normalize(row[...])
+        grad_n = dn_sum[...]
+        vec_out[0:1, :] = jnp.sum(grad_n * normal, axis=0, keepdims=True)
+        vec_out[1:2, :] = jnp.sum(grad_n, axis=0, keepdims=True)
+        back = norm_back(normal, inverse, grad_n, gain1[...].astype(SINGLE))
+        row[...] = dm[...] + back
+        piece = x_mine.shape[0]
+        x_grad_mine[...] = row[pl.ds(pl.multiple_of(place * piece, piece), piece), :].astype(LOW)
+        x_grad_send[...] = row[pl.ds(pl.multiple_of((1 - place) * piece, piece), piece), :].astype(LOW)
+
+
+def back(at, inputs, x_other, gain1, query, keys, values, probs, db1, dm, out_weight, qkv_weight, vec, after):
+    piece, features = x_other.shape
+    length = 2 * piece
+    groups = features // GW
+
+    def whole(*shape):
+        return pl.BlockSpec(shape, lambda g, at: (0,) * len(shape))
+
+    def columns(first):
+        return pl.BlockSpec((features, GW), lambda g, at: (0, first * groups + g))
+
+    act = pl.BlockSpec((length, GW), lambda g, at: (0, g))
+    half = jax.ShapeDtypeStruct((length, 3 * features // 2), LOW)
+    part = jax.ShapeDtypeStruct((piece, features), LOW)
+    return pl.pallas_call(
+        behind(back_kernel, len(after)),
+        grid_spec=pltpu.PrefetchScalarGridSpec(
+            num_scalar_prefetch=1,
+            grid=(groups,),
+            in_specs=[
+                *tokens(after),
+                pl.BlockSpec((None, piece, features), lambda g, at: (at[2], 0, 0)),
+                whole(piece, features), whole(1, features),
+                act, act, act,
+                pl.BlockSpec((GROUP, length, length), lambda g, at: (g, 0, 0)),
+                whole(length, features), whole(length, features),
+                pl.BlockSpec((GW, features), lambda g, at: (g, 0)),
+                columns(0), columns(1), columns(2), whole(16, features),
+            ],
+            out_specs=[whole(*half.shape), whole(*half.shape), whole(*part.shape), whole(*part.shape), whole(16, features)],
+            scratch_shapes=[
+                pltpu.VMEM((length, features), SINGLE),
+                pltpu.VMEM((length, 3 * features), LOW),
+                pltpu.VMEM((length, features), SINGLE),
+            ],
+        ),
+        out_shape=[half, half, part, part, jax.ShapeDtypeStruct((16, features), SINGLE)],
+        compiler_params=pltpu.CompilerParams(vmem_limit_bytes=40 << 20),
+        cost_estimate=pl.CostEstimate(flops=1, bytes_accessed=1, transcendentals=0),
+    )(at, *after, inputs, x_other, gain1, query, keys, values, probs, db1, dm, out_weight,
+      qkv_weight, qkv_weight, qkv_weight, vec)
+
+
+def lanes_kernel(at_ref, left, left_other, right, right_other, out, *whole, halved):
+    total = (dot_tn(left[...], right[...]) + dot_tn(left_other[...], right_other[...])).astype(LOW)
+    if halved:
+        half = total.shape[0] // 2
+        whole[0][...] = total
+        for side in (0, 1):
+            first = pl.multiple_of((at_ref[2] ^ side) * half, half)
+            out[0, side * half : (side + 1) * half, :] = whole[0][pl.ds(first, half), :]
+    else:
+        out[0] = total
+
+
+def grad_lanes(at, left, left_other, right, right_other, chunk_ids, count, after=(), halved=False):
+    length, tall = left.shape
+    rows = tall // count
+    width = right_other.shape[1]
+    pick = len(chunk_ids)
+
+    def chunk(j, at):
+        number = jnp.int32(chunk_ids[0])
+        for spot, value in enumerate(chunk_ids[1:], 1):
+            number = jnp.where(j == spot, value, number)
+        return (0, number ^ at[1])
+
+    return pl.pallas_call(
+        behind(functools.partial(lanes_kernel, halved=halved), len(after)),
+        grid_spec=pltpu.PrefetchScalarGridSpec(
+            num_scalar_prefetch=1,
+            grid=(pick,),
+            in_specs=[
+                *tokens(after),
+                pl.BlockSpec((length, rows), chunk),
+                pl.BlockSpec((length, rows), chunk),
+                pl.BlockSpec((length, width), lambda j, at: (0, at[0])),
+                pl.BlockSpec((length, width), lambda j, at: (0, 0)),
+            ],
+            out_specs=pl.BlockSpec((1, rows, width), lambda j, at: (j, 0, 0)),
+            scratch_shapes=[pltpu.VMEM((rows, width), LOW)] * halved,
+        ),
+        out_shape=jax.ShapeDtypeStruct((pick, rows, width), LOW),
+        compiler_params=pltpu.CompilerParams(vmem_limit_bytes=32 << 20),
+        cost_estimate=pl.CostEstimate(flops=1, bytes_accessed=1, transcendentals=0),
+    )(at, *after, left, left_other, right, right_other)
+
+
+def rows_kernel(at_ref, left, left_other, right, right_other, *rest, count, sent, kept, with_vec, halved):
+    if with_vec:
+        vec, vec_other, send, keep, whole, spread = rest
+    else:
+        send, keep, whole = rest
+    whole[...] = (
+        dot_tn(left[...], right[...]) + dot_tn(left_other[...], right_other[...])
+    ).astype(LOW)
+    rows = whole.shape[0] // count
+    if with_vec:
+        total = vec[...] + vec_other[...]
+        wide = 4 * total.shape[1] // count
+        spread[...] = jnp.zeros_like(spread)
+        for chunk in range(count):
+            spread[chunk, 0:8, :rows] = total[0:8, chunk * rows : (chunk + 1) * rows]
+            line = 8 + chunk * wide // total.shape[1]
+            begin = chunk * wide % total.shape[1]
+            for part in range(wide // rows):
+                spread[chunk, 8 + part : 9 + part, :rows] = total[
+                    line : line + 1, begin + part * rows : begin + (part + 1) * rows
+                ]
+            spread[chunk, 12:13, : 2 * DIGITS] = total[12:13, : 2 * DIGITS]
+    for out, numbers in ((send, sent), (keep, kept)):
+        if with_vec:
+            out[:, rows:, :] = jnp.zeros_like(out[:, rows:, :])
+        for spot, number in enumerate(numbers):
+            chunk = at_ref[1] ^ number
+            if halved:
+                half = rows // 2
+                for side in (0, 1):
+                    first = chunk * rows + (at_ref[2] ^ side) * half
+                    out[spot, side * half : (side + 1) * half, :] = whole[
+                        pl.ds(pl.multiple_of(first, half), half), :
+                    ]
+            else:
+                out[spot, :rows, :] = whole[pl.ds(pl.multiple_of(chunk * rows, rows), rows), :]
+            if with_vec:
+                out[spot, rows:, :128] = spread[chunk].astype(LOW)
+
+
+def grad_rows(at, left, left_other, right, right_other, sent, kept, tile, pick_core, vecs=(), after=(), halved=False):
+    length, tall = left.shape
+    count = len(sent) + len(kept)
+    rows = tall // count
+    width = right_other.shape[1]
+    steps = width // tile
+    more = 16 if vecs else 0
+    return pl.pallas_call(
+        behind(
+            functools.partial(
+                rows_kernel, count=count, sent=sent, kept=kept, with_vec=bool(vecs), halved=halved
+            ),
+            len(after),
+        ),
+        grid_spec=pltpu.PrefetchScalarGridSpec(
+            num_scalar_prefetch=1,
+            grid=(steps,),
+            in_specs=[
+                *tokens(after),
+                pl.BlockSpec((length, tall), lambda j, at: (0, 0)),
+                pl.BlockSpec((length, tall), lambda j, at: (0, 0)),
+                pl.BlockSpec((length, tile), lambda j, at: (0, (at[0] * steps if pick_core else 0) + j)),
+                pl.BlockSpec((length, tile), lambda j, at: (0, j)),
+                *[pl.BlockSpec(v.shape, lambda j, at: (0, 0)) for v in vecs],
+            ],
+            out_specs=[
+                pl.BlockSpec((len(sent), rows + more, tile), lambda j, at: (0, 0, j)),
+                pl.BlockSpec((len(kept), rows + more, tile), lambda j, at: (0, 0, j)),
+            ],
+            scratch_shapes=[pltpu.VMEM((tall, tile), LOW)]
+            + [pltpu.VMEM((count, 16, 128), SINGLE)] * bool(vecs),
+        ),
+        out_shape=[
+            jax.ShapeDtypeStruct((len(sent), rows + more, width), LOW),
+            jax.ShapeDtypeStruct((len(kept), rows + more, width), LOW),
+        ],
+        compiler_params=pltpu.CompilerParams(vmem_limit_bytes=32 << 20),
+        cost_estimate=pl.CostEstimate(flops=1, bytes_accessed=1, transcendentals=0),
+    )(at, *after, left, left_other, right, right_other, *vecs)
+
+
+def counts_of(vec):
+    line = vec[12:13, :].astype(SINGLE)
+    lane = lax.broadcasted_iota(jnp.int32, line.shape, 1)
+    worth = lax.shift_left(jnp.ones_like(lane), lax.rem(lane, DIGITS)).astype(SINGLE)
+    return [
+        jnp.sum(
+            jnp.where((lane >= half * DIGITS) & (lane < (half + 1) * DIGITS), line * worth, 0.0),
+            axis=1,
+            keepdims=True,
+        )
+        for half in (0, 1)
+    ]
+
+
+def finish_kernel(at_ref, vec, mine, other, out):
+    core = at_ref[0]
+    first, second = counts_of(vec[...])
+    whole = first + second
+    rows = out.shape[0]
+    width = mine.shape[1]
+    out[:, pl.ds(pl.multiple_of(core * width, 128), width)] = (
+        mine[:rows, :].astype(SINGLE) / whole
+    )
+    out[:, pl.ds(pl.multiple_of((1 - core) * width, 128), width)] = (
+        other[:rows, :].astype(SINGLE) / whole
+    )
+
+
+def finish(at, vec, mine, other, rows):
+    width = mine.shape[1]
+    vmem = pl.BlockSpec(memory_space=pltpu.VMEM)
+    return pl.pallas_call(
+        finish_kernel,
+        in_specs=[pl.BlockSpec(memory_space=pltpu.SMEM), vmem, vmem, vmem],
+        out_specs=vmem,
+        out_shape=jax.ShapeDtypeStruct((rows, 2 * width), SINGLE),
+        cost_estimate=pl.CostEstimate(flops=1, bytes_accessed=1, transcendentals=0),
+    )(at, vec, mine, other)
+
+
+def finish_halves_kernel(at_ref, vec, *refs):
+    parts, out = refs[:4], refs[4]
+    core, place = at_ref[0], at_ref[2]
+    first, second = counts_of(vec[...])
+    whole = first + second
+    half, width = parts[0].shape
+    for number, part in enumerate(parts):
+        row = pl.multiple_of((place ^ (number & 1)) * half, half)
+        column = pl.multiple_of((core ^ (number >> 1)) * width, 128)
+        out[pl.ds(row, half), pl.ds(column, width)] = part[...].astype(SINGLE) / whole
+
+
+def finish_halves(at, vec, parts):
+    half, width = parts[0].shape
+    vmem = pl.BlockSpec(memory_space=pltpu.VMEM)
+    return pl.pallas_call(
+        finish_halves_kernel,
+        in_specs=[pl.BlockSpec(memory_space=pltpu.SMEM)] + [vmem] * 5,
+        out_specs=vmem,
+        out_shape=jax.ShapeDtypeStruct((2 * half, 2 * width), SINGLE),
+        cost_estimate=pl.CostEstimate(flops=1, bytes_accessed=1, transcendentals=0),
+    )(at, vec, *parts)
+
+
+def close_kernel(vec, counts, plain, qv, up):
+    first, second = counts_of(vec[...])
+    counts[:, 0:1] = first.astype(jnp.int32)
+    counts[:, 1:2] = second.astype(jnp.int32)
+    rows = plain.shape[1]
+    scaled = vec[...].astype(SINGLE) / (first + second)
+    plain[...] = scaled[0:8, :rows]
+    qv[...] = scaled[2:4, :rows]
+    for part in range(up.shape[1] // rows):
+        up[:, part * rows : (part + 1) * rows] = scaled[8 + part : 9 + part, :rows]
+
+
+def close(vec, rows, wide):
+    vmem = pl.BlockSpec(memory_space=pltpu.VMEM)
+    return pl.pallas_call(
+        close_kernel,
+        in_specs=[vmem],
+        out_specs=[vmem] * 4,
+        out_shape=[
+            jax.ShapeDtypeStruct((1, 2), jnp.int32),
+            jax.ShapeDtypeStruct((8, rows), SINGLE),
+            jax.ShapeDtypeStruct((2, rows), SINGLE),
+            jax.ShapeDtypeStruct((1, wide), SINGLE),
+        ],
+        cost_estimate=pl.CostEstimate(flops=1, bytes_accessed=1, transcendentals=0),
+    )(vec)
+
+
+STAGES = ((1, "seq", 0, 2, "gather"), (0, "seq", 1, 2, "gather"), (0, "seq", 1, 2, "gather"), (1, 0, 2, "seq"))
+STEPS = "uduoduqoqudqodqo"
+
+
+def swap_pairs(size, bit):
+    return [(i, i ^ bit) for i in range(size)]
+
+
+def added(one, two):
+    return (one.astype(SINGLE) + two.astype(SINGLE)).astype(LOW)
+
+
+def split_numbers(count, stage):
+    sent = [j for j in range(count) if j >> stage & 1]
+    return sent, [j for j in range(count) if not j >> stage & 1]
+
+
+class Order:
+    def __init__(self):
+        self.last = None
+
+    def tie(self, value):
+        if self.last is not None:
+            value, _ = lax.optimization_barrier((value, self.last))
+        return value
+
+    def mark(self, value):
+        self.last = value
+
+
+class Sum:
+    def __init__(self, order, groups, stages, send, keep):
+        self.order, self.groups, self.stages = order, groups, list(stages)
+        self.given = tuple(stages)
+        self.left = [b for b in range(groups.bit_length() - 2, -1, -1) if b != stages[0]]
+        self.keep = keep
+        self.done = []
+        self.go(send)
+
+    def go(self, send):
+        stage = self.stages[0]
+        if stage in ("seq", "gather"):
+            self.flying = lax.ppermute(send, "seq", swap_pairs(2, 1))
+        else:
+            self.flying = lax.ppermute(send, "dp", swap_pairs(self.groups, 1 << stage))
+
+    def split(self, value, stage):
+        if stage == "gather" or (stage == "seq" and len(self.stages) == 1):
+            return value, value
+        if stage == "seq":
+            half = value.shape[-2] // 2
+            return value[..., :half, :], value[..., half:, :]
+        spot = self.left.index(stage)
+        cut = value.reshape((2,) * len(self.left) + value.shape[1:])
+        shape = (-1,) + value.shape[1:]
+        return tuple(
+            lax.index_in_dim(cut, side, spot, keepdims=False).reshape(shape) for side in (0, 1)
+        )
+
+    def step(self):
+        other = self.order.tie(self.flying)
+        self.stages.pop(0)
+        if not self.stages:
+            self.total = added(self.keep, other)
+            if self.total.ndim == 3:
+                self.total = self.total[0]
+            self.order.mark(self.total)
+            return
+        following = self.stages[0]
+        if following == "gather":
+            self.total = added(self.keep, other)[0]
+            self.order.mark(self.total)
+            self.go(self.total)
+            return
+        one, two = self.split(self.keep, following), self.split(other, following)
+        send = added(one[1], two[1])
+        same = following == "seq" and len(self.stages) == 1
+        self.keep = send if same else added(one[0], two[0])
+        if following != "seq":
+            self.left.remove(following)
+        self.order.mark(send)
+        self.go(send)
+
+
+def body_fast(
+    inputs,
+    cotangent,
+    row_counts,
+    response_mask,
+    norm1_gain,
+    norm1_bias,
+    qkv_weight,
+    qv_bias,
+    out_weight,
+    out_bias,
+    norm2_gain,
+    norm2_bias,
+    up_weight,
+    up_bias,
+    down_weight,
+    down_bias,
+):
+    groups = lax.axis_size("dp")
+    pair = swap_pairs(2, 1)
+    core, own, place = (lax.axis_index(a) for a in ("src", "dp", "seq"))
+    at = jnp.stack([core, own, place]).astype(jnp.int32)
+    gain1, bias1, gain2, bias2, out_bias, down_bias, up_bias = (
+        v[None]
+        for v in (norm1_gain, norm1_bias, norm2_gain, norm2_bias, out_bias, down_bias, up_bias)
+    )
+
+    x_both = inputs[0, 0]
+    x_other = lax.ppermute(
+        lax.dynamic_index_in_dim(x_both, 1 - place, 0, keepdims=False), "seq", pair
+    )
+    c_send, c_mine, count = prepare(at, row_counts, cotangent[0, 0], response_mask[0, 0])
+    c_other = lax.ppermute(c_send, "seq", pair)
+
+    order = Order()
+
+    n1, query, keys, values, probs, mixed, middle, n2 = attend(
+        at, x_both, x_other, gain1, bias1, qkv_weight, qv_bias[:, None], out_weight, out_bias, gain2, bias2
+    )
+    active, du_theirs, du_mine, y_mine, y_send, dm, db1, db1_theirs, db2, db2_theirs, vec = feed(
+        at, row_counts, n2, middle, c_mine, c_other, up_weight, up_bias, down_weight, down_bias, gain2, count
+    )
+
+    def from_core(value):
+        return lax.ppermute(value, "src", pair)
+
+    def numbers(stages):
+        return split_numbers(groups, stages[0])
+
+    up_stages, down_stages, qkv_stages, out_stages = STAGES
+    up_parts = grad_rows(
+        at, n2, from_core(n2), du_mine, from_core(du_theirs), *numbers(up_stages), 512, False,
+        halved="gather" in up_stages,
+    )
+    order.mark(up_parts[0])
+    up_sum = Sum(order, groups, up_stages, *up_parts)
+    active_other, db2_other = from_core(active), from_core(db2_theirs)
+    down_parts = []
+    for ids in numbers(down_stages):
+        down_parts.append(
+            grad_lanes(
+                order.tie(at), active, active_other, db2, db2_other, ids, groups,
+                halved="gather" in down_stages,
+            )
+        )
+        order.mark(down_parts[-1])
+    down_sum = Sum(order, groups, down_stages, *down_parts)
+    dp_theirs, dp_mine, x_grad_mine, x_grad_send, vec = back(
+        order.tie(at), x_both, x_other, gain1, query, keys, values, probs, db1, dm, out_weight, qkv_weight, vec, ()
+    )
+    order.mark(vec)
+    out_parts = grad_rows(
+        order.tie(at), mixed, from_core(mixed), db1, from_core(db1_theirs), *numbers(out_stages), 384, True,
+        (vec, from_core(vec)), halved="gather" in out_stages,
+    )
+    order.mark(out_parts[0])
+    out_sum = Sum(order, groups, out_stages, *out_parts)
+    qkv_parts = grad_rows(
+        order.tie(at), n1, from_core(n1), dp_mine, from_core(dp_theirs), *numbers(qkv_stages), 384, False,
+        halved="gather" in qkv_stages,
+    )
+    order.mark(qkv_parts[0])
+    qkv_sum = Sum(order, groups, qkv_stages, *qkv_parts)
+    sums = {"u": up_sum, "d": down_sum, "o": out_sum, "q": qkv_sum}
+    for name in STEPS:
+        sums[name].step()
+
+    rows = out_weight.shape[0] // groups
+    vec = out_sum.total[rows:, :128]
+
+    def joined(done, rows):
+        if "gather" in done.given:
+            parts = [done.total, done.flying]
+            return finish_halves(at, vec, parts + [from_core(p) for p in parts])
+        return finish(at, vec, done.total, from_core(done.total), rows)
+
+    def rows_home(mine, send):
+        other = lax.ppermute(send, "seq", pair)
+        both = jnp.where(place == 0, jnp.stack([mine, other]), jnp.stack([other, mine]))
+        return both[None, None]
+
+    counts, plain, qv, up_small = close(vec, rows, up_bias.shape[1] // groups)
+    return (
+        rows_home(y_mine, y_send),
+        rows_home(x_grad_mine, x_grad_send),
+        counts[0],
+        plain[0],
+        plain[1],
+        joined(qkv_sum, rows),
+        qv,
+        joined(out_sum, rows),
+        plain[4],
+        plain[5],
+        plain[6],
+        joined(up_sum, rows),
+        up_small[0],
+        joined(down_sum, 4 * rows),
+        plain[7],
+    )
+
+
 def solution(mesh):
     placed = (
         P("src", "dp", None, "seq", None),
@@ -327,8 +1194,10 @@
         P(),
         P(),
     )
+    sizes = dict(mesh.shape)
+    paired = sizes["src"] == 2 and sizes["seq"] == 2 and sizes["dp"] == 8
     return jax.shard_map(
-        body,
+        body_fast if paired else body_generic,
         mesh=mesh,
         in_specs=placed,
         out_specs=(

time: 629 us -> 174 us (0.28)
  waiting for transfers between devices: 334 us -> 66.9 us
  blocking collectives: 112 us -> 0 us
  matrix products: 74.9 us -> 0 us
  Pallas kernels: 0 us -> 51.7 us
  other arithmetic: 43.9 us -> 7.83 us
  starting transfers between devices: 0.55 us -> 27.1 us
  local copies, waits for them, and re-layouts: 44.2 us -> 18.2 us
  between operations: 17.6 us -> 1.85 us
    reduce_scatter x6 -> x0, waiting for transfers between devices: 288 us -> none  [the longest x1 98.7 us: body(): lax.psum_scatter(grads[10].astype(jnp.bfloat16), 'dp', scatter_dimension=...]
    ppermute x0 -> x39, waiting for transfers between devices: none -> 66.9 us  [the longest x12 44 us: go(): self.flying = lax.ppermute(send, 'dp', swap_pairs(self.groups, 1 << stage))]
    dot_general x27 -> x0, matrix products: 66.7 us -> none  [the longest x3 7.75 us: attend_backward(): jnp.einsum('rhqk,rqhd->rkhd', probs_low, grad_part, preferred_element_typ...]
    pallas_call x0 -> x14, Pallas kernels: none -> 51.7 us  [the longest x1 11 us: feed(): pl.pallas_call(feed_kernel, grid_spec=pltpu.PrefetchScalarGridSpec(num_sc...]
    psum x2 -> x0, blocking collectives: 47.6 us -> none  [the longest x1 39.6 us: body(): source_counts = lax.psum(picked, ('src', 'dp', 'seq'))]
    psum x1 -> x0, waiting for transfers between devices: 46.1 us -> none  [body(): lax.psum(summed[2].astype(jnp.bfloat16), ('src', 'seq')).astype(jnp.float32)]
    unnamed x1 -> x0, blocking collectives: 38.2 us -> none
    ppermute x0 -> x39, starting transfers between devices: none -> 27.1 us  [the longest x12 12.9 us: go(): self.flying = lax.ppermute(send, 'dp', swap_pairs(self.groups, 1 << stage))]
  transfers between devices with their start and end apart: 8 -> 39, of which waited for: 6 -> 16; matrix products, arithmetic and copies ran while one was open for 11% -> 9% of each run, Pallas kernels for 0% -> 22%
where the time goes in v2:
time: 174 us; the launch traced here: 173 us
  waiting for transfers between devices  66.9 us (38%)
  Pallas kernels  51.7 us (30%)
  starting transfers between devices  27.1 us (16%)
  local copies, waits for them, and re-layouts  18.2 us (10%)
  other arithmetic  7.83 us (4%)
  between operations  1.85 us (1%)
    ppermute x12, waiting for transfers between devices, go(): self.flying = lax.ppermute(send, 'dp', swap_pairs(self.groups, 1 << stage))  44 us
    ppermute x7, waiting for transfers between devices, go(): self.flying = lax.ppermute(send, 'seq', swap_pairs(2, 1))  14.3 us
    ppermute x12, starting transfers between devices, go(): self.flying = lax.ppermute(send, 'dp', swap_pairs(self.groups, 1 << stage))  12.9 us
    pallas_call x1, Pallas kernels, feed(): pl.pallas_call(feed_kernel, grid_spec=pltpu.PrefetchScalarGridSpec(num_sc...  11 us
    pallas_call x1, Pallas kernels, back(): pl.pallas_call(behind(back_kernel, len(after)), grid_spec=pltpu.PrefetchS...  9.72 us
    unnamed x80, local copies, waits for them, and re-layouts  9.67 us
    ppermute x16, waiting for transfers between devices, from_core(): return lax.ppermute(value, 'src', pair)  8.54 us
    pallas_call x3, Pallas kernels, grad_rows(): pl.pallas_call(behind(functools.partial(rows_kernel, count=count, sent=se...  7.15 us
  transfers between devices with their start and end apart: 39, of which 16 were waited for; matrix products, arithmetic and copies ran while one was open for 9% of the time, Pallas kernels for 22%

profile of v2, /device:TPU:0, one launch (start us, length us, event | category | flops | bytes accessed | tf_op | source)
XLA Modules:
  0.0 173.5 jit_solution(1182502243224277173)
XLA Ops:
  1.6 3.0 %collective-permute-start = (bf16[128,768]{1,0:T(8,128)(2,1)S(1)}, bf16[128,768]{1,0:T(8,128)(2,1)S(1)}, u32[]{:S(2)}, u32[]{:S(2)}) collective-permute-start(bf16[128,768]{1,0:T(8,128)(2,1)S(1)} %dynamic-slice_bitcast_fusion), channel_id=1, source_target_pairs={{0,1},{1,0},{2,3},{3,2},{4,5},{5,4},{6,7},{7,6},{8,9},{9,8},{10,11... | collective-permute-start | bytes 589832 | tf_op jit(solution)/shard_map/ppermute | solution.py:1085
  5.9 1.9 %shard_map.272 = (bf16[128,768]{1,0:T(8,128)(2,1)}, bf16[128,768]{1,0:T(8,128)(2,1)}, f32[1,128]{1,0:T(1,128)}) custom-call(s32[3]{0:T(128)} %pad_add_fusion.at_ref, s32[1,1]{1,0:T(1,128)S(6)} %copy.33.rows_ref, bf16[2,128,768]{2,1,0:T(8,128)(2,1)} %bitcast.100, s32[2,128]{1,0:T(2,128)} %bitcast.105), custom_call_target="tpu_custom_call" | custom-call | flops 1 | bytes 1 | tf_op jit(solution)/shard_map/pallas_call | solution.py:401
  13.3 2.0 %copy-done = bf16[768,2304]{1,0:T(8,128)(2,1)S(1)} copy-done((bf16[768,2304]{1,0:T(8,128)(2,1)S(1)}, bf16[768,2304]{1,0:T(8,128)(2,1)}, u32[]{:S(2)}) %copy-start) | copy-done | bytes 3538968
  18.3 6.7 %shard_map.271 = (bf16[256,768]{1,0:T(8,128)(2,1)S(1)}, bf16[256,768]{1,0:T(8,128)(2,1)S(1)}, bf16[256,768]{1,0:T(8,128)(2,1)S(1)}, bf16[256,768]{1,0:T(8,128)(2...) custom-call(s32[3]{0:T(128)S(1)} %copy-done.16, ...), custom_call_target="tpu_custom_call" | custom-call | flops 1 | bytes 1 | tf_op jit(solution)/shard_map/pallas_call | solution.py:468
  25.8 11.0 %shard_map.273 = (bf16[256,3072]{1,0:T(8,128)(2,1)S(1)}, bf16[256,1536]{1,0:T(8,128)(2,1)S(1)}, bf16[256,1536]{1,0:T(8,128)(2,1)S(1)}, bf16[128,768]{1,0:T(8,128...) custom-call(s32[3]{0:T(128)S(1)} %copy-done.16, ...), custom_call_target="tpu_custom_call" | custom-call | flops 1 | bytes 1 | tf_op jit(solution)/shard_map/pallas_call | solution.py:606
  38.0 4.6 %collective-permute-done.3.refs_1_ = bf16[256,768]{1,0:T(8,128)(2,1)S(1)} collective-permute-done((bf16[256,768]{1,0:T(8,128)(2,1)S(1)}, bf16[256,768]{1,0:T(8,128)(2,1)S(1)}, u32[]{:S(2)}, u32[]{:S(2)}) %collective-permute-start.3) | collective-permute-done | bytes 393248 | tf_op jit(solution)/shard_map/ppermute | solution.py:1101
  42.6 2.9 %shard_map.274 = (bf16[4,96,1536]{2,1,0:T(8,128)(2,1)S(1)}, bf16[4,96,1536]{2,1,0:T(8,128)(2,1)S(1)}) custom-call(s32[3]{0:T(128)S(1)} %copy-done.16, bf16[256,768]{1,0:T(8,128)(2,1)S(1)} %get-tuple-element.73.n2_ref.refs_0_, bf16[256,768]{1,0:T(8,128)(2,1)S(1)} %collective-permute-done.3.refs_1_, bf16[256,1536]{1,0:T(8,128)(2,1)S(1)} %get-tuple-element.80.refs_2_, ...), custom_call_target="tpu_custom_call" | custom-call | flops 1 | bytes 1 | tf_op jit(solution)/shard_map/pallas_call | solution.py:847
  45.4 2.2 %collective-permute-start.12 = (bf16[4,96,1536]{2,1,0:T(8,128)(2,1)S(1)}, bf16[4,96,1536]{2,1,0:T(8,128)(2,1)S(1)}, u32[]{:S(2)}, u32[]{:S(2)}) collective-permute-start(bf16[4,96,1536]{2,1,0:T(8,128)(2,1)S(1)} %get-tuple-element.82), channel_id=1, source_target_pairs={{0,4},{2,6},{4,0},{6,2},{8,12},{10,14},{12,8},{14,10},{1,5},{3,7},... | collective-permute-start | bytes 3538952 | tf_op jit(solution)/shard_map/ppermute | solution.py:1017
  49.1 2.6 %shard_map.275 = bf16[4,384,384]{2,1,0:T(8,128)(2,1)S(1)} custom-call(s32[3]{0:T(128)S(1)} %copy-done.16, bf16[256,3072]{1,0:T(8,128)(2,1)S(1)} %get-tuple-element.84.refs_0_, bf16[256,3072]{1,0:T(8,128)(2,1)S(1)} %collective-permute-done.5.refs_1_, bf16[256,768]{1,0:T(8,128)(2,1)S(1)} %get-tuple-element.85.refs_2_, ...), custom_call_target="tpu_custom_call" | custom-call | flops 1 | bytes 1 | tf_op jit(solution)/shard_map/pallas_call | solution.py:779
  51.7 2.6 %shard_map.276 = bf16[4,384,384]{2,1,0:T(8,128)(2,1)S(1)} custom-call(s32[3]{0:T(128)S(1)} %copy-done.16, bf16[256,3072]{1,0:T(8,128)(2,1)S(1)} %get-tuple-element.84.refs_0_, bf16[256,3072]{1,0:T(8,128)(2,1)S(1)} %collective-permute-done.5.refs_1_, bf16[256,768]{1,0:T(8,128)(2,1)S(1)} %get-tuple-element.85.refs_2_, ...), custom_call_target="tpu_custom_call" | custom-call | flops 1 | bytes 1 | tf_op jit(solution)/shard_map/pallas_call | solution.py:779
  54.4 9.7 %shard_map.277 = (bf16[256,1152]{1,0:T(8,128)(2,1)S(1)}, bf16[256,1152]{1,0:T(8,128)(2,1)S(1)}, bf16[128,768]{1,0:T(8,128)(2,1)S(1)}, bf16[128,768]{1,0:T(8,128)(2,1)S(1)}, f32[16,768]{1,0:T(8,128)S(1)}) custom-call(s32[3]{0:T(128)S(1)} %copy-done.16, bf16[2,128,768]{2,1,0:T(8,128)(2,1)S(1)} %bitcast.91, ...), custom_call_target="tpu_custom_call" | custom-call | flops 1 | bytes 1 | tf_op jit(solution)/shard_map/pallas_call | solution.py:726
  66.5 1.5 collective-permute-start.16
  70.5 3.1 %shard_map.279 = (bf16[4,96,1152]{2,1,0:T(8,128)(2,1)S(1)}, bf16[4,96,1152]{2,1,0:T(8,128)(2,1)S(1)}) custom-call(s32[3]{0:T(128)S(1)} %copy-done.16, bf16[256,768]{1,0:T(8,128)(2,1)S(1)} %get-tuple-element.106.refs_0_, bf16[256,768]{1,0:T(8,128)(2,1)S(1)} %collective-permute-done.13.refs_1_, bf16[256,1152]{1,0:T(8,128)(2,1)S(1)} %get-tuple-element.107.refs_2_, ...), custom_call_target="tpu_custom_call" | custom-call | flops 1 | bytes 1 | tf_op jit(solution)/shard_map/pallas_call | solution.py:847
  75.2 1.7 collective-permute-start.15
  77.3 1.7 collective-permute-start.7
  79.0 1.6 collective-permute-start.11
  80.5 14.1 %collective-permute-done.16 = bf16[4,384,384]{2,1,0:T(8,128)(2,1)} collective-permute-done((bf16[4,384,384]{2,1,0:T(8,128)(2,1)S(1)}, bf16[4,384,384]{2,1,0:T(8,128)(2,1)}, u32[]{:S(2)}, u32[]{:S(2)}) %collective-permute-start.16) | collective-permute-done | bytes 1179680 | tf_op jit(solution)/shard_map/ppermute | solution.py:1017
  96.1 1.5 add_convert_fusion
  97.7 1.6 collective-permute-start.20
  101.1 10.9 %collective-permute-done.20 = bf16[4,192,384]{2,1,0:T(8,128)(2,1)S(1)} collective-permute-done((bf16[4,192,384]{2,1,0:T(8,128)(2,1)S(1)}, bf16[4,192,384]{2,1,0:T(8,128)(2,1)S(1)}, u32[]{:S(2)}, u32[]{:S(2)}) %collective-permute-start.20) | collective-permute-done | bytes 589856 | tf_op jit(solution)/shard_map/ppermute | solution.py:1015
  113.0 10.7 %collective-permute-done.19 = bf16[2,48,1536]{2,1,0:T(8,128)(2,1)S(1)} collective-permute-done((bf16[2,48,1536]{2,1,0:T(8,128)(2,1)S(1)}, bf16[2,48,1536]{2,1,0:T(8,128)(2,1)S(1)}, u32[]{:S(2)}, u32[]{:S(2)}) %collective-permute-start.19) | collective-permute-done | bytes 294944 | tf_op jit(solution)/shard_map/ppermute | solution.py:1017
  124.1 1.6 collective-permute-start.22
  127.2 2.6 %collective-permute-start.25 = (bf16[1,48,1536]{2,1,0:T(8,128)(2,1)S(1)}, bf16[1,48,1536]{2,1,0:T(8,128)(2,1)S(1)}, u32[]{:S(2)}, u32[]{:S(2)}) collective-permute-start(bf16[1,48,1536]{2,1,0:T(8,128)(2,1)S(1)} %fusion.5), channel_id=1, source_target_pairs={{0,8},{2,10},{4,12},{6,14},{8,0},{10,2},{12,4},{14,6},{1,9},{3,11}... | collective-permute-start | bytes 442376 | tf_op jit(solution)/shard_map/ppermute | solution.py:1017
  130.7 2.2 %collective-permute-done.22 = bf16[4,48,1152]{2,1,0:T(8,128)(2,1)S(1)} collective-permute-done((bf16[4,48,1152]{2,1,0:T(8,128)(2,1)S(1)}, bf16[4,48,1152]{2,1,0:T(8,128)(2,1)S(1)}, u32[]{:S(2)}, u32[]{:S(2)}) %collective-permute-start.22) | collective-permute-done | bytes 442400 | tf_op jit(solution)/shard_map/ppermute | solution.py:1015
  133.7 2.1 %collective-permute-done.25 = bf16[1,48,1536]{2,1,0:T(8,128)(2,1)S(1)} collective-permute-done((bf16[1,48,1536]{2,1,0:T(8,128)(2,1)S(1)}, bf16[1,48,1536]{2,1,0:T(8,128)(2,1)S(1)}, u32[]{:S(2)}, u32[]{:S(2)}) %collective-permute-start.25) | collective-permute-done | bytes 147488 | tf_op jit(solution)/shard_map/ppermute | solution.py:1017
  136.4 7.0 %collective-permute-done.24 = bf16[2,192,384]{2,1,0:T(8,128)(2,1)S(1)} collective-permute-done((bf16[2,192,384]{2,1,0:T(8,128)(2,1)S(1)}, bf16[2,192,384]{2,1,0:T(8,128)(2,1)S(1)}, u32[]{:S(2)}, u32[]{:S(2)}) %collective-permute-start.24) | collective-permute-done | bytes 294944 | tf_op jit(solution)/shard_map/ppermute | solution.py:1017
  143.6 2.4 %collective-permute-done.23 = bf16[2,48,1152]{2,1,0:T(8,128)(2,1)S(1)} collective-permute-done((bf16[2,48,1152]{2,1,0:T(8,128)(2,1)S(1)}, bf16[2,48,1152]{2,1,0:T(8,128)(2,1)S(1)}, u32[]{:S(2)}, u32[]{:S(2)}) %collective-permute-start.23) | collective-permute-done | bytes 221216 | tf_op jit(solution)/shard_map/ppermute | solution.py:1017
  146.8 6.4 %collective-permute-done.28 = bf16[1,192,384]{2,1,0:T(8,128)(2,1)S(1)} collective-permute-done((bf16[1,192,384]{2,1,0:T(8,128)(2,1)S(1)}, bf16[1,192,384]{2,1,0:T(8,128)(2,1)S(1)}, u32[]{:S(2)}, u32[]{:S(2)}) %collective-permute-start.28) | collective-permute-done | bytes 147488 | tf_op jit(solution)/shard_map/ppermute | solution.py:1017
  161.1 2.3 %shard_map.283 = f32[96,3072]{1,0:T(8,128)} custom-call(s32[3]{0:T(128)} %pad_add_fusion.at_ref, bf16[16,128]{1,0:T(8,128)(2,1)} %slice.238.vec, bf16[48,1536]{1,0:T(8,128)(2,1)} %copy-done.25, bf16[48,1536]{1,0:T(8,128)(2,1)} %copy-done.29, bf16[48,1536]{1,0:T(8,128)(2,1)} %copy-done.30, bf16[48,1536]{1,0:T(8,128)(2,1)} %copy-done.31), custom_call_target="tpu_custom_call" | custom-call | flops 1 | bytes 1 | tf_op jit(solution)/shard_map/pallas_call | solution.py:936
  164.7 1.8 %shard_map.282 = f32[96,768]{1,0:T(8,128)} custom-call(s32[3]{0:T(128)} %pad_add_fusion.at_ref, bf16[16,128]{1,0:T(8,128)(2,1)} %slice.238.vec, bf16[112,384]{1,0:T(8,128)(2,1)} %copy-done.28, bf16[112,384]{1,0:T(8,128)(2,1)} %copy-done.38), custom_call_target="tpu_custom_call" | custom-call | flops 1 | bytes 1 | tf_op jit(solution)/shard_map/pallas_call | solution.py:912
  167.8 2.3 %shard_map.284 = f32[384,768]{1,0:T(8,128)} custom-call(s32[3]{0:T(128)} %pad_add_fusion.at_ref, bf16[16,128]{1,0:T(8,128)(2,1)} %slice.238.vec, bf16[192,384]{1,0:T(8,128)(2,1)} %copy-done.26, bf16[192,384]{1,0:T(8,128)(2,1)} %copy-done.32, bf16[192,384]{1,0:T(8,128)(2,1)} %copy-done.33, bf16[192,384]{1,0:T(8,128)(2,1)} %copy-done.34), custom_call_target="tpu_custom_call" | custom-call | flops 1 | bytes 1 | tf_op jit(solution)/shard_map/pallas_call | solution.py:936
  171.4 2.1 %shard_map.281 = f32[96,2304]{1,0:T(8,128)} custom-call(s32[3]{0:T(128)} %pad_add_fusion.at_ref, bf16[16,128]{1,0:T(8,128)(2,1)} %slice.238.vec, bf16[48,1152]{1,0:T(8,128)(2,1)} %copy-done.27, bf16[48,1152]{1,0:T(8,128)(2,1)} %copy-done.35, bf16[48,1152]{1,0:T(8,128)(2,1)} %copy-done.36, bf16[48,1152]{1,0:T(8,128)(2,1)} %copy-done.37), custom_call_target="tpu_custom_call" | custom-call | flops 1 | bytes 1 | tf_op jit(solution)/shard_map/pallas_call | solution.py:936
  (171 shorter events, 41.4 us)
Async XLA Ops:
  1.6 11.7 %collective-permute-start = (bf16[128,768]{1,0:T(8,128)(2,1)S(1)}, bf16[128,768]{1,0:T(8,128)(2,1)S(1)}, u32[]{:S(2)}, u32[]{:S(2)}) collective-permute-start(bf16[128,768]{1,0:T(8,128)(2,1)S(1)} %dynamic-slice_bitcast_fusion), channel_id=1, source_target_pairs={{0,1},{1,0},{2,3},{3,2},{4,5},{5,4},{6,7},{7,6},{8,9},{9,8},{10,11... | collective-permute-start | bytes 589832 | tf_op jit(solution)/shard_map/ppermute | solution.py:1085
  7.8 18.0 %collective-permute-start.1 = (bf16[128,768]{1,0:T(8,128)(2,1)}, bf16[128,768]{1,0:T(8,128)(2,1)S(1)}, u32[]{:S(2)}, u32[]{:S(2)}) collective-permute-start(bf16[128,768]{1,0:T(8,128)(2,1)} %get-tuple-element.76), channel_id=1, source_target_pairs={{0,1},{1,0},{2,3},{3,2},{4,5},{5,4},{6,7},{7,6},{8,9},{9,8},{10,11... | collective-permute-start | bytes 589832 | tf_op jit(solution)/shard_map/ppermute | solution.py:1089
  37.5 11.6 %collective-permute-start.5 = (bf16[256,3072]{1,0:T(8,128)(2,1)S(1)}, bf16[256,3072]{1,0:T(8,128)(2,1)S(1)}, u32[]{:S(2)}, u32[]{:S(2)}) collective-permute-start(bf16[256,3072]{1,0:T(8,128)(2,1)S(1)} %get-tuple-element.84.refs_0_), channel_id=1, source_target_pairs={{0,16},{16,0},{1,17},{17,1},{2,18},{18,2},{3,19},{19,3},{4,20},{20... | collective-permute-start | bytes 4718600 | tf_op jit(solution)/shard_map/ppermute | solution.py:1101
  45.4 28.4 %collective-permute-start.12 = (bf16[4,96,1536]{2,1,0:T(8,128)(2,1)S(1)}, bf16[4,96,1536]{2,1,0:T(8,128)(2,1)S(1)}, u32[]{:S(2)}, u32[]{:S(2)}) collective-permute-start(bf16[4,96,1536]{2,1,0:T(8,128)(2,1)S(1)} %get-tuple-element.82), channel_id=1, source_target_pairs={{0,4},{2,6},{4,0},{6,2},{8,12},{10,14},{12,8},{14,10},{1,5},{3,7},... | collective-permute-start | bytes 3538952 | tf_op jit(solution)/shard_map/ppermute | solution.py:1017
  64.2 6.3 %collective-permute-start.14 = (bf16[256,1152]{1,0:T(8,128)(2,1)S(1)}, bf16[256,1152]{1,0:T(8,128)(2,1)S(1)}, u32[]{:S(2)}, u32[]{:S(2)}) collective-permute-start(bf16[256,1152]{1,0:T(8,128)(2,1)S(1)} %get-tuple-element.108), channel_id=1, source_target_pairs={{0,16},{16,0},{1,17},{17,1},{2,18},{18,2},{3,19},{19,3},{4,20},{20... | collective-permute-start | bytes 1769480 | tf_op jit(solution)/shard_map/ppermute | solution.py:1101
  64.9 5.6 %collective-permute-start.13 = (bf16[256,768]{1,0:T(8,128)(2,1)S(1)}, bf16[256,768]{1,0:T(8,128)(2,1)S(1)}, u32[]{:S(2)}, u32[]{:S(2)}) collective-permute-start(bf16[256,768]{1,0:T(8,128)(2,1)S(1)} %get-tuple-element.106.refs_0_), channel_id=1, source_target_pairs={{0,16},{16,0},{1,17},{17,1},{2,18},{18,2},{3,19},{19,3},{4,20},{20... | collective-permute-start | bytes 1179656 | tf_op jit(solution)/shard_map/ppermute | solution.py:1101
  66.5 28.1 %collective-permute-start.16 = (bf16[4,384,384]{2,1,0:T(8,128)(2,1)S(1)}, bf16[4,384,384]{2,1,0:T(8,128)(2,1)}, u32[]{:S(2)}, u32[]{:S(2)}) collective-permute-start(bf16[4,384,384]{2,1,0:T(8,128)(2,1)S(1)} %shard_map.275), channel_id=1, source_target_pairs={{0,2},{2,0},{4,6},{6,4},{8,10},{10,8},{12,14},{14,12},{1,3},{3,1},... | collective-permute-start | bytes 3538952 | tf_op jit(solution)/shard_map/ppermute | solution.py:1017
  75.2 22.5 %collective-permute-start.15 = (bf16[4,48,1536]{2,1,0:T(8,128)(2,1)}, bf16[4,48,1536]{2,1,0:T(8,128)(2,1)}, u32[]{:S(2)}, u32[]{:S(2)}) collective-permute-start(bf16[4,48,1536]{2,1,0:T(8,128)(2,1)} %get-tuple-element.134), channel_id=1, source_target_pairs={{0,1},{1,0},{2,3},{3,2},{4,5},{5,4},{6,7},{7,6},{8,9},{9,8},{10,11... | collective-permute-start | bytes 1769480 | tf_op jit(solution)/shard_map/ppermute | solution.py:1015
  76.9 48.7 %collective-permute-start.2 = (bf16[128,768]{1,0:T(8,128)(2,1)}, bf16[128,768]{1,0:T(8,128)(2,1)S(1)}, u32[]{:S(2)}, u32[]{:S(2)}) collective-permute-start(bf16[128,768]{1,0:T(8,128)(2,1)} %copy-done.20), channel_id=1, source_target_pairs={{0,1},{1,0},{2,3},{3,2},{4,5},{5,4},{6,7},{7,6},{8,9},{9,8},{10,11... | collective-permute-start | bytes 589832 | tf_op jit(solution)/shard_map/ppermute | solution.py:1154
  77.3 49.1 %collective-permute-start.7 = (bf16[128,768]{1,0:T(8,128)(2,1)}, bf16[128,768]{1,0:T(8,128)(2,1)S(1)}, u32[]{:S(2)}, u32[]{:S(2)}) collective-permute-start(bf16[128,768]{1,0:T(8,128)(2,1)} %copy-done.21), channel_id=1, source_target_pairs={{0,1},{1,0},{2,3},{3,2},{4,5},{5,4},{6,7},{7,6},{8,9},{9,8},{10,11... | collective-permute-start | bytes 589832 | tf_op jit(solution)/shard_map/ppermute | solution.py:1154
  79.0 21.5 %collective-permute-start.11 = (bf16[4,112,384]{2,1,0:T(8,128)(2,1)}, bf16[4,112,384]{2,1,0:T(8,128)(2,1)S(1)}, u32[]{:S(2)}, u32[]{:S(2)}) collective-permute-start(bf16[4,112,384]{2,1,0:T(8,128)(2,1)} %copy-done.19), channel_id=1, source_target_pairs={{0,4},{2,6},{4,0},{6,2},{8,12},{10,14},{12,8},{14,10},{1,5},{3,7},... | collective-permute-start | bytes 1032200 | tf_op jit(solution)/shard_map/ppermute | solution.py:1017
  94.6 29.2 %collective-permute-start.18 = (bf16[4,96,1152]{2,1,0:T(8,128)(2,1)}, bf16[4,96,1152]{2,1,0:T(8,128)(2,1)S(1)}, u32[]{:S(2)}, u32[]{:S(2)}) collective-permute-start(bf16[4,96,1152]{2,1,0:T(8,128)(2,1)} %copy-done.18), channel_id=1, source_target_pairs={{0,2},{2,0},{4,6},{6,4},{8,10},{10,8},{12,14},{14,12},{1,3},{3,1},... | collective-permute-start | bytes 2654216 | tf_op jit(solution)/shard_map/ppermute | solution.py:1017
  97.7 14.3 %collective-permute-start.20 = (bf16[4,192,384]{2,1,0:T(8,128)(2,1)S(1)}, bf16[4,192,384]{2,1,0:T(8,128)(2,1)S(1)}, u32[]{:S(2)}, u32[]{:S(2)}) collective-permute-start(bf16[4,192,384]{2,1,0:T(8,128)(2,1)S(1)} %get-tuple-element.132), channel_id=1, source_target_pairs={{0,1},{1,0},{2,3},{3,2},{4,5},{5,4},{6,7},{7,6},{8,9},{9,8},{10,11... | collective-permute-start | bytes 1769480 | tf_op jit(solution)/shard_map/ppermute | solution.py:1015
  100.5 23.3 %collective-permute-start.19 = (bf16[2,48,1536]{2,1,0:T(8,128)(2,1)S(1)}, bf16[2,48,1536]{2,1,0:T(8,128)(2,1)S(1)}, u32[]{:S(2)}, u32[]{:S(2)}) collective-permute-start(bf16[2,48,1536]{2,1,0:T(8,128)(2,1)S(1)} %get-tuple-element.140), channel_id=1, source_target_pairs={{0,2},{2,0},{4,6},{6,4},{8,10},{10,8},{12,14},{14,12},{1,3},{3,1},... | collective-permute-start | bytes 884744 | tf_op jit(solution)/shard_map/ppermute | solution.py:1017
  112.0 18.2 %collective-permute-start.17 = (bf16[2,112,384]{2,1,0:T(8,128)(2,1)S(1)}, bf16[2,112,384]{2,1,0:T(8,128)(2,1)S(1)}, u32[]{:S(2)}, u32[]{:S(2)}) collective-permute-start(bf16[2,112,384]{2,1,0:T(8,128)(2,1)S(1)} %get-tuple-element.143), channel_id=1, source_target_pairs={{0,2},{2,0},{4,6},{6,4},{8,10},{10,8},{12,14},{14,12},{1,3},{3,1},... | collective-permute-start | bytes 516104 | tf_op jit(solution)/shard_map/ppermute | solution.py:1017
  124.1 8.8 %collective-permute-start.22 = (bf16[4,48,1152]{2,1,0:T(8,128)(2,1)S(1)}, bf16[4,48,1152]{2,1,0:T(8,128)(2,1)S(1)}, u32[]{:S(2)}, u32[]{:S(2)}) collective-permute-start(bf16[4,48,1152]{2,1,0:T(8,128)(2,1)S(1)} %get-tuple-element.136), channel_id=1, source_target_pairs={{0,1},{1,0},{2,3},{3,2},{4,5},{5,4},{6,7},{7,6},{8,9},{9,8},{10,11... | collective-permute-start | bytes 1327112 | tf_op jit(solution)/shard_map/ppermute | solution.py:1015
  127.2 8.6 %collective-permute-start.25 = (bf16[1,48,1536]{2,1,0:T(8,128)(2,1)S(1)}, bf16[1,48,1536]{2,1,0:T(8,128)(2,1)S(1)}, u32[]{:S(2)}, u32[]{:S(2)}) collective-permute-start(bf16[1,48,1536]{2,1,0:T(8,128)(2,1)S(1)} %fusion.5), channel_id=1, source_target_pairs={{0,8},{2,10},{4,12},{6,14},{8,0},{10,2},{12,4},{14,6},{1,9},{3,11}... | collective-permute-start | bytes 442376 | tf_op jit(solution)/shard_map/ppermute | solution.py:1017
  129.8 13.6 %collective-permute-start.24 = (bf16[2,192,384]{2,1,0:T(8,128)(2,1)S(1)}, bf16[2,192,384]{2,1,0:T(8,128)(2,1)S(1)}, u32[]{:S(2)}, u32[]{:S(2)}) collective-permute-start(bf16[2,192,384]{2,1,0:T(8,128)(2,1)S(1)} %get-tuple-element.138), channel_id=1, source_target_pairs={{0,4},{2,6},{4,0},{6,2},{8,12},{10,14},{12,8},{14,10},{1,5},{3,7},... | collective-permute-start | bytes 884744 | tf_op jit(solution)/shard_map/ppermute | solution.py:1017
  130.3 16.3 %collective-permute-start.21 = (bf16[1,112,384]{2,1,0:T(8,128)(2,1)S(1)}, bf16[1,112,384]{2,1,0:T(8,128)(2,1)S(1)}, u32[]{:S(2)}, u32[]{:S(2)}) collective-permute-start(bf16[1,112,384]{2,1,0:T(8,128)(2,1)S(1)} %fusion.10), channel_id=1, source_target_pairs={{0,8},{2,10},{4,12},{6,14},{8,0},{10,2},{12,4},{14,6},{1,9},{3,11}... | collective-permute-start | bytes 258056 | tf_op jit(solution)/shard_map/ppermute | solution.py:1017
  133.0 13.1 %collective-permute-start.23 = (bf16[2,48,1152]{2,1,0:T(8,128)(2,1)S(1)}, bf16[2,48,1152]{2,1,0:T(8,128)(2,1)S(1)}, u32[]{:S(2)}, u32[]{:S(2)}) collective-permute-start(bf16[2,48,1152]{2,1,0:T(8,128)(2,1)S(1)} %get-tuple-element.141), channel_id=1, source_target_pairs={{0,4},{2,6},{4,0},{6,2},{8,12},{10,14},{12,8},{14,10},{1,5},{3,7},... | collective-permute-start | bytes 663560 | tf_op jit(solution)/shard_map/ppermute | solution.py:1017
  135.9 7.6 %collective-permute-start.33 = (bf16[48,1536]{1,0:T(8,128)(2,1)S(1)}, bf16[48,1536]{1,0:T(8,128)(2,1)S(1)}, u32[]{:S(2)}, u32[]{:S(2)}) collective-permute-start(bf16[48,1536]{1,0:T(8,128)(2,1)S(1)} %fusion.12.refs_0_), channel_id=1, source_target_pairs={{0,1},{1,0},{2,3},{3,2},{4,5},{5,4},{6,7},{7,6},{8,9},{9,8},{10,11... | collective-permute-start | bytes 442376 | tf_op jit(solution)/shard_map/ppermute | solution.py:1015
  136.4 21.2 %collective-permute-start.34 = (bf16[48,1536]{1,0:T(8,128)(2,1)S(1)}, bf16[48,1536]{1,0:T(8,128)(2,1)S(1)}, u32[]{:S(2)}, u32[]{:S(2)}) collective-permute-start(bf16[48,1536]{1,0:T(8,128)(2,1)S(1)} %fusion.12.refs_0_), channel_id=1, source_target_pairs={{0,16},{16,0},{1,17},{17,1},{2,18},{18,2},{3,19},{19,3},{4,20},{20... | collective-permute-start | bytes 442376 | tf_op jit(solution)/shard_map/ppermute | solution.py:1101
  143.4 9.7 %collective-permute-start.28 = (bf16[1,192,384]{2,1,0:T(8,128)(2,1)S(1)}, bf16[1,192,384]{2,1,0:T(8,128)(2,1)S(1)}, u32[]{:S(2)}, u32[]{:S(2)}) collective-permute-start(bf16[1,192,384]{2,1,0:T(8,128)(2,1)S(1)} %fusion.4), channel_id=1, source_target_pairs={{0,8},{2,10},{4,12},{6,14},{8,0},{10,2},{12,4},{14,6},{1,9},{3,11}... | collective-permute-start | bytes 442376 | tf_op jit(solution)/shard_map/ppermute | solution.py:1017
  143.5 14.6 %collective-permute-start.35 = (bf16[48,1536]{1,0:T(8,128)(2,1)S(1)}, bf16[48,1536]{1,0:T(8,128)(2,1)S(1)}, u32[]{:S(2)}, u32[]{:S(2)}) collective-permute-start(bf16[48,1536]{1,0:T(8,128)(2,1)S(1)} %collective-permute-done.33.refs_1_), channel_id=1, source_target_pairs={{0,16},{16,0},{1,17},{17,1},{2,18},{18,2},{3,19},{19,3},{4,20},{20... | collective-permute-start | bytes 442376 | tf_op jit(solution)/shard_map/ppermute | solution.py:1101
  146.1 8.3 %collective-permute-start.27 = (bf16[1,48,1152]{2,1,0:T(8,128)(2,1)S(1)}, bf16[1,48,1152]{2,1,0:T(8,128)(2,1)S(1)}, u32[]{:S(2)}, u32[]{:S(2)}) collective-permute-start(bf16[1,48,1152]{2,1,0:T(8,128)(2,1)S(1)} %fusion.8), channel_id=1, source_target_pairs={{0,8},{2,10},{4,12},{6,14},{8,0},{10,2},{12,4},{14,6},{1,9},{3,11}... | collective-permute-start | bytes 331784 | tf_op jit(solution)/shard_map/ppermute | solution.py:1017
  146.6 8.9 %collective-permute-start.26 = (bf16[1,112,384]{2,1,0:T(8,128)(2,1)S(1)}, bf16[1,112,384]{2,1,0:T(8,128)(2,1)S(1)}, u32[]{:S(2)}, u32[]{:S(2)}) collective-permute-start(bf16[1,112,384]{2,1,0:T(8,128)(2,1)S(1)} %add_convert_fusion.18), channel_id=1, source_target_pairs={{0,1},{1,0},{2,3},{3,2},{4,5},{5,4},{6,7},{7,6},{8,9},{9,8},{10,11... | collective-permute-start | bytes 258056 | tf_op jit(solution)/shard_map/ppermute | solution.py:1015
  154.4 5.2 %collective-permute-start.29 = (bf16[48,1152]{1,0:T(8,128)(2,1)S(1)}, bf16[48,1152]{1,0:T(8,128)(2,1)S(1)}, u32[]{:S(2)}, u32[]{:S(2)}) collective-permute-start(bf16[48,1152]{1,0:T(8,128)(2,1)S(1)} %fusion.14.refs_0_), channel_id=1, source_target_pairs={{0,1},{1,0},{2,3},{3,2},{4,5},{5,4},{6,7},{7,6},{8,9},{9,8},{10,11... | collective-permute-start | bytes 331784 | tf_op jit(solution)/shard_map/ppermute | solution.py:1015
  156.1 10.3 %collective-permute-start.37 = (bf16[192,384]{1,0:T(8,128)(2,1)S(1)}, bf16[192,384]{1,0:T(8,128)(2,1)S(1)}, u32[]{:S(2)}, u32[]{:S(2)}) collective-permute-start(bf16[192,384]{1,0:T(8,128)(2,1)S(1)} %fusion.13.refs_0_), channel_id=1, source_target_pairs={{0,16},{16,0},{1,17},{17,1},{2,18},{18,2},{3,19},{19,3},{4,20},{20... | collective-permute-start | bytes 442376 | tf_op jit(solution)/shard_map/ppermute | solution.py:1101
  157.5 6.5 %collective-permute-start.32 = (bf16[112,384]{1,0:T(8,128)(2,1)S(1)}, bf16[112,384]{1,0:T(8,128)(2,1)S(1)}, u32[]{:S(2)}, u32[]{:S(2)}) collective-permute-start(bf16[112,384]{1,0:T(8,128)(2,1)S(1)} %fusion.15.mine), channel_id=1, source_target_pairs={{0,16},{16,0},{1,17},{17,1},{2,18},{18,2},{3,19},{19,3},{4,20},{20... | collective-permute-start | bytes 258056 | tf_op jit(solution)/shard_map/ppermute | solution.py:1101
  158.1 12.0 %collective-permute-start.30 = (bf16[48,1152]{1,0:T(8,128)(2,1)S(1)}, bf16[48,1152]{1,0:T(8,128)(2,1)S(1)}, u32[]{:S(2)}, u32[]{:S(2)}) collective-permute-start(bf16[48,1152]{1,0:T(8,128)(2,1)S(1)} %fusion.14.refs_0_), channel_id=1, source_target_pairs={{0,16},{16,0},{1,17},{17,1},{2,18},{18,2},{3,19},{19,3},{4,20},{20... | collective-permute-start | bytes 331784 | tf_op jit(solution)/shard_map/ppermute | solution.py:1101
  158.4 8.0 %collective-permute-start.38 = (bf16[192,384]{1,0:T(8,128)(2,1)S(1)}, bf16[192,384]{1,0:T(8,128)(2,1)S(1)}, u32[]{:S(2)}, u32[]{:S(2)}) collective-permute-start(bf16[192,384]{1,0:T(8,128)(2,1)S(1)} %collective-permute-done.36.refs_1_), channel_id=1, source_target_pairs={{0,16},{16,0},{1,17},{17,1},{2,18},{18,2},{3,19},{19,3},{4,20},{20... | collective-permute-start | bytes 442376 | tf_op jit(solution)/shard_map/ppermute | solution.py:1101
  159.6 10.5 %collective-permute-start.31 = (bf16[48,1152]{1,0:T(8,128)(2,1)S(1)}, bf16[48,1152]{1,0:T(8,128)(2,1)S(1)}, u32[]{:S(2)}, u32[]{:S(2)}) collective-permute-start(bf16[48,1152]{1,0:T(8,128)(2,1)S(1)} %collective-permute-done.29.refs_1_), channel_id=1, source_target_pairs={{0,16},{16,0},{1,17},{17,1},{2,18},{18,2},{3,19},{19,3},{4,20},{20... | collective-permute-start | bytes 331784 | tf_op jit(solution)/shard_map/ppermute | solution.py:1101
  (47 other events, 269.9 us)

commit v3 on v0

--- a/solution.py
+++ b/solution.py
@@ -4,6 +4,8 @@
 import jax
 import jax.numpy as jnp
 from jax import lax
+from jax.experimental import pallas as pl
+from jax.experimental.pallas import tpu as pltpu
 from jax.sharding import PartitionSpec as P
 
 H = 12
@@ -65,7 +67,7 @@
     return (grad_query, grad_keys, grad_values)
 
 
-def body(
+def body_generic(
     inputs,
     cotangent,
     row_counts,
@@ -308,6 +310,845 @@
     )
 
 
+WAYS = {
+    "u": ("x12y", "12xy"),
+    "d": ("yx12", "1yx2"),
+    "o": ("yx12", "y12x"),
+    "q": ("yx12", "xy12"),
+}
+EVENTS = "UDCIuQOdoqdouqYduoqudoqodouqioyuqd"
+BITS = {"y": 1, "1": 2, "2": 4}
+
+
+COSTS = {"prepare": 2, "load": 4, "attend": 8, "feed_one": 5, "feed_two": 5, "back": 0, "input": 0, "lanes": 4, "rows": 4, "result": 0}
+AXES = ("src", "dp", "seq")
+SINGLE = jnp.float32
+LOW = jnp.bfloat16
+GROUP = 4
+GW = GROUP * HD
+DIGITS = 16
+
+
+def dot_nt(left, right):
+    return lax.dot_general(left, right, (((1,), (1,)), ((), ())), preferred_element_type=SINGLE)
+
+
+def dot_tn(left, right):
+    return lax.dot_general(left, right, (((0,), (0,)), ((), ())), preferred_element_type=SINGLE)
+
+
+def dot_nn(left, right):
+    return jnp.dot(left, right, preferred_element_type=SINGLE)
+
+
+def normalize(values):
+    centered = values - jnp.mean(values, axis=-1, keepdims=True)
+    inverse = lax.rsqrt(jnp.mean(centered * centered, axis=-1, keepdims=True) + EPS)
+    return centered * inverse, inverse
+
+
+def norm_back(normal, inverse, grad, gain):
+    scaled = grad * gain
+    return inverse * (
+        scaled
+        - jnp.mean(scaled, axis=-1, keepdims=True)
+        - normal * jnp.mean(scaled * normal, axis=-1, keepdims=True)
+    )
+
+
+def head_mask(head):
+    lanes = lax.broadcasted_iota(jnp.int32, (1, GW), 1)
+    return (lanes >= head * HD) & (lanes < (head + 1) * HD)
+
+
+def rows_at(first, count):
+    return pl.ds(pl.multiple_of(first, count), count)
+
+
+def where_am_i():
+    return tuple(lax.axis_index(axis) for axis in AXES)
+
+
+def call(name, kernel, operands, outs, scratch=(), loaded=()):
+    vmem = pl.BlockSpec(memory_space=pltpu.VMEM)
+    return pl.pallas_call(
+        kernel,
+        in_specs=[pl.BlockSpec(memory_space=pl.ANY)] * len(loaded) + [vmem] * len(operands),
+        out_specs=[vmem] * (len(loaded) + len(outs)),
+        out_shape=[jax.ShapeDtypeStruct(v.shape, v.dtype) for v in loaded]
+        + [jax.ShapeDtypeStruct(*o) for o in outs],
+        scratch_shapes=[pltpu.VMEM(*s) for s in scratch]
+        + [pltpu.SemaphoreType.DMA((len(loaded),))] * bool(loaded),
+        compiler_params=pltpu.CompilerParams(vmem_limit_bytes=16 << 20),
+        cost_estimate=pl.CostEstimate(
+            flops=int(COSTS[name] * 10**9) + 1, bytes_accessed=1, transcendentals=0
+        ),
+    )(*in_hbm(loaded), *operands)
+
+
+def prepare_kernel(*refs):
+    rows_ref, ins, refs = refs[0], refs[1:14], refs[14:]
+    x_mine, c_send, c_mine, count_ref, small, wqkv, wo = refs[:7]
+    held, sems = refs[7:18], refs[18]
+    core, _, place = where_am_i()
+    copies = [
+        pltpu.make_async_copy(source, target, sems.at[i])
+        for i, (source, target) in enumerate(zip(ins, held + (wqkv, wo)))
+    ]
+    for copy in copies:
+        copy.start()
+    for copy in copies[:11]:
+        copy.wait()
+    (
+        mask_ref, x_ref, cot_ref, gain1, bias1, qv_bias, out_bias, gain2, bias2, down_bias, up_bias,
+    ) = held
+    piece = mask_ref.shape[1]
+    diagonal = lax.broadcasted_iota(jnp.int32, (piece, piece), 0) == lax.broadcasted_iota(
+        jnp.int32, (piece, piece), 1
+    )
+    rows = rows_ref[0, 0]
+
+    def column(row):
+        kept = mask_ref[pl.ds(row, 1), :].astype(SINGLE) * (row < rows).astype(SINGLE)
+        return jnp.sum(jnp.where(diagonal, kept, 0.0), axis=1, keepdims=True), kept
+
+    weight_send, kept_send = column(1 - place)
+    c_send[...] = (cot_ref[1 - place].astype(SINGLE) * weight_send).astype(LOW)
+    weight_mine, kept_mine = column(place)
+    c_mine[...] = (cot_ref[place].astype(SINGLE) * weight_mine).astype(LOW)
+    x_mine[...] = x_ref[place]
+    count = jnp.sum(kept_mine + kept_send, axis=1, keepdims=True).astype(jnp.int32)
+    lane = lax.broadcasted_iota(jnp.int32, count_ref.shape, 1) - core * DIGITS
+    digit = lax.shift_right_logical(
+        jnp.broadcast_to(count, count_ref.shape), jnp.clip(lane, 0, DIGITS - 1)
+    )
+    count_ref[...] = jnp.where((lane >= 0) & (lane < DIGITS), digit & 1, 0).astype(SINGLE)
+    features = small.shape[1]
+    small[12:16, :] = jnp.broadcast_to((place < rows).astype(SINGLE), (4, features))
+    small[2:4, :] = qv_bias[...].astype(SINGLE)
+    for line, value in ((0, gain1), (1, bias1), (4, out_bias), (5, gain2), (6, bias2), (7, down_bias)):
+        small[line : line + 1, :] = value[...].astype(SINGLE)[None, :]
+    ups = up_bias[...].astype(SINGLE)[None, :]
+    for part in range(ups.shape[1] // features):
+        small[8 + part : 9 + part, :] = ups[:, part * features : (part + 1) * features]
+    for copy in copies[11:]:
+        copy.wait()
+
+
+def in_hbm(values):
+    return [pltpu.with_memory_space_constraint(value, pltpu.HBM) for value in values]
+
+
+def prepare(rows, mask, x, cot, vectors, weights):
+    piece, features = cot.shape[1:]
+    part = jax.ShapeDtypeStruct((piece, features), LOW)
+    vmem = pl.BlockSpec(memory_space=pltpu.VMEM)
+    held = (mask, x, cot, *vectors)
+    return pl.pallas_call(
+        prepare_kernel,
+        in_specs=[pl.BlockSpec(memory_space=pltpu.SMEM)] + [pl.BlockSpec(memory_space=pl.ANY)] * 13,
+        out_specs=[vmem] * 7,
+        out_shape=[
+            part,
+            part,
+            part,
+            jax.ShapeDtypeStruct((1, 128), SINGLE),
+            jax.ShapeDtypeStruct((16, features), SINGLE),
+        ]
+        + [jax.ShapeDtypeStruct(w.shape, w.dtype) for w in weights],
+        scratch_shapes=[pltpu.VMEM(v.shape, v.dtype) for v in held]
+        + [pltpu.SemaphoreType.DMA((13,))],
+        compiler_params=pltpu.CompilerParams(vmem_limit_bytes=8 << 20),
+        cost_estimate=pl.CostEstimate(flops=2 * 10**9, bytes_accessed=1, transcendentals=0),
+    )(rows, *in_hbm(held), *in_hbm(weights))
+
+
+def join_row(place, mine_ref, other_ref, row_ref):
+    piece = mine_ref.shape[0]
+    row_ref[rows_at(place * piece, piece), :] = mine_ref[...].astype(row_ref.dtype)
+    row_ref[rows_at((1 - place) * piece, piece), :] = other_ref[...].astype(row_ref.dtype)
+
+
+def attend_kernel(
+    up_ref, down_ref, x_mine, x_other, small, wqkv, wo,
+    up, down, n1, qkv, probs, mixed_low, middle, n2, sems,
+):
+    _, _, place = where_am_i()
+    copies = [
+        pltpu.make_async_copy(up_ref, up, sems.at[0]),
+        pltpu.make_async_copy(down_ref, down, sems.at[1]),
+    ]
+    for copy in copies:
+        copy.start()
+    length, features = n1.shape
+    groups = features // GW
+    join_row(place, x_mine, x_other, middle)
+    normal, _ = normalize(middle[...])
+    n1[...] = (normal * small[0:1, :] + small[1:2, :]).astype(LOW)
+    for which in range(3):
+        value = dot_nn(n1[...], wqkv[:, which * features : (which + 1) * features])
+        if which != 1:
+            line = 2 + which // 2
+            value = value + small[line : line + 1, :]
+        value = value.astype(LOW)
+        for group in range(groups):
+            qkv[which * groups + group] = value[:, group * GW : (group + 1) * GW]
+    allowed = lax.broadcasted_iota(jnp.int32, (length, length), 0) >= lax.broadcasted_iota(
+        jnp.int32, (length, length), 1
+    )
+
+    def one_group(group, carry):
+        query, keys, values = (qkv[which * groups + group] for which in range(3))
+        scaled = query * HD**-0.5
+        mixed = None
+        for head in range(GROUP):
+            mask = head_mask(head)
+            scores = dot_nt(jnp.where(mask, scaled, 0), keys)
+            scores = jnp.where(allowed, scores, NEGATIVE)
+            powers = jnp.exp(scores - jnp.max(scores, axis=-1, keepdims=True))
+            low = (powers * (1.0 / jnp.sum(powers, axis=-1, keepdims=True))).astype(LOW)
+            probs[group * GROUP + head] = low
+            part = dot_nn(low, values)
+            mixed = part if head == 0 else jnp.where(mask, part, mixed)
+        mixed_low[:, rows_at(group * GW, GW)] = mixed.astype(LOW)
+        return carry
+
+    lax.fori_loop(0, groups, one_group, 0)
+    middle[...] += dot_nn(mixed_low[...], wo[...]) + small[4:5, :]
+    normal, _ = normalize(middle[...])
+    n2[...] = (normal * small[5:6, :] + small[6:7, :]).astype(LOW)
+    for copy in copies:
+        copy.wait()
+
+
+def attend(x_mine, x_other, small, qkv_weight, out_weight, up_weight, down_weight):
+    piece, features = x_other.shape
+    length = 2 * piece
+    groups = features // GW
+    act = ((length, features), LOW)
+    return call(
+        "attend",
+        attend_kernel,
+        (x_mine, x_other, small, qkv_weight, out_weight),
+        [
+            act,
+            ((3 * groups, length, GW), LOW),
+            ((groups * GROUP, length, length), LOW),
+            act,
+            ((length, features), SINGLE),
+            act,
+        ],
+        loaded=(up_weight, down_weight),
+    )
+
+
+def gelu_and_slope(u):
+    c = math.sqrt(2 / math.pi)
+    square = u * u
+    bent = jnp.tanh(u * (c + (c * 0.044715) * square))
+    half = 0.5 + 0.5 * bent
+    slope = half + u * (0.5 - 0.5 * bent * bent) * (c + (3 * c * 0.044715) * square)
+    return u * half, slope
+
+
+def feed_tiles(side, n2, db2, small, up, down, g, du, vec, total):
+    tiles, _, features = g.shape
+
+    def one_tile(tile, carry):
+        number = side * tiles + tile
+        cut = rows_at(number * features, features)
+        line = pl.ds(8 + number, 1)
+        hidden = dot_nn(n2[...], up[:, cut]) + small[line, :]
+        active, slope = gelu_and_slope(hidden)
+        g[tile] = active.astype(LOW)
+        grad = (dot_nt(db2[...], down[cut, :]) * slope).astype(LOW)
+        du[tile] = grad
+        vec[line, :] = jnp.sum(grad.astype(SINGLE), axis=0, keepdims=True)
+        total[...] += dot_nt(grad, up[:, cut])
+        return carry
+
+    lax.fori_loop(0, tiles, one_tile, 0)
+
+
+def feed_one_kernel(
+    n2, c_mine, c_other, small, count, up, down, g, du, db2, theirs, dn, vec,
+):
+    core, _, place = where_am_i()
+    half = theirs.shape[1]
+    join_row(place, c_mine, c_other, db2)
+    theirs[...] = db2[:, rows_at((1 - core) * half, half)]
+    vec[...] = jnp.zeros_like(vec)
+    vec[7:8, :] = jnp.sum(db2[...].astype(SINGLE), axis=0, keepdims=True)
+    vec[12:13, 0:128] = count[...]
+    dn[...] = jnp.zeros_like(dn)
+    feed_tiles(1 - core, n2, db2, small, up, down, g, du, vec, dn)
+
+
+def feed_one(n2, c_mine, c_other, small, count, up, down):
+    length, features = n2.shape
+    tiles = up.shape[1] // 2 // features
+    hid = ((tiles, length, features), LOW)
+    return call(
+        "feed_one",
+        feed_one_kernel,
+        (n2, c_mine, c_other, small, count, up, down),
+        [
+            hid, hid, ((length, features), LOW), ((length, features // 2), LOW),
+            ((length, features), SINGLE), ((16, features), SINGLE),
+        ],
+    )
+
+
+def feed_two_kernel(
+    n2, db2, small, up, down, middle, dn, vec_in, g, du, dm, db1, theirs, vec,
+):
+    core, _, _ = where_am_i()
+    half = theirs.shape[1]
+    vec[...] = vec_in[...]
+    dm[...] = dn[...]
+    feed_tiles(core, n2, db2, small, up, down, g, du, vec, dm)
+    grad_n = dm[...]
+    normal, inverse = normalize(middle[...])
+    vec[5:6, :] = jnp.sum(grad_n * normal, axis=0, keepdims=True)
+    vec[6:7, :] = jnp.sum(grad_n, axis=0, keepdims=True)
+    grad = db2[...].astype(SINGLE) + norm_back(normal, inverse, grad_n, small[5:6, :])
+    dm[...] = grad
+    low = grad.astype(LOW)
+    db1[...] = low
+    theirs[...] = db1[:, rows_at((1 - core) * half, half)]
+    vec[4:5, :] = jnp.sum(low.astype(SINGLE), axis=0, keepdims=True)
+
+
+def feed_two(n2, db2, small, up, down, middle, dn, vec_in):
+    length, features = n2.shape
+    tiles = up.shape[1] // 2 // features
+    hid = ((tiles, length, features), LOW)
+    return call(
+        "feed_two",
+        feed_two_kernel,
+        (n2, db2, small, up, down, middle, dn, vec_in),
+        [
+            hid, hid, ((length, features), SINGLE), ((length, features), LOW),
+            ((length, features // 2), LOW), ((16, features), SINGLE),
+        ],
+    )
+
+
+def result_kernel(g_mine, g_theirs, middle, small, down, y_mine, y_send, total):
+    core, _, place = where_am_i()
+    tiles, _, features = g_mine.shape
+    piece = y_mine.shape[0]
+    total[...] = middle[...] + small[7:8, :]
+
+    def one_tile(tile, carry):
+        for side, active in ((core, g_mine), (1 - core, g_theirs)):
+            cut = rows_at((side * tiles + tile) * features, features)
+            total[...] += dot_nn(active[tile], down[cut, :])
+        return carry
+
+    lax.fori_loop(0, tiles, one_tile, 0)
+    present = small[12:13, :]
+    y_mine[...] = (total[rows_at(place * piece, piece), :] * present).astype(LOW)
+    y_send[...] = (total[rows_at((1 - place) * piece, piece), :] * present).astype(LOW)
+
+
+def result(g_mine, g_theirs, middle, small, down):
+    length, features = middle.shape
+    part = ((length // 2, features), LOW)
+    return call(
+        "result",
+        result_kernel,
+        (g_mine, g_theirs, middle, small, down),
+        [part, part],
+        [((length, features), SINGLE)],
+    )
+
+
+def back_kernel(qkv, probs, db1, wo, vec_in, theirs, mine, vec, dp):
+    core, _, _ = where_am_i()
+    features = db1.shape[1]
+    groups = features // GW
+    vec[...] = vec_in[...]
+
+    def one_group(group, carry):
+        cut = rows_at(group * GW, GW)
+        grad_mixed = dot_nt(db1[...], wo[cut, :]).astype(LOW)
+        query, keys, values = (qkv[which * groups + group] for which in range(3))
+        query = query * HD**-0.5
+        keys = keys * HD**-0.5
+        dq = dk = dv = None
+        for head in range(GROUP):
+            mask = head_mask(head)
+            grad_head = jnp.where(mask, grad_mixed, 0)
+            probs_low = probs[group * GROUP + head]
+            weights = probs_low.astype(SINGLE)
+            grad_probs = dot_nt(grad_head, values)
+            inner = jnp.sum(weights * grad_probs, axis=-1, keepdims=True)
+            grad_scores = (weights * (grad_probs - inner)).astype(LOW)
+            part = dot_nn(grad_scores, keys)
+            dq = part if head == 0 else jnp.where(mask, part, dq)
+            part = dot_tn(grad_scores, query)
+            dk = part if head == 0 else jnp.where(mask, part, dk)
+            part = dot_tn(probs_low, grad_mixed)
+            dv = part if head == 0 else jnp.where(mask, part, dv)
+        for which, value in enumerate((dq, dk, dv)):
+            low = value.astype(LOW)
+            dp[:, rows_at(which * features + group * GW, GW)] = low
+            if which != 1:
+                line = 2 + which // 2
+                vec[line : line + 1, cut] = jnp.sum(low.astype(SINGLE), axis=0, keepdims=True)
+        return carry
+
+    lax.fori_loop(0, groups, one_group, 0)
+    half = mine.shape[1]
+    theirs[...] = dp[:, rows_at((1 - core) * half, half)]
+    mine[...] = dp[:, rows_at(core * half, half)]
+
+
+def back(qkv, probs, db1, out_weight, vec_in):
+    length, features = db1.shape
+    half = ((length, 3 * features // 2), LOW)
+    return call(
+        "back",
+        back_kernel,
+        (qkv, probs, db1, out_weight, vec_in),
+        [half, half, ((16, features), SINGLE)],
+        [((length, 3 * features), LOW)],
+    )
+
+
+def input_kernel(
+    x_mine, x_other, small, dp_mine, dp_theirs, wqkv, dm, vec_in, mine, send, vec, row,
+):
+    core, _, place = where_am_i()
+    half = dp_mine.shape[1]
+    piece = mine.shape[0]
+    grad_n = dot_nt(dp_mine[...], wqkv[:, rows_at(core * half, half)])
+    grad_n = grad_n + dot_nt(dp_theirs[...], wqkv[:, rows_at((1 - core) * half, half)])
+    join_row(place, x_mine, x_other, row)
+    normal, inverse = normalize(row[...])
+    vec[...] = vec_in[...]
+    vec[0:1, :] = jnp.sum(grad_n * normal, axis=0, keepdims=True)
+    vec[1:2, :] = jnp.sum(grad_n, axis=0, keepdims=True)
+    row[...] = dm[...] + norm_back(normal, inverse, grad_n, small[0:1, :])
+    mine[...] = row[rows_at(place * piece, piece), :].astype(LOW)
+    send[...] = row[rows_at((1 - place) * piece, piece), :].astype(LOW)
+
+
+def input_gradient(x_mine, x_other, small, dp_mine, dp_theirs, qkv_weight, dm, vec_in):
+    piece, features = x_other.shape
+    part = ((piece, features), LOW)
+    return call(
+        "input",
+        input_kernel,
+        (x_mine, x_other, small, dp_mine, dp_theirs, qkv_weight, dm, vec_in),
+        [part, part, ((16, features), SINGLE)],
+        [((2 * piece, features), SINGLE)],
+    )
+
+
+UNITS = 16
+
+
+def unit_of(name, number):
+    core, own, place = where_am_i()
+    units = []
+    for order in WAYS[name]:
+        unit = 0
+        for stage, axis in enumerate(order):
+            if number >> (3 - stage) & 1:
+                unit |= 1 if axis == "x" else BITS[axis] << 1
+        units.append(unit)
+    return jnp.where(core == 0, units[0], units[1]) ^ (own * 2 + place)
+
+
+def lanes_kernel(
+    g_mine, g_theirs, other_mine, other_theirs, right, right_other, send, keep, turned, whole, *, name
+):
+    core, _, _ = where_am_i()
+    chunks, tall, wide = whole.shape
+    tiles, length, features = g_mine.shape
+    per_tile = features // wide
+    half = tall // 2
+    turned[:, :length] = right[:, rows_at(core * tall, tall)].T
+    turned[:, length:] = right_other[...].T
+    for side, one, two in ((core, g_mine, other_theirs), (1 - core, g_theirs, other_mine)):
+
+        def one_tile(tile, carry, side=side, one=one, two=two):
+            total = dot_nn(turned[:, :length], one[tile]) + dot_nn(turned[:, length:], two[tile])
+            total = total.astype(LOW)
+            for chunk in range(per_tile):
+                whole[(side * tiles + tile) * per_tile + chunk] = total[:, chunk * wide : (chunk + 1) * wide]
+            return carry
+
+        lax.fori_loop(0, tiles, one_tile, 0)
+    for number in range(UNITS):
+        unit = unit_of(name, number)
+        out = send if number >= UNITS // 2 else keep
+        out[number % (UNITS // 2)] = whole[lax.div(unit, 2), rows_at(lax.rem(unit, 2) * half, half), :]
+
+
+def grad_lanes(name, mine, theirs, other_mine, other_theirs, right, right_other):
+    tiles, length, features = mine.shape
+    tall = right_other.shape[1]
+    chunks = UNITS // 2
+    wide = 2 * tiles * features // chunks
+    unit = ((UNITS // 2, tall // 2, wide), LOW)
+    return call(
+        "lanes",
+        functools.partial(lanes_kernel, name=name),
+        (mine, theirs, other_mine, other_theirs, right, right_other),
+        [unit, unit],
+        [((tall, 2 * length), LOW), ((chunks, tall, wide), LOW)],
+    )
+
+
+def rows_kernel(left, left_other, right, right_other, *rest, name, pick_core):
+    if len(rest) > 4:
+        vec, vec_other, send, keep, turned, whole, spread = rest
+    else:
+        send, keep, turned, whole = rest
+        vec = None
+    core, _, _ = where_am_i()
+    length = left.shape[0]
+    split = len(right_other.shape) == 2
+    tiles, tile = (1, right_other.shape[1]) if split else (right_other.shape[0], right_other.shape[2])
+    turned[:, :length] = left[...].T
+    turned[:, length:] = left_other[...].T
+    rows = turned.shape[0] // UNITS
+    units = [unit_of(name, number) for number in range(UNITS)]
+    if vec is not None:
+        total = vec[...] + vec_other[...]
+        features = total.shape[1]
+        part = 2 * rows
+        spread[...] = jnp.zeros_like(spread)
+        for chunk in range(UNITS // 2):
+            spread[2 * chunk, 0:8, :part] = total[0:8, chunk * part : (chunk + 1) * part]
+            for piece in range(4):
+                line, begin = divmod((4 * chunk + piece) * part, features)
+                spread[2 * chunk + 1, piece : piece + 1, :part] = total[
+                    8 + line : 9 + line, begin : begin + part
+                ]
+            spread[2 * chunk + 1, 4:5, : 2 * DIGITS] = total[12:13, : 2 * DIGITS]
+        for out in (send, keep):
+            out[:, rows:, :] = jnp.zeros_like(out[:, rows:, :])
+
+    def one_tile(step, carry):
+        if split:
+            here = right[:, rows_at(core * tile, tile)] if pick_core else right[...]
+            there = right_other[...]
+        else:
+            here, there = right[step], right_other[step]
+        whole[...] = (dot_nn(turned[:, :length], here) + dot_nn(turned[:, length:], there)).astype(LOW)
+        columns = rows_at(step * tile, tile)
+        for number, unit in enumerate(units):
+            out = send if number >= UNITS // 2 else keep
+            out[number % (UNITS // 2), :rows, columns] = whole[rows_at(unit * rows, rows), :]
+        return carry
+
+    if tiles == 1:
+        one_tile(0, 0)
+    else:
+        lax.fori_loop(0, tiles, one_tile, 0)
+    if vec is not None:
+        for number, unit in enumerate(units):
+            out = send if number >= UNITS // 2 else keep
+            out[number % (UNITS // 2), rows:, :128] = spread[unit].astype(LOW)
+
+
+def grad_rows(name, left, left_other, right, right_other, pick_core=False, vecs=()):
+    length, tall = left.shape
+    rows = tall // UNITS
+    tile = right_other.shape[-1]
+    width = math.prod(right_other.shape) // length
+    unit = ((UNITS // 2, rows + (16 if vecs else 0), width), LOW)
+    return call(
+        "rows",
+        functools.partial(rows_kernel, name=name, pick_core=pick_core),
+        (left, left_other, right, right_other, *vecs),
+        [unit, unit],
+        [((tall, 2 * length), LOW), ((tall, tile), LOW)] + [((UNITS, 16, 128), SINGLE)] * bool(vecs),
+    )
+
+
+def close_kernel(mine, other, *outs):
+    vec = outs[-1]
+    counts, whole, up, qv = outs[:4]
+    plain = outs[4:-1]
+    _, _, place = where_am_i()
+    rows = mine.shape[0] - 16
+    vec[rows_at(place * 8, 8), :] = mine[rows:, :128].astype(SINGLE)[:8]
+    vec[rows_at((1 - place) * 8, 8), :] = other[rows:, :128].astype(SINGLE)[:8]
+    line = vec[12:13, :]
+    lane = lax.broadcasted_iota(jnp.int32, line.shape, 1)
+    worth = lax.shift_left(jnp.ones_like(lane), lax.rem(lane, DIGITS)).astype(SINGLE)
+    first, second = (
+        jnp.sum(jnp.where(lane // DIGITS == half, line * worth, 0.0), axis=1, keepdims=True)
+        for half in (0, 1)
+    )
+    total = first + second
+    spot = lax.broadcasted_iota(jnp.int32, (1, 128), 1)
+    both = jnp.where(spot == 0, first, second).astype(jnp.int32)
+    counts[...] = both[0, :2]
+    whole[...] = jnp.broadcast_to(total, whole.shape)
+    width = qv.shape[1]
+    scaled = vec[...] / total
+    qv[...] = scaled[2:4, :width]
+    for number, out in zip((0, 1, 4, 5, 6, 7), plain):
+        out[...] = scaled[number, :width]
+    up[...] = jnp.concatenate([scaled[8 + part : 9 + part, :width] for part in range(4)], axis=1)[0]
+
+
+def close(mine, other, width):
+    return call(
+        "result",
+        close_kernel,
+        (mine, other),
+        [((2,), jnp.int32), ((8, 128), SINGLE), ((4 * width,), SINGLE), ((2, width), SINGLE)]
+        + [((width,), SINGLE)] * 6,
+        [((16, 128), SINGLE)],
+    )
+
+
+def finish_kernel(whole, *refs, rows, turned):
+    parts, out = refs[:4], refs[4]
+    core, _, place = where_am_i()
+    total = whole[0:1, 0:1]
+    for number, part in enumerate(parts):
+        side, half = core ^ (number >> 1), place ^ (number & 1)
+        if turned:
+            refs[5][rows_at((side * 2 + half) * rows, rows), :] = part[...].astype(SINGLE)
+        else:
+            width = part.shape[1]
+            out[rows_at(half * rows, rows), rows_at(side * width, width)] = (
+                part[:rows, :].astype(SINGLE) / total
+            )
+    if turned:
+        out[...] = refs[5][...].T / total
+
+
+def finish(whole, parts, rows, turned=False):
+    width = parts[0].shape[1]
+    shape = (width, 4 * rows) if turned else (2 * rows, 2 * width)
+    return call(
+        "result",
+        functools.partial(finish_kernel, rows=rows, turned=turned),
+        (whole, *parts),
+        [(shape, SINGLE)],
+        [((4 * rows, width), SINGLE)] * turned,
+    )[0]
+
+
+def swap_pairs(size, bit):
+    return [(i, i ^ bit) for i in range(size)]
+
+
+def partners(name, stage, groups):
+    pairs = []
+    for core in range(2):
+        axis = WAYS[name][core][stage]
+        for own in range(groups):
+            for place in range(2):
+                to = (own, place ^ 1) if axis == "x" else (own ^ BITS[axis], place)
+                pairs.append(((core * groups + own) * 2 + place, (core * groups + to[0]) * 2 + to[1]))
+    return pairs
+
+
+def added(one, two):
+    return (one.astype(SINGLE) + two.astype(SINGLE)).astype(LOW)
+
+
+class Order:
+    def __init__(self):
+        self.last = None
+
+    def tie(self, value):
+        if self.last is not None:
+            value, _ = lax.optimization_barrier((value, self.last))
+        return value
+
+    def mark(self, value):
+        self.last = value
+
+
+class Sum:
+    def __init__(self, order, name, groups, send, keep):
+        self.order, self.name, self.groups = order, name, groups
+        self.keep = keep
+        self.stage = 0
+        self.go(send)
+
+    def go(self, send):
+        self.flying = lax.ppermute(send, AXES, partners(self.name, self.stage, self.groups))
+
+    def step(self):
+        other = self.order.tie(self.flying)
+        keep = self.keep
+        self.stage += 1
+        pair = swap_pairs(2, 1)
+        if self.stage == 5:
+            self.order.mark(other)
+            self.parts = [self.total, other, self.across, lax.ppermute(other, "src", pair)]
+            return
+        if self.stage == 4:
+            self.total = added(keep[0], other[0])
+            self.order.mark(self.total)
+            self.flying = lax.ppermute(self.total, "seq", pair)
+            self.across = lax.ppermute(self.total, "src", pair)
+            return
+        half = keep.shape[0] // 2
+        send = added(keep[half:], other[half:])
+        self.keep = added(keep[:half], other[:half])
+        self.order.mark(send)
+        self.go(send)
+
+
+def body_fast(
+    inputs,
+    cotangent,
+    row_counts,
+    response_mask,
+    norm1_gain,
+    norm1_bias,
+    qkv_weight,
+    qv_bias,
+    out_weight,
+    out_bias,
+    norm2_gain,
+    norm2_bias,
+    up_weight,
+    up_bias,
+    down_weight,
+    down_bias,
+):
+    groups = lax.axis_size("dp")
+    pair = swap_pairs(2, 1)
+    core, own, place = (lax.axis_index(a) for a in ("src", "dp", "seq"))
+    x_both = inputs[0, 0]
+    x_other = lax.ppermute(
+        lax.dynamic_index_in_dim(x_both, 1 - place, 0, keepdims=False), "seq", pair
+    )
+    x_mine, c_send, c_mine, count, small, qkv_weight, out_weight = prepare(
+        row_counts,
+        response_mask[0, 0],
+        x_both,
+        cotangent[0, 0],
+        (norm1_gain, norm1_bias, qv_bias, out_bias, norm2_gain, norm2_bias, down_bias, up_bias),
+        (qkv_weight, out_weight),
+    )
+    c_other = lax.ppermute(c_send, "seq", pair)
+    order = Order()
+
+    def from_core(value):
+        return lax.ppermute(value, "src", pair)
+
+    up_weight, down_weight, n1, qkv, probs, mixed, middle, n2 = attend(
+        x_mine, x_other, small, qkv_weight, out_weight, up_weight, down_weight
+    )
+    g_theirs, du_theirs, db2, db2_theirs, dn, vec = feed_one(
+        n2, c_mine, c_other, small, count, up_weight, down_weight
+    )
+    order.mark(vec)
+    n2_other = order.tie(from_core(n2))
+    order.mark(n2_other)
+    g_mine, du_mine, dm, db1, db1_theirs, vec = feed_two(
+        order.tie(n2), db2, small, up_weight, down_weight, middle, dn, vec
+    )
+    order.mark(vec)
+    du_other = from_core(du_theirs)
+    other_theirs, other_mine = from_core(g_theirs), from_core(g_mine)
+    db2_other = from_core(db2_theirs)
+    n1_other, mixed_other, db1_other = from_core(n1), from_core(mixed), from_core(db1_theirs)
+
+    sums = {}
+    done = {}
+    rows = out_weight.shape[0] // groups
+
+    def rows_home(mine, send):
+        other = order.tie(lax.ppermute(send, "seq", pair))
+        both = jnp.where(place == 0, jnp.stack([mine, other]), jnp.stack([other, mine]))
+        order.mark(both)
+        return both[None, None]
+
+    def finished(name):
+        parts = sums[name].parts
+        parts[3] = order.tie(parts[3])
+        turned = name == "d"
+        shard = finish(done["whole"], parts, 2 * rows if turned else rows // 2, turned)
+        order.mark(shard)
+        return shard
+
+    for event in EVENTS:
+        if event == "y":
+            done["output"] = rows_home(y_mine, y_send)
+            continue
+        if event == "i":
+            done["input_grad"] = rows_home(x_grad_mine, x_grad_send)
+            continue
+        if event.islower():
+            if event in sums and sums[event].stage < 5:
+                sums[event].step()
+                if event == "o" and sums[event].stage == 5:
+                    counts, done["whole"], up_small, qv, *plain = close(*sums["o"].parts[:2], rows)
+                    order.mark(done["whole"])
+            else:
+                done[event] = finished(event)
+            continue
+        name = event.lower()
+        if event == "U":
+            parts = grad_rows(name, order.tie(n2), n2_other, du_mine, du_other)
+        elif event == "D":
+            parts = grad_lanes(
+                name, order.tie(g_mine), g_theirs, other_mine, other_theirs, db2, db2_other
+            )
+        elif event == "C":
+            n1_other, mixed_other, db1_other = order.tie((n1_other, mixed_other, db1_other))
+            here, n1_other, mixed_other, db1_other = lax.optimization_barrier(
+                (qkv, n1_other, mixed_other, db1_other)
+            )
+            dp_theirs, dp_mine, vec = back(here, probs, db1, out_weight, vec)
+            dp_other = from_core(dp_theirs)
+            order.mark(vec)
+            continue
+        elif event == "I":
+            x_grad_mine, x_grad_send, vec = input_gradient(
+                order.tie(x_mine), x_other, small, dp_mine, dp_theirs, qkv_weight, dm, vec
+            )
+            vec_other = from_core(vec)
+            order.mark(vec)
+            continue
+        elif event == "Y":
+            y_mine, y_send = result(order.tie(g_mine), g_theirs, middle, small, down_weight)
+            order.mark(y_send)
+            continue
+        elif event == "O":
+            parts = grad_rows(
+                name, order.tie(mixed), mixed_other, db1, db1_other, True, (vec, vec_other)
+            )
+        else:
+            parts = grad_rows(name, order.tie(n1), n1_other, dp_mine, dp_other)
+        order.mark(parts[0])
+        sums[name] = Sum(order, name, groups, *parts)
+
+    return (
+        done["output"],
+        done["input_grad"],
+        counts,
+        plain[0],
+        plain[1],
+        done["q"],
+        qv,
+        done["o"],
+        plain[2],
+        plain[3],
+        plain[4],
+        done["u"],
+        up_small,
+        done["d"],
+        plain[5],
+    )
+
+
 def solution(mesh):
     placed = (
         P("src", "dp", None, "seq", None),
@@ -327,8 +1168,10 @@
         P(),
         P(),
     )
+    sizes = dict(mesh.shape)
+    paired = sizes["src"] == 2 and sizes["seq"] == 2 and sizes["dp"] == 8
     return jax.shard_map(
-        body,
+        body_fast if paired else body_generic,
         mesh=mesh,
         in_specs=placed,
         out_specs=(

time: 629 us -> 126 us (0.20)
  waiting for transfers between devices: 334 us -> 46.2 us
  blocking collectives: 112 us -> 0 us
  matrix products: 74.9 us -> 0 us
  local copies, waits for them, and re-layouts: 44.2 us -> 0.94 us
  other arithmetic: 43.9 us -> 3.24 us
  starting transfers between devices: 0.55 us -> 38.5 us
  Pallas kernels: 0 us -> 35.1 us
  between operations: 17.6 us -> 1.62 us
    reduce_scatter x6 -> x0, waiting for transfers between devices: 288 us -> none  [the longest x1 98.7 us: body(): lax.psum_scatter(grads[10].astype(jnp.bfloat16), 'dp', scatter_dimension=...]
    dot_general x27 -> x0, matrix products: 66.7 us -> none  [the longest x3 7.75 us: attend_backward(): jnp.einsum('rhqk,rqhd->rkhd', probs_low, grad_part, preferred_element_typ...]
    psum x2 -> x0, blocking collectives: 47.6 us -> none  [the longest x1 39.6 us: body(): source_counts = lax.psum(picked, ('src', 'dp', 'seq'))]
    ppermute x0 -> x42, waiting for transfers between devices: none -> 46.2 us  [the longest x16 40.4 us: go(): lax.ppermute(send, AXES, partners(self.name, self.stage, self.groups))]
    psum x1 -> x0, waiting for transfers between devices: 46.1 us -> none  [body(): lax.psum(summed[2].astype(jnp.bfloat16), ('src', 'seq')).astype(jnp.float32)]
    ppermute x0 -> x42, starting transfers between devices: none -> 38.5 us  [the longest x16 25.2 us: go(): lax.ppermute(send, AXES, partners(self.name, self.stage, self.groups))]
    unnamed x1 -> x0, blocking collectives: 38.2 us -> none
    pallas_call x0 -> x16, Pallas kernels: none -> 35.1 us  [the longest x15 32.3 us: call(): pl.pallas_call(kernel, in_specs=[pl.BlockSpec(memory_space=pl.ANY)] * len...]
  transfers between devices with their start and end apart: 8 -> 42, of which waited for: 6 -> 12; matrix products, arithmetic and copies ran while one was open for 11% -> 3% of each run, Pallas kernels for 0% -> 27%
where the time goes in v3:
time: 126 us
  waiting for transfers between devices  46.2 us (37%)
  starting transfers between devices  38.5 us (31%)
  Pallas kernels  35.1 us (28%)
  other arithmetic  3.24 us (3%)
  between operations  1.62 us (1%)
    ppermute x16, waiting for transfers between devices, go(): lax.ppermute(send, AXES, partners(self.name, self.stage, self.groups))  40.4 us
    pallas_call x15, Pallas kernels, call(): pl.pallas_call(kernel, in_specs=[pl.BlockSpec(memory_space=pl.ANY)] * len...  32.3 us
    ppermute x16, starting transfers between devices, go(): lax.ppermute(send, AXES, partners(self.name, self.stage, self.groups))  25.2 us
    ppermute x4, starting transfers between devices, step(): self.flying = lax.ppermute(self.total, 'seq', pair)  4.48 us
    ppermute x1, starting transfers between devices, body_fast(): lax.ppermute(lax.dynamic_index_in_dim(x_both, 1 - place, 0, keepdims=Fals...  3 us
    pallas_call x1, Pallas kernels, prepare(): pl.pallas_call(prepare_kernel, in_specs=[pl.BlockSpec(memory_space=pltpu....  2.82 us
    ppermute x4, waiting for transfers between devices, step(): self.flying = lax.ppermute(self.total, 'seq', pair)  2.69 us
    ppermute x10, starting transfers between devices, from_core(): return lax.ppermute(value, 'src', pair)  2.65 us
  transfers between devices with their start and end apart: 42, of which 12 were waited for; matrix products, arithmetic and copies ran while one was open for 3% of the time, Pallas kernels for 27%

profile of v3, /device:TPU:0, one launch (start us, length us, event | category | flops | bytes accessed | tf_op | source)
XLA Modules:
  0.0 125.6 jit_solution(10400864180770269131)
XLA Ops:
  1.6 3.0 %collective-permute-start = (bf16[128,768]{1,0:T(8,128)(2,1)S(1)}, bf16[128,768]{1,0:T(8,128)(2,1)S(1)}, u32[]{:S(2)}, u32[]{:S(2)}) collective-permute-start(bf16[128,768]{1,0:T(8,128)(2,1)S(1)} %dynamic-slice_bitcast_fusion), channel_id=1, source_target_pairs={{0,1},{1,0},{2,3},{3,2},{4,5},{5,4},{6,7},{7,6},{8,9},{9,8},{10,11... | collective-permute-start | bytes 589832 | tf_op jit(solution)/shard_map/ppermute | solution.py:1028
  5.3 2.8 %shard_map.271 = (bf16[128,768]{1,0:T(8,128)(2,1)S(1)}, bf16[128,768]{1,0:T(8,128)(2,1)S(1)}, bf16[128,768]{1,0:T(8,128)(2,1)S(1)}, f32[1,128]{1,0:T(1,128)S(1)}...) custom-call(s32[1,1]{1,0:T(1,128)S(6)} %copy.31.refs_0_, s32[2,128]{1,0:T(2,128)} %bitcast.23, ...), custom_call_target="tpu_custom_call" | custom-call | flops 2000000000 | bytes 1 | tf_op jit(solution)/shard_map/pallas_call | solution.py:447
  8.2 1.3 %collective-permute-done.x_other = bf16[128,768]{1,0:T(8,128)(2,1)S(1)} collective-permute-done((bf16[128,768]{1,0:T(8,128)(2,1)S(1)}, bf16[128,768]{1,0:T(8,128)(2,1)S(1)}, u32[]{:S(2)}, u32[]{:S(2)}) %collective-permute-start) | collective-permute-done | bytes 196640 | tf_op jit(solution)/shard_map/ppermute | solution.py:1028
  9.5 5.4 %shard_map.272 = (bf16[768,3072]{1,0:T(8,128)(2,1)S(1)}, bf16[3072,768]{1,0:T(8,128)(2,1)S(1)}, bf16[256,768]{1,0:T(8,128)(2,1)S(1)}, bf16[9,256,256]{2,1,0:T(8,...) custom-call(bf16[768,3072]{1,0:T(8,128)(2,1)} %up_ref.1, ...), custom_call_target="tpu_custom_call" | custom-call | flops 8000000000 | bytes 1 | tf_op jit(solution)/shard_map/pallas_call | solution.py:374
  15.0 2.8 %shard_map.273 = (bf16[2,256,768]{2,1,0:T(8,128)(2,1)S(1)}, bf16[2,256,768]{2,1,0:T(8,128)(2,1)S(1)}, bf16[256,768]{1,0:T(8,128)(2,1)S(1)}, bf16[256,384]{1,0:T(...) custom-call(bf16[256,768]{1,0:T(8,128)(2,1)S(1)} %get-tuple-element.126.n2.left, ...), custom_call_target="tpu_custom_call" | custom-call | flops 5000000000 | bytes 1 | tf_op jit(solution)/shard_map/pallas_call | solution.py:374
  18.4 3.3 %shard_map.274 = (bf16[2,256,768]{2,1,0:T(8,128)(2,1)S(1)}, bf16[2,256,768]{2,1,0:T(8,128)(2,1)S(1)}, f32[256,768]{1,0:T(8,128)S(1)}, bf16[256,768]{1,0:T(8,128)...) custom-call(bf16[256,768]{1,0:T(8,128)(2,1)S(1)} %get-tuple-element.126.n2.left, ...), custom_call_target="tpu_custom_call" | custom-call | flops 5000000000 | bytes 1 | tf_op jit(solution)/shard_map/pallas_call | solution.py:374
  22.2 2.0 %shard_map.275 = (bf16[8,48,1536]{2,1,0:T(8,128)(2,1)S(1)}, bf16[8,48,1536]{2,1,0:T(8,128)(2,1)S(1)}) custom-call(bf16[256,768]{1,0:T(8,128)(2,1)S(1)} %get-tuple-element.126.n2.left, bf16[256,768]{1,0:T(8,128)(2,1)S(1)} %collective-permute-done.1.left_other, bf16[2,256,768]{2,1,0:T(8,128)(2,1)S(1)} %get-tuple-element.127.right, ...), custom_call_target="tpu_custom_call" | custom-call | flops 4000000000 | bytes 1 | tf_op jit(solution)/shard_map/pallas_call | solution.py:374
  24.2 2.4 %collective-permute-start.4 = (bf16[8,48,1536]{2,1,0:T(8,128)(2,1)S(1)}, bf16[8,48,1536]{2,1,0:T(8,128)(2,1)S(1)}, u32[]{:S(2)}, u32[]{:S(2)}) collective-permute-start(bf16[8,48,1536]{2,1,0:T(8,128)(2,1)S(1)} %get-tuple-element.130), channel_id=1, source_target_pairs={{0,1},{1,0},{2,3},{3,2},{4,5},{5,4},{6,7},{7,6},{8,9},{9,8},{10,11... | collective-permute-start | bytes 3538952 | tf_op jit(solution)/shard_map/ppermute | solution.py:982
  28.5 2.3 %shard_map.276 = (bf16[8,192,384]{2,1,0:T(8,128)(2,1)S(1)}, bf16[8,192,384]{2,1,0:T(8,128)(2,1)S(1)}) custom-call(bf16[2,256,768]{2,1,0:T(8,128)(2,1)S(1)} %get-tuple-element.168.g_mine, bf16[2,256,768]{2,1,0:T(8,128)(2,1)S(1)} %get-tuple-element.135.g_theirs, bf16[2,256,768]{2,1,0:T(8,128)(2,1)S(1)} %collective-permute-done.8.other_mine, ...), custom_call_target="tpu_custom_call" | custom-call | flops 4000000000 | bytes 1 | tf_op jit(solution)/shard_map/pallas_call | solution.py:374
  30.9 6.2 %shard_map.277 = (bf16[256,1152]{1,0:T(8,128)(2,1)S(1)}, bf16[256,1152]{1,0:T(8,128)(2,1)S(1)}, f32[16,768]{1,0:T(8,128)S(1)}) custom-call(bf16[9,256,256]{2,1,0:T(8,128)(2,1)S(1)} %get-tuple-element.141.qkv, bf16[12,256,256]{2,1,0:T(8,128)(2,1)S(1)} %get-tuple-element.142.probs, bf16[256,768]{1,0:T(8,128)(2,1)S(1)} %get-tuple-element.143.db1.right, ...), custom_call_target="tpu_custom_call" | custom-call | flops 1 | bytes 1 | tf_op jit(solution)/shard_map/pallas_call | solution.py:374
  37.3 1.3 %collective-permute-start.15 = (bf16[8,192,384]{2,1,0:T(8,128)(2,1)S(1)}, bf16[8,192,384]{2,1,0:T(8,128)(2,1)S(1)}, u32[]{:S(2)}, u32[]{:S(2)}) collective-permute-start(bf16[8,192,384]{2,1,0:T(8,128)(2,1)S(1)} %get-tuple-element.137), channel_id=1, source_target_pairs={{0,2},{1,3},{2,0},{3,1},{4,6},{5,7},{6,4},{7,5},{8,10},{9,11},{10,... | collective-permute-start | bytes 3538952 | tf_op jit(solution)/shard_map/ppermute | solution.py:982
  38.6 1.6 %shard_map.278 = (bf16[128,768]{1,0:T(8,128)(2,1)S(1)}, bf16[128,768]{1,0:T(8,128)(2,1)S(1)}, f32[16,768]{1,0:T(8,128)S(1)}) custom-call(bf16[128,768]{1,0:T(8,128)(2,1)S(1)} %get-tuple-element.145.x_mine, bf16[128,768]{1,0:T(8,128)(2,1)S(1)} %collective-permute-done.x_other, f32[16,768]{1,0:T(8,128)S(1)} %get-tuple-element.108.small, ...), custom_call_target="tpu_custom_call" | custom-call | flops 1 | bytes 1 | tf_op jit(solution)/shard_map/pallas_call | solution.py:374
  41.1 1.3 %shard_map.279 = (bf16[8,48,1152]{2,1,0:T(8,128)(2,1)S(1)}, bf16[8,48,1152]{2,1,0:T(8,128)(2,1)S(1)}) custom-call(bf16[256,768]{1,0:T(8,128)(2,1)S(1)} %get-tuple-element.151.left, bf16[256,768]{1,0:T(8,128)(2,1)S(1)} %collective-permute-done.5.left_other, bf16[256,1152]{1,0:T(8,128)(2,1)S(1)} %get-tuple-element.146.dp_mine.right, ...), custom_call_target="tpu_custom_call" | custom-call | flops 4000000000 | bytes 1 | tf_op jit(solution)/shard_map/pallas_call | solution.py:374
  42.4 1.5 %collective-permute-start.12 = (bf16[8,48,1152]{2,1,0:T(8,128)(2,1)S(1)}, bf16[8,48,1152]{2,1,0:T(8,128)(2,1)S(1)}, u32[]{:S(2)}, u32[]{:S(2)}) collective-permute-start(bf16[8,48,1152]{2,1,0:T(8,128)(2,1)S(1)} %get-tuple-element.154), channel_id=1, source_target_pairs={{0,2},{1,3},{2,0},{3,1},{4,6},{5,7},{6,4},{7,5},{8,10},{9,11},{10,... | collective-permute-start | bytes 2654216 | tf_op jit(solution)/shard_map/ppermute | solution.py:982
  45.2 1.5 %collective-permute-start.17 = (bf16[4,48,1536]{2,1,0:T(8,128)(2,1)S(1)}, bf16[4,48,1536]{2,1,0:T(8,128)(2,1)S(1)}, u32[]{:S(2)}, u32[]{:S(2)}) collective-permute-start(bf16[4,48,1536]{2,1,0:T(8,128)(2,1)S(1)} %get-tuple-element.202), channel_id=1, source_target_pairs={{0,4},{1,5},{2,6},{3,7},{4,0},{5,1},{6,2},{7,3},{8,12},{9,13},{10,... | collective-permute-start | bytes 1769480 | tf_op jit(solution)/shard_map/ppermute | solution.py:982
  46.7 11.0 %collective-permute-done.15 = bf16[8,192,384]{2,1,0:T(8,128)(2,1)S(1)} collective-permute-done((bf16[8,192,384]{2,1,0:T(8,128)(2,1)S(1)}, bf16[8,192,384]{2,1,0:T(8,128)(2,1)S(1)}, u32[]{:S(2)}, u32[]{:S(2)}) %collective-permute-start.15) | collective-permute-done | bytes 1179680 | tf_op jit(solution)/shard_map/ppermute | solution.py:982
  59.0 17.3 %collective-permute-done.14 = bf16[8,64,384]{2,1,0:T(8,128)(2,1)S(1)} collective-permute-done((bf16[8,64,384]{2,1,0:T(8,128)(2,1)S(1)}, bf16[8,64,384]{2,1,0:T(8,128)(2,1)S(1)}, u32[]{:S(2)}, u32[]{:S(2)}) %collective-permute-start.14) | collective-permute-done | bytes 393248 | tf_op jit(solution)/shard_map/ppermute | solution.py:982
  76.7 2.1 %collective-permute-start.16 = (bf16[4,48,1152]{2,1,0:T(8,128)(2,1)S(1)}, bf16[4,48,1152]{2,1,0:T(8,128)(2,1)S(1)}, u32[]{:S(2)}, u32[]{:S(2)}) collective-permute-start(bf16[4,48,1152]{2,1,0:T(8,128)(2,1)S(1)} %get-tuple-element.203), channel_id=1, source_target_pairs={{0,1},{1,0},{2,3},{3,2},{4,5},{5,4},{6,7},{7,6},{8,9},{9,8},{10,11... | collective-permute-start | bytes 1327112 | tf_op jit(solution)/shard_map/ppermute | solution.py:982
  78.9 3.1 %collective-permute-start.23 = (bf16[2,192,384]{2,1,0:T(8,128)(2,1)S(1)}, bf16[2,192,384]{2,1,0:T(8,128)(2,1)S(1)}, u32[]{:S(2)}, u32[]{:S(2)}) collective-permute-start(bf16[2,192,384]{2,1,0:T(8,128)(2,1)S(1)} %get-tuple-element.206), channel_id=1, source_target_pairs={{0,4},{1,5},{2,6},{3,7},{4,0},{5,1},{6,2},{7,3},{8,12},{9,13},{10,... | collective-permute-start | bytes 884744 | tf_op jit(solution)/shard_map/ppermute | solution.py:982
  82.1 1.8 %collective-permute-done.18 = bf16[4,64,384]{2,1,0:T(8,128)(2,1)S(1)} collective-permute-done((bf16[4,64,384]{2,1,0:T(8,128)(2,1)S(1)}, bf16[4,64,384]{2,1,0:T(8,128)(2,1)S(1)}, u32[]{:S(2)}, u32[]{:S(2)}) %collective-permute-start.18) | collective-permute-done | bytes 196640 | tf_op jit(solution)/shard_map/ppermute | solution.py:982
  83.9 3.5 %collective-permute-start.21 = (bf16[2,64,384]{2,1,0:T(8,128)(2,1)S(1)}, bf16[2,64,384]{2,1,0:T(8,128)(2,1)S(1)}, u32[]{:S(2)}, u32[]{:S(2)}) collective-permute-start(bf16[2,64,384]{2,1,0:T(8,128)(2,1)S(1)} %get-tuple-element.214), channel_id=1, source_target_pairs={{0,4},{1,5},{2,6},{3,7},{4,0},{5,1},{6,2},{7,3},{8,12},{9,13},{10,... | collective-permute-start | bytes 294920 | tf_op jit(solution)/shard_map/ppermute | solution.py:982
  87.7 5.7 %collective-permute-done.16 = bf16[4,48,1152]{2,1,0:T(8,128)(2,1)S(1)} collective-permute-done((bf16[4,48,1152]{2,1,0:T(8,128)(2,1)S(1)}, bf16[4,48,1152]{2,1,0:T(8,128)(2,1)S(1)}, u32[]{:S(2)}, u32[]{:S(2)}) %collective-permute-start.16) | collective-permute-done | bytes 442400 | tf_op jit(solution)/shard_map/ppermute | solution.py:982
  93.5 3.5 %collective-permute-start.27 = (bf16[2,48,1152]{2,1,0:T(8,128)(2,1)S(1)}, bf16[2,48,1152]{2,1,0:T(8,128)(2,1)S(1)}, u32[]{:S(2)}, u32[]{:S(2)}) collective-permute-start(bf16[2,48,1152]{2,1,0:T(8,128)(2,1)S(1)} %get-tuple-element.210), channel_id=1, source_target_pairs={{0,4},{1,5},{2,6},{3,7},{4,0},{5,1},{6,2},{7,3},{8,12},{9,13},{10,... | collective-permute-start | bytes 663560 | tf_op jit(solution)/shard_map/ppermute | solution.py:982
  97.0 1.7 %shard_map.281 = (bf16[128,768]{1,0:T(8,128)(2,1)S(1)}, bf16[128,768]{1,0:T(8,128)(2,1)S(1)}) custom-call(bf16[2,256,768]{2,1,0:T(8,128)(2,1)S(1)} %get-tuple-element.168.g_mine, bf16[2,256,768]{2,1,0:T(8,128)(2,1)S(1)} %get-tuple-element.135.g_theirs, f32[256,768]{1,0:T(8,128)S(1)} %get-tuple-element.121.middle, f32[16,768]{1,0:T(8,128)S(1)} %get-tuple-element.108.small, ...), custom_call_target="tpu_custom_call" | custom-call | flops 1 | bytes 1 | tf_op jit(solution)/shard_map/pallas_call | solution.py:374
  98.9 3.5 %collective-permute-done.22 = bf16[2,48,1536]{2,1,0:T(8,128)(2,1)S(1)} collective-permute-done((bf16[2,48,1536]{2,1,0:T(8,128)(2,1)S(1)}, bf16[2,48,1536]{2,1,0:T(8,128)(2,1)S(1)}, u32[]{:S(2)}, u32[]{:S(2)}) %collective-permute-start.22) | collective-permute-done | bytes 294944 | tf_op jit(solution)/shard_map/ppermute | solution.py:982
  102.4 1.4 %collective-permute-start.26 = (bf16[1,48,1536]{2,1,0:T(8,128)(2,1)S(1)}, bf16[1,48,1536]{2,1,0:T(8,128)(2,1)S(1)}, u32[]{:S(2)}, u32[]{:S(2)}) collective-permute-start(bf16[1,48,1536]{2,1,0:T(8,128)(2,1)S(1)} %add_convert_fusion.18), channel_id=1, source_target_pairs={{0,2},{1,3},{2,0},{3,1},{4,6},{5,7},{6,4},{7,5},{8,10},{9,11},{10,... | collective-permute-start | bytes 442376 | tf_op jit(solution)/shard_map/ppermute | solution.py:982
  103.9 3.0 %collective-permute-start.29 = (bf16[1,48,1152]{2,1,0:T(8,128)(2,1)S(1)}, bf16[1,48,1152]{2,1,0:T(8,128)(2,1)S(1)}, u32[]{:S(2)}, u32[]{:S(2)}) collective-permute-start(bf16[1,48,1152]{2,1,0:T(8,128)(2,1)S(1)} %add_convert_fusion.22), channel_id=1, source_target_pairs={{0,8},{1,9},{2,10},{3,11},{4,12},{5,13},{6,14},{7,15},{8,0},{9,1},... | collective-permute-start | bytes 331784 | tf_op jit(solution)/shard_map/ppermute | solution.py:982
  108.7 1.1 collective-permute-start.32
  109.9 1.2 collective-permute-start.28
  111.1 1.2 collective-permute-start.34
  112.3 2.7 %collective-permute-done.28.other.refs_1_ = bf16[64,384]{1,0:T(8,128)(2,1)S(1)} collective-permute-done((bf16[64,384]{1,0:T(8,128)(2,1)S(1)}, bf16[64,384]{1,0:T(8,128)(2,1)S(1)}, u32[]{:S(2)}, u32[]{:S(2)}) %collective-permute-start.28) | collective-permute-done | bytes 49184 | tf_op jit(solution)/shard_map/ppermute | solution.py:996
  124.1 1.5 %shard_map.286 = f32[384,768]{1,0:T(8,128)} custom-call(f32[8,128]{1,0:T(8,128)S(1)} %get-tuple-element.180.whole, bf16[192,384]{1,0:T(8,128)(2,1)S(1)} %fusion.1.refs_0_, bf16[192,384]{1,0:T(8,128)(2,1)S(1)} %collective-permute-done.32.refs_1_, bf16[192,384]{1,0:T(8,128)(2,1)S(1)} %collective-permute-done.40.refs_2_, ...), custom_call_target="tpu_custom_call" | custom-call | flops 1 | bytes 1 | tf_op jit(solution)/shard_map/pallas_call | solution.py:374
  (87 shorter events, 20.2 us)
Async XLA Ops:
  1.6 7.9 %collective-permute-start = (bf16[128,768]{1,0:T(8,128)(2,1)S(1)}, bf16[128,768]{1,0:T(8,128)(2,1)S(1)}, u32[]{:S(2)}, u32[]{:S(2)}) collective-permute-start(bf16[128,768]{1,0:T(8,128)(2,1)S(1)} %dynamic-slice_bitcast_fusion), channel_id=1, source_target_pairs={{0,1},{1,0},{2,3},{3,2},{4,5},{5,4},{6,7},{7,6},{8,9},{9,8},{10,11... | collective-permute-start | bytes 589832 | tf_op jit(solution)/shard_map/ppermute | solution.py:1028
  8.1 6.9 %collective-permute-start.2 = (bf16[128,768]{1,0:T(8,128)(2,1)S(1)}, bf16[128,768]{1,0:T(8,128)(2,1)S(1)}, u32[]{:S(2)}, u32[]{:S(2)}) collective-permute-start(bf16[128,768]{1,0:T(8,128)(2,1)S(1)} %get-tuple-element.113), channel_id=1, source_target_pairs={{0,1},{1,0},{2,3},{3,2},{4,5},{5,4},{6,7},{7,6},{8,9},{9,8},{10,11... | collective-permute-start | bytes 589832 | tf_op jit(solution)/shard_map/ppermute | solution.py:1039
  17.8 4.4 %collective-permute-start.3 = (bf16[2,256,768]{2,1,0:T(8,128)(2,1)S(1)}, bf16[2,256,768]{2,1,0:T(8,128)(2,1)S(1)}, u32[]{:S(2)}, u32[]{:S(2)}) collective-permute-start(bf16[2,256,768]{2,1,0:T(8,128)(2,1)S(1)} %get-tuple-element.128), channel_id=1, source_target_pairs={{0,16},{16,0},{1,17},{17,1},{2,18},{18,2},{3,19},{19,3},{4,20},{20... | collective-permute-start | bytes 2359304 | tf_op jit(solution)/shard_map/ppermute | solution.py:1043
  18.3 9.9 %collective-permute-start.9 = (bf16[2,256,768]{2,1,0:T(8,128)(2,1)S(1)}, bf16[2,256,768]{2,1,0:T(8,128)(2,1)S(1)}, u32[]{:S(2)}, u32[]{:S(2)}) collective-permute-start(bf16[2,256,768]{2,1,0:T(8,128)(2,1)S(1)} %get-tuple-element.135.g_theirs), channel_id=1, source_target_pairs={{0,16},{16,0},{1,17},{17,1},{2,18},{18,2},{3,19},{19,3},{4,20},{20... | collective-permute-start | bytes 2359304 | tf_op jit(solution)/shard_map/ppermute | solution.py:1043
  21.6 6.9 %collective-permute-start.8 = (bf16[2,256,768]{2,1,0:T(8,128)(2,1)S(1)}, bf16[2,256,768]{2,1,0:T(8,128)(2,1)S(1)}, u32[]{:S(2)}, u32[]{:S(2)}) collective-permute-start(bf16[2,256,768]{2,1,0:T(8,128)(2,1)S(1)} %get-tuple-element.168.g_mine), channel_id=1, source_target_pairs={{0,16},{16,0},{1,17},{17,1},{2,18},{18,2},{3,19},{19,3},{4,20},{20... | collective-permute-start | bytes 2359304 | tf_op jit(solution)/shard_map/ppermute | solution.py:1043
  24.2 16.6 %collective-permute-start.4 = (bf16[8,48,1536]{2,1,0:T(8,128)(2,1)S(1)}, bf16[8,48,1536]{2,1,0:T(8,128)(2,1)S(1)}, u32[]{:S(2)}, u32[]{:S(2)}) collective-permute-start(bf16[8,48,1536]{2,1,0:T(8,128)(2,1)S(1)} %get-tuple-element.130), channel_id=1, source_target_pairs={{0,1},{1,0},{2,3},{3,2},{4,5},{5,4},{6,7},{7,6},{8,9},{9,8},{10,11... | collective-permute-start | bytes 3538952 | tf_op jit(solution)/shard_map/ppermute | solution.py:982
  26.6 4.3 %collective-permute-start.5 = (bf16[256,768]{1,0:T(8,128)(2,1)S(1)}, bf16[256,768]{1,0:T(8,128)(2,1)S(1)}, u32[]{:S(2)}, u32[]{:S(2)}) collective-permute-start(bf16[256,768]{1,0:T(8,128)(2,1)S(1)} %get-tuple-element.151.left), channel_id=1, source_target_pairs={{0,16},{16,0},{1,17},{17,1},{2,18},{18,2},{3,19},{19,3},{4,20},{20... | collective-permute-start | bytes 1179656 | tf_op jit(solution)/shard_map/ppermute | solution.py:1043
  37.1 4.0 %collective-permute-start.11 = (bf16[256,1152]{1,0:T(8,128)(2,1)S(1)}, bf16[256,1152]{1,0:T(8,128)(2,1)S(1)}, u32[]{:S(2)}, u32[]{:S(2)}) collective-permute-start(bf16[256,1152]{1,0:T(8,128)(2,1)S(1)} %get-tuple-element.147.dp_theirs), channel_id=1, source_target_pairs={{0,16},{16,0},{1,17},{17,1},{2,18},{18,2},{3,19},{19,3},{4,20},{20... | collective-permute-start | bytes 1769480 | tf_op jit(solution)/shard_map/ppermute | solution.py:1043
  37.3 20.4 %collective-permute-start.15 = (bf16[8,192,384]{2,1,0:T(8,128)(2,1)S(1)}, bf16[8,192,384]{2,1,0:T(8,128)(2,1)S(1)}, u32[]{:S(2)}, u32[]{:S(2)}) collective-permute-start(bf16[8,192,384]{2,1,0:T(8,128)(2,1)S(1)} %get-tuple-element.137), channel_id=1, source_target_pairs={{0,2},{1,3},{2,0},{3,1},{4,6},{5,7},{6,4},{7,5},{8,10},{9,11},{10,... | collective-permute-start | bytes 3538952 | tf_op jit(solution)/shard_map/ppermute | solution.py:982
  42.4 34.1 %collective-permute-start.12 = (bf16[8,48,1152]{2,1,0:T(8,128)(2,1)S(1)}, bf16[8,48,1152]{2,1,0:T(8,128)(2,1)S(1)}, u32[]{:S(2)}, u32[]{:S(2)}) collective-permute-start(bf16[8,48,1152]{2,1,0:T(8,128)(2,1)S(1)} %get-tuple-element.154), channel_id=1, source_target_pairs={{0,2},{1,3},{2,0},{3,1},{4,6},{5,7},{6,4},{7,5},{8,10},{9,11},{10,... | collective-permute-start | bytes 2654216 | tf_op jit(solution)/shard_map/ppermute | solution.py:982
  44.6 31.7 %collective-permute-start.14 = (bf16[8,64,384]{2,1,0:T(8,128)(2,1)S(1)}, bf16[8,64,384]{2,1,0:T(8,128)(2,1)S(1)}, u32[]{:S(2)}, u32[]{:S(2)}) collective-permute-start(bf16[8,64,384]{2,1,0:T(8,128)(2,1)S(1)} %get-tuple-element.159), channel_id=1, source_target_pairs={{0,2},{1,3},{2,0},{3,1},{4,6},{5,7},{6,4},{7,5},{8,10},{9,11},{10,... | collective-permute-start | bytes 1179656 | tf_op jit(solution)/shard_map/ppermute | solution.py:982
  45.2 42.2 %collective-permute-start.17 = (bf16[4,48,1536]{2,1,0:T(8,128)(2,1)S(1)}, bf16[4,48,1536]{2,1,0:T(8,128)(2,1)S(1)}, u32[]{:S(2)}, u32[]{:S(2)}) collective-permute-start(bf16[4,48,1536]{2,1,0:T(8,128)(2,1)S(1)} %get-tuple-element.202), channel_id=1, source_target_pairs={{0,4},{1,5},{2,6},{3,7},{4,0},{5,1},{6,2},{7,3},{8,12},{9,13},{10,... | collective-permute-start | bytes 1769480 | tf_op jit(solution)/shard_map/ppermute | solution.py:982
  58.0 20.8 %collective-permute-start.19 = (bf16[4,192,384]{2,1,0:T(8,128)(2,1)S(1)}, bf16[4,192,384]{2,1,0:T(8,128)(2,1)S(1)}, u32[]{:S(2)}, u32[]{:S(2)}) collective-permute-start(bf16[4,192,384]{2,1,0:T(8,128)(2,1)S(1)} %get-tuple-element.200), channel_id=1, source_target_pairs={{0,1},{1,0},{2,3},{3,2},{4,5},{5,4},{6,7},{7,6},{8,9},{9,8},{10,11... | collective-permute-start | bytes 1769480 | tf_op jit(solution)/shard_map/ppermute | solution.py:982
  76.4 7.5 %collective-permute-start.18 = (bf16[4,64,384]{2,1,0:T(8,128)(2,1)S(1)}, bf16[4,64,384]{2,1,0:T(8,128)(2,1)S(1)}, u32[]{:S(2)}, u32[]{:S(2)}) collective-permute-start(bf16[4,64,384]{2,1,0:T(8,128)(2,1)S(1)} %get-tuple-element.212), channel_id=1, source_target_pairs={{0,1},{1,0},{2,3},{3,2},{4,5},{5,4},{6,7},{7,6},{8,9},{9,8},{10,11... | collective-permute-start | bytes 589832 | tf_op jit(solution)/shard_map/ppermute | solution.py:982
  76.7 16.7 %collective-permute-start.16 = (bf16[4,48,1152]{2,1,0:T(8,128)(2,1)S(1)}, bf16[4,48,1152]{2,1,0:T(8,128)(2,1)S(1)}, u32[]{:S(2)}, u32[]{:S(2)}) collective-permute-start(bf16[4,48,1152]{2,1,0:T(8,128)(2,1)S(1)} %get-tuple-element.203), channel_id=1, source_target_pairs={{0,1},{1,0},{2,3},{3,2},{4,5},{5,4},{6,7},{7,6},{8,9},{9,8},{10,11... | collective-permute-start | bytes 1327112 | tf_op jit(solution)/shard_map/ppermute | solution.py:982
  78.9 19.8 %collective-permute-start.23 = (bf16[2,192,384]{2,1,0:T(8,128)(2,1)S(1)}, bf16[2,192,384]{2,1,0:T(8,128)(2,1)S(1)}, u32[]{:S(2)}, u32[]{:S(2)}) collective-permute-start(bf16[2,192,384]{2,1,0:T(8,128)(2,1)S(1)} %get-tuple-element.206), channel_id=1, source_target_pairs={{0,4},{1,5},{2,6},{3,7},{4,0},{5,1},{6,2},{7,3},{8,12},{9,13},{10,... | collective-permute-start | bytes 884744 | tf_op jit(solution)/shard_map/ppermute | solution.py:982
  83.9 19.8 %collective-permute-start.21 = (bf16[2,64,384]{2,1,0:T(8,128)(2,1)S(1)}, bf16[2,64,384]{2,1,0:T(8,128)(2,1)S(1)}, u32[]{:S(2)}, u32[]{:S(2)}) collective-permute-start(bf16[2,64,384]{2,1,0:T(8,128)(2,1)S(1)} %get-tuple-element.214), channel_id=1, source_target_pairs={{0,4},{1,5},{2,6},{3,7},{4,0},{5,1},{6,2},{7,3},{8,12},{9,13},{10,... | collective-permute-start | bytes 294920 | tf_op jit(solution)/shard_map/ppermute | solution.py:982
  87.6 14.7 %collective-permute-start.22 = (bf16[2,48,1536]{2,1,0:T(8,128)(2,1)S(1)}, bf16[2,48,1536]{2,1,0:T(8,128)(2,1)S(1)}, u32[]{:S(2)}, u32[]{:S(2)}) collective-permute-start(bf16[2,48,1536]{2,1,0:T(8,128)(2,1)S(1)} %get-tuple-element.208), channel_id=1, source_target_pairs={{0,8},{1,9},{2,10},{3,11},{4,12},{5,13},{6,14},{7,15},{8,0},{9,1},... | collective-permute-start | bytes 884744 | tf_op jit(solution)/shard_map/ppermute | solution.py:982
  93.5 10.4 %collective-permute-start.27 = (bf16[2,48,1152]{2,1,0:T(8,128)(2,1)S(1)}, bf16[2,48,1152]{2,1,0:T(8,128)(2,1)S(1)}, u32[]{:S(2)}, u32[]{:S(2)}) collective-permute-start(bf16[2,48,1152]{2,1,0:T(8,128)(2,1)S(1)} %get-tuple-element.210), channel_id=1, source_target_pairs={{0,4},{1,5},{2,6},{3,7},{4,0},{5,1},{6,2},{7,3},{8,12},{9,13},{10,... | collective-permute-start | bytes 663560 | tf_op jit(solution)/shard_map/ppermute | solution.py:982
  98.7 20.6 %collective-permute-start.20 = (bf16[128,768]{1,0:T(8,128)(2,1)S(1)}, bf16[128,768]{1,0:T(8,128)(2,1)S(1)}, u32[]{:S(2)}, u32[]{:S(2)}) collective-permute-start(bf16[128,768]{1,0:T(8,128)(2,1)S(1)} %get-tuple-element.170), channel_id=1, source_target_pairs={{0,1},{1,0},{2,3},{3,2},{4,5},{5,4},{6,7},{7,6},{8,9},{9,8},{10,11... | collective-permute-start | bytes 589832 | tf_op jit(solution)/shard_map/ppermute | solution.py:1068
  98.8 9.9 %collective-permute-start.25 = (bf16[1,192,384]{2,1,0:T(8,128)(2,1)S(1)}, bf16[1,192,384]{2,1,0:T(8,128)(2,1)S(1)}, u32[]{:S(2)}, u32[]{:S(2)}) collective-permute-start(bf16[1,192,384]{2,1,0:T(8,128)(2,1)S(1)} %add_convert_fusion.19), channel_id=1, source_target_pairs={{0,8},{1,9},{2,10},{3,11},{4,12},{5,13},{6,14},{7,15},{8,0},{9,1},... | collective-permute-start | bytes 442376 | tf_op jit(solution)/shard_map/ppermute | solution.py:982
  102.4 5.2 %collective-permute-start.26 = (bf16[1,48,1536]{2,1,0:T(8,128)(2,1)S(1)}, bf16[1,48,1536]{2,1,0:T(8,128)(2,1)S(1)}, u32[]{:S(2)}, u32[]{:S(2)}) collective-permute-start(bf16[1,48,1536]{2,1,0:T(8,128)(2,1)S(1)} %add_convert_fusion.18), channel_id=1, source_target_pairs={{0,2},{1,3},{2,0},{3,1},{4,6},{5,7},{6,4},{7,5},{8,10},{9,11},{10,... | collective-permute-start | bytes 442376 | tf_op jit(solution)/shard_map/ppermute | solution.py:982
  103.8 6.1 %collective-permute-start.24 = (bf16[1,64,384]{2,1,0:T(8,128)(2,1)S(1)}, bf16[1,64,384]{2,1,0:T(8,128)(2,1)S(1)}, u32[]{:S(2)}, u32[]{:S(2)}) collective-permute-start(bf16[1,64,384]{2,1,0:T(8,128)(2,1)S(1)} %add_convert_fusion.26), channel_id=1, source_target_pairs={{0,8},{1,9},{2,10},{3,11},{4,12},{5,13},{6,14},{7,15},{8,0},{9,1},... | collective-permute-start | bytes 147464 | tf_op jit(solution)/shard_map/ppermute | solution.py:982
  103.9 7.2 %collective-permute-start.29 = (bf16[1,48,1152]{2,1,0:T(8,128)(2,1)S(1)}, bf16[1,48,1152]{2,1,0:T(8,128)(2,1)S(1)}, u32[]{:S(2)}, u32[]{:S(2)}) collective-permute-start(bf16[1,48,1152]{2,1,0:T(8,128)(2,1)S(1)} %add_convert_fusion.22), channel_id=1, source_target_pairs={{0,8},{1,9},{2,10},{3,11},{4,12},{5,13},{6,14},{7,15},{8,0},{9,1},... | collective-permute-start | bytes 331784 | tf_op jit(solution)/shard_map/ppermute | solution.py:982
  107.7 8.3 %collective-permute-start.35 = (bf16[48,1536]{1,0:T(8,128)(2,1)S(1)}, bf16[48,1536]{1,0:T(8,128)(2,1)S(1)}, u32[]{:S(2)}, u32[]{:S(2)}) collective-permute-start(bf16[48,1536]{1,0:T(8,128)(2,1)S(1)} %fusion.refs_0_), channel_id=1, source_target_pairs={{0,1},{1,0},{2,3},{3,2},{4,5},{5,4},{6,7},{7,6},{8,9},{9,8},{10,11... | collective-permute-start | bytes 442376 | tf_op jit(solution)/shard_map/ppermute | solution.py:996
  108.7 7.2 %collective-permute-start.32 = (bf16[192,384]{1,0:T(8,128)(2,1)S(1)}, bf16[192,384]{1,0:T(8,128)(2,1)S(1)}, u32[]{:S(2)}, u32[]{:S(2)}) collective-permute-start(bf16[192,384]{1,0:T(8,128)(2,1)S(1)} %fusion.1.refs_0_), channel_id=1, source_target_pairs={{0,1},{1,0},{2,3},{3,2},{4,5},{5,4},{6,7},{7,6},{8,9},{9,8},{10,11... | collective-permute-start | bytes 442376 | tf_op jit(solution)/shard_map/ppermute | solution.py:996
  109.9 5.1 %collective-permute-start.28 = (bf16[64,384]{1,0:T(8,128)(2,1)S(1)}, bf16[64,384]{1,0:T(8,128)(2,1)S(1)}, u32[]{:S(2)}, u32[]{:S(2)}) collective-permute-start(bf16[64,384]{1,0:T(8,128)(2,1)S(1)} %fusion.3.mine.refs_0_), channel_id=1, source_target_pairs={{0,1},{1,0},{2,3},{3,2},{4,5},{5,4},{6,7},{7,6},{8,9},{9,8},{10,11... | collective-permute-start | bytes 147464 | tf_op jit(solution)/shard_map/ppermute | solution.py:996
  111.1 8.3 %collective-permute-start.34 = (bf16[48,1152]{1,0:T(8,128)(2,1)S(1)}, bf16[48,1152]{1,0:T(8,128)(2,1)S(1)}, u32[]{:S(2)}, u32[]{:S(2)}) collective-permute-start(bf16[48,1152]{1,0:T(8,128)(2,1)S(1)} %fusion.2.refs_0_), channel_id=1, source_target_pairs={{0,1},{1,0},{2,3},{3,2},{4,5},{5,4},{6,7},{7,6},{8,9},{9,8},{10,11... | collective-permute-start | bytes 331784 | tf_op jit(solution)/shard_map/ppermute | solution.py:996
  115.0 5.7 %collective-permute-start.33 = (bf16[128,768]{1,0:T(8,128)(2,1)S(1)}, bf16[128,768]{1,0:T(8,128)(2,1)S(1)}, u32[]{:S(2)}, u32[]{:S(2)}) collective-permute-start(bf16[128,768]{1,0:T(8,128)(2,1)S(1)} %get-tuple-element.185), channel_id=1, source_target_pairs={{0,1},{1,0},{2,3},{3,2},{4,5},{5,4},{6,7},{7,6},{8,9},{9,8},{10,11... | collective-permute-start | bytes 589832 | tf_op jit(solution)/shard_map/ppermute | solution.py:1068
  118.1 3.9 %collective-permute-start.38 = (bf16[48,1536]{1,0:T(8,128)(2,1)S(1)}, bf16[48,1536]{1,0:T(8,128)(2,1)S(1)}, u32[]{:S(2)}, u32[]{:S(2)}) collective-permute-start(bf16[48,1536]{1,0:T(8,128)(2,1)S(1)} %fusion.refs_0_), channel_id=1, source_target_pairs={{0,16},{16,0},{1,17},{17,1},{2,18},{18,2},{3,19},{19,3},{4,20},{20... | collective-permute-start | bytes 442376 | tf_op jit(solution)/shard_map/ppermute | solution.py:997
  119.3 4.9 %collective-permute-start.40 = (bf16[192,384]{1,0:T(8,128)(2,1)S(1)}, bf16[192,384]{1,0:T(8,128)(2,1)S(1)}, u32[]{:S(2)}, u32[]{:S(2)}) collective-permute-start(bf16[192,384]{1,0:T(8,128)(2,1)S(1)} %fusion.1.refs_0_), channel_id=1, source_target_pairs={{0,16},{16,0},{1,17},{17,1},{2,18},{18,2},{3,19},{19,3},{4,20},{20... | collective-permute-start | bytes 442376 | tf_op jit(solution)/shard_map/ppermute | solution.py:997
  119.4 4.7 %collective-permute-start.41 = (bf16[192,384]{1,0:T(8,128)(2,1)S(1)}, bf16[192,384]{1,0:T(8,128)(2,1)S(1)}, u32[]{:S(2)}, u32[]{:S(2)}) collective-permute-start(bf16[192,384]{1,0:T(8,128)(2,1)S(1)} %collective-permute-done.32.refs_1_), channel_id=1, source_target_pairs={{0,16},{16,0},{1,17},{17,1},{2,18},{18,2},{3,19},{19,3},{4,20},{20... | collective-permute-start | bytes 442376 | tf_op jit(solution)/shard_map/ppermute | solution.py:991
  (10 other events, 26.0 us)

commit v4 on v3

--- a/solution.py
+++ b/solution.py
@@ -311,16 +311,16 @@
 
 
 WAYS = {
-    "u": ("x12y", "12xy"),
-    "d": ("yx12", "1yx2"),
-    "o": ("yx12", "y12x"),
+    "u": ("x12y", "yx12"),
+    "d": ("y1x2", "12yx"),
+    "o": ("xy12", "1xy2"),
     "q": ("yx12", "xy12"),
 }
-EVENTS = "UDCIuQOdoqdouqYduoqudoqodouqioyuqd"
+EVENTS = "UDCIOQudoqudoqYudoqiudoqyudoq+"
 BITS = {"y": 1, "1": 2, "2": 4}
 
 
-COSTS = {"prepare": 2, "load": 4, "attend": 8, "feed_one": 5, "feed_two": 5, "back": 0, "input": 0, "lanes": 4, "rows": 4, "result": 0}
+COSTS = {"prepare": 2, "load": 4, "attend": 8, "feed_one": 5, "feed_two": 5, "back": 0, "input": 0, "lanes": 0, "rows_u": 4, "rows_q": 0, "rows_o": 0, "result": 0}
 AXES = ("src", "dp", "seq")
 SINGLE = jnp.float32
 LOW = jnp.bfloat16
@@ -356,9 +356,18 @@
     )
 
 
-def head_mask(head):
+def spread_heads(value, out, scale=1.0):
+    length = value.shape[0]
     lanes = lax.broadcasted_iota(jnp.int32, (1, GW), 1)
-    return (lanes >= head * HD) & (lanes < (head + 1) * HD)
+    for head in range(GROUP):
+        keep = jnp.where((lanes >= head * HD) & (lanes < (head + 1) * HD), scale, 0.0).astype(LOW)
+        out[head * length : (head + 1) * length, :] = value * keep
+
+
+def side_by_side(stacked, out):
+    length = out.shape[0]
+    for head in range(GROUP):
+        out[:, head * length : (head + 1) * length] = stacked[head * length : (head + 1) * length, :]
 
 
 def rows_at(first, count):
@@ -471,7 +480,7 @@
 
 def attend_kernel(
     up_ref, down_ref, x_mine, x_other, small, wqkv, wo,
-    up, down, n1, qkv, probs, mixed_low, middle, n2, sems,
+    up, down, n1, qkv, probs, mixed_low, middle, n2, heads_q, sems,
 ):
     _, _, place = where_am_i()
     copies = [
@@ -496,20 +505,22 @@
     allowed = lax.broadcasted_iota(jnp.int32, (length, length), 0) >= lax.broadcasted_iota(
         jnp.int32, (length, length), 1
     )
+    lanes = lax.broadcasted_iota(jnp.int32, (1, GW), 1)
 
     def one_group(group, carry):
         query, keys, values = (qkv[which * groups + group] for which in range(3))
-        scaled = query * HD**-0.5
-        mixed = None
+        spread_heads(query, heads_q, HD**-0.5)
+        parts = []
         for head in range(GROUP):
-            mask = head_mask(head)
-            scores = dot_nt(jnp.where(mask, scaled, 0), keys)
-            scores = jnp.where(allowed, scores, NEGATIVE)
+            cut = slice(head * length, (head + 1) * length)
+            scores = jnp.where(allowed, dot_nt(heads_q[cut, :], keys), NEGATIVE)
             powers = jnp.exp(scores - jnp.max(scores, axis=-1, keepdims=True))
             low = (powers * (1.0 / jnp.sum(powers, axis=-1, keepdims=True))).astype(LOW)
-            probs[group * GROUP + head] = low
-            part = dot_nn(low, values)
-            mixed = part if head == 0 else jnp.where(mask, part, mixed)
+            probs[group, cut, :] = low
+            parts.append(low)
+        mixed = dot_nn(parts[0], values)
+        for head in range(1, GROUP):
+            mixed = jnp.where(lanes >= head * HD, dot_nn(parts[head], values), mixed)
         mixed_low[:, rows_at(group * GW, GW)] = mixed.astype(LOW)
         return carry
 
@@ -533,11 +544,12 @@
         [
             act,
             ((3 * groups, length, GW), LOW),
-            ((groups * GROUP, length, length), LOW),
+            ((groups, GROUP * length, length), LOW),
             act,
             ((length, features), SINGLE),
             act,
         ],
+        [((GROUP * length, GW), LOW)],
         loaded=(up_weight, down_weight),
     )
 
@@ -664,7 +676,9 @@
     )
 
 
-def back_kernel(qkv, probs, db1, wo, vec_in, theirs, mine, vec, dp):
+def back_kernel(
+    qkv, probs, db1, wo, vec_in, theirs, mine, vec, dp, heads_q, heads_k, heads_g, side,
+):
     core, _, _ = where_am_i()
     features = db1.shape[1]
     groups = features // GW
@@ -674,23 +688,17 @@
         cut = rows_at(group * GW, GW)
         grad_mixed = dot_nt(db1[...], wo[cut, :]).astype(LOW)
         query, keys, values = (qkv[which * groups + group] for which in range(3))
-        query = query * HD**-0.5
-        keys = keys * HD**-0.5
-        dq = dk = dv = None
-        for head in range(GROUP):
-            mask = head_mask(head)
-            grad_head = jnp.where(mask, grad_mixed, 0)
-            probs_low = probs[group * GROUP + head]
-            weights = probs_low.astype(SINGLE)
-            grad_probs = dot_nt(grad_head, values)
-            inner = jnp.sum(weights * grad_probs, axis=-1, keepdims=True)
-            grad_scores = (weights * (grad_probs - inner)).astype(LOW)
-            part = dot_nn(grad_scores, keys)
-            dq = part if head == 0 else jnp.where(mask, part, dq)
-            part = dot_tn(grad_scores, query)
-            dk = part if head == 0 else jnp.where(mask, part, dk)
-            part = dot_tn(probs_low, grad_mixed)
-            dv = part if head == 0 else jnp.where(mask, part, dv)
+        spread_heads(grad_mixed, heads_g)
+        spread_heads(query, heads_q, HD**-0.5)
+        spread_heads(keys, heads_k, HD**-0.5)
+        weights = probs[group].astype(SINGLE)
+        grad_probs = dot_nt(heads_g[...], values)
+        inner = jnp.sum(weights * grad_probs, axis=-1, keepdims=True)
+        grad_scores = (weights * (grad_probs - inner)).astype(LOW)
+        side_by_side(grad_scores, side)
+        dv = dot_tn(probs[group], heads_g[...])
+        dk = dot_tn(grad_scores, heads_q[...])
+        dq = dot_nn(side[...], heads_k[...])
         for which, value in enumerate((dq, dk, dv)):
             low = value.astype(LOW)
             dp[:, rows_at(which * features + group * GW, GW)] = low
@@ -713,7 +721,9 @@
         back_kernel,
         (qkv, probs, db1, out_weight, vec_in),
         [half, half, ((16, features), SINGLE)],
-        [((length, 3 * features), LOW)],
+        [((length, 3 * features), LOW)]
+        + [((GROUP * length, GW), LOW)] * 3
+        + [((length, GROUP * length), LOW)],
     )
 
 
@@ -863,7 +873,7 @@
     width = math.prod(right_other.shape) // length
     unit = ((UNITS // 2, rows + (16 if vecs else 0), width), LOW)
     return call(
-        "rows",
+        "rows_" + name,
         functools.partial(rows_kernel, name=name, pick_core=pick_core),
         (left, left_other, right, right_other, *vecs),
         [unit, unit],
@@ -939,6 +949,16 @@
     )[0]
 
 
+def home_kernel(mine, other, out):
+    _, _, place = where_am_i()
+    out[place] = mine[...]
+    out[1 - place] = other[...]
+
+
+def home(mine, other):
+    return call("result", home_kernel, (mine, other), [((2,) + mine.shape, LOW)])[0]
+
+
 def swap_pairs(size, bit):
     return [(i, i ^ bit) for i in range(size)]
 
@@ -976,31 +996,39 @@
         self.order, self.name, self.groups = order, name, groups
         self.keep = keep
         self.stage = 0
+        self.whole_last = all(way[3] == "x" for way in WAYS[name])
+        self.parts = None
         self.go(send)
 
     def go(self, send):
         self.flying = lax.ppermute(send, AXES, partners(self.name, self.stage, self.groups))
 
     def step(self):
+        if self.parts is not None:
+            return
         other = self.order.tie(self.flying)
         keep = self.keep
         self.stage += 1
-        pair = swap_pairs(2, 1)
         if self.stage == 5:
             self.order.mark(other)
-            self.parts = [self.total, other, self.across, lax.ppermute(other, "src", pair)]
-            return
-        if self.stage == 4:
+            self.parts = [self.total, other]
+        elif self.stage == 4 and self.whole_last:
+            self.parts = [added(keep[0], other[1]), added(keep[1], other[0])]
+            self.order.mark(self.parts[0])
+        elif self.stage == 4:
             self.total = added(keep[0], other[0])
             self.order.mark(self.total)
-            self.flying = lax.ppermute(self.total, "seq", pair)
-            self.across = lax.ppermute(self.total, "src", pair)
-            return
-        half = keep.shape[0] // 2
-        send = added(keep[half:], other[half:])
-        self.keep = added(keep[:half], other[:half])
-        self.order.mark(send)
-        self.go(send)
+            self.flying = lax.ppermute(self.total, "seq", swap_pairs(2, 1))
+        elif self.stage == 3 and self.whole_last:
+            self.keep = added(keep, other)
+            self.order.mark(self.keep)
+            self.go(self.keep)
+        else:
+            half = keep.shape[0] // 2
+            send = added(keep[half:], other[half:])
+            self.keep = added(keep[:half], other[:half])
+            self.order.mark(send)
+            self.go(send)
 
 
 def body_fast(
@@ -1049,16 +1077,23 @@
         n2, c_mine, c_other, small, count, up_weight, down_weight
     )
     order.mark(vec)
-    n2_other = order.tie(from_core(n2))
-    order.mark(n2_other)
+    n2_other, n1_other, mixed_other = order.tie(
+        (from_core(n2), from_core(n1), from_core(mixed))
+    )
+    here, n2_other, n1_other, mixed_other = lax.optimization_barrier(
+        (n2, n2_other, n1_other, mixed_other)
+    )
     g_mine, du_mine, dm, db1, db1_theirs, vec = feed_two(
-        order.tie(n2), db2, small, up_weight, down_weight, middle, dn, vec
+        here, db2, small, up_weight, down_weight, middle, dn, vec
     )
     order.mark(vec)
-    du_other = from_core(du_theirs)
-    other_theirs, other_mine = from_core(g_theirs), from_core(g_mine)
-    db2_other = from_core(db2_theirs)
-    n1_other, mixed_other, db1_other = from_core(n1), from_core(mixed), from_core(db1_theirs)
+    du_other, db2_other, other_theirs = order.tie(
+        (from_core(du_theirs), from_core(db2_theirs), from_core(g_theirs))
+    )
+    here, du_other, db2_other, other_theirs = lax.optimization_barrier(
+        (n2, du_other, db2_other, other_theirs)
+    )
+    other_mine, db1_other = from_core(g_mine), from_core(db1_theirs)
 
     sums = {}
     done = {}
@@ -1066,17 +1101,21 @@
 
     def rows_home(mine, send):
         other = order.tie(lax.ppermute(send, "seq", pair))
-        both = jnp.where(place == 0, jnp.stack([mine, other]), jnp.stack([other, mine]))
+        both = home(mine, other)
         order.mark(both)
         return both[None, None]
 
-    def finished(name):
-        parts = sums[name].parts
-        parts[3] = order.tie(parts[3])
-        turned = name == "d"
-        shard = finish(done["whole"], parts, 2 * rows if turned else rows // 2, turned)
-        order.mark(shard)
-        return shard
+    def finish_all():
+        names = [n for n in sums if sums[n].parts is not None and n not in done]
+        mine = order.tie([sums[n].parts for n in names])
+        theirs = [[from_core(p) for p in parts] for parts in mine]
+        for name, here, there in zip(names, mine, theirs):
+            there = order.tie(there)
+            turned = name == "d"
+            done[name] = finish(
+                done["whole"], here + there, 2 * rows if turned else rows // 2, turned
+            )
+            order.mark(done[name])
 
     for event in EVENTS:
         if event == "y":
@@ -1085,27 +1124,24 @@
         if event == "i":
             done["input_grad"] = rows_home(x_grad_mine, x_grad_send)
             continue
+        if event == "+":
+            finish_all()
+            continue
         if event.islower():
-            if event in sums and sums[event].stage < 5:
-                sums[event].step()
-                if event == "o" and sums[event].stage == 5:
-                    counts, done["whole"], up_small, qv, *plain = close(*sums["o"].parts[:2], rows)
-                    order.mark(done["whole"])
-            else:
-                done[event] = finished(event)
+            sums[event].step()
+            if event == "o" and sums["o"].parts is not None and "whole" not in done:
+                counts, done["whole"], up_small, qv, *plain = close(*sums["o"].parts, rows)
+                order.mark(done["whole"])
             continue
         name = event.lower()
         if event == "U":
-            parts = grad_rows(name, order.tie(n2), n2_other, du_mine, du_other)
+            parts = grad_rows(name, order.tie(here), n2_other, du_mine, du_other)
         elif event == "D":
-            parts = grad_lanes(
-                name, order.tie(g_mine), g_theirs, other_mine, other_theirs, db2, db2_other
-            )
+            other_mine = order.tie(other_mine)
+            here, other_mine = lax.optimization_barrier((g_mine, other_mine))
+            parts = grad_lanes(name, here, g_theirs, other_mine, other_theirs, db2, db2_other)
         elif event == "C":
-            n1_other, mixed_other, db1_other = order.tie((n1_other, mixed_other, db1_other))
-            here, n1_other, mixed_other, db1_other = lax.optimization_barrier(
-                (qkv, n1_other, mixed_other, db1_other)
-            )
+            here = order.tie(qkv)
             dp_theirs, dp_mine, vec = back(here, probs, db1, out_weight, vec)
             dp_other = from_core(dp_theirs)
             order.mark(vec)
@@ -1126,7 +1162,9 @@
                 name, order.tie(mixed), mixed_other, db1, db1_other, True, (vec, vec_other)
             )
         else:
-            parts = grad_rows(name, order.tie(n1), n1_other, dp_mine, dp_other)
+            dp_other, db1_other = order.tie((dp_other, db1_other))
+            here, dp_other, db1_other = lax.optimization_barrier((n1, dp_other, db1_other))
+            parts = grad_rows(name, here, n1_other, dp_mine, dp_other)
         order.mark(parts[0])
         sums[name] = Sum(order, name, groups, *parts)
 

time: 126 us -> 107 us (0.85)
  waiting for transfers between devices: 46.2 us -> 26.6 us
  starting transfers between devices: 38.5 us -> 42.9 us
  Pallas kernels: 35.1 us -> 32.8 us
  other arithmetic: 3.24 us -> 1.66 us
    ppermute x16, waiting for transfers between devices: 40.4 us -> 21.5 us  [go(): lax.ppermute(send, AXES, partners(self.name, self.stage, self.groups))]
    ppermute x16, starting transfers between devices: 25.2 us -> 30.2 us  [go(): lax.ppermute(send, AXES, partners(self.name, self.stage, self.groups))]
    ppermute x12 -> x4, starting transfers between devices: 6.59 us -> 2.23 us  [step(): self.flying = lax.ppermute(self.total, 'seq', swap_pairs(2, 1))]
    pallas_call x15 -> x17, Pallas kernels: 32.3 us -> 30 us  [call(): pl.pallas_call(kernel, in_specs=[pl.BlockSpec(memory_space=pl.ANY)] * len...]
    ppermute x2, starting transfers between devices: 1.01 us -> 2.99 us  [rows_home(): other = order.tie(lax.ppermute(send, 'seq', pair))]
    ppermute x10 -> x18, starting transfers between devices: 2.65 us -> 4.41 us  [from_core(): return lax.ppermute(value, 'src', pair)]
    select_n x2 -> x0, other arithmetic: 1.59 us -> none  [rows_home(): jnp.where(place == 0, jnp.stack([mine, other]), jnp.stack([other, mine]))]
    ppermute x12 -> x4, waiting for transfers between devices: 3.42 us -> 3.25 us  [step(): self.flying = lax.ppermute(self.total, 'seq', swap_pairs(2, 1))]
  transfers between devices with their start and end apart: 42 -> 42, of which waited for: 12 -> 14; matrix products, arithmetic and copies ran while one was open for 3% -> 2% of each run, Pallas kernels for 27% -> 30%
where the time goes in v4:
time: 107 us
  starting transfers between devices  42.9 us (40%)
  Pallas kernels  32.8 us (31%)
  waiting for transfers between devices  26.6 us (25%)
  other arithmetic  1.66 us (2%)
  between operations  1.58 us (1%)
    ppermute x16, starting transfers between devices, go(): lax.ppermute(send, AXES, partners(self.name, self.stage, self.groups))  30.2 us
    pallas_call x17, Pallas kernels, call(): pl.pallas_call(kernel, in_specs=[pl.BlockSpec(memory_space=pl.ANY)] * len...  30 us
    ppermute x16, waiting for transfers between devices, go(): lax.ppermute(send, AXES, partners(self.name, self.stage, self.groups))  21.5 us
    ppermute x18, starting transfers between devices, from_core(): return lax.ppermute(value, 'src', pair)  4.41 us
    ppermute x4, waiting for transfers between devices, step(): self.flying = lax.ppermute(self.total, 'seq', swap_pairs(2, 1))  3.25 us
    ppermute x1, starting transfers between devices, body_fast(): lax.ppermute(lax.dynamic_index_in_dim(x_both, 1 - place, 0, keepdims=Fals...  3 us
    ppermute x2, starting transfers between devices, rows_home(): other = order.tie(lax.ppermute(send, 'seq', pair))  2.99 us
    pallas_call x1, Pallas kernels, prepare(): pl.pallas_call(prepare_kernel, in_specs=[pl.BlockSpec(memory_space=pltpu....  2.82 us
  transfers between devices with their start and end apart: 42, of which 14 were waited for; matrix products, arithmetic and copies ran while one was open for 2% of the time, Pallas kernels for 30%

profile of v4, /device:TPU:0, one launch (start us, length us, event | category | flops | bytes accessed | tf_op | source)
XLA Modules:
  0.0 106.5 jit_solution(5053823729043988352)
XLA Ops:
  1.6 3.0 %collective-permute-start = (bf16[128,768]{1,0:T(8,128)(2,1)S(1)}, bf16[128,768]{1,0:T(8,128)(2,1)S(1)}, u32[]{:S(2)}, u32[]{:S(2)}) collective-permute-start(bf16[128,768]{1,0:T(8,128)(2,1)S(1)} %dynamic-slice_bitcast_fusion), channel_id=1, source_target_pairs={{0,1},{1,0},{2,3},{3,2},{4,5},{5,4},{6,7},{7,6},{8,9},{9,8},{10,11... | collective-permute-start | bytes 589832 | tf_op jit(solution)/shard_map/ppermute | solution.py:1056
  5.3 2.8 %shard_map.271 = (bf16[128,768]{1,0:T(8,128)(2,1)S(1)}, bf16[128,768]{1,0:T(8,128)(2,1)S(1)}, bf16[128,768]{1,0:T(8,128)(2,1)S(1)}, f32[1,128]{1,0:T(1,128)S(1)}...) custom-call(s32[1,1]{1,0:T(1,128)S(6)} %copy.31.refs_0_, s32[2,128]{1,0:T(2,128)} %bitcast.19, ...), custom_call_target="tpu_custom_call" | custom-call | flops 2000000000 | bytes 1 | tf_op jit(solution)/shard_map/pallas_call | solution.py:456
  8.2 1.3 %collective-permute-done.x_other = bf16[128,768]{1,0:T(8,128)(2,1)S(1)} collective-permute-done((bf16[128,768]{1,0:T(8,128)(2,1)S(1)}, bf16[128,768]{1,0:T(8,128)(2,1)S(1)}, u32[]{:S(2)}, u32[]{:S(2)}) %collective-permute-start) | collective-permute-done | bytes 196640 | tf_op jit(solution)/shard_map/ppermute | solution.py:1056
  9.5 4.2 %shard_map.272 = (bf16[768,3072]{1,0:T(8,128)(2,1)S(1)}, bf16[3072,768]{1,0:T(8,128)(2,1)S(1)}, bf16[256,768]{1,0:T(8,128)(2,1)S(1)}, bf16[9,256,256]{2,1,0:T(8,...) custom-call(bf16[768,3072]{1,0:T(8,128)(2,1)} %up_ref.1, ...), custom_call_target="tpu_custom_call" | custom-call | flops 8000000000 | bytes 1 | tf_op jit(solution)/shard_map/pallas_call | solution.py:383
  14.5 2.7 %shard_map.273 = (bf16[2,256,768]{2,1,0:T(8,128)(2,1)S(1)}, bf16[2,256,768]{2,1,0:T(8,128)(2,1)S(1)}, bf16[256,768]{1,0:T(8,128)(2,1)S(1)}, bf16[256,384]{1,0:T(...) custom-call(bf16[256,768]{1,0:T(8,128)(2,1)S(1)} %get-tuple-element.161.n2.left, ...), custom_call_target="tpu_custom_call" | custom-call | flops 5000000000 | bytes 1 | tf_op jit(solution)/shard_map/pallas_call | solution.py:383
  18.1 3.2 %shard_map.274 = (bf16[2,256,768]{2,1,0:T(8,128)(2,1)S(1)}, bf16[2,256,768]{2,1,0:T(8,128)(2,1)S(1)}, f32[256,768]{1,0:T(8,128)S(1)}, bf16[256,768]{1,0:T(8,128)...) custom-call(bf16[256,768]{1,0:T(8,128)(2,1)S(1)} %get-tuple-element.161.n2.left, ...), custom_call_target="tpu_custom_call" | custom-call | flops 5000000000 | bytes 1 | tf_op jit(solution)/shard_map/pallas_call | solution.py:383
  21.7 2.0 %shard_map.275 = (bf16[8,48,1536]{2,1,0:T(8,128)(2,1)S(1)}, bf16[8,48,1536]{2,1,0:T(8,128)(2,1)S(1)}) custom-call(bf16[256,768]{1,0:T(8,128)(2,1)S(1)} %get-tuple-element.161.n2.left, bf16[256,768]{1,0:T(8,128)(2,1)S(1)} %collective-permute-done.1.left_other, bf16[2,256,768]{2,1,0:T(8,128)(2,1)S(1)} %get-tuple-element.163.right, ...), custom_call_target="tpu_custom_call" | custom-call | flops 4000000000 | bytes 1 | tf_op jit(solution)/shard_map/pallas_call | solution.py:383
  23.7 2.2 %collective-permute-start.15 = (bf16[8,48,1536]{2,1,0:T(8,128)(2,1)S(1)}, bf16[8,48,1536]{2,1,0:T(8,128)(2,1)S(1)}, u32[]{:S(2)}, u32[]{:S(2)}) collective-permute-start(bf16[8,48,1536]{2,1,0:T(8,128)(2,1)S(1)} %get-tuple-element.165), channel_id=1, source_target_pairs={{0,1},{1,0},{2,3},{3,2},{4,5},{5,4},{6,7},{7,6},{8,9},{9,8},{10,11... | collective-permute-start | bytes 3538952 | tf_op jit(solution)/shard_map/ppermute | solution.py:1004
  25.9 2.3 %shard_map.276 = (bf16[8,192,384]{2,1,0:T(8,128)(2,1)S(1)}, bf16[8,192,384]{2,1,0:T(8,128)(2,1)S(1)}) custom-call(bf16[2,256,768]{2,1,0:T(8,128)(2,1)S(1)} %get-tuple-element.202.g_mine, bf16[2,256,768]{2,1,0:T(8,128)(2,1)S(1)} %get-tuple-element.155.g_theirs, bf16[2,256,768]{2,1,0:T(8,128)(2,1)S(1)} %collective-permute-done.5.other_mine, ...), custom_call_target="tpu_custom_call" | custom-call | flops 1 | bytes 1 | tf_op jit(solution)/shard_map/pallas_call | solution.py:383
  28.2 1.3 %collective-permute-start.14 = (bf16[8,192,384]{2,1,0:T(8,128)(2,1)S(1)}, bf16[8,192,384]{2,1,0:T(8,128)(2,1)S(1)}, u32[]{:S(2)}, u32[]{:S(2)}) collective-permute-start(bf16[8,192,384]{2,1,0:T(8,128)(2,1)S(1)} %get-tuple-element.171), channel_id=1, source_target_pairs={{0,2},{1,3},{2,0},{3,1},{4,6},{5,7},{6,4},{7,5},{8,10},{9,11},{10,... | collective-permute-start | bytes 3538952 | tf_op jit(solution)/shard_map/ppermute | solution.py:1004
  29.6 3.6 %shard_map.277 = (bf16[256,1152]{1,0:T(8,128)(2,1)S(1)}, bf16[256,1152]{1,0:T(8,128)(2,1)S(1)}, f32[16,768]{1,0:T(8,128)S(1)}) custom-call(bf16[9,256,256]{2,1,0:T(8,128)(2,1)S(1)} %get-tuple-element.172.qkv, bf16[3,1024,256]{2,1,0:T(8,128)(2,1)S(1)} %get-tuple-element.173.probs, bf16[256,768]{1,0:T(8,128)(2,1)S(1)} %get-tuple-element.174.db1.right, ...), custom_call_target="tpu_custom_call" | custom-call | flops 1 | bytes 1 | tf_op jit(solution)/shard_map/pallas_call | solution.py:383
  33.8 1.6 %shard_map.278 = (bf16[128,768]{1,0:T(8,128)(2,1)S(1)}, bf16[128,768]{1,0:T(8,128)(2,1)S(1)}, f32[16,768]{1,0:T(8,128)S(1)}) custom-call(bf16[128,768]{1,0:T(8,128)(2,1)S(1)} %get-tuple-element.178.x_mine, bf16[128,768]{1,0:T(8,128)(2,1)S(1)} %collective-permute-done.x_other, f32[16,768]{1,0:T(8,128)S(1)} %get-tuple-element.132.small, ...), custom_call_target="tpu_custom_call" | custom-call | flops 1 | bytes 1 | tf_op jit(solution)/shard_map/pallas_call | solution.py:383
  38.4 1.3 %shard_map.280 = (bf16[8,48,1152]{2,1,0:T(8,128)(2,1)S(1)}, bf16[8,48,1152]{2,1,0:T(8,128)(2,1)S(1)}) custom-call(bf16[256,768]{1,0:T(8,128)(2,1)S(1)} %get-tuple-element.186.left, bf16[256,768]{1,0:T(8,128)(2,1)S(1)} %collective-permute-done.2.left_other, bf16[256,1152]{1,0:T(8,128)(2,1)S(1)} %get-tuple-element.179.dp_mine.right, ...), custom_call_target="tpu_custom_call" | custom-call | flops 1 | bytes 1 | tf_op jit(solution)/shard_map/pallas_call | solution.py:383
  40.5 1.7 %collective-permute-done.15 = bf16[8,48,1536]{2,1,0:T(8,128)(2,1)S(1)} collective-permute-done((bf16[8,48,1536]{2,1,0:T(8,128)(2,1)S(1)}, bf16[8,48,1536]{2,1,0:T(8,128)(2,1)S(1)}, u32[]{:S(2)}, u32[]{:S(2)}) %collective-permute-start.15) | collective-permute-done | bytes 1179680 | tf_op jit(solution)/shard_map/ppermute | solution.py:1004
  42.5 1.8 %collective-permute-start.19 = (bf16[4,48,1536]{2,1,0:T(8,128)(2,1)S(1)}, bf16[4,48,1536]{2,1,0:T(8,128)(2,1)S(1)}, u32[]{:S(2)}, u32[]{:S(2)}) collective-permute-start(bf16[4,48,1536]{2,1,0:T(8,128)(2,1)S(1)} %get-tuple-element.248), channel_id=1, source_target_pairs={{0,4},{1,5},{2,6},{3,7},{4,0},{5,1},{6,2},{7,3},{8,12},{9,13},{10,... | collective-permute-start | bytes 1769480 | tf_op jit(solution)/shard_map/ppermute | solution.py:1004
  44.4 7.5 %collective-permute-done.14 = bf16[8,192,384]{2,1,0:T(8,128)(2,1)S(1)} collective-permute-done((bf16[8,192,384]{2,1,0:T(8,128)(2,1)S(1)}, bf16[8,192,384]{2,1,0:T(8,128)(2,1)S(1)}, u32[]{:S(2)}, u32[]{:S(2)}) %collective-permute-start.14) | collective-permute-done | bytes 1179680 | tf_op jit(solution)/shard_map/ppermute | solution.py:1004
  52.1 1.8 %collective-permute-start.18 = (bf16[4,192,384]{2,1,0:T(8,128)(2,1)S(1)}, bf16[4,192,384]{2,1,0:T(8,128)(2,1)S(1)}, u32[]{:S(2)}, u32[]{:S(2)}) collective-permute-start(bf16[4,192,384]{2,1,0:T(8,128)(2,1)S(1)} %get-tuple-element.250), channel_id=1, source_target_pairs={{0,4},{1,5},{2,6},{3,7},{4,0},{5,1},{6,2},{7,3},{8,12},{9,13},{10,... | collective-permute-start | bytes 1769480 | tf_op jit(solution)/shard_map/ppermute | solution.py:1004
  55.0 2.1 %collective-permute-start.17 = (bf16[4,64,384]{2,1,0:T(8,128)(2,1)S(1)}, bf16[4,64,384]{2,1,0:T(8,128)(2,1)S(1)}, u32[]{:S(2)}, u32[]{:S(2)}) collective-permute-start(bf16[4,64,384]{2,1,0:T(8,128)(2,1)S(1)} %get-tuple-element.260), channel_id=1, source_target_pairs={{0,2},{1,3},{2,0},{3,1},{4,6},{5,7},{6,4},{7,5},{8,10},{9,11},{10,... | collective-permute-start | bytes 589832 | tf_op jit(solution)/shard_map/ppermute | solution.py:1004
  57.1 4.4 %collective-permute-done.12 = bf16[8,48,1152]{2,1,0:T(8,128)(2,1)S(1)} collective-permute-done((bf16[8,48,1152]{2,1,0:T(8,128)(2,1)S(1)}, bf16[8,48,1152]{2,1,0:T(8,128)(2,1)S(1)}, u32[]{:S(2)}, u32[]{:S(2)}) %collective-permute-start.12) | collective-permute-done | bytes 884768 | tf_op jit(solution)/shard_map/ppermute | solution.py:1004
  61.8 2.6 %collective-permute-start.16 = (bf16[4,48,1152]{2,1,0:T(8,128)(2,1)S(1)}, bf16[4,48,1152]{2,1,0:T(8,128)(2,1)S(1)}, u32[]{:S(2)}, u32[]{:S(2)}) collective-permute-start(bf16[4,48,1152]{2,1,0:T(8,128)(2,1)S(1)} %get-tuple-element.251), channel_id=1, source_target_pairs={{0,1},{1,0},{2,3},{3,2},{4,5},{5,4},{6,7},{7,6},{8,9},{9,8},{10,11... | collective-permute-start | bytes 1327112 | tf_op jit(solution)/shard_map/ppermute | solution.py:1004
  64.6 2.4 %collective-permute-start.24 = (bf16[2,48,1536]{2,1,0:T(8,128)(2,1)S(1)}, bf16[2,48,1536]{2,1,0:T(8,128)(2,1)S(1)}, u32[]{:S(2)}, u32[]{:S(2)}) collective-permute-start(bf16[2,48,1536]{2,1,0:T(8,128)(2,1)S(1)} %get-tuple-element.254), channel_id=1, source_target_pairs={{0,8},{1,9},{2,10},{3,11},{4,12},{5,13},{6,14},{7,15},{8,0},{9,1},... | collective-permute-start | bytes 884744 | tf_op jit(solution)/shard_map/ppermute | solution.py:1004
  67.1 2.1 %collective-permute-start.23 = (bf16[2,192,384]{2,1,0:T(8,128)(2,1)S(1)}, bf16[2,192,384]{2,1,0:T(8,128)(2,1)S(1)}, u32[]{:S(2)}, u32[]{:S(2)}) collective-permute-start(bf16[2,192,384]{2,1,0:T(8,128)(2,1)S(1)} %get-tuple-element.256), channel_id=1, source_target_pairs={{0,1},{1,0},{2,3},{3,2},{4,5},{5,4},{6,7},{7,6},{8,9},{9,8},{10,11... | collective-permute-start | bytes 884744 | tf_op jit(solution)/shard_map/ppermute | solution.py:1004
  71.3 1.6 %collective-permute-start.21 = (bf16[2,48,1152]{2,1,0:T(8,128)(2,1)S(1)}, bf16[2,48,1152]{2,1,0:T(8,128)(2,1)S(1)}, u32[]{:S(2)}, u32[]{:S(2)}) collective-permute-start(bf16[2,48,1152]{2,1,0:T(8,128)(2,1)S(1)} %get-tuple-element.258), channel_id=1, source_target_pairs={{0,4},{1,5},{2,6},{3,7},{4,0},{5,1},{6,2},{7,3},{8,12},{9,13},{10,... | collective-permute-start | bytes 663560 | tf_op jit(solution)/shard_map/ppermute | solution.py:1004
  72.9 1.6 %shard_map.281 = (bf16[128,768]{1,0:T(8,128)(2,1)S(1)}, bf16[128,768]{1,0:T(8,128)(2,1)S(1)}) custom-call(bf16[2,256,768]{2,1,0:T(8,128)(2,1)S(1)} %get-tuple-element.202.g_mine, bf16[2,256,768]{2,1,0:T(8,128)(2,1)S(1)} %get-tuple-element.155.g_theirs, f32[256,768]{1,0:T(8,128)S(1)} %get-tuple-element.149.middle, f32[16,768]{1,0:T(8,128)S(1)} %get-tuple-element.132.small, ...), custom_call_target="tpu_custom_call" | custom-call | flops 1 | bytes 1 | tf_op jit(solution)/shard_map/pallas_call | solution.py:383
  74.7 1.7 %collective-permute-start.20 = (bf16[128,768]{1,0:T(8,128)(2,1)S(1)}, bf16[128,768]{1,0:T(8,128)(2,1)S(1)}, u32[]{:S(2)}, u32[]{:S(2)}) collective-permute-start(bf16[128,768]{1,0:T(8,128)(2,1)S(1)} %get-tuple-element.204), channel_id=1, source_target_pairs={{0,1},{1,0},{2,3},{3,2},{4,5},{5,4},{6,7},{7,6},{8,9},{9,8},{10,11... | collective-permute-start | bytes 589832 | tf_op jit(solution)/shard_map/ppermute | solution.py:1103
  76.5 1.6 %collective-permute-start.28 = (bf16[1,48,1536]{2,1,0:T(8,128)(2,1)S(1)}, bf16[1,48,1536]{2,1,0:T(8,128)(2,1)S(1)}, u32[]{:S(2)}, u32[]{:S(2)}) collective-permute-start(bf16[1,48,1536]{2,1,0:T(8,128)(2,1)S(1)} %add_convert_fusion.19), channel_id=1, source_target_pairs={{0,2},{1,3},{2,0},{3,1},{4,6},{5,7},{6,4},{7,5},{8,10},{9,11},{10,... | collective-permute-start | bytes 442376 | tf_op jit(solution)/shard_map/ppermute | solution.py:1004
  78.2 2.7 %collective-permute-start.27 = (bf16[1,192,384]{2,1,0:T(8,128)(2,1)S(1)}, bf16[1,192,384]{2,1,0:T(8,128)(2,1)S(1)}, u32[]{:S(2)}, u32[]{:S(2)}) collective-permute-start(bf16[1,192,384]{2,1,0:T(8,128)(2,1)S(1)} %add_convert_fusion.18), channel_id=1, source_target_pairs={{0,8},{1,9},{2,10},{3,11},{4,12},{5,13},{6,14},{7,15},{8,0},{9,1},... | collective-permute-start | bytes 442376 | tf_op jit(solution)/shard_map/ppermute | solution.py:1004
  80.8 5.4 %collective-permute-start.26 = (bf16[1,64,384]{2,1,0:T(8,128)(2,1)S(1)}, bf16[1,64,384]{2,1,0:T(8,128)(2,1)S(1)}, u32[]{:S(2)}, u32[]{:S(2)}) collective-permute-start(bf16[1,64,384]{2,1,0:T(8,128)(2,1)S(1)} %add_convert_fusion.27), channel_id=1, source_target_pairs={{0,8},{1,9},{2,10},{3,11},{4,12},{5,13},{6,14},{7,15},{8,0},{9,1},... | collective-permute-start | bytes 147464 | tf_op jit(solution)/shard_map/ppermute | solution.py:1004
  87.3 4.0 %collective-permute-done.27 = bf16[1,192,384]{2,1,0:T(8,128)(2,1)S(1)} collective-permute-done((bf16[1,192,384]{2,1,0:T(8,128)(2,1)S(1)}, bf16[1,192,384]{2,1,0:T(8,128)(2,1)S(1)}, u32[]{:S(2)}, u32[]{:S(2)}) %collective-permute-start.27) | collective-permute-done | bytes 147488 | tf_op jit(solution)/shard_map/ppermute | solution.py:1004
  96.0 1.5 %collective-permute-done.31.refs_1_ = bf16[192,384]{1,0:T(8,128)(2,1)S(1)} collective-permute-done((bf16[192,384]{1,0:T(8,128)(2,1)S(1)}, bf16[192,384]{1,0:T(8,128)(2,1)S(1)}, u32[]{:S(2)}, u32[]{:S(2)}) %collective-permute-start.31) | collective-permute-done | bytes 147488 | tf_op jit(solution)/shard_map/ppermute | solution.py:1021
  97.5 1.7 %collective-permute-done.30.other.refs_1_ = bf16[64,384]{1,0:T(8,128)(2,1)S(1)} collective-permute-done((bf16[64,384]{1,0:T(8,128)(2,1)S(1)}, bf16[64,384]{1,0:T(8,128)(2,1)S(1)}, u32[]{:S(2)}, u32[]{:S(2)}) %collective-permute-start.30) | collective-permute-done | bytes 49184 | tf_op jit(solution)/shard_map/ppermute | solution.py:1021
  103.3 1.5 %shard_map.286 = f32[384,768]{1,0:T(8,128)} custom-call(f32[8,128]{1,0:T(8,128)S(1)} %get-tuple-element.223.whole, bf16[192,384]{1,0:T(8,128)(2,1)S(1)} %fusion.1.refs_0_, bf16[192,384]{1,0:T(8,128)(2,1)S(1)} %collective-permute-done.31.refs_1_, bf16[192,384]{1,0:T(8,128)(2,1)S(1)} %collective-permute-done.38.refs_2_, ...), custom_call_target="tpu_custom_call" | custom-call | flops 1 | bytes 1 | tf_op jit(solution)/shard_map/pallas_call | solution.py:383
  (87 shorter events, 23.3 us)
Async XLA Ops:
  1.6 7.9 %collective-permute-start = (bf16[128,768]{1,0:T(8,128)(2,1)S(1)}, bf16[128,768]{1,0:T(8,128)(2,1)S(1)}, u32[]{:S(2)}, u32[]{:S(2)}) collective-permute-start(bf16[128,768]{1,0:T(8,128)(2,1)S(1)} %dynamic-slice_bitcast_fusion), channel_id=1, source_target_pairs={{0,1},{1,0},{2,3},{3,2},{4,5},{5,4},{6,7},{7,6},{8,9},{9,8},{10,11... | collective-permute-start | bytes 589832 | tf_op jit(solution)/shard_map/ppermute | solution.py:1056
  8.1 6.4 %collective-permute-start.4 = (bf16[128,768]{1,0:T(8,128)(2,1)S(1)}, bf16[128,768]{1,0:T(8,128)(2,1)S(1)}, u32[]{:S(2)}, u32[]{:S(2)}) collective-permute-start(bf16[128,768]{1,0:T(8,128)(2,1)S(1)} %get-tuple-element.139), channel_id=1, source_target_pairs={{0,1},{1,0},{2,3},{3,2},{4,5},{5,4},{6,7},{7,6},{8,9},{9,8},{10,11... | collective-permute-start | bytes 589832 | tf_op jit(solution)/shard_map/ppermute | solution.py:1067
  13.7 4.1 %collective-permute-start.2 = (bf16[256,768]{1,0:T(8,128)(2,1)S(1)}, bf16[256,768]{1,0:T(8,128)(2,1)S(1)}, u32[]{:S(2)}, u32[]{:S(2)}) collective-permute-start(bf16[256,768]{1,0:T(8,128)(2,1)S(1)} %get-tuple-element.186.left), channel_id=1, source_target_pairs={{0,16},{16,0},{1,17},{17,1},{2,18},{18,2},{3,19},{19,3},{4,20},{20... | collective-permute-start | bytes 1179656 | tf_op jit(solution)/shard_map/ppermute | solution.py:1071
  13.8 4.3 %collective-permute-start.3 = (bf16[256,768]{1,0:T(8,128)(2,1)S(1)}, bf16[256,768]{1,0:T(8,128)(2,1)S(1)}, u32[]{:S(2)}, u32[]{:S(2)}) collective-permute-start(bf16[256,768]{1,0:T(8,128)(2,1)S(1)} %get-tuple-element.182.left), channel_id=1, source_target_pairs={{0,16},{16,0},{1,17},{17,1},{2,18},{18,2},{3,19},{19,3},{4,20},{20... | collective-permute-start | bytes 1179656 | tf_op jit(solution)/shard_map/ppermute | solution.py:1071
  17.3 4.5 %collective-permute-start.6 = (bf16[2,256,768]{2,1,0:T(8,128)(2,1)S(1)}, bf16[2,256,768]{2,1,0:T(8,128)(2,1)S(1)}, u32[]{:S(2)}, u32[]{:S(2)}) collective-permute-start(bf16[2,256,768]{2,1,0:T(8,128)(2,1)S(1)} %get-tuple-element.153), channel_id=1, source_target_pairs={{0,16},{16,0},{1,17},{17,1},{2,18},{18,2},{3,19},{19,3},{4,20},{20... | collective-permute-start | bytes 2359304 | tf_op jit(solution)/shard_map/ppermute | solution.py:1071
  17.5 4.2 %collective-permute-start.8 = (bf16[2,256,768]{2,1,0:T(8,128)(2,1)S(1)}, bf16[2,256,768]{2,1,0:T(8,128)(2,1)S(1)}, u32[]{:S(2)}, u32[]{:S(2)}) collective-permute-start(bf16[2,256,768]{2,1,0:T(8,128)(2,1)S(1)} %get-tuple-element.155.g_theirs), channel_id=1, source_target_pairs={{0,16},{16,0},{1,17},{17,1},{2,18},{18,2},{3,19},{19,3},{4,20},{20... | collective-permute-start | bytes 2359304 | tf_op jit(solution)/shard_map/ppermute | solution.py:1071
  21.3 4.6 %collective-permute-start.5 = (bf16[2,256,768]{2,1,0:T(8,128)(2,1)S(1)}, bf16[2,256,768]{2,1,0:T(8,128)(2,1)S(1)}, u32[]{:S(2)}, u32[]{:S(2)}) collective-permute-start(bf16[2,256,768]{2,1,0:T(8,128)(2,1)S(1)} %get-tuple-element.202.g_mine), channel_id=1, source_target_pairs={{0,16},{16,0},{1,17},{17,1},{2,18},{18,2},{3,19},{19,3},{4,20},{20... | collective-permute-start | bytes 2359304 | tf_op jit(solution)/shard_map/ppermute | solution.py:1071
  23.7 18.5 %collective-permute-start.15 = (bf16[8,48,1536]{2,1,0:T(8,128)(2,1)S(1)}, bf16[8,48,1536]{2,1,0:T(8,128)(2,1)S(1)}, u32[]{:S(2)}, u32[]{:S(2)}) collective-permute-start(bf16[8,48,1536]{2,1,0:T(8,128)(2,1)S(1)} %get-tuple-element.165), channel_id=1, source_target_pairs={{0,1},{1,0},{2,3},{3,2},{4,5},{5,4},{6,7},{7,6},{8,9},{9,8},{10,11... | collective-permute-start | bytes 3538952 | tf_op jit(solution)/shard_map/ppermute | solution.py:1004
  28.2 23.6 %collective-permute-start.14 = (bf16[8,192,384]{2,1,0:T(8,128)(2,1)S(1)}, bf16[8,192,384]{2,1,0:T(8,128)(2,1)S(1)}, u32[]{:S(2)}, u32[]{:S(2)}) collective-permute-start(bf16[8,192,384]{2,1,0:T(8,128)(2,1)S(1)} %get-tuple-element.171), channel_id=1, source_target_pairs={{0,2},{1,3},{2,0},{3,1},{4,6},{5,7},{6,4},{7,5},{8,10},{9,11},{10,... | collective-permute-start | bytes 3538952 | tf_op jit(solution)/shard_map/ppermute | solution.py:1004
  33.2 5.2 %collective-permute-start.9 = (bf16[256,1152]{1,0:T(8,128)(2,1)S(1)}, bf16[256,1152]{1,0:T(8,128)(2,1)S(1)}, u32[]{:S(2)}, u32[]{:S(2)}) collective-permute-start(bf16[256,1152]{1,0:T(8,128)(2,1)S(1)} %get-tuple-element.175.dp_theirs), channel_id=1, source_target_pairs={{0,16},{16,0},{1,17},{17,1},{2,18},{18,2},{3,19},{19,3},{4,20},{20... | collective-permute-start | bytes 1769480 | tf_op jit(solution)/shard_map/ppermute | solution.py:1071
  35.6 50.7 %collective-permute-start.29 = (bf16[128,768]{1,0:T(8,128)(2,1)S(1)}, bf16[128,768]{1,0:T(8,128)(2,1)S(1)}, u32[]{:S(2)}, u32[]{:S(2)}) collective-permute-start(bf16[128,768]{1,0:T(8,128)(2,1)S(1)} %get-tuple-element.210), channel_id=1, source_target_pairs={{0,1},{1,0},{2,3},{3,2},{4,5},{5,4},{6,7},{7,6},{8,9},{9,8},{10,11... | collective-permute-start | bytes 589832 | tf_op jit(solution)/shard_map/ppermute | solution.py:1103
  37.5 17.4 %collective-permute-start.13 = (bf16[8,64,384]{2,1,0:T(8,128)(2,1)S(1)}, bf16[8,64,384]{2,1,0:T(8,128)(2,1)S(1)}, u32[]{:S(2)}, u32[]{:S(2)}) collective-permute-start(bf16[8,64,384]{2,1,0:T(8,128)(2,1)S(1)} %get-tuple-element.184), channel_id=1, source_target_pairs={{0,1},{1,0},{2,3},{3,2},{4,5},{5,4},{6,7},{7,6},{8,9},{9,8},{10,11... | collective-permute-start | bytes 1179656 | tf_op jit(solution)/shard_map/ppermute | solution.py:1004
  39.8 21.8 %collective-permute-start.12 = (bf16[8,48,1152]{2,1,0:T(8,128)(2,1)S(1)}, bf16[8,48,1152]{2,1,0:T(8,128)(2,1)S(1)}, u32[]{:S(2)}, u32[]{:S(2)}) collective-permute-start(bf16[8,48,1152]{2,1,0:T(8,128)(2,1)S(1)} %get-tuple-element.190), channel_id=1, source_target_pairs={{0,2},{1,3},{2,0},{3,1},{4,6},{5,7},{6,4},{7,5},{8,10},{9,11},{10,... | collective-permute-start | bytes 2654216 | tf_op jit(solution)/shard_map/ppermute | solution.py:1004
  42.5 21.9 %collective-permute-start.19 = (bf16[4,48,1536]{2,1,0:T(8,128)(2,1)S(1)}, bf16[4,48,1536]{2,1,0:T(8,128)(2,1)S(1)}, u32[]{:S(2)}, u32[]{:S(2)}) collective-permute-start(bf16[4,48,1536]{2,1,0:T(8,128)(2,1)S(1)} %get-tuple-element.248), channel_id=1, source_target_pairs={{0,4},{1,5},{2,6},{3,7},{4,0},{5,1},{6,2},{7,3},{8,12},{9,13},{10,... | collective-permute-start | bytes 1769480 | tf_op jit(solution)/shard_map/ppermute | solution.py:1004
  52.1 14.8 %collective-permute-start.18 = (bf16[4,192,384]{2,1,0:T(8,128)(2,1)S(1)}, bf16[4,192,384]{2,1,0:T(8,128)(2,1)S(1)}, u32[]{:S(2)}, u32[]{:S(2)}) collective-permute-start(bf16[4,192,384]{2,1,0:T(8,128)(2,1)S(1)} %get-tuple-element.250), channel_id=1, source_target_pairs={{0,4},{1,5},{2,6},{3,7},{4,0},{5,1},{6,2},{7,3},{8,12},{9,13},{10,... | collective-permute-start | bytes 1769480 | tf_op jit(solution)/shard_map/ppermute | solution.py:1004
  55.0 14.3 %collective-permute-start.17 = (bf16[4,64,384]{2,1,0:T(8,128)(2,1)S(1)}, bf16[4,64,384]{2,1,0:T(8,128)(2,1)S(1)}, u32[]{:S(2)}, u32[]{:S(2)}) collective-permute-start(bf16[4,64,384]{2,1,0:T(8,128)(2,1)S(1)} %get-tuple-element.260), channel_id=1, source_target_pairs={{0,2},{1,3},{2,0},{3,1},{4,6},{5,7},{6,4},{7,5},{8,10},{9,11},{10,... | collective-permute-start | bytes 589832 | tf_op jit(solution)/shard_map/ppermute | solution.py:1004
  61.8 9.4 %collective-permute-start.16 = (bf16[4,48,1152]{2,1,0:T(8,128)(2,1)S(1)}, bf16[4,48,1152]{2,1,0:T(8,128)(2,1)S(1)}, u32[]{:S(2)}, u32[]{:S(2)}) collective-permute-start(bf16[4,48,1152]{2,1,0:T(8,128)(2,1)S(1)} %get-tuple-element.251), channel_id=1, source_target_pairs={{0,1},{1,0},{2,3},{3,2},{4,5},{5,4},{6,7},{7,6},{8,9},{9,8},{10,11... | collective-permute-start | bytes 1327112 | tf_op jit(solution)/shard_map/ppermute | solution.py:1004
  64.6 10.2 %collective-permute-start.24 = (bf16[2,48,1536]{2,1,0:T(8,128)(2,1)S(1)}, bf16[2,48,1536]{2,1,0:T(8,128)(2,1)S(1)}, u32[]{:S(2)}, u32[]{:S(2)}) collective-permute-start(bf16[2,48,1536]{2,1,0:T(8,128)(2,1)S(1)} %get-tuple-element.254), channel_id=1, source_target_pairs={{0,8},{1,9},{2,10},{3,11},{4,12},{5,13},{6,14},{7,15},{8,0},{9,1},... | collective-permute-start | bytes 884744 | tf_op jit(solution)/shard_map/ppermute | solution.py:1004
  67.1 9.4 %collective-permute-start.23 = (bf16[2,192,384]{2,1,0:T(8,128)(2,1)S(1)}, bf16[2,192,384]{2,1,0:T(8,128)(2,1)S(1)}, u32[]{:S(2)}, u32[]{:S(2)}) collective-permute-start(bf16[2,192,384]{2,1,0:T(8,128)(2,1)S(1)} %get-tuple-element.256), channel_id=1, source_target_pairs={{0,1},{1,0},{2,3},{3,2},{4,5},{5,4},{6,7},{7,6},{8,9},{9,8},{10,11... | collective-permute-start | bytes 884744 | tf_op jit(solution)/shard_map/ppermute | solution.py:1004
  69.3 8.8 %collective-permute-start.22 = (bf16[2,64,384]{2,1,0:T(8,128)(2,1)S(1)}, bf16[2,64,384]{2,1,0:T(8,128)(2,1)S(1)}, u32[]{:S(2)}, u32[]{:S(2)}) collective-permute-start(bf16[2,64,384]{2,1,0:T(8,128)(2,1)S(1)} %get-tuple-element.262), channel_id=1, source_target_pairs={{0,4},{1,5},{2,6},{3,7},{4,0},{5,1},{6,2},{7,3},{8,12},{9,13},{10,... | collective-permute-start | bytes 294920 | tf_op jit(solution)/shard_map/ppermute | solution.py:1004
  71.3 9.5 %collective-permute-start.21 = (bf16[2,48,1152]{2,1,0:T(8,128)(2,1)S(1)}, bf16[2,48,1152]{2,1,0:T(8,128)(2,1)S(1)}, u32[]{:S(2)}, u32[]{:S(2)}) collective-permute-start(bf16[2,48,1152]{2,1,0:T(8,128)(2,1)S(1)} %get-tuple-element.258), channel_id=1, source_target_pairs={{0,4},{1,5},{2,6},{3,7},{4,0},{5,1},{6,2},{7,3},{8,12},{9,13},{10,... | collective-permute-start | bytes 663560 | tf_op jit(solution)/shard_map/ppermute | solution.py:1004
  74.7 20.4 %collective-permute-start.20 = (bf16[128,768]{1,0:T(8,128)(2,1)S(1)}, bf16[128,768]{1,0:T(8,128)(2,1)S(1)}, u32[]{:S(2)}, u32[]{:S(2)}) collective-permute-start(bf16[128,768]{1,0:T(8,128)(2,1)S(1)} %get-tuple-element.204), channel_id=1, source_target_pairs={{0,1},{1,0},{2,3},{3,2},{4,5},{5,4},{6,7},{7,6},{8,9},{9,8},{10,11... | collective-permute-start | bytes 589832 | tf_op jit(solution)/shard_map/ppermute | solution.py:1103
  76.5 10.6 %collective-permute-start.28 = (bf16[1,48,1536]{2,1,0:T(8,128)(2,1)S(1)}, bf16[1,48,1536]{2,1,0:T(8,128)(2,1)S(1)}, u32[]{:S(2)}, u32[]{:S(2)}) collective-permute-start(bf16[1,48,1536]{2,1,0:T(8,128)(2,1)S(1)} %add_convert_fusion.19), channel_id=1, source_target_pairs={{0,2},{1,3},{2,0},{3,1},{4,6},{5,7},{6,4},{7,5},{8,10},{9,11},{10,... | collective-permute-start | bytes 442376 | tf_op jit(solution)/shard_map/ppermute | solution.py:1004
  78.2 13.1 %collective-permute-start.27 = (bf16[1,192,384]{2,1,0:T(8,128)(2,1)S(1)}, bf16[1,192,384]{2,1,0:T(8,128)(2,1)S(1)}, u32[]{:S(2)}, u32[]{:S(2)}) collective-permute-start(bf16[1,192,384]{2,1,0:T(8,128)(2,1)S(1)} %add_convert_fusion.18), channel_id=1, source_target_pairs={{0,8},{1,9},{2,10},{3,11},{4,12},{5,13},{6,14},{7,15},{8,0},{9,1},... | collective-permute-start | bytes 442376 | tf_op jit(solution)/shard_map/ppermute | solution.py:1004
  80.8 11.0 %collective-permute-start.26 = (bf16[1,64,384]{2,1,0:T(8,128)(2,1)S(1)}, bf16[1,64,384]{2,1,0:T(8,128)(2,1)S(1)}, u32[]{:S(2)}, u32[]{:S(2)}) collective-permute-start(bf16[1,64,384]{2,1,0:T(8,128)(2,1)S(1)} %add_convert_fusion.27), channel_id=1, source_target_pairs={{0,8},{1,9},{2,10},{3,11},{4,12},{5,13},{6,14},{7,15},{8,0},{9,1},... | collective-permute-start | bytes 147464 | tf_op jit(solution)/shard_map/ppermute | solution.py:1004
  86.3 6.8 %collective-permute-start.25 = (bf16[1,48,1152]{2,1,0:T(8,128)(2,1)S(1)}, bf16[1,48,1152]{2,1,0:T(8,128)(2,1)S(1)}, u32[]{:S(2)}, u32[]{:S(2)}) collective-permute-start(bf16[1,48,1152]{2,1,0:T(8,128)(2,1)S(1)} %add_convert_fusion.21), channel_id=1, source_target_pairs={{0,8},{1,9},{2,10},{3,11},{4,12},{5,13},{6,14},{7,15},{8,0},{9,1},... | collective-permute-start | bytes 331784 | tf_op jit(solution)/shard_map/ppermute | solution.py:1004
  87.2 8.8 %collective-permute-start.32 = (bf16[48,1536]{1,0:T(8,128)(2,1)S(1)}, bf16[48,1536]{1,0:T(8,128)(2,1)S(1)}, u32[]{:S(2)}, u32[]{:S(2)}) collective-permute-start(bf16[48,1536]{1,0:T(8,128)(2,1)S(1)} %fusion.refs_0_), channel_id=1, source_target_pairs={{0,1},{1,0},{2,3},{3,2},{4,5},{5,4},{6,7},{7,6},{8,9},{9,8},{10,11... | collective-permute-start | bytes 442376 | tf_op jit(solution)/shard_map/ppermute | solution.py:1021
  91.3 6.2 %collective-permute-start.31 = (bf16[192,384]{1,0:T(8,128)(2,1)S(1)}, bf16[192,384]{1,0:T(8,128)(2,1)S(1)}, u32[]{:S(2)}, u32[]{:S(2)}) collective-permute-start(bf16[192,384]{1,0:T(8,128)(2,1)S(1)} %fusion.1.refs_0_), channel_id=1, source_target_pairs={{0,1},{1,0},{2,3},{3,2},{4,5},{5,4},{6,7},{7,6},{8,9},{9,8},{10,11... | collective-permute-start | bytes 442376 | tf_op jit(solution)/shard_map/ppermute | solution.py:1021
  93.1 6.9 %collective-permute-start.33 = (bf16[48,1152]{1,0:T(8,128)(2,1)S(1)}, bf16[48,1152]{1,0:T(8,128)(2,1)S(1)}, u32[]{:S(2)}, u32[]{:S(2)}) collective-permute-start(bf16[48,1152]{1,0:T(8,128)(2,1)S(1)} %fusion.2.refs_0_), channel_id=1, source_target_pairs={{0,1},{1,0},{2,3},{3,2},{4,5},{5,4},{6,7},{7,6},{8,9},{9,8},{10,11... | collective-permute-start | bytes 331784 | tf_op jit(solution)/shard_map/ppermute | solution.py:1021
  93.9 5.3 %collective-permute-start.30 = (bf16[64,384]{1,0:T(8,128)(2,1)S(1)}, bf16[64,384]{1,0:T(8,128)(2,1)S(1)}, u32[]{:S(2)}, u32[]{:S(2)}) collective-permute-start(bf16[64,384]{1,0:T(8,128)(2,1)S(1)} %fusion.3.mine.refs_0_), channel_id=1, source_target_pairs={{0,1},{1,0},{2,3},{3,2},{4,5},{5,4},{6,7},{7,6},{8,9},{9,8},{10,11... | collective-permute-start | bytes 147464 | tf_op jit(solution)/shard_map/ppermute | solution.py:1021
  101.0 4.5 %collective-permute-start.34 = (bf16[48,1152]{1,0:T(8,128)(2,1)S(1)}, bf16[48,1152]{1,0:T(8,128)(2,1)S(1)}, u32[]{:S(2)}, u32[]{:S(2)}) collective-permute-start(bf16[48,1152]{1,0:T(8,128)(2,1)S(1)} %fusion.2.refs_0_), channel_id=1, source_target_pairs={{0,16},{16,0},{1,17},{17,1},{2,18},{18,2},{3,19},{19,3},{4,20},{20... | collective-permute-start | bytes 331784 | tf_op jit(solution)/shard_map/ppermute | solution.py:1071
  101.4 4.1 %collective-permute-start.35 = (bf16[48,1152]{1,0:T(8,128)(2,1)S(1)}, bf16[48,1152]{1,0:T(8,128)(2,1)S(1)}, u32[]{:S(2)}, u32[]{:S(2)}) collective-permute-start(bf16[48,1152]{1,0:T(8,128)(2,1)S(1)} %collective-permute-done.33.refs_1_), channel_id=1, source_target_pairs={{0,16},{16,0},{1,17},{17,1},{2,18},{18,2},{3,19},{19,3},{4,20},{20... | collective-permute-start | bytes 331784 | tf_op jit(solution)/shard_map/ppermute | solution.py:1071
  (10 other events, 24.4 us)

commit v5 on v4

--- a/solution.py
+++ b/solution.py
@@ -311,12 +311,12 @@
 
 
 WAYS = {
-    "u": ("x12y", "yx12"),
-    "d": ("y1x2", "12yx"),
-    "o": ("xy12", "1xy2"),
-    "q": ("yx12", "xy12"),
+    "u": ("xy12", "12yx"),
+    "d": ("yx12", "1yx2"),
+    "o": ("x12y", "yx12"),
+    "q": ("x1y2", "yx12"),
 }
-EVENTS = "UDCIOQudoqudoqYudoqiudoqyudoq+"
+EVENTS = "UDCIOQYudoqudoqhudqoduoqiduoq"
 BITS = {"y": 1, "1": 2, "2": 4}
 
 
@@ -646,7 +646,7 @@
     )
 
 
-def result_kernel(g_mine, g_theirs, middle, small, down, y_mine, y_send, total):
+def result_kernel(g_mine, g_theirs, middle, small, down, x_grad_send, y_mine, send, total):
     core, _, place = where_am_i()
     tiles, _, features = g_mine.shape
     piece = y_mine.shape[0]
@@ -661,17 +661,18 @@
     lax.fori_loop(0, tiles, one_tile, 0)
     present = small[12:13, :]
     y_mine[...] = (total[rows_at(place * piece, piece), :] * present).astype(LOW)
-    y_send[...] = (total[rows_at((1 - place) * piece, piece), :] * present).astype(LOW)
-
-
-def result(g_mine, g_theirs, middle, small, down):
+    send[0] = (total[rows_at((1 - place) * piece, piece), :] * present).astype(LOW)
+    send[1] = x_grad_send[...]
+
+
+def result(g_mine, g_theirs, middle, small, down, x_grad_send):
     length, features = middle.shape
-    part = ((length // 2, features), LOW)
+    piece = length // 2
     return call(
         "result",
         result_kernel,
-        (g_mine, g_theirs, middle, small, down),
-        [part, part],
+        (g_mine, g_theirs, middle, small, down, x_grad_send),
+        [((piece, features), LOW), ((2, piece, features), LOW)],
         [((length, features), SINGLE)],
     )
 
@@ -881,82 +882,133 @@
     )
 
 
-def close_kernel(mine, other, *outs):
-    vec = outs[-1]
-    counts, whole, up, qv = outs[:4]
-    plain = outs[4:-1]
-    _, _, place = where_am_i()
-    rows = mine.shape[0] - 16
-    vec[rows_at(place * 8, 8), :] = mine[rows:, :128].astype(SINGLE)[:8]
-    vec[rows_at((1 - place) * 8, 8), :] = other[rows:, :128].astype(SINGLE)[:8]
+FIRST = ("o", "q", "d", "u")
+
+
+PACK = 384
+
+
+def packed_rows(name, shape):
+    tall, width = shape
+    return (tall - 16 if name == "o" else tall) * (width // PACK)
+
+
+def pack_kernel(*refs):
+    out = refs[-1]
+    first = 0
+    for number, part in enumerate(refs[:-1]):
+        name = FIRST[number // 2]
+        tall = part.shape[0] - (16 if name == "o" else 0)
+        for block in range(part.shape[1] // PACK):
+            out[first : first + tall, :] = part[:tall, block * PACK : (block + 1) * PACK]
+            first += tall
+
+
+def pack(parts):
+    operands = [p for name in FIRST for p in parts[name]]
+    rows = sum(packed_rows(name, p.shape) for name in FIRST for p in parts[name])
+    return call("result", pack_kernel, operands, [((rows, PACK), LOW)])[0]
+
+
+def finale_kernel(*refs):
+    homes, theirs, refs = refs[:3], refs[3], refs[4:]
+    parts = {name: refs[2 * i : 2 * i + 2] for i, name in enumerate(FIRST)}
+    refs = refs[2 * len(FIRST) :]
+    count = (len(refs) - 3) // 2
+    results, held = refs[:count], refs[count : 2 * count]
+    vec, turned, sems = refs[2 * count :]
+    core, _, place = where_am_i()
+    copies = []
+
+    def send(*numbers):
+        for number in numbers:
+            copies.append(pltpu.make_async_copy(held[number], results[number], sems.at[number]))
+            copies[-1].start()
+
+    for number in (0, 1):
+        held[number][place] = homes[number][...]
+        held[number][1 - place] = homes[2][number]
+    send(0, 1)
+    mine, other = parts["o"][:2]
+    half = mine.shape[0] - 16
+    vec[rows_at(place * 8, 8), :] = mine[half:, :128].astype(SINGLE)[:8]
+    vec[rows_at((1 - place) * 8, 8), :] = other[half:, :128].astype(SINGLE)[:8]
     line = vec[12:13, :]
     lane = lax.broadcasted_iota(jnp.int32, line.shape, 1)
     worth = lax.shift_left(jnp.ones_like(lane), lax.rem(lane, DIGITS)).astype(SINGLE)
     first, second = (
-        jnp.sum(jnp.where(lane // DIGITS == half, line * worth, 0.0), axis=1, keepdims=True)
-        for half in (0, 1)
+        jnp.sum(jnp.where(lane // DIGITS == side, line * worth, 0.0), axis=1, keepdims=True)
+        for side in (0, 1)
     )
     total = first + second
+    share = 1.0 / total
+    first_row = 0
+    for number, name in enumerate(FIRST):
+        out = held[2 + number]
+        tall, width = parts[name][0].shape
+        tall = tall - 16 if name == "o" else tall
+        for spot in range(4):
+            side, low = core ^ (spot >> 1), place ^ (spot & 1)
+            for block in range(width // PACK):
+                if spot < 2:
+                    piece = parts[name][spot][:tall, block * PACK : (block + 1) * PACK]
+                else:
+                    piece = theirs[first_row : first_row + tall, :]
+                    first_row += tall
+                piece = piece.astype(SINGLE)
+                if name == "d":
+                    turned[rows_at((side * 2 + low) * tall, tall), :] = piece
+                else:
+                    column = pl.multiple_of(side * width + block * PACK, 128)
+                    out[rows_at(low * tall, tall), pl.ds(column, PACK)] = piece * share
+        if name == "d":
+            out[...] = turned[...].T * share
+        send(2 + number)
+    counts, up, qv, *plain = held[2 + len(FIRST) :]
     spot = lax.broadcasted_iota(jnp.int32, (1, 128), 1)
-    both = jnp.where(spot == 0, first, second).astype(jnp.int32)
-    counts[...] = both[0, :2]
-    whole[...] = jnp.broadcast_to(total, whole.shape)
+    counts[...] = jnp.where(spot == 0, first, second).astype(jnp.int32)[0, : counts.shape[0]]
     width = qv.shape[1]
-    scaled = vec[...] / total
+    scaled = vec[...] * share
     qv[...] = scaled[2:4, :width]
     for number, out in zip((0, 1, 4, 5, 6, 7), plain):
         out[...] = scaled[number, :width]
     up[...] = jnp.concatenate([scaled[8 + part : 9 + part, :width] for part in range(4)], axis=1)[0]
-
-
-def close(mine, other, width):
-    return call(
-        "result",
-        close_kernel,
-        (mine, other),
-        [((2,), jnp.int32), ((8, 128), SINGLE), ((4 * width,), SINGLE), ((2, width), SINGLE)]
-        + [((width,), SINGLE)] * 6,
-        [((16, 128), SINGLE)],
-    )
-
-
-def finish_kernel(whole, *refs, rows, turned):
-    parts, out = refs[:4], refs[4]
-    core, _, place = where_am_i()
-    total = whole[0:1, 0:1]
-    for number, part in enumerate(parts):
-        side, half = core ^ (number >> 1), place ^ (number & 1)
-        if turned:
-            refs[5][rows_at((side * 2 + half) * rows, rows), :] = part[...].astype(SINGLE)
-        else:
-            width = part.shape[1]
-            out[rows_at(half * rows, rows), rows_at(side * width, width)] = (
-                part[:rows, :].astype(SINGLE) / total
-            )
-    if turned:
-        out[...] = refs[5][...].T / total
-
-
-def finish(whole, parts, rows, turned=False):
-    width = parts[0].shape[1]
-    shape = (width, 4 * rows) if turned else (2 * rows, 2 * width)
-    return call(
-        "result",
-        functools.partial(finish_kernel, rows=rows, turned=turned),
-        (whole, *parts),
-        [(shape, SINGLE)],
-        [((4 * rows, width), SINGLE)] * turned,
-    )[0]
-
-
-def home_kernel(mine, other, out):
-    _, _, place = where_am_i()
-    out[place] = mine[...]
-    out[1 - place] = other[...]
-
-
-def home(mine, other):
-    return call("result", home_kernel, (mine, other), [((2,) + mine.shape, LOW)])[0]
+    send(*range(2 + len(FIRST), count))
+    for copy in copies:
+        copy.wait()
+
+
+def finale(homes, theirs, parts, rows):
+    piece, features = homes[0].shape
+    home = jax.ShapeDtypeStruct((2, piece, features), LOW)
+    results = [home, home]
+    for name in FIRST:
+        tall, width = parts[name][0].shape
+        shape = (width, 4 * tall) if name == "d" else (2 * rows, 2 * width)
+        results.append(jax.ShapeDtypeStruct(shape, SINGLE))
+    chunk = 2 * rows
+    results += [
+        jax.ShapeDtypeStruct((2,), jnp.int32),
+        jax.ShapeDtypeStruct((4 * chunk,), SINGLE),
+        jax.ShapeDtypeStruct((2, chunk), SINGLE),
+    ] + [jax.ShapeDtypeStruct((chunk,), SINGLE)] * 6
+    vmem = pl.BlockSpec(memory_space=pltpu.VMEM)
+    tall, width = parts["d"][0].shape
+    operands = [*homes, theirs, *[p for name in FIRST for p in parts[name]]]
+    return pl.pallas_call(
+        finale_kernel,
+        in_specs=[vmem] * len(operands),
+        out_specs=[pl.BlockSpec(memory_space=pl.ANY)] * len(results),
+        out_shape=results,
+        scratch_shapes=[pltpu.VMEM(r.shape, r.dtype) for r in results]
+        + [
+            pltpu.VMEM((16, 128), SINGLE),
+            pltpu.VMEM((4 * tall, width), SINGLE),
+            pltpu.SemaphoreType.DMA((len(results),)),
+        ],
+        compiler_params=pltpu.CompilerParams(vmem_limit_bytes=16 << 20),
+        cost_estimate=pl.CostEstimate(flops=1, bytes_accessed=1, transcendentals=0),
+    )(*operands)
 
 
 def swap_pairs(size, bit):
@@ -1096,42 +1148,16 @@
     other_mine, db1_other = from_core(g_mine), from_core(db1_theirs)
 
     sums = {}
-    done = {}
-    rows = out_weight.shape[0] // groups
-
-    def rows_home(mine, send):
-        other = order.tie(lax.ppermute(send, "seq", pair))
-        both = home(mine, other)
-        order.mark(both)
-        return both[None, None]
-
-    def finish_all():
-        names = [n for n in sums if sums[n].parts is not None and n not in done]
-        mine = order.tie([sums[n].parts for n in names])
-        theirs = [[from_core(p) for p in parts] for parts in mine]
-        for name, here, there in zip(names, mine, theirs):
-            there = order.tie(there)
-            turned = name == "d"
-            done[name] = finish(
-                done["whole"], here + there, 2 * rows if turned else rows // 2, turned
-            )
-            order.mark(done[name])
-
     for event in EVENTS:
-        if event == "y":
-            done["output"] = rows_home(y_mine, y_send)
+        if event == "h":
+            homes = lax.ppermute(order.tie(home_send), "seq", pair)
             continue
         if event == "i":
-            done["input_grad"] = rows_home(x_grad_mine, x_grad_send)
-            continue
-        if event == "+":
-            finish_all()
+            homes = order.tie(homes)
+            order.mark(homes)
             continue
         if event.islower():
             sums[event].step()
-            if event == "o" and sums["o"].parts is not None and "whole" not in done:
-                counts, done["whole"], up_small, qv, *plain = close(*sums["o"].parts, rows)
-                order.mark(done["whole"])
             continue
         name = event.lower()
         if event == "U":
@@ -1154,8 +1180,10 @@
             order.mark(vec)
             continue
         elif event == "Y":
-            y_mine, y_send = result(order.tie(g_mine), g_theirs, middle, small, down_weight)
-            order.mark(y_send)
+            y_mine, home_send = result(
+                order.tie(g_mine), g_theirs, middle, small, down_weight, x_grad_send
+            )
+            order.mark(home_send)
             continue
         elif event == "O":
             parts = grad_rows(
@@ -1168,21 +1196,26 @@
         order.mark(parts[0])
         sums[name] = Sum(order, name, groups, *parts)
 
+    parts = order.tie({name: sums[name].parts for name in FIRST})
+    rows = out_weight.shape[0] // groups // 2
+    output, input_grad, out, qkv, down, up, counts, up_small, qv, *plain = finale(
+        (y_mine, x_grad_mine, homes), from_core(pack(parts)), parts, rows
+    )
     return (
-        done["output"],
-        done["input_grad"],
+        output[None, None],
+        input_grad[None, None],
         counts,
         plain[0],
         plain[1],
-        done["q"],
+        qkv,
         qv,
-        done["o"],
+        out,
         plain[2],
         plain[3],
         plain[4],
-        done["u"],
+        up,
         up_small,
-        done["d"],
+        down,
         plain[5],
     )
 

time: 107 us -> 103 us (0.963)
  Pallas kernels: 32.8 us -> 29 us
  waiting for transfers between devices: 26.6 us -> 28.3 us
  starting transfers between devices: 42.9 us -> 41.2 us
    ppermute x16, starting transfers between devices: 30.2 us -> 22.7 us  [go(): lax.ppermute(send, AXES, partners(self.name, self.stage, self.groups))]
    pallas_call x17 -> x11, Pallas kernels: 30 us -> 23.3 us  [call(): pl.pallas_call(kernel, in_specs=[pl.BlockSpec(memory_space=pl.ANY)] * len...]
    ppermute x16, waiting for transfers between devices: 21.5 us -> 16.7 us  [go(): lax.ppermute(send, AXES, partners(self.name, self.stage, self.groups))]
    ppermute x4, waiting for transfers between devices: 3.25 us -> 6.91 us  [step(): self.flying = lax.ppermute(self.total, 'seq', swap_pairs(2, 1))]
    ppermute x4, starting transfers between devices: 2.23 us -> 5.85 us  [step(): self.flying = lax.ppermute(self.total, 'seq', swap_pairs(2, 1))]
    ppermute x18 -> x11, starting transfers between devices: 4.41 us -> 7.55 us  [from_core(): return lax.ppermute(value, 'src', pair)]
    pallas_call x0 -> x1, Pallas kernels: none -> 2.85 us  [finale(): pl.pallas_call(finale_kernel, in_specs=[vmem] * len(operands), out_specs=...]
    ppermute x18 -> x11, waiting for transfers between devices: 0.38 us -> 3.21 us  [from_core(): return lax.ppermute(value, 'src', pair)]
  transfers between devices with their start and end apart: 42 -> 34, of which waited for: 14 -> 13; matrix products, arithmetic and copies ran while one was open for 2% -> 2% of each run, Pallas kernels for 30% -> 25%
where the time goes in v5:
time: 103 us
  starting transfers between devices  41.2 us (40%)
  Pallas kernels  29 us (28%)
  waiting for transfers between devices  28.3 us (27%)
  between operations  1.7 us (2%)
  other arithmetic  1.66 us (2%)
    pallas_call x11, Pallas kernels, call(): pl.pallas_call(kernel, in_specs=[pl.BlockSpec(memory_space=pl.ANY)] * len...  23.3 us
    ppermute x16, starting transfers between devices, go(): lax.ppermute(send, AXES, partners(self.name, self.stage, self.groups))  22.7 us
    ppermute x16, waiting for transfers between devices, go(): lax.ppermute(send, AXES, partners(self.name, self.stage, self.groups))  16.7 us
    ppermute x11, starting transfers between devices, from_core(): return lax.ppermute(value, 'src', pair)  7.55 us
    ppermute x4, waiting for transfers between devices, step(): self.flying = lax.ppermute(self.total, 'seq', swap_pairs(2, 1))  6.91 us
    ppermute x4, starting transfers between devices, step(): self.flying = lax.ppermute(self.total, 'seq', swap_pairs(2, 1))  5.85 us
    ppermute x11, waiting for transfers between devices, from_core(): return lax.ppermute(value, 'src', pair)  3.21 us
    ppermute x1, starting transfers between devices, body_fast(): lax.ppermute(lax.dynamic_index_in_dim(x_both, 1 - place, 0, keepdims=Fals...  3 us
  transfers between devices with their start and end apart: 34, of which 13 were waited for; matrix products, arithmetic and copies ran while one was open for 2% of the time, Pallas kernels for 25%

profile of v5, /device:TPU:0, one launch (start us, length us, event | category | flops | bytes accessed | tf_op | source)
XLA Modules:
  0.0 102.8 jit_solution(12054717735459973281)
XLA Ops:
  1.6 3.0 %collective-permute-start = (bf16[128,768]{1,0:T(8,128)(2,1)S(1)}, bf16[128,768]{1,0:T(8,128)(2,1)S(1)}, u32[]{:S(2)}, u32[]{:S(2)}) collective-permute-start(bf16[128,768]{1,0:T(8,128)(2,1)S(1)} %dynamic-slice_bitcast_fusion), channel_id=1, source_target_pairs={{0,1},{1,0},{2,3},{3,2},{4,5},{5,4},{6,7},{7,6},{8,9},{9,8},{10,11... | collective-permute-start | bytes 589832 | tf_op jit(solution)/shard_map/ppermute | solution.py:1108
  5.3 2.8 %shard_map.271 = (bf16[128,768]{1,0:T(8,128)(2,1)S(1)}, bf16[128,768]{1,0:T(8,128)(2,1)S(1)}, bf16[128,768]{1,0:T(8,128)(2,1)S(1)}, f32[1,128]{1,0:T(1,128)S(1)}...) custom-call(s32[1,1]{1,0:T(1,128)S(6)} %copy.31.refs_0_, s32[2,128]{1,0:T(2,128)} %bitcast.19, ...), custom_call_target="tpu_custom_call" | custom-call | flops 2000000000 | bytes 1 | tf_op jit(solution)/shard_map/pallas_call | solution.py:456
  8.2 1.3 %collective-permute-done.x_other = bf16[128,768]{1,0:T(8,128)(2,1)S(1)} collective-permute-done((bf16[128,768]{1,0:T(8,128)(2,1)S(1)}, bf16[128,768]{1,0:T(8,128)(2,1)S(1)}, u32[]{:S(2)}, u32[]{:S(2)}) %collective-permute-start) | collective-permute-done | bytes 196640 | tf_op jit(solution)/shard_map/ppermute | solution.py:1108
  9.5 4.2 %shard_map.272 = (bf16[768,3072]{1,0:T(8,128)(2,1)S(1)}, bf16[3072,768]{1,0:T(8,128)(2,1)S(1)}, bf16[256,768]{1,0:T(8,128)(2,1)S(1)}, bf16[9,256,256]{2,1,0:T(8,...) custom-call(bf16[768,3072]{1,0:T(8,128)(2,1)} %up_ref.1, ...), custom_call_target="tpu_custom_call" | custom-call | flops 8000000000 | bytes 1 | tf_op jit(solution)/shard_map/pallas_call | solution.py:383
  14.5 2.7 %shard_map.273 = (bf16[2,256,768]{2,1,0:T(8,128)(2,1)S(1)}, bf16[2,256,768]{2,1,0:T(8,128)(2,1)S(1)}, bf16[256,768]{1,0:T(8,128)(2,1)S(1)}, bf16[256,384]{1,0:T(...) custom-call(bf16[256,768]{1,0:T(8,128)(2,1)S(1)} %get-tuple-element.158.n2.left, ...), custom_call_target="tpu_custom_call" | custom-call | flops 5000000000 | bytes 1 | tf_op jit(solution)/shard_map/pallas_call | solution.py:383
  18.1 3.2 %shard_map.274 = (bf16[2,256,768]{2,1,0:T(8,128)(2,1)S(1)}, bf16[2,256,768]{2,1,0:T(8,128)(2,1)S(1)}, f32[256,768]{1,0:T(8,128)S(1)}, bf16[256,768]{1,0:T(8,128)...) custom-call(bf16[256,768]{1,0:T(8,128)(2,1)S(1)} %get-tuple-element.158.n2.left, ...), custom_call_target="tpu_custom_call" | custom-call | flops 5000000000 | bytes 1 | tf_op jit(solution)/shard_map/pallas_call | solution.py:383
  21.7 2.0 %shard_map.275 = (bf16[8,48,1536]{2,1,0:T(8,128)(2,1)S(1)}, bf16[8,48,1536]{2,1,0:T(8,128)(2,1)S(1)}) custom-call(bf16[256,768]{1,0:T(8,128)(2,1)S(1)} %get-tuple-element.158.n2.left, bf16[256,768]{1,0:T(8,128)(2,1)S(1)} %collective-permute-done.1.left_other, bf16[2,256,768]{2,1,0:T(8,128)(2,1)S(1)} %get-tuple-element.160.right, ...), custom_call_target="tpu_custom_call" | custom-call | flops 4000000000 | bytes 1 | tf_op jit(solution)/shard_map/pallas_call | solution.py:383
  23.7 2.2 %collective-permute-start.15 = (bf16[8,48,1536]{2,1,0:T(8,128)(2,1)S(1)}, bf16[8,48,1536]{2,1,0:T(8,128)(2,1)S(1)}, u32[]{:S(2)}, u32[]{:S(2)}) collective-permute-start(bf16[8,48,1536]{2,1,0:T(8,128)(2,1)S(1)} %get-tuple-element.162), channel_id=1, source_target_pairs={{0,1},{1,0},{2,3},{3,2},{4,5},{5,4},{6,7},{7,6},{8,9},{9,8},{10,11... | collective-permute-start | bytes 3538952 | tf_op jit(solution)/shard_map/ppermute | solution.py:1056
  25.9 2.3 %shard_map.276 = (bf16[8,192,384]{2,1,0:T(8,128)(2,1)S(1)}, bf16[8,192,384]{2,1,0:T(8,128)(2,1)S(1)}) custom-call(bf16[2,256,768]{2,1,0:T(8,128)(2,1)S(1)} %get-tuple-element.187.g_mine, bf16[2,256,768]{2,1,0:T(8,128)(2,1)S(1)} %get-tuple-element.152.g_theirs, bf16[2,256,768]{2,1,0:T(8,128)(2,1)S(1)} %collective-permute-done.5.other_mine, ...), custom_call_target="tpu_custom_call" | custom-call | flops 1 | bytes 1 | tf_op jit(solution)/shard_map/pallas_call | solution.py:383
  28.2 1.4 %collective-permute-start.14 = (bf16[8,192,384]{2,1,0:T(8,128)(2,1)S(1)}, bf16[8,192,384]{2,1,0:T(8,128)(2,1)S(1)}, u32[]{:S(2)}, u32[]{:S(2)}) collective-permute-start(bf16[8,192,384]{2,1,0:T(8,128)(2,1)S(1)} %get-tuple-element.168), channel_id=1, source_target_pairs={{0,2},{1,3},{2,0},{3,1},{4,6},{5,7},{6,4},{7,5},{8,10},{9,11},{10,... | collective-permute-start | bytes 3538952 | tf_op jit(solution)/shard_map/ppermute | solution.py:1056
  29.6 3.4 %shard_map.277 = (bf16[256,1152]{1,0:T(8,128)(2,1)S(1)}, bf16[256,1152]{1,0:T(8,128)(2,1)S(1)}, f32[16,768]{1,0:T(8,128)S(1)}) custom-call(bf16[9,256,256]{2,1,0:T(8,128)(2,1)S(1)} %get-tuple-element.169.qkv, bf16[3,1024,256]{2,1,0:T(8,128)(2,1)S(1)} %get-tuple-element.170.probs, bf16[256,768]{1,0:T(8,128)(2,1)S(1)} %get-tuple-element.171.db1.right, ...), custom_call_target="tpu_custom_call" | custom-call | flops 1 | bytes 1 | tf_op jit(solution)/shard_map/pallas_call | solution.py:383
  33.6 1.6 %shard_map.278 = (bf16[128,768]{1,0:T(8,128)(2,1)S(1)}, bf16[128,768]{1,0:T(8,128)(2,1)S(1)}, f32[16,768]{1,0:T(8,128)S(1)}) custom-call(bf16[128,768]{1,0:T(8,128)(2,1)S(1)} %get-tuple-element.175.x_mine, bf16[128,768]{1,0:T(8,128)(2,1)S(1)} %collective-permute-done.x_other, f32[16,768]{1,0:T(8,128)S(1)} %get-tuple-element.129.small, ...), custom_call_target="tpu_custom_call" | custom-call | flops 1 | bytes 1 | tf_op jit(solution)/shard_map/pallas_call | solution.py:383
  38.8 1.9 %collective-permute-start.12 = (bf16[8,48,1152]{2,1,0:T(8,128)(2,1)S(1)}, bf16[8,48,1152]{2,1,0:T(8,128)(2,1)S(1)}, u32[]{:S(2)}, u32[]{:S(2)}) collective-permute-start(bf16[8,48,1152]{2,1,0:T(8,128)(2,1)S(1)} %get-tuple-element.186), channel_id=1, source_target_pairs={{0,1},{1,0},{2,3},{3,2},{4,5},{5,4},{6,7},{7,6},{8,9},{9,8},{10,11... | collective-permute-start | bytes 2654216 | tf_op jit(solution)/shard_map/ppermute | solution.py:1056
  40.7 1.8 %shard_map.281 = (bf16[128,768]{1,0:T(8,128)(2,1)S(1)}, bf16[2,128,768]{2,1,0:T(8,128)(2,1)S(1)}) custom-call(bf16[2,256,768]{2,1,0:T(8,128)(2,1)S(1)} %get-tuple-element.187.g_mine, bf16[2,256,768]{2,1,0:T(8,128)(2,1)S(1)} %get-tuple-element.152.g_theirs, f32[256,768]{1,0:T(8,128)S(1)} %get-tuple-element.146.middle, ...), custom_call_target="tpu_custom_call" | custom-call | flops 1 | bytes 1 | tf_op jit(solution)/shard_map/pallas_call | solution.py:383
  43.6 5.4 %collective-permute-done.14 = bf16[8,192,384]{2,1,0:T(8,128)(2,1)S(1)} collective-permute-done((bf16[8,192,384]{2,1,0:T(8,128)(2,1)S(1)}, bf16[8,192,384]{2,1,0:T(8,128)(2,1)S(1)}, u32[]{:S(2)}, u32[]{:S(2)}) %collective-permute-start.14) | collective-permute-done | bytes 1179680 | tf_op jit(solution)/shard_map/ppermute | solution.py:1056
  50.8 3.7 %collective-permute-done.12 = bf16[8,48,1152]{2,1,0:T(8,128)(2,1)S(1)} collective-permute-done((bf16[8,48,1152]{2,1,0:T(8,128)(2,1)S(1)}, bf16[8,48,1152]{2,1,0:T(8,128)(2,1)S(1)}, u32[]{:S(2)}, u32[]{:S(2)}) %collective-permute-start.12) | collective-permute-done | bytes 884768 | tf_op jit(solution)/shard_map/ppermute | solution.py:1056
  54.7 1.6 %collective-permute-start.16 = (bf16[4,48,1152]{2,1,0:T(8,128)(2,1)S(1)}, bf16[4,48,1152]{2,1,0:T(8,128)(2,1)S(1)}, u32[]{:S(2)}, u32[]{:S(2)}) collective-permute-start(bf16[4,48,1152]{2,1,0:T(8,128)(2,1)S(1)} %get-tuple-element.245), channel_id=1, source_target_pairs={{0,4},{1,5},{2,6},{3,7},{4,0},{5,1},{6,2},{7,3},{8,12},{9,13},{10,... | collective-permute-start | bytes 1327112 | tf_op jit(solution)/shard_map/ppermute | solution.py:1056
  56.3 5.3 %collective-permute-done.19 = bf16[4,48,1536]{2,1,0:T(8,128)(2,1)S(1)} collective-permute-done((bf16[4,48,1536]{2,1,0:T(8,128)(2,1)S(1)}, bf16[4,48,1536]{2,1,0:T(8,128)(2,1)S(1)}, u32[]{:S(2)}, u32[]{:S(2)}) %collective-permute-start.19) | collective-permute-done | bytes 589856 | tf_op jit(solution)/shard_map/ppermute | solution.py:1056
  64.1 2.3 %collective-permute-start.25 = (bf16[2,64,384]{2,1,0:T(8,128)(2,1)S(1)}, bf16[2,64,384]{2,1,0:T(8,128)(2,1)S(1)}, u32[]{:S(2)}, u32[]{:S(2)}) collective-permute-start(bf16[2,64,384]{2,1,0:T(8,128)(2,1)S(1)} %get-tuple-element.256), channel_id=1, source_target_pairs={{0,8},{1,9},{2,10},{3,11},{4,12},{5,13},{6,14},{7,15},{8,0},{9,1},... | collective-permute-start | bytes 294920 | tf_op jit(solution)/shard_map/ppermute | solution.py:1056
  66.5 2.5 %collective-permute-start.21 = (bf16[2,48,1152]{2,1,0:T(8,128)(2,1)S(1)}, bf16[2,48,1152]{2,1,0:T(8,128)(2,1)S(1)}, u32[]{:S(2)}, u32[]{:S(2)}) collective-permute-start(bf16[2,48,1152]{2,1,0:T(8,128)(2,1)S(1)} %get-tuple-element.252), channel_id=1, source_target_pairs={{0,2},{1,3},{2,0},{3,1},{4,6},{5,7},{6,4},{7,5},{8,10},{9,11},{10,... | collective-permute-start | bytes 663560 | tf_op jit(solution)/shard_map/ppermute | solution.py:1056
  69.1 2.0 %collective-permute-start.27 = (bf16[1,48,1536]{2,1,0:T(8,128)(2,1)S(1)}, bf16[1,48,1536]{2,1,0:T(8,128)(2,1)S(1)}, u32[]{:S(2)}, u32[]{:S(2)}) collective-permute-start(bf16[1,48,1536]{2,1,0:T(8,128)(2,1)S(1)} %add_convert_fusion.19), channel_id=1, source_target_pairs={{0,8},{1,9},{2,10},{3,11},{4,12},{5,13},{6,14},{7,15},{8,0},{9,1},... | collective-permute-start | bytes 442376 | tf_op jit(solution)/shard_map/ppermute | solution.py:1056
  71.1 2.0 %collective-permute-start.20 = (bf16[2,128,768]{2,1,0:T(8,128)(2,1)S(1)}, bf16[2,128,768]{2,1,0:T(8,128)(2,1)S(1)}, u32[]{:S(2)}, u32[]{:S(2)}) collective-permute-start(bf16[2,128,768]{2,1,0:T(8,128)(2,1)S(1)} %get-tuple-element.204), channel_id=1, source_target_pairs={{0,1},{1,0},{2,3},{3,2},{4,5},{5,4},{6,7},{7,6},{8,9},{9,8},{10,11... | collective-permute-start | bytes 1179656 | tf_op jit(solution)/shard_map/ppermute | solution.py:1153
  73.1 1.5 %collective-permute-start.28 = (bf16[1,192,384]{2,1,0:T(8,128)(2,1)S(1)}, bf16[1,192,384]{2,1,0:T(8,128)(2,1)S(1)}, u32[]{:S(2)}, u32[]{:S(2)}) collective-permute-start(bf16[1,192,384]{2,1,0:T(8,128)(2,1)S(1)} %add_convert_fusion.18), channel_id=1, source_target_pairs={{0,8},{1,9},{2,10},{3,11},{4,12},{5,13},{6,14},{7,15},{8,0},{9,1},... | collective-permute-start | bytes 442376 | tf_op jit(solution)/shard_map/ppermute | solution.py:1056
  76.5 1.6 %collective-permute-start.26 = (bf16[1,64,384]{2,1,0:T(8,128)(2,1)S(1)}, bf16[1,64,384]{2,1,0:T(8,128)(2,1)S(1)}, u32[]{:S(2)}, u32[]{:S(2)}) collective-permute-start(bf16[1,64,384]{2,1,0:T(8,128)(2,1)S(1)} %add_convert_fusion.26), channel_id=1, source_target_pairs={{0,2},{1,3},{2,0},{3,1},{4,6},{5,7},{6,4},{7,5},{8,10},{9,11},{10,... | collective-permute-start | bytes 147464 | tf_op jit(solution)/shard_map/ppermute | solution.py:1056
  79.4 3.7 %collective-permute-start.29 = (bf16[192,384]{1,0:T(8,128)(2,1)S(1)}, bf16[192,384]{1,0:T(8,128)(2,1)S(1)}, u32[]{:S(2)}, u32[]{:S(2)}) collective-permute-start(bf16[192,384]{1,0:T(8,128)(2,1)S(1)} %fusion.refs_4_.refs_8_), channel_id=1, source_target_pairs={{0,1},{1,0},{2,3},{3,2},{4,5},{5,4},{6,7},{7,6},{8,9},{9,8},{10,11... | collective-permute-start | bytes 442376 | tf_op jit(solution)/shard_map/ppermute | solution.py:1073
  83.7 1.7 %collective-permute-start.32 = (bf16[48,1152]{1,0:T(8,128)(2,1)S(1)}, bf16[48,1152]{1,0:T(8,128)(2,1)S(1)}, u32[]{:S(2)}, u32[]{:S(2)}) collective-permute-start(bf16[48,1152]{1,0:T(8,128)(2,1)S(1)} %fusion.2.refs_2_.refs_6_), channel_id=1, source_target_pairs={{0,1},{1,0},{2,3},{3,2},{4,5},{5,4},{6,7},{7,6},{8,9},{9,8},{10,11... | collective-permute-start | bytes 331784 | tf_op jit(solution)/shard_map/ppermute | solution.py:1073
  85.8 2.1 %collective-permute-done.29.refs_5_.refs_9_ = bf16[192,384]{1,0:T(8,128)(2,1)S(1)} collective-permute-done((bf16[192,384]{1,0:T(8,128)(2,1)S(1)}, bf16[192,384]{1,0:T(8,128)(2,1)S(1)}, u32[]{:S(2)}, u32[]{:S(2)}) %collective-permute-start.29) | collective-permute-done | bytes 147488 | tf_op jit(solution)/shard_map/ppermute | solution.py:1073
  87.9 3.1 %collective-permute-done.31.refs_7_.refs_11_ = bf16[48,1536]{1,0:T(8,128)(2,1)S(1)} collective-permute-done((bf16[48,1536]{1,0:T(8,128)(2,1)S(1)}, bf16[48,1536]{1,0:T(8,128)(2,1)S(1)}, u32[]{:S(2)}, u32[]{:S(2)}) %collective-permute-start.31) | collective-permute-done | bytes 147488 | tf_op jit(solution)/shard_map/ppermute | solution.py:1073
  91.0 1.7 %collective-permute-done.30.refs_1_.refs_5_ = bf16[64,384]{1,0:T(8,128)(2,1)S(1)} collective-permute-done((bf16[64,384]{1,0:T(8,128)(2,1)S(1)}, bf16[64,384]{1,0:T(8,128)(2,1)S(1)}, u32[]{:S(2)}, u32[]{:S(2)}) %collective-permute-start.30) | collective-permute-done | bytes 49184 | tf_op jit(solution)/shard_map/ppermute | solution.py:1073
  92.8 5.0 %collective-permute-start.33 = (bf16[1152,384]{1,0:T(8,128)(2,1)S(1)}, bf16[1152,384]{1,0:T(8,128)(2,1)S(1)}, u32[]{:S(2)}, u32[]{:S(2)}) collective-permute-start(bf16[1152,384]{1,0:T(8,128)(2,1)S(1)} %shard_map.282), channel_id=1, source_target_pairs={{0,16},{16,0},{1,17},{17,1},{2,18},{18,2},{3,19},{19,3},{4,20},{20... | collective-permute-start | bytes 2654216 | tf_op jit(solution)/shard_map/ppermute | solution.py:1123
  97.7 2.1 %collective-permute-done.33.refs_3_ = bf16[1152,384]{1,0:T(8,128)(2,1)S(1)} collective-permute-done((bf16[1152,384]{1,0:T(8,128)(2,1)S(1)}, bf16[1152,384]{1,0:T(8,128)(2,1)S(1)}, u32[]{:S(2)}, u32[]{:S(2)}) %collective-permute-start.33) | collective-permute-done | bytes 884768 | tf_op jit(solution)/shard_map/ppermute | solution.py:1123
  99.8 2.8 %shard_map.283 = (bf16[2,128,768]{2,1,0:T(8,128)(2,1)}, bf16[2,128,768]{2,1,0:T(8,128)(2,1)}, f32[96,768]{1,0:T(8,128)}, f32[96,2304]{1,0:T(8,128)}, f32[384,768...) custom-call(bf16[128,768]{1,0:T(8,128)(2,1)S(1)} %get-tuple-element., ...), custom_call_target="tpu_custom_call" | custom-call | flops 1 | bytes 1 | tf_op jit(solution)/shard_map/pallas_call | solution.py:998
  (66 shorter events, 17.1 us)
Async XLA Ops:
  1.6 7.9 %collective-permute-start = (bf16[128,768]{1,0:T(8,128)(2,1)S(1)}, bf16[128,768]{1,0:T(8,128)(2,1)S(1)}, u32[]{:S(2)}, u32[]{:S(2)}) collective-permute-start(bf16[128,768]{1,0:T(8,128)(2,1)S(1)} %dynamic-slice_bitcast_fusion), channel_id=1, source_target_pairs={{0,1},{1,0},{2,3},{3,2},{4,5},{5,4},{6,7},{7,6},{8,9},{9,8},{10,11... | collective-permute-start | bytes 589832 | tf_op jit(solution)/shard_map/ppermute | solution.py:1108
  8.1 6.4 %collective-permute-start.4 = (bf16[128,768]{1,0:T(8,128)(2,1)S(1)}, bf16[128,768]{1,0:T(8,128)(2,1)S(1)}, u32[]{:S(2)}, u32[]{:S(2)}) collective-permute-start(bf16[128,768]{1,0:T(8,128)(2,1)S(1)} %get-tuple-element.136), channel_id=1, source_target_pairs={{0,1},{1,0},{2,3},{3,2},{4,5},{5,4},{6,7},{7,6},{8,9},{9,8},{10,11... | collective-permute-start | bytes 589832 | tf_op jit(solution)/shard_map/ppermute | solution.py:1119
  13.7 4.1 %collective-permute-start.2 = (bf16[256,768]{1,0:T(8,128)(2,1)S(1)}, bf16[256,768]{1,0:T(8,128)(2,1)S(1)}, u32[]{:S(2)}, u32[]{:S(2)}) collective-permute-start(bf16[256,768]{1,0:T(8,128)(2,1)S(1)} %get-tuple-element.183.left), channel_id=1, source_target_pairs={{0,16},{16,0},{1,17},{17,1},{2,18},{18,2},{3,19},{19,3},{4,20},{20... | collective-permute-start | bytes 1179656 | tf_op jit(solution)/shard_map/ppermute | solution.py:1123
  13.8 4.3 %collective-permute-start.3 = (bf16[256,768]{1,0:T(8,128)(2,1)S(1)}, bf16[256,768]{1,0:T(8,128)(2,1)S(1)}, u32[]{:S(2)}, u32[]{:S(2)}) collective-permute-start(bf16[256,768]{1,0:T(8,128)(2,1)S(1)} %get-tuple-element.179.left), channel_id=1, source_target_pairs={{0,16},{16,0},{1,17},{17,1},{2,18},{18,2},{3,19},{19,3},{4,20},{20... | collective-permute-start | bytes 1179656 | tf_op jit(solution)/shard_map/ppermute | solution.py:1123
  14.3 3.8 %collective-permute-start.1 = (bf16[256,768]{1,0:T(8,128)(2,1)S(1)}, bf16[256,768]{1,0:T(8,128)(2,1)S(1)}, u32[]{:S(2)}, u32[]{:S(2)}) collective-permute-start(bf16[256,768]{1,0:T(8,128)(2,1)S(1)} %get-tuple-element.158.n2.left), channel_id=1, source_target_pairs={{0,16},{16,0},{1,17},{17,1},{2,18},{18,2},{3,19},{19,3},{4,20},{20... | collective-permute-start | bytes 1179656 | tf_op jit(solution)/shard_map/ppermute | solution.py:1123
  17.2 4.5 %collective-permute-start.6 = (bf16[2,256,768]{2,1,0:T(8,128)(2,1)S(1)}, bf16[2,256,768]{2,1,0:T(8,128)(2,1)S(1)}, u32[]{:S(2)}, u32[]{:S(2)}) collective-permute-start(bf16[2,256,768]{2,1,0:T(8,128)(2,1)S(1)} %get-tuple-element.150), channel_id=1, source_target_pairs={{0,16},{16,0},{1,17},{17,1},{2,18},{18,2},{3,19},{19,3},{4,20},{20... | collective-permute-start | bytes 2359304 | tf_op jit(solution)/shard_map/ppermute | solution.py:1123
  17.5 4.2 %collective-permute-start.8 = (bf16[2,256,768]{2,1,0:T(8,128)(2,1)S(1)}, bf16[2,256,768]{2,1,0:T(8,128)(2,1)S(1)}, u32[]{:S(2)}, u32[]{:S(2)}) collective-permute-start(bf16[2,256,768]{2,1,0:T(8,128)(2,1)S(1)} %get-tuple-element.152.g_theirs), channel_id=1, source_target_pairs={{0,16},{16,0},{1,17},{17,1},{2,18},{18,2},{3,19},{19,3},{4,20},{20... | collective-permute-start | bytes 2359304 | tf_op jit(solution)/shard_map/ppermute | solution.py:1123
  17.8 3.9 %collective-permute-start.7 = (bf16[256,384]{1,0:T(8,128)(2,1)S(1)}, bf16[256,384]{1,0:T(8,128)(2,1)S(1)}, u32[]{:S(2)}, u32[]{:S(2)}) collective-permute-start(bf16[256,384]{1,0:T(8,128)(2,1)S(1)} %get-tuple-element.151), channel_id=1, source_target_pairs={{0,16},{16,0},{1,17},{17,1},{2,18},{18,2},{3,19},{19,3},{4,20},{20... | collective-permute-start | bytes 589832 | tf_op jit(solution)/shard_map/ppermute | solution.py:1123
  21.3 4.7 %collective-permute-start.5 = (bf16[2,256,768]{2,1,0:T(8,128)(2,1)S(1)}, bf16[2,256,768]{2,1,0:T(8,128)(2,1)S(1)}, u32[]{:S(2)}, u32[]{:S(2)}) collective-permute-start(bf16[2,256,768]{2,1,0:T(8,128)(2,1)S(1)} %get-tuple-element.187.g_mine), channel_id=1, source_target_pairs={{0,16},{16,0},{1,17},{17,1},{2,18},{18,2},{3,19},{19,3},{4,20},{20... | collective-permute-start | bytes 2359304 | tf_op jit(solution)/shard_map/ppermute | solution.py:1123
  23.7 18.8 %collective-permute-start.15 = (bf16[8,48,1536]{2,1,0:T(8,128)(2,1)S(1)}, bf16[8,48,1536]{2,1,0:T(8,128)(2,1)S(1)}, u32[]{:S(2)}, u32[]{:S(2)}) collective-permute-start(bf16[8,48,1536]{2,1,0:T(8,128)(2,1)S(1)} %get-tuple-element.162), channel_id=1, source_target_pairs={{0,1},{1,0},{2,3},{3,2},{4,5},{5,4},{6,7},{7,6},{8,9},{9,8},{10,11... | collective-permute-start | bytes 3538952 | tf_op jit(solution)/shard_map/ppermute | solution.py:1056
  28.2 20.7 %collective-permute-start.14 = (bf16[8,192,384]{2,1,0:T(8,128)(2,1)S(1)}, bf16[8,192,384]{2,1,0:T(8,128)(2,1)S(1)}, u32[]{:S(2)}, u32[]{:S(2)}) collective-permute-start(bf16[8,192,384]{2,1,0:T(8,128)(2,1)S(1)} %get-tuple-element.168), channel_id=1, source_target_pairs={{0,2},{1,3},{2,0},{3,1},{4,6},{5,7},{6,4},{7,5},{8,10},{9,11},{10,... | collective-permute-start | bytes 3538952 | tf_op jit(solution)/shard_map/ppermute | solution.py:1056
  33.0 4.4 %collective-permute-start.9 = (bf16[256,1152]{1,0:T(8,128)(2,1)S(1)}, bf16[256,1152]{1,0:T(8,128)(2,1)S(1)}, u32[]{:S(2)}, u32[]{:S(2)}) collective-permute-start(bf16[256,1152]{1,0:T(8,128)(2,1)S(1)} %get-tuple-element.172.dp_theirs), channel_id=1, source_target_pairs={{0,16},{16,0},{1,17},{17,1},{2,18},{18,2},{3,19},{19,3},{4,20},{20... | collective-permute-start | bytes 1769480 | tf_op jit(solution)/shard_map/ppermute | solution.py:1123
  37.2 12.2 %collective-permute-start.13 = (bf16[8,64,384]{2,1,0:T(8,128)(2,1)S(1)}, bf16[8,64,384]{2,1,0:T(8,128)(2,1)S(1)}, u32[]{:S(2)}, u32[]{:S(2)}) collective-permute-start(bf16[8,64,384]{2,1,0:T(8,128)(2,1)S(1)} %get-tuple-element.181), channel_id=1, source_target_pairs={{0,1},{1,0},{2,3},{3,2},{4,5},{5,4},{6,7},{7,6},{8,9},{9,8},{10,11... | collective-permute-start | bytes 1179656 | tf_op jit(solution)/shard_map/ppermute | solution.py:1056
  38.8 15.7 %collective-permute-start.12 = (bf16[8,48,1152]{2,1,0:T(8,128)(2,1)S(1)}, bf16[8,48,1152]{2,1,0:T(8,128)(2,1)S(1)}, u32[]{:S(2)}, u32[]{:S(2)}) collective-permute-start(bf16[8,48,1152]{2,1,0:T(8,128)(2,1)S(1)} %get-tuple-element.186), channel_id=1, source_target_pairs={{0,1},{1,0},{2,3},{3,2},{4,5},{5,4},{6,7},{7,6},{8,9},{9,8},{10,11... | collective-permute-start | bytes 2654216 | tf_op jit(solution)/shard_map/ppermute | solution.py:1056
  42.8 18.8 %collective-permute-start.19 = (bf16[4,48,1536]{2,1,0:T(8,128)(2,1)S(1)}, bf16[4,48,1536]{2,1,0:T(8,128)(2,1)S(1)}, u32[]{:S(2)}, u32[]{:S(2)}) collective-permute-start(bf16[4,48,1536]{2,1,0:T(8,128)(2,1)S(1)} %get-tuple-element.242), channel_id=1, source_target_pairs={{0,2},{1,3},{2,0},{3,1},{4,6},{5,7},{6,4},{7,5},{8,10},{9,11},{10,... | collective-permute-start | bytes 1769480 | tf_op jit(solution)/shard_map/ppermute | solution.py:1056
  49.3 13.7 %collective-permute-start.18 = (bf16[4,192,384]{2,1,0:T(8,128)(2,1)S(1)}, bf16[4,192,384]{2,1,0:T(8,128)(2,1)S(1)}, u32[]{:S(2)}, u32[]{:S(2)}) collective-permute-start(bf16[4,192,384]{2,1,0:T(8,128)(2,1)S(1)} %get-tuple-element.244), channel_id=1, source_target_pairs={{0,1},{1,0},{2,3},{3,2},{4,5},{5,4},{6,7},{7,6},{8,9},{9,8},{10,11... | collective-permute-start | bytes 1769480 | tf_op jit(solution)/shard_map/ppermute | solution.py:1056
  49.5 14.6 %collective-permute-start.17 = (bf16[4,64,384]{2,1,0:T(8,128)(2,1)S(1)}, bf16[4,64,384]{2,1,0:T(8,128)(2,1)S(1)}, u32[]{:S(2)}, u32[]{:S(2)}) collective-permute-start(bf16[4,64,384]{2,1,0:T(8,128)(2,1)S(1)} %get-tuple-element.254), channel_id=1, source_target_pairs={{0,4},{1,5},{2,6},{3,7},{4,0},{5,1},{6,2},{7,3},{8,12},{9,13},{10,... | collective-permute-start | bytes 589832 | tf_op jit(solution)/shard_map/ppermute | solution.py:1056
  54.7 11.7 %collective-permute-start.16 = (bf16[4,48,1152]{2,1,0:T(8,128)(2,1)S(1)}, bf16[4,48,1152]{2,1,0:T(8,128)(2,1)S(1)}, u32[]{:S(2)}, u32[]{:S(2)}) collective-permute-start(bf16[4,48,1152]{2,1,0:T(8,128)(2,1)S(1)} %get-tuple-element.245), channel_id=1, source_target_pairs={{0,4},{1,5},{2,6},{3,7},{4,0},{5,1},{6,2},{7,3},{8,12},{9,13},{10,... | collective-permute-start | bytes 1327112 | tf_op jit(solution)/shard_map/ppermute | solution.py:1056
  61.8 7.3 %collective-permute-start.23 = (bf16[2,48,1536]{2,1,0:T(8,128)(2,1)S(1)}, bf16[2,48,1536]{2,1,0:T(8,128)(2,1)S(1)}, u32[]{:S(2)}, u32[]{:S(2)}) collective-permute-start(bf16[2,48,1536]{2,1,0:T(8,128)(2,1)S(1)} %get-tuple-element.248), channel_id=1, source_target_pairs={{0,4},{1,5},{2,6},{3,7},{4,0},{5,1},{6,2},{7,3},{8,12},{9,13},{10,... | collective-permute-start | bytes 884744 | tf_op jit(solution)/shard_map/ppermute | solution.py:1056
  63.2 9.9 %collective-permute-start.22 = (bf16[2,192,384]{2,1,0:T(8,128)(2,1)S(1)}, bf16[2,192,384]{2,1,0:T(8,128)(2,1)S(1)}, u32[]{:S(2)}, u32[]{:S(2)}) collective-permute-start(bf16[2,192,384]{2,1,0:T(8,128)(2,1)S(1)} %get-tuple-element.250), channel_id=1, source_target_pairs={{0,4},{1,5},{2,6},{3,7},{4,0},{5,1},{6,2},{7,3},{8,12},{9,13},{10,... | collective-permute-start | bytes 884744 | tf_op jit(solution)/shard_map/ppermute | solution.py:1056
  64.1 12.3 %collective-permute-start.25 = (bf16[2,64,384]{2,1,0:T(8,128)(2,1)S(1)}, bf16[2,64,384]{2,1,0:T(8,128)(2,1)S(1)}, u32[]{:S(2)}, u32[]{:S(2)}) collective-permute-start(bf16[2,64,384]{2,1,0:T(8,128)(2,1)S(1)} %get-tuple-element.256), channel_id=1, source_target_pairs={{0,8},{1,9},{2,10},{3,11},{4,12},{5,13},{6,14},{7,15},{8,0},{9,1},... | collective-permute-start | bytes 294920 | tf_op jit(solution)/shard_map/ppermute | solution.py:1056
  66.5 8.9 %collective-permute-start.21 = (bf16[2,48,1152]{2,1,0:T(8,128)(2,1)S(1)}, bf16[2,48,1152]{2,1,0:T(8,128)(2,1)S(1)}, u32[]{:S(2)}, u32[]{:S(2)}) collective-permute-start(bf16[2,48,1152]{2,1,0:T(8,128)(2,1)S(1)} %get-tuple-element.252), channel_id=1, source_target_pairs={{0,2},{1,3},{2,0},{3,1},{4,6},{5,7},{6,4},{7,5},{8,10},{9,11},{10,... | collective-permute-start | bytes 663560 | tf_op jit(solution)/shard_map/ppermute | solution.py:1056
  69.1 14.0 %collective-permute-start.27 = (bf16[1,48,1536]{2,1,0:T(8,128)(2,1)S(1)}, bf16[1,48,1536]{2,1,0:T(8,128)(2,1)S(1)}, u32[]{:S(2)}, u32[]{:S(2)}) collective-permute-start(bf16[1,48,1536]{2,1,0:T(8,128)(2,1)S(1)} %add_convert_fusion.19), channel_id=1, source_target_pairs={{0,8},{1,9},{2,10},{3,11},{4,12},{5,13},{6,14},{7,15},{8,0},{9,1},... | collective-permute-start | bytes 442376 | tf_op jit(solution)/shard_map/ppermute | solution.py:1056
  71.1 14.7 %collective-permute-start.20 = (bf16[2,128,768]{2,1,0:T(8,128)(2,1)S(1)}, bf16[2,128,768]{2,1,0:T(8,128)(2,1)S(1)}, u32[]{:S(2)}, u32[]{:S(2)}) collective-permute-start(bf16[2,128,768]{2,1,0:T(8,128)(2,1)S(1)} %get-tuple-element.204), channel_id=1, source_target_pairs={{0,1},{1,0},{2,3},{3,2},{4,5},{5,4},{6,7},{7,6},{8,9},{9,8},{10,11... | collective-permute-start | bytes 1179656 | tf_op jit(solution)/shard_map/ppermute | solution.py:1153
  73.1 6.2 %collective-permute-start.28 = (bf16[1,192,384]{2,1,0:T(8,128)(2,1)S(1)}, bf16[1,192,384]{2,1,0:T(8,128)(2,1)S(1)}, u32[]{:S(2)}, u32[]{:S(2)}) collective-permute-start(bf16[1,192,384]{2,1,0:T(8,128)(2,1)S(1)} %add_convert_fusion.18), channel_id=1, source_target_pairs={{0,8},{1,9},{2,10},{3,11},{4,12},{5,13},{6,14},{7,15},{8,0},{9,1},... | collective-permute-start | bytes 442376 | tf_op jit(solution)/shard_map/ppermute | solution.py:1056
  75.4 8.2 %collective-permute-start.24 = (bf16[1,48,1152]{2,1,0:T(8,128)(2,1)S(1)}, bf16[1,48,1152]{2,1,0:T(8,128)(2,1)S(1)}, u32[]{:S(2)}, u32[]{:S(2)}) collective-permute-start(bf16[1,48,1152]{2,1,0:T(8,128)(2,1)S(1)} %add_convert_fusion.21), channel_id=1, source_target_pairs={{0,8},{1,9},{2,10},{3,11},{4,12},{5,13},{6,14},{7,15},{8,0},{9,1},... | collective-permute-start | bytes 331784 | tf_op jit(solution)/shard_map/ppermute | solution.py:1056
  76.5 6.8 %collective-permute-start.26 = (bf16[1,64,384]{2,1,0:T(8,128)(2,1)S(1)}, bf16[1,64,384]{2,1,0:T(8,128)(2,1)S(1)}, u32[]{:S(2)}, u32[]{:S(2)}) collective-permute-start(bf16[1,64,384]{2,1,0:T(8,128)(2,1)S(1)} %add_convert_fusion.26), channel_id=1, source_target_pairs={{0,2},{1,3},{2,0},{3,1},{4,6},{5,7},{6,4},{7,5},{8,10},{9,11},{10,... | collective-permute-start | bytes 147464 | tf_op jit(solution)/shard_map/ppermute | solution.py:1056
  79.4 8.4 %collective-permute-start.29 = (bf16[192,384]{1,0:T(8,128)(2,1)S(1)}, bf16[192,384]{1,0:T(8,128)(2,1)S(1)}, u32[]{:S(2)}, u32[]{:S(2)}) collective-permute-start(bf16[192,384]{1,0:T(8,128)(2,1)S(1)} %fusion.refs_4_.refs_8_), channel_id=1, source_target_pairs={{0,1},{1,0},{2,3},{3,2},{4,5},{5,4},{6,7},{7,6},{8,9},{9,8},{10,11... | collective-permute-start | bytes 442376 | tf_op jit(solution)/shard_map/ppermute | solution.py:1073
  83.2 7.8 %collective-permute-start.31 = (bf16[48,1536]{1,0:T(8,128)(2,1)S(1)}, bf16[48,1536]{1,0:T(8,128)(2,1)S(1)}, u32[]{:S(2)}, u32[]{:S(2)}) collective-permute-start(bf16[48,1536]{1,0:T(8,128)(2,1)S(1)} %fusion.1.refs_6_.refs_10_), channel_id=1, source_target_pairs={{0,1},{1,0},{2,3},{3,2},{4,5},{5,4},{6,7},{7,6},{8,9},{9,8},{10,11... | collective-permute-start | bytes 442376 | tf_op jit(solution)/shard_map/ppermute | solution.py:1073
  83.7 9.0 %collective-permute-start.32 = (bf16[48,1152]{1,0:T(8,128)(2,1)S(1)}, bf16[48,1152]{1,0:T(8,128)(2,1)S(1)}, u32[]{:S(2)}, u32[]{:S(2)}) collective-permute-start(bf16[48,1152]{1,0:T(8,128)(2,1)S(1)} %fusion.2.refs_2_.refs_6_), channel_id=1, source_target_pairs={{0,1},{1,0},{2,3},{3,2},{4,5},{5,4},{6,7},{7,6},{8,9},{9,8},{10,11... | collective-permute-start | bytes 331784 | tf_op jit(solution)/shard_map/ppermute | solution.py:1073
  85.4 7.3 %collective-permute-start.30 = (bf16[64,384]{1,0:T(8,128)(2,1)S(1)}, bf16[64,384]{1,0:T(8,128)(2,1)S(1)}, u32[]{:S(2)}, u32[]{:S(2)}) collective-permute-start(bf16[64,384]{1,0:T(8,128)(2,1)S(1)} %fusion.3.refs_0_.refs_4_), channel_id=1, source_target_pairs={{0,1},{1,0},{2,3},{3,2},{4,5},{5,4},{6,7},{7,6},{8,9},{9,8},{10,11... | collective-permute-start | bytes 147464 | tf_op jit(solution)/shard_map/ppermute | solution.py:1073
  92.8 7.0 %collective-permute-start.33 = (bf16[1152,384]{1,0:T(8,128)(2,1)S(1)}, bf16[1152,384]{1,0:T(8,128)(2,1)S(1)}, u32[]{:S(2)}, u32[]{:S(2)}) collective-permute-start(bf16[1152,384]{1,0:T(8,128)(2,1)S(1)} %shard_map.282), channel_id=1, source_target_pairs={{0,16},{16,0},{1,17},{17,1},{2,18},{18,2},{3,19},{19,3},{4,20},{20... | collective-permute-start | bytes 2654216 | tf_op jit(solution)/shard_map/ppermute | solution.py:1123
  (2 other events, 3.6 us)

commit v6 on v5

--- a/solution.py
+++ b/solution.py
@@ -311,12 +311,12 @@
 
 
 WAYS = {
-    "u": ("xy12", "12yx"),
-    "d": ("yx12", "1yx2"),
-    "o": ("x12y", "yx12"),
+    "u": ("yx12", "12yx"),
+    "d": ("xy12", "1yx2"),
+    "o": ("yx12", "yx12"),
     "q": ("x1y2", "yx12"),
 }
-EVENTS = "UDCIOQYudoqudoqhudqoduoqiduoq"
+EVENTS = "UDCIOQYudoqudqohudqoduoqiduoq"
 BITS = {"y": 1, "1": 2, "2": 4}
 
 
@@ -910,26 +910,54 @@
     return call("result", pack_kernel, operands, [((rows, PACK), LOW)])[0]
 
 
-def finale_kernel(*refs):
-    homes, theirs, refs = refs[:3], refs[3], refs[4:]
-    parts = {name: refs[2 * i : 2 * i + 2] for i, name in enumerate(FIRST)}
+def finish_side(side, parts, share, out, turned, scratch, sems, copies):
+    _, _, place = where_am_i()
+    for number, name in enumerate(FIRST):
+        tall, width = 0, 0
+        for spot in (0, 1):
+            low = place ^ spot
+            blocks = parts(name, spot)
+            tall, width = blocks[0].shape[0], PACK * len(blocks)
+            for block, value in enumerate(blocks):
+                value = value.astype(SINGLE)
+                if name == "d":
+                    turned[rows_at(low * tall, tall), :] = value
+                else:
+                    scratch[number][rows_at(low * tall, tall), block * PACK : (block + 1) * PACK] = (
+                        value * share
+                    )
+        if name == "d":
+            scratch[number][...] = turned[...].T * share
+            width = scratch[number].shape[1]
+        target = out[number].at[:, rows_at(side * width, width)]
+        copies.append(pltpu.make_async_copy(scratch[number], target, sems.at[number]))
+        copies[-1].start()
+
+
+def own_kernel(*refs):
+    homes, refs = refs[:3], refs[3:]
+    given = {name: refs[2 * i : 2 * i + 2] for i, name in enumerate(FIRST)}
     refs = refs[2 * len(FIRST) :]
-    count = (len(refs) - 3) // 2
-    results, held = refs[:count], refs[count : 2 * count]
-    vec, turned, sems = refs[2 * count :]
+    grads, refs = refs[: len(FIRST)], refs[len(FIRST) :]
+    count = (len(refs) - 4 - len(FIRST)) // 2
+    results, share_out, refs = refs[:count], refs[count], refs[count + 1 :]
+    scratch, held = refs[: len(FIRST)], refs[len(FIRST) : len(FIRST) + count]
+    vec, turned, sems = refs[len(FIRST) + count :]
     core, _, place = where_am_i()
     copies = []
 
     def send(*numbers):
         for number in numbers:
-            copies.append(pltpu.make_async_copy(held[number], results[number], sems.at[number]))
+            copies.append(
+                pltpu.make_async_copy(held[number], results[number], sems.at[len(FIRST) + number])
+            )
             copies[-1].start()
 
     for number in (0, 1):
         held[number][place] = homes[number][...]
         held[number][1 - place] = homes[2][number]
     send(0, 1)
-    mine, other = parts["o"][:2]
+    mine, other = given["o"]
     half = mine.shape[0] - 16
     vec[rows_at(place * 8, 8), :] = mine[half:, :128].astype(SINGLE)[:8]
     vec[rows_at((1 - place) * 8, 8), :] = other[half:, :128].astype(SINGLE)[:8]
@@ -940,31 +968,16 @@
         jnp.sum(jnp.where(lane // DIGITS == side, line * worth, 0.0), axis=1, keepdims=True)
         for side in (0, 1)
     )
-    total = first + second
-    share = 1.0 / total
-    first_row = 0
-    for number, name in enumerate(FIRST):
-        out = held[2 + number]
-        tall, width = parts[name][0].shape
-        tall = tall - 16 if name == "o" else tall
-        for spot in range(4):
-            side, low = core ^ (spot >> 1), place ^ (spot & 1)
-            for block in range(width // PACK):
-                if spot < 2:
-                    piece = parts[name][spot][:tall, block * PACK : (block + 1) * PACK]
-                else:
-                    piece = theirs[first_row : first_row + tall, :]
-                    first_row += tall
-                piece = piece.astype(SINGLE)
-                if name == "d":
-                    turned[rows_at((side * 2 + low) * tall, tall), :] = piece
-                else:
-                    column = pl.multiple_of(side * width + block * PACK, 128)
-                    out[rows_at(low * tall, tall), pl.ds(column, PACK)] = piece * share
-        if name == "d":
-            out[...] = turned[...].T * share
-        send(2 + number)
-    counts, up, qv, *plain = held[2 + len(FIRST) :]
+    share = 1.0 / (first + second)
+    share_out[...] = jnp.broadcast_to(share, share_out.shape)
+
+    def parts(name, spot):
+        part = given[name][spot]
+        tall = part.shape[0] - (16 if name == "o" else 0)
+        return [part[:tall, at : at + PACK] for at in range(0, part.shape[1], PACK)]
+
+    finish_side(core, parts, share, grads, turned, scratch, sems, copies)
+    counts, up, qv, *plain = held[2:]
     spot = lax.broadcasted_iota(jnp.int32, (1, 128), 1)
     counts[...] = jnp.where(spot == 0, first, second).astype(jnp.int32)[0, : counts.shape[0]]
     width = qv.shape[1]
@@ -973,42 +986,85 @@
     for number, out in zip((0, 1, 4, 5, 6, 7), plain):
         out[...] = scaled[number, :width]
     up[...] = jnp.concatenate([scaled[8 + part : 9 + part, :width] for part in range(4)], axis=1)[0]
-    send(*range(2 + len(FIRST), count))
+    send(*range(2, count))
     for copy in copies:
         copy.wait()
 
 
+def other_kernel(theirs, share, *refs):
+    refs = refs[len(FIRST) :]
+    grads, refs = refs[: len(FIRST)], refs[len(FIRST) :]
+    scratch, (turned, sems) = refs[: len(FIRST)], refs[len(FIRST) :]
+    core, _, _ = where_am_i()
+    first = [0]
+
+    def parts(name, spot):
+        place = FIRST.index(name)
+        tall, width = scratch[place].shape
+        if name == "d":
+            tall, width = turned.shape
+        blocks = []
+        for _ in range(width // PACK):
+            blocks.append(theirs[first[0] : first[0] + tall // 2, :])
+            first[0] += tall // 2
+        return blocks
+
+    copies = []
+    finish_side(1 - core, parts, share[0:1, 0:1], grads, turned, scratch, sems, copies)
+    for copy in copies:
+        copy.wait()
+
+
 def finale(homes, theirs, parts, rows):
     piece, features = homes[0].shape
-    home = jax.ShapeDtypeStruct((2, piece, features), LOW)
-    results = [home, home]
+    shapes, halves = [], []
     for name in FIRST:
         tall, width = parts[name][0].shape
-        shape = (width, 4 * tall) if name == "d" else (2 * rows, 2 * width)
-        results.append(jax.ShapeDtypeStruct(shape, SINGLE))
+        shapes.append((width, 4 * tall) if name == "d" else (2 * rows, 2 * width))
+        halves.append(pltpu.VMEM((shapes[-1][0], shapes[-1][1] // 2), SINGLE))
+    grads = [jax.ShapeDtypeStruct(s, SINGLE) for s in shapes]
     chunk = 2 * rows
-    results += [
+    home = jax.ShapeDtypeStruct((2, piece, features), LOW)
+    results = [
+        home,
+        home,
         jax.ShapeDtypeStruct((2,), jnp.int32),
         jax.ShapeDtypeStruct((4 * chunk,), SINGLE),
         jax.ShapeDtypeStruct((2, chunk), SINGLE),
     ] + [jax.ShapeDtypeStruct((chunk,), SINGLE)] * 6
     vmem = pl.BlockSpec(memory_space=pltpu.VMEM)
+    anywhere = pl.BlockSpec(memory_space=pl.ANY)
     tall, width = parts["d"][0].shape
-    operands = [*homes, theirs, *[p for name in FIRST for p in parts[name]]]
-    return pl.pallas_call(
-        finale_kernel,
+    turned = pltpu.VMEM((2 * tall, width), SINGLE)
+    operands = [*homes, *[p for name in FIRST for p in parts[name]]]
+    params = pltpu.CompilerParams(vmem_limit_bytes=16 << 20)
+    own = pl.pallas_call(
+        own_kernel,
         in_specs=[vmem] * len(operands),
-        out_specs=[pl.BlockSpec(memory_space=pl.ANY)] * len(results),
-        out_shape=results,
-        scratch_shapes=[pltpu.VMEM(r.shape, r.dtype) for r in results]
+        out_specs=[anywhere] * (len(grads) + len(results)) + [vmem],
+        out_shape=grads + results + [jax.ShapeDtypeStruct((8, 128), SINGLE)],
+        scratch_shapes=halves
+        + [pltpu.VMEM(r.shape, r.dtype) for r in results]
         + [
             pltpu.VMEM((16, 128), SINGLE),
-            pltpu.VMEM((4 * tall, width), SINGLE),
-            pltpu.SemaphoreType.DMA((len(results),)),
+            turned,
+            pltpu.SemaphoreType.DMA((len(grads) + len(results),)),
         ],
-        compiler_params=pltpu.CompilerParams(vmem_limit_bytes=16 << 20),
+        compiler_params=params,
+        cost_estimate=pl.CostEstimate(flops=40 * 10**9, bytes_accessed=1, transcendentals=0),
+    )(*operands)
+    grads_own, rest, share = own[: len(grads)], own[len(grads) : -1], own[-1]
+    whole = pl.pallas_call(
+        other_kernel,
+        in_specs=[vmem, vmem] + [anywhere] * len(grads),
+        out_specs=[anywhere] * len(grads),
+        out_shape=grads,
+        scratch_shapes=halves + [turned, pltpu.SemaphoreType.DMA((len(grads),))],
+        input_output_aliases={2 + i: i for i in range(len(grads))},
+        compiler_params=params,
         cost_estimate=pl.CostEstimate(flops=1, bytes_accessed=1, transcendentals=0),
-    )(*operands)
+    )(theirs, share, *grads_own)
+    return [*rest[:2], *whole, *rest[2:]]
 
 
 def swap_pairs(size, bit):

time: 103 us -> 99.7 us (0.968)
  waiting for transfers between devices: 28.3 us -> 24.1 us
    ppermute x16, starting transfers between devices: 22.7 us -> 26 us  [go(): lax.ppermute(send, AXES, partners(self.name, self.stage, self.groups))]
    ppermute x16, waiting for transfers between devices: 16.7 us -> 14 us  [go(): lax.ppermute(send, AXES, partners(self.name, self.stage, self.groups))]
    ppermute x11, waiting for transfers between devices: 3.21 us -> 1.26 us  [from_core(): return lax.ppermute(value, 'src', pair)]
    ppermute x4, starting transfers between devices: 5.85 us -> 4.23 us  [step(): self.flying = lax.ppermute(self.total, 'seq', swap_pairs(2, 1))]
    ppermute x11, starting transfers between devices: 7.55 us -> 6.18 us  [from_core(): return lax.ppermute(value, 'src', pair)]
    pallas_call x1 -> x2, Pallas kernels: 2.85 us -> 3.41 us  [the longest x1 1.94 us: finale(): pl.pallas_call(own_kernel, in_specs=[vmem] * len(operands), out_specs=[an...]
  transfers between devices with their start and end apart: 34 -> 34, of which waited for: 13 -> 15; matrix products, arithmetic and copies ran while one was open for 2% -> 2% of each run, Pallas kernels for 25% -> 28%
where the time goes in v6:
time: 99.7 us; the launch traced here: 99.5 us
  starting transfers between devices  41.6 us (42%)
  Pallas kernels  29.5 us (30%)
  waiting for transfers between devices  24.1 us (24%)
  between operations  1.72 us (2%)
  other arithmetic  1.66 us (2%)
    ppermute x16, starting transfers between devices, go(): lax.ppermute(send, AXES, partners(self.name, self.stage, self.groups))  26 us
    pallas_call x11, Pallas kernels, call(): pl.pallas_call(kernel, in_specs=[pl.BlockSpec(memory_space=pl.ANY)] * len...  23.3 us
    ppermute x16, waiting for transfers between devices, go(): lax.ppermute(send, AXES, partners(self.name, self.stage, self.groups))  14 us
    ppermute x4, waiting for transfers between devices, step(): self.flying = lax.ppermute(self.total, 'seq', swap_pairs(2, 1))  7.34 us
    ppermute x11, starting transfers between devices, from_core(): return lax.ppermute(value, 'src', pair)  6.18 us
    ppermute x4, starting transfers between devices, step(): self.flying = lax.ppermute(self.total, 'seq', swap_pairs(2, 1))  4.23 us
    ppermute x1, starting transfers between devices, body_fast(): lax.ppermute(lax.dynamic_index_in_dim(x_both, 1 - place, 0, keepdims=Fals...  3 us
    pallas_call x1, Pallas kernels, prepare(): pl.pallas_call(prepare_kernel, in_specs=[pl.BlockSpec(memory_space=pltpu....  2.82 us
  transfers between devices with their start and end apart: 34, of which 15 were waited for; matrix products, arithmetic and copies ran while one was open for 2% of the time, Pallas kernels for 28%

profile of v6, /device:TPU:0, one launch (start us, length us, event | category | flops | bytes accessed | tf_op | source)
XLA Modules:
  0.0 99.5 jit_solution(6827553846268921434)
XLA Ops:
  1.6 3.0 %collective-permute-start = (bf16[128,768]{1,0:T(8,128)(2,1)S(1)}, bf16[128,768]{1,0:T(8,128)(2,1)S(1)}, u32[]{:S(2)}, u32[]{:S(2)}) collective-permute-start(bf16[128,768]{1,0:T(8,128)(2,1)S(1)} %dynamic-slice_bitcast_fusion), channel_id=1, source_target_pairs={{0,1},{1,0},{2,3},{3,2},{4,5},{5,4},{6,7},{7,6},{8,9},{9,8},{10,11... | collective-permute-start | bytes 589832 | tf_op jit(solution)/shard_map/ppermute | solution.py:1164
  5.3 2.8 %shard_map.271 = (bf16[128,768]{1,0:T(8,128)(2,1)S(1)}, bf16[128,768]{1,0:T(8,128)(2,1)S(1)}, bf16[128,768]{1,0:T(8,128)(2,1)S(1)}, f32[1,128]{1,0:T(1,128)S(1)}...) custom-call(s32[1,1]{1,0:T(1,128)S(6)} %copy.39.refs_0_, s32[2,128]{1,0:T(2,128)} %bitcast.17, ...), custom_call_target="tpu_custom_call" | custom-call | flops 2000000000 | bytes 1 | tf_op jit(solution)/shard_map/pallas_call | solution.py:456
  9.5 4.2 %shard_map.272 = (bf16[768,3072]{1,0:T(8,128)(2,1)S(1)}, bf16[3072,768]{1,0:T(8,128)(2,1)S(1)}, bf16[256,768]{1,0:T(8,128)(2,1)S(1)}, bf16[9,256,256]{2,1,0:T(8,...) custom-call(bf16[768,3072]{1,0:T(8,128)(2,1)} %up_ref.1, ...), custom_call_target="tpu_custom_call" | custom-call | flops 8000000000 | bytes 1 | tf_op jit(solution)/shard_map/pallas_call | solution.py:383
  14.5 2.7 %shard_map.273 = (bf16[2,256,768]{2,1,0:T(8,128)(2,1)S(1)}, bf16[2,256,768]{2,1,0:T(8,128)(2,1)S(1)}, bf16[256,768]{1,0:T(8,128)(2,1)S(1)}, bf16[256,384]{1,0:T(...) custom-call(bf16[256,768]{1,0:T(8,128)(2,1)S(1)} %get-tuple-element.163.n2.left, ...), custom_call_target="tpu_custom_call" | custom-call | flops 5000000000 | bytes 1 | tf_op jit(solution)/shard_map/pallas_call | solution.py:383
  18.1 3.2 %shard_map.274 = (bf16[2,256,768]{2,1,0:T(8,128)(2,1)S(1)}, bf16[2,256,768]{2,1,0:T(8,128)(2,1)S(1)}, f32[256,768]{1,0:T(8,128)S(1)}, bf16[256,768]{1,0:T(8,128)...) custom-call(bf16[256,768]{1,0:T(8,128)(2,1)S(1)} %get-tuple-element.163.n2.left, ...), custom_call_target="tpu_custom_call" | custom-call | flops 5000000000 | bytes 1 | tf_op jit(solution)/shard_map/pallas_call | solution.py:383
  21.7 2.0 %shard_map.275 = (bf16[8,48,1536]{2,1,0:T(8,128)(2,1)S(1)}, bf16[8,48,1536]{2,1,0:T(8,128)(2,1)S(1)}) custom-call(bf16[256,768]{1,0:T(8,128)(2,1)S(1)} %get-tuple-element.163.n2.left, bf16[256,768]{1,0:T(8,128)(2,1)S(1)} %collective-permute-done.1.left_other, bf16[2,256,768]{2,1,0:T(8,128)(2,1)S(1)} %get-tuple-element.165.right, ...), custom_call_target="tpu_custom_call" | custom-call | flops 4000000000 | bytes 1 | tf_op jit(solution)/shard_map/pallas_call | solution.py:383
  23.7 1.7 %collective-permute-start.14 = (bf16[8,48,1536]{2,1,0:T(8,128)(2,1)S(1)}, bf16[8,48,1536]{2,1,0:T(8,128)(2,1)S(1)}, u32[]{:S(2)}, u32[]{:S(2)}) collective-permute-start(bf16[8,48,1536]{2,1,0:T(8,128)(2,1)S(1)} %get-tuple-element.167), channel_id=1, source_target_pairs={{0,2},{1,3},{2,0},{3,1},{4,6},{5,7},{6,4},{7,5},{8,10},{9,11},{10,... | collective-permute-start | bytes 3538952 | tf_op jit(solution)/shard_map/ppermute | solution.py:1112
  25.4 2.3 %shard_map.276 = (bf16[8,192,384]{2,1,0:T(8,128)(2,1)S(1)}, bf16[8,192,384]{2,1,0:T(8,128)(2,1)S(1)}) custom-call(bf16[2,256,768]{2,1,0:T(8,128)(2,1)S(1)} %get-tuple-element.192.g_mine, bf16[2,256,768]{2,1,0:T(8,128)(2,1)S(1)} %get-tuple-element.157.g_theirs, bf16[2,256,768]{2,1,0:T(8,128)(2,1)S(1)} %collective-permute-done.5.other_mine, ...), custom_call_target="tpu_custom_call" | custom-call | flops 1 | bytes 1 | tf_op jit(solution)/shard_map/pallas_call | solution.py:383
  27.7 1.9 %collective-permute-start.13 = (bf16[8,192,384]{2,1,0:T(8,128)(2,1)S(1)}, bf16[8,192,384]{2,1,0:T(8,128)(2,1)S(1)}, u32[]{:S(2)}, u32[]{:S(2)}) collective-permute-start(bf16[8,192,384]{2,1,0:T(8,128)(2,1)S(1)} %get-tuple-element.173), channel_id=1, source_target_pairs={{0,1},{1,0},{2,3},{3,2},{4,5},{5,4},{6,7},{7,6},{8,9},{9,8},{10,11... | collective-permute-start | bytes 3538952 | tf_op jit(solution)/shard_map/ppermute | solution.py:1112
  29.6 3.4 %shard_map.277 = (bf16[256,1152]{1,0:T(8,128)(2,1)S(1)}, bf16[256,1152]{1,0:T(8,128)(2,1)S(1)}, f32[16,768]{1,0:T(8,128)S(1)}) custom-call(bf16[9,256,256]{2,1,0:T(8,128)(2,1)S(1)} %get-tuple-element.174.qkv, bf16[3,1024,256]{2,1,0:T(8,128)(2,1)S(1)} %get-tuple-element.175.probs, bf16[256,768]{1,0:T(8,128)(2,1)S(1)} %get-tuple-element.176.db1.right, ...), custom_call_target="tpu_custom_call" | custom-call | flops 1 | bytes 1 | tf_op jit(solution)/shard_map/pallas_call | solution.py:383
  33.6 1.6 %shard_map.278 = (bf16[128,768]{1,0:T(8,128)(2,1)S(1)}, bf16[128,768]{1,0:T(8,128)(2,1)S(1)}, f32[16,768]{1,0:T(8,128)S(1)}) custom-call(bf16[128,768]{1,0:T(8,128)(2,1)S(1)} %get-tuple-element.180.x_mine, bf16[128,768]{1,0:T(8,128)(2,1)S(1)} %collective-permute-done.x_other, f32[16,768]{1,0:T(8,128)S(1)} %get-tuple-element.134.small, ...), custom_call_target="tpu_custom_call" | custom-call | flops 1 | bytes 1 | tf_op jit(solution)/shard_map/pallas_call | solution.py:383
  40.1 1.8 %shard_map.281 = (bf16[128,768]{1,0:T(8,128)(2,1)S(1)}, bf16[2,128,768]{2,1,0:T(8,128)(2,1)S(1)}) custom-call(bf16[2,256,768]{2,1,0:T(8,128)(2,1)S(1)} %get-tuple-element.192.g_mine, bf16[2,256,768]{2,1,0:T(8,128)(2,1)S(1)} %get-tuple-element.157.g_theirs, f32[256,768]{1,0:T(8,128)S(1)} %get-tuple-element.151.middle, ...), custom_call_target="tpu_custom_call" | custom-call | flops 1 | bytes 1 | tf_op jit(solution)/shard_map/pallas_call | solution.py:383
  42.2 2.0 %collective-permute-start.19 = (bf16[4,48,1536]{2,1,0:T(8,128)(2,1)S(1)}, bf16[4,48,1536]{2,1,0:T(8,128)(2,1)S(1)}, u32[]{:S(2)}, u32[]{:S(2)}) collective-permute-start(bf16[4,48,1536]{2,1,0:T(8,128)(2,1)S(1)} %get-tuple-element.252), channel_id=1, source_target_pairs={{0,1},{1,0},{2,3},{3,2},{4,5},{5,4},{6,7},{7,6},{8,9},{9,8},{10,11... | collective-permute-start | bytes 1769480 | tf_op jit(solution)/shard_map/ppermute | solution.py:1112
  44.5 1.4 %collective-permute-start.18 = (bf16[4,192,384]{2,1,0:T(8,128)(2,1)S(1)}, bf16[4,192,384]{2,1,0:T(8,128)(2,1)S(1)}, u32[]{:S(2)}, u32[]{:S(2)}) collective-permute-start(bf16[4,192,384]{2,1,0:T(8,128)(2,1)S(1)} %get-tuple-element.254), channel_id=1, source_target_pairs={{0,2},{1,3},{2,0},{3,1},{4,6},{5,7},{6,4},{7,5},{8,10},{9,11},{10,... | collective-permute-start | bytes 1769480 | tf_op jit(solution)/shard_map/ppermute | solution.py:1112
  45.9 3.3 %collective-permute-done.12 = bf16[8,64,384]{2,1,0:T(8,128)(2,1)S(1)} collective-permute-done((bf16[8,64,384]{2,1,0:T(8,128)(2,1)S(1)}, bf16[8,64,384]{2,1,0:T(8,128)(2,1)S(1)}, u32[]{:S(2)}, u32[]{:S(2)}) %collective-permute-start.12) | collective-permute-done | bytes 393248 | tf_op jit(solution)/shard_map/ppermute | solution.py:1112
  49.3 3.2 %collective-permute-start.15 = (bf16[4,64,384]{2,1,0:T(8,128)(2,1)S(1)}, bf16[4,64,384]{2,1,0:T(8,128)(2,1)S(1)}, u32[]{:S(2)}, u32[]{:S(2)}) collective-permute-start(bf16[4,64,384]{2,1,0:T(8,128)(2,1)S(1)} %get-tuple-element.263), channel_id=1, source_target_pairs={{0,1},{1,0},{2,3},{3,2},{4,5},{5,4},{6,7},{7,6},{8,9},{9,8},{10,11... | collective-permute-start | bytes 589832 | tf_op jit(solution)/shard_map/ppermute | solution.py:1112
  53.6 1.6 %collective-permute-start.17 = (bf16[4,48,1152]{2,1,0:T(8,128)(2,1)S(1)}, bf16[4,48,1152]{2,1,0:T(8,128)(2,1)S(1)}, u32[]{:S(2)}, u32[]{:S(2)}) collective-permute-start(bf16[4,48,1152]{2,1,0:T(8,128)(2,1)S(1)} %get-tuple-element.255), channel_id=1, source_target_pairs={{0,4},{1,5},{2,6},{3,7},{4,0},{5,1},{6,2},{7,3},{8,12},{9,13},{10,... | collective-permute-start | bytes 1327112 | tf_op jit(solution)/shard_map/ppermute | solution.py:1112
  55.3 4.5 %collective-permute-done.19 = bf16[4,48,1536]{2,1,0:T(8,128)(2,1)S(1)} collective-permute-done((bf16[4,48,1536]{2,1,0:T(8,128)(2,1)S(1)}, bf16[4,48,1536]{2,1,0:T(8,128)(2,1)S(1)}, u32[]{:S(2)}, u32[]{:S(2)}) %collective-permute-start.19) | collective-permute-done | bytes 589856 | tf_op jit(solution)/shard_map/ppermute | solution.py:1112
  59.9 1.6 %collective-permute-start.23 = (bf16[2,48,1536]{2,1,0:T(8,128)(2,1)S(1)}, bf16[2,48,1536]{2,1,0:T(8,128)(2,1)S(1)}, u32[]{:S(2)}, u32[]{:S(2)}) collective-permute-start(bf16[2,48,1536]{2,1,0:T(8,128)(2,1)S(1)} %get-tuple-element.258), channel_id=1, source_target_pairs={{0,4},{1,5},{2,6},{3,7},{4,0},{5,1},{6,2},{7,3},{8,12},{9,13},{10,... | collective-permute-start | bytes 884744 | tf_op jit(solution)/shard_map/ppermute | solution.py:1112
  62.0 1.6 %collective-permute-start.22 = (bf16[2,192,384]{2,1,0:T(8,128)(2,1)S(1)}, bf16[2,192,384]{2,1,0:T(8,128)(2,1)S(1)}, u32[]{:S(2)}, u32[]{:S(2)}) collective-permute-start(bf16[2,192,384]{2,1,0:T(8,128)(2,1)S(1)} %get-tuple-element.260), channel_id=1, source_target_pairs={{0,4},{1,5},{2,6},{3,7},{4,0},{5,1},{6,2},{7,3},{8,12},{9,13},{10,... | collective-permute-start | bytes 884744 | tf_op jit(solution)/shard_map/ppermute | solution.py:1112
  65.0 1.5 %collective-permute-start.21 = (bf16[2,48,1152]{2,1,0:T(8,128)(2,1)S(1)}, bf16[2,48,1152]{2,1,0:T(8,128)(2,1)S(1)}, u32[]{:S(2)}, u32[]{:S(2)}) collective-permute-start(bf16[2,48,1152]{2,1,0:T(8,128)(2,1)S(1)} %get-tuple-element.262), channel_id=1, source_target_pairs={{0,2},{1,3},{2,0},{3,1},{4,6},{5,7},{6,4},{7,5},{8,10},{9,11},{10,... | collective-permute-start | bytes 663560 | tf_op jit(solution)/shard_map/ppermute | solution.py:1112
  66.7 2.7 %collective-permute-start.27 = (bf16[1,48,1536]{2,1,0:T(8,128)(2,1)S(1)}, bf16[1,48,1536]{2,1,0:T(8,128)(2,1)S(1)}, u32[]{:S(2)}, u32[]{:S(2)}) collective-permute-start(bf16[1,48,1536]{2,1,0:T(8,128)(2,1)S(1)} %add_convert_fusion.19), channel_id=1, source_target_pairs={{0,8},{1,9},{2,10},{3,11},{4,12},{5,13},{6,14},{7,15},{8,0},{9,1},... | collective-permute-start | bytes 442376 | tf_op jit(solution)/shard_map/ppermute | solution.py:1112
  69.4 2.1 %collective-permute-start.20 = (bf16[2,128,768]{2,1,0:T(8,128)(2,1)S(1)}, bf16[2,128,768]{2,1,0:T(8,128)(2,1)S(1)}, u32[]{:S(2)}, u32[]{:S(2)}) collective-permute-start(bf16[2,128,768]{2,1,0:T(8,128)(2,1)S(1)} %get-tuple-element.209), channel_id=1, source_target_pairs={{0,1},{1,0},{2,3},{3,2},{4,5},{5,4},{6,7},{7,6},{8,9},{9,8},{10,11... | collective-permute-start | bytes 1179656 | tf_op jit(solution)/shard_map/ppermute | solution.py:1209
  73.4 2.6 %collective-permute-start.24 = (bf16[1,48,1152]{2,1,0:T(8,128)(2,1)S(1)}, bf16[1,48,1152]{2,1,0:T(8,128)(2,1)S(1)}, u32[]{:S(2)}, u32[]{:S(2)}) collective-permute-start(bf16[1,48,1152]{2,1,0:T(8,128)(2,1)S(1)} %add_convert_fusion.21), channel_id=1, source_target_pairs={{0,8},{1,9},{2,10},{3,11},{4,12},{5,13},{6,14},{7,15},{8,0},{9,1},... | collective-permute-start | bytes 331784 | tf_op jit(solution)/shard_map/ppermute | solution.py:1112
  76.5 3.7 %collective-permute-done.28 = bf16[1,192,384]{2,1,0:T(8,128)(2,1)S(1)} collective-permute-done((bf16[1,192,384]{2,1,0:T(8,128)(2,1)S(1)}, bf16[1,192,384]{2,1,0:T(8,128)(2,1)S(1)}, u32[]{:S(2)}, u32[]{:S(2)}) %collective-permute-start.28) | collective-permute-done | bytes 147488 | tf_op jit(solution)/shard_map/ppermute | solution.py:1112
  80.4 2.1 %collective-permute-start.31 = (bf16[48,1536]{1,0:T(8,128)(2,1)S(1)}, bf16[48,1536]{1,0:T(8,128)(2,1)S(1)}, u32[]{:S(2)}, u32[]{:S(2)}) collective-permute-start(bf16[48,1536]{1,0:T(8,128)(2,1)S(1)} %fusion.1.refs_9_.refs_6_), channel_id=1, source_target_pairs={{0,1},{1,0},{2,3},{3,2},{4,5},{5,4},{6,7},{7,6},{8,9},{9,8},{10,11... | collective-permute-start | bytes 442376 | tf_op jit(solution)/shard_map/ppermute | solution.py:1129
  84.8 2.3 %collective-permute-done.29.refs_8_.refs_5_ = bf16[192,384]{1,0:T(8,128)(2,1)S(1)} collective-permute-done((bf16[192,384]{1,0:T(8,128)(2,1)S(1)}, bf16[192,384]{1,0:T(8,128)(2,1)S(1)}, u32[]{:S(2)}, u32[]{:S(2)}) %collective-permute-start.29) | collective-permute-done | bytes 147488 | tf_op jit(solution)/shard_map/ppermute | solution.py:1129
  87.1 2.2 %collective-permute-done.31.refs_10_.refs_7_ = bf16[48,1536]{1,0:T(8,128)(2,1)S(1)} collective-permute-done((bf16[48,1536]{1,0:T(8,128)(2,1)S(1)}, bf16[48,1536]{1,0:T(8,128)(2,1)S(1)}, u32[]{:S(2)}, u32[]{:S(2)}) %collective-permute-start.31) | collective-permute-done | bytes 147488 | tf_op jit(solution)/shard_map/ppermute | solution.py:1129
  89.3 2.9 %collective-permute-done.30.refs_4_.refs_1_ = bf16[64,384]{1,0:T(8,128)(2,1)S(1)} collective-permute-done((bf16[64,384]{1,0:T(8,128)(2,1)S(1)}, bf16[64,384]{1,0:T(8,128)(2,1)S(1)}, u32[]{:S(2)}, u32[]{:S(2)}) %collective-permute-start.30) | collective-permute-done | bytes 49184 | tf_op jit(solution)/shard_map/ppermute | solution.py:1129
  92.3 3.6 %collective-permute-start.33 = (bf16[1152,384]{1,0:T(8,128)(2,1)S(1)}, bf16[1152,384]{1,0:T(8,128)(2,1)S(1)}, u32[]{:S(2)}, u32[]{:S(2)}) collective-permute-start(bf16[1152,384]{1,0:T(8,128)(2,1)S(1)} %shard_map.283), channel_id=1, source_target_pairs={{0,16},{16,0},{1,17},{17,1},{2,18},{18,2},{3,19},{19,3},{4,20},{20... | collective-permute-start | bytes 2654216 | tf_op jit(solution)/shard_map/ppermute | solution.py:1179
  95.9 1.9 %shard_map.282 = (f32[96,768]{1,0:T(8,128)}, f32[96,2304]{1,0:T(8,128)}, f32[384,768]{1,0:T(8,128)}, f32[96,3072]{1,0:T(8,128)}, bf16[2,128,768]{2,1,0:T(8,128)(...) custom-call(bf16[128,768]{1,0:T(8,128)(2,1)S(1)} %get-tuple-element., ...), custom_call_target="tpu_custom_call" | custom-call | flops 40000000000 | bytes 1 | tf_op jit(solution)/shard_map/pallas_call | solution.py:1041
  97.9 1.5 %shard_map.284 = (f32[96,768]{1,0:T(8,128)}, f32[96,2304]{1,0:T(8,128)}, f32[384,768]{1,0:T(8,128)}, f32[96,3072]{1,0:T(8,128)}) custom-call(bf16[1152,384]{1,0:T(8,128)(2,1)S(1)} %collective-permute-done.33.theirs, f32[8,128]{1,0:T(8,128)S(1)} %get-tuple-element.236.share, ...), custom_call_target="tpu_custom_call", output_to_operand_aliasing={{0}: (2, {}), {1}: (3, {}), {2}: (4, {}), {3}: (5, {})} | custom-call | flops 1 | bytes 1 | tf_op jit(solution)/shard_map/pallas_call | solution.py:1057
  (67 shorter events, 19.0 us)
Async XLA Ops:
  1.6 7.9 %collective-permute-start = (bf16[128,768]{1,0:T(8,128)(2,1)S(1)}, bf16[128,768]{1,0:T(8,128)(2,1)S(1)}, u32[]{:S(2)}, u32[]{:S(2)}) collective-permute-start(bf16[128,768]{1,0:T(8,128)(2,1)S(1)} %dynamic-slice_bitcast_fusion), channel_id=1, source_target_pairs={{0,1},{1,0},{2,3},{3,2},{4,5},{5,4},{6,7},{7,6},{8,9},{9,8},{10,11... | collective-permute-start | bytes 589832 | tf_op jit(solution)/shard_map/ppermute | solution.py:1164
  8.1 6.4 %collective-permute-start.4 = (bf16[128,768]{1,0:T(8,128)(2,1)S(1)}, bf16[128,768]{1,0:T(8,128)(2,1)S(1)}, u32[]{:S(2)}, u32[]{:S(2)}) collective-permute-start(bf16[128,768]{1,0:T(8,128)(2,1)S(1)} %get-tuple-element.141), channel_id=1, source_target_pairs={{0,1},{1,0},{2,3},{3,2},{4,5},{5,4},{6,7},{7,6},{8,9},{9,8},{10,11... | collective-permute-start | bytes 589832 | tf_op jit(solution)/shard_map/ppermute | solution.py:1175
  13.7 4.1 %collective-permute-start.2 = (bf16[256,768]{1,0:T(8,128)(2,1)S(1)}, bf16[256,768]{1,0:T(8,128)(2,1)S(1)}, u32[]{:S(2)}, u32[]{:S(2)}) collective-permute-start(bf16[256,768]{1,0:T(8,128)(2,1)S(1)} %get-tuple-element.188.left), channel_id=1, source_target_pairs={{0,16},{16,0},{1,17},{17,1},{2,18},{18,2},{3,19},{19,3},{4,20},{20... | collective-permute-start | bytes 1179656 | tf_op jit(solution)/shard_map/ppermute | solution.py:1179
  13.8 4.3 %collective-permute-start.3 = (bf16[256,768]{1,0:T(8,128)(2,1)S(1)}, bf16[256,768]{1,0:T(8,128)(2,1)S(1)}, u32[]{:S(2)}, u32[]{:S(2)}) collective-permute-start(bf16[256,768]{1,0:T(8,128)(2,1)S(1)} %get-tuple-element.184.left), channel_id=1, source_target_pairs={{0,16},{16,0},{1,17},{17,1},{2,18},{18,2},{3,19},{19,3},{4,20},{20... | collective-permute-start | bytes 1179656 | tf_op jit(solution)/shard_map/ppermute | solution.py:1179
  14.3 3.8 %collective-permute-start.1 = (bf16[256,768]{1,0:T(8,128)(2,1)S(1)}, bf16[256,768]{1,0:T(8,128)(2,1)S(1)}, u32[]{:S(2)}, u32[]{:S(2)}) collective-permute-start(bf16[256,768]{1,0:T(8,128)(2,1)S(1)} %get-tuple-element.163.n2.left), channel_id=1, source_target_pairs={{0,16},{16,0},{1,17},{17,1},{2,18},{18,2},{3,19},{19,3},{4,20},{20... | collective-permute-start | bytes 1179656 | tf_op jit(solution)/shard_map/ppermute | solution.py:1179
  17.2 4.5 %collective-permute-start.6 = (bf16[2,256,768]{2,1,0:T(8,128)(2,1)S(1)}, bf16[2,256,768]{2,1,0:T(8,128)(2,1)S(1)}, u32[]{:S(2)}, u32[]{:S(2)}) collective-permute-start(bf16[2,256,768]{2,1,0:T(8,128)(2,1)S(1)} %get-tuple-element.155), channel_id=1, source_target_pairs={{0,16},{16,0},{1,17},{17,1},{2,18},{18,2},{3,19},{19,3},{4,20},{20... | collective-permute-start | bytes 2359304 | tf_op jit(solution)/shard_map/ppermute | solution.py:1179
  17.5 4.2 %collective-permute-start.8 = (bf16[2,256,768]{2,1,0:T(8,128)(2,1)S(1)}, bf16[2,256,768]{2,1,0:T(8,128)(2,1)S(1)}, u32[]{:S(2)}, u32[]{:S(2)}) collective-permute-start(bf16[2,256,768]{2,1,0:T(8,128)(2,1)S(1)} %get-tuple-element.157.g_theirs), channel_id=1, source_target_pairs={{0,16},{16,0},{1,17},{17,1},{2,18},{18,2},{3,19},{19,3},{4,20},{20... | collective-permute-start | bytes 2359304 | tf_op jit(solution)/shard_map/ppermute | solution.py:1179
  17.8 3.9 %collective-permute-start.7 = (bf16[256,384]{1,0:T(8,128)(2,1)S(1)}, bf16[256,384]{1,0:T(8,128)(2,1)S(1)}, u32[]{:S(2)}, u32[]{:S(2)}) collective-permute-start(bf16[256,384]{1,0:T(8,128)(2,1)S(1)} %get-tuple-element.156), channel_id=1, source_target_pairs={{0,16},{16,0},{1,17},{17,1},{2,18},{18,2},{3,19},{19,3},{4,20},{20... | collective-permute-start | bytes 589832 | tf_op jit(solution)/shard_map/ppermute | solution.py:1179
  21.3 4.1 %collective-permute-start.5 = (bf16[2,256,768]{2,1,0:T(8,128)(2,1)S(1)}, bf16[2,256,768]{2,1,0:T(8,128)(2,1)S(1)}, u32[]{:S(2)}, u32[]{:S(2)}) collective-permute-start(bf16[2,256,768]{2,1,0:T(8,128)(2,1)S(1)} %get-tuple-element.192.g_mine), channel_id=1, source_target_pairs={{0,16},{16,0},{1,17},{17,1},{2,18},{18,2},{3,19},{19,3},{4,20},{20... | collective-permute-start | bytes 2359304 | tf_op jit(solution)/shard_map/ppermute | solution.py:1179
  23.7 18.2 %collective-permute-start.14 = (bf16[8,48,1536]{2,1,0:T(8,128)(2,1)S(1)}, bf16[8,48,1536]{2,1,0:T(8,128)(2,1)S(1)}, u32[]{:S(2)}, u32[]{:S(2)}) collective-permute-start(bf16[8,48,1536]{2,1,0:T(8,128)(2,1)S(1)} %get-tuple-element.167), channel_id=1, source_target_pairs={{0,2},{1,3},{2,0},{3,1},{4,6},{5,7},{6,4},{7,5},{8,10},{9,11},{10,... | collective-permute-start | bytes 3538952 | tf_op jit(solution)/shard_map/ppermute | solution.py:1112
  27.7 16.5 %collective-permute-start.13 = (bf16[8,192,384]{2,1,0:T(8,128)(2,1)S(1)}, bf16[8,192,384]{2,1,0:T(8,128)(2,1)S(1)}, u32[]{:S(2)}, u32[]{:S(2)}) collective-permute-start(bf16[8,192,384]{2,1,0:T(8,128)(2,1)S(1)} %get-tuple-element.173), channel_id=1, source_target_pairs={{0,1},{1,0},{2,3},{3,2},{4,5},{5,4},{6,7},{7,6},{8,9},{9,8},{10,11... | collective-permute-start | bytes 3538952 | tf_op jit(solution)/shard_map/ppermute | solution.py:1112
  33.0 4.9 %collective-permute-start.9 = (bf16[256,1152]{1,0:T(8,128)(2,1)S(1)}, bf16[256,1152]{1,0:T(8,128)(2,1)S(1)}, u32[]{:S(2)}, u32[]{:S(2)}) collective-permute-start(bf16[256,1152]{1,0:T(8,128)(2,1)S(1)} %get-tuple-element.177.dp_theirs), channel_id=1, source_target_pairs={{0,16},{16,0},{1,17},{17,1},{2,18},{18,2},{3,19},{19,3},{4,20},{20... | collective-permute-start | bytes 1769480 | tf_op jit(solution)/shard_map/ppermute | solution.py:1179
  37.2 12.0 %collective-permute-start.12 = (bf16[8,64,384]{2,1,0:T(8,128)(2,1)S(1)}, bf16[8,64,384]{2,1,0:T(8,128)(2,1)S(1)}, u32[]{:S(2)}, u32[]{:S(2)}) collective-permute-start(bf16[8,64,384]{2,1,0:T(8,128)(2,1)S(1)} %get-tuple-element.186), channel_id=1, source_target_pairs={{0,2},{1,3},{2,0},{3,1},{4,6},{5,7},{6,4},{7,5},{8,10},{9,11},{10,... | collective-permute-start | bytes 1179656 | tf_op jit(solution)/shard_map/ppermute | solution.py:1112
  39.3 14.1 %collective-permute-start.16 = (bf16[8,48,1152]{2,1,0:T(8,128)(2,1)S(1)}, bf16[8,48,1152]{2,1,0:T(8,128)(2,1)S(1)}, u32[]{:S(2)}, u32[]{:S(2)}) collective-permute-start(bf16[8,48,1152]{2,1,0:T(8,128)(2,1)S(1)} %get-tuple-element.191), channel_id=1, source_target_pairs={{0,1},{1,0},{2,3},{3,2},{4,5},{5,4},{6,7},{7,6},{8,9},{9,8},{10,11... | collective-permute-start | bytes 2654216 | tf_op jit(solution)/shard_map/ppermute | solution.py:1112
  42.2 17.5 %collective-permute-start.19 = (bf16[4,48,1536]{2,1,0:T(8,128)(2,1)S(1)}, bf16[4,48,1536]{2,1,0:T(8,128)(2,1)S(1)}, u32[]{:S(2)}, u32[]{:S(2)}) collective-permute-start(bf16[4,48,1536]{2,1,0:T(8,128)(2,1)S(1)} %get-tuple-element.252), channel_id=1, source_target_pairs={{0,1},{1,0},{2,3},{3,2},{4,5},{5,4},{6,7},{7,6},{8,9},{9,8},{10,11... | collective-permute-start | bytes 1769480 | tf_op jit(solution)/shard_map/ppermute | solution.py:1112
  44.5 17.3 %collective-permute-start.18 = (bf16[4,192,384]{2,1,0:T(8,128)(2,1)S(1)}, bf16[4,192,384]{2,1,0:T(8,128)(2,1)S(1)}, u32[]{:S(2)}, u32[]{:S(2)}) collective-permute-start(bf16[4,192,384]{2,1,0:T(8,128)(2,1)S(1)} %get-tuple-element.254), channel_id=1, source_target_pairs={{0,2},{1,3},{2,0},{3,1},{4,6},{5,7},{6,4},{7,5},{8,10},{9,11},{10,... | collective-permute-start | bytes 1769480 | tf_op jit(solution)/shard_map/ppermute | solution.py:1112
  49.3 14.5 %collective-permute-start.15 = (bf16[4,64,384]{2,1,0:T(8,128)(2,1)S(1)}, bf16[4,64,384]{2,1,0:T(8,128)(2,1)S(1)}, u32[]{:S(2)}, u32[]{:S(2)}) collective-permute-start(bf16[4,64,384]{2,1,0:T(8,128)(2,1)S(1)} %get-tuple-element.263), channel_id=1, source_target_pairs={{0,1},{1,0},{2,3},{3,2},{4,5},{5,4},{6,7},{7,6},{8,9},{9,8},{10,11... | collective-permute-start | bytes 589832 | tf_op jit(solution)/shard_map/ppermute | solution.py:1112
  53.6 10.0 %collective-permute-start.17 = (bf16[4,48,1152]{2,1,0:T(8,128)(2,1)S(1)}, bf16[4,48,1152]{2,1,0:T(8,128)(2,1)S(1)}, u32[]{:S(2)}, u32[]{:S(2)}) collective-permute-start(bf16[4,48,1152]{2,1,0:T(8,128)(2,1)S(1)} %get-tuple-element.255), channel_id=1, source_target_pairs={{0,4},{1,5},{2,6},{3,7},{4,0},{5,1},{6,2},{7,3},{8,12},{9,13},{10,... | collective-permute-start | bytes 1327112 | tf_op jit(solution)/shard_map/ppermute | solution.py:1112
  59.9 6.8 %collective-permute-start.23 = (bf16[2,48,1536]{2,1,0:T(8,128)(2,1)S(1)}, bf16[2,48,1536]{2,1,0:T(8,128)(2,1)S(1)}, u32[]{:S(2)}, u32[]{:S(2)}) collective-permute-start(bf16[2,48,1536]{2,1,0:T(8,128)(2,1)S(1)} %get-tuple-element.258), channel_id=1, source_target_pairs={{0,4},{1,5},{2,6},{3,7},{4,0},{5,1},{6,2},{7,3},{8,12},{9,13},{10,... | collective-permute-start | bytes 884744 | tf_op jit(solution)/shard_map/ppermute | solution.py:1112
  62.0 9.5 %collective-permute-start.22 = (bf16[2,192,384]{2,1,0:T(8,128)(2,1)S(1)}, bf16[2,192,384]{2,1,0:T(8,128)(2,1)S(1)}, u32[]{:S(2)}, u32[]{:S(2)}) collective-permute-start(bf16[2,192,384]{2,1,0:T(8,128)(2,1)S(1)} %get-tuple-element.260), channel_id=1, source_target_pairs={{0,4},{1,5},{2,6},{3,7},{4,0},{5,1},{6,2},{7,3},{8,12},{9,13},{10,... | collective-permute-start | bytes 884744 | tf_op jit(solution)/shard_map/ppermute | solution.py:1112
  63.8 12.2 %collective-permute-start.25 = (bf16[2,64,384]{2,1,0:T(8,128)(2,1)S(1)}, bf16[2,64,384]{2,1,0:T(8,128)(2,1)S(1)}, u32[]{:S(2)}, u32[]{:S(2)}) collective-permute-start(bf16[2,64,384]{2,1,0:T(8,128)(2,1)S(1)} %get-tuple-element.266), channel_id=1, source_target_pairs={{0,4},{1,5},{2,6},{3,7},{4,0},{5,1},{6,2},{7,3},{8,12},{9,13},{10,... | collective-permute-start | bytes 294920 | tf_op jit(solution)/shard_map/ppermute | solution.py:1112
  65.0 8.4 %collective-permute-start.21 = (bf16[2,48,1152]{2,1,0:T(8,128)(2,1)S(1)}, bf16[2,48,1152]{2,1,0:T(8,128)(2,1)S(1)}, u32[]{:S(2)}, u32[]{:S(2)}) collective-permute-start(bf16[2,48,1152]{2,1,0:T(8,128)(2,1)S(1)} %get-tuple-element.262), channel_id=1, source_target_pairs={{0,2},{1,3},{2,0},{3,1},{4,6},{5,7},{6,4},{7,5},{8,10},{9,11},{10,... | collective-permute-start | bytes 663560 | tf_op jit(solution)/shard_map/ppermute | solution.py:1112
  66.7 13.6 %collective-permute-start.27 = (bf16[1,48,1536]{2,1,0:T(8,128)(2,1)S(1)}, bf16[1,48,1536]{2,1,0:T(8,128)(2,1)S(1)}, u32[]{:S(2)}, u32[]{:S(2)}) collective-permute-start(bf16[1,48,1536]{2,1,0:T(8,128)(2,1)S(1)} %add_convert_fusion.19), channel_id=1, source_target_pairs={{0,8},{1,9},{2,10},{3,11},{4,12},{5,13},{6,14},{7,15},{8,0},{9,1},... | collective-permute-start | bytes 442376 | tf_op jit(solution)/shard_map/ppermute | solution.py:1112
  69.4 15.5 %collective-permute-start.20 = (bf16[2,128,768]{2,1,0:T(8,128)(2,1)S(1)}, bf16[2,128,768]{2,1,0:T(8,128)(2,1)S(1)}, u32[]{:S(2)}, u32[]{:S(2)}) collective-permute-start(bf16[2,128,768]{2,1,0:T(8,128)(2,1)S(1)} %get-tuple-element.209), channel_id=1, source_target_pairs={{0,1},{1,0},{2,3},{3,2},{4,5},{5,4},{6,7},{7,6},{8,9},{9,8},{10,11... | collective-permute-start | bytes 1179656 | tf_op jit(solution)/shard_map/ppermute | solution.py:1209
  71.5 8.7 %collective-permute-start.28 = (bf16[1,192,384]{2,1,0:T(8,128)(2,1)S(1)}, bf16[1,192,384]{2,1,0:T(8,128)(2,1)S(1)}, u32[]{:S(2)}, u32[]{:S(2)}) collective-permute-start(bf16[1,192,384]{2,1,0:T(8,128)(2,1)S(1)} %add_convert_fusion.18), channel_id=1, source_target_pairs={{0,8},{1,9},{2,10},{3,11},{4,12},{5,13},{6,14},{7,15},{8,0},{9,1},... | collective-permute-start | bytes 442376 | tf_op jit(solution)/shard_map/ppermute | solution.py:1112
  73.4 9.3 %collective-permute-start.24 = (bf16[1,48,1152]{2,1,0:T(8,128)(2,1)S(1)}, bf16[1,48,1152]{2,1,0:T(8,128)(2,1)S(1)}, u32[]{:S(2)}, u32[]{:S(2)}) collective-permute-start(bf16[1,48,1152]{2,1,0:T(8,128)(2,1)S(1)} %add_convert_fusion.21), channel_id=1, source_target_pairs={{0,8},{1,9},{2,10},{3,11},{4,12},{5,13},{6,14},{7,15},{8,0},{9,1},... | collective-permute-start | bytes 331784 | tf_op jit(solution)/shard_map/ppermute | solution.py:1112
  76.0 6.6 %collective-permute-start.26 = (bf16[1,64,384]{2,1,0:T(8,128)(2,1)S(1)}, bf16[1,64,384]{2,1,0:T(8,128)(2,1)S(1)}, u32[]{:S(2)}, u32[]{:S(2)}) collective-permute-start(bf16[1,64,384]{2,1,0:T(8,128)(2,1)S(1)} %add_convert_fusion.26), channel_id=1, source_target_pairs={{0,8},{1,9},{2,10},{3,11},{4,12},{5,13},{6,14},{7,15},{8,0},{9,1},... | collective-permute-start | bytes 147464 | tf_op jit(solution)/shard_map/ppermute | solution.py:1112
  80.3 6.8 %collective-permute-start.29 = (bf16[192,384]{1,0:T(8,128)(2,1)S(1)}, bf16[192,384]{1,0:T(8,128)(2,1)S(1)}, u32[]{:S(2)}, u32[]{:S(2)}) collective-permute-start(bf16[192,384]{1,0:T(8,128)(2,1)S(1)} %fusion.refs_7_.refs_4_), channel_id=1, source_target_pairs={{0,1},{1,0},{2,3},{3,2},{4,5},{5,4},{6,7},{7,6},{8,9},{9,8},{10,11... | collective-permute-start | bytes 442376 | tf_op jit(solution)/shard_map/ppermute | solution.py:1129
  80.4 8.9 %collective-permute-start.31 = (bf16[48,1536]{1,0:T(8,128)(2,1)S(1)}, bf16[48,1536]{1,0:T(8,128)(2,1)S(1)}, u32[]{:S(2)}, u32[]{:S(2)}) collective-permute-start(bf16[48,1536]{1,0:T(8,128)(2,1)S(1)} %fusion.1.refs_9_.refs_6_), channel_id=1, source_target_pairs={{0,1},{1,0},{2,3},{3,2},{4,5},{5,4},{6,7},{7,6},{8,9},{9,8},{10,11... | collective-permute-start | bytes 442376 | tf_op jit(solution)/shard_map/ppermute | solution.py:1129
  82.8 9.4 %collective-permute-start.32 = (bf16[48,1152]{1,0:T(8,128)(2,1)S(1)}, bf16[48,1152]{1,0:T(8,128)(2,1)S(1)}, u32[]{:S(2)}, u32[]{:S(2)}) collective-permute-start(bf16[48,1152]{1,0:T(8,128)(2,1)S(1)} %fusion.2.refs_5_.refs_2_), channel_id=1, source_target_pairs={{0,1},{1,0},{2,3},{3,2},{4,5},{5,4},{6,7},{7,6},{8,9},{9,8},{10,11... | collective-permute-start | bytes 331784 | tf_op jit(solution)/shard_map/ppermute | solution.py:1129
  83.8 8.4 %collective-permute-start.30 = (bf16[64,384]{1,0:T(8,128)(2,1)S(1)}, bf16[64,384]{1,0:T(8,128)(2,1)S(1)}, u32[]{:S(2)}, u32[]{:S(2)}) collective-permute-start(bf16[64,384]{1,0:T(8,128)(2,1)S(1)} %fusion.3.refs_3_.refs_0_), channel_id=1, source_target_pairs={{0,1},{1,0},{2,3},{3,2},{4,5},{5,4},{6,7},{7,6},{8,9},{9,8},{10,11... | collective-permute-start | bytes 147464 | tf_op jit(solution)/shard_map/ppermute | solution.py:1129
  92.3 5.6 %collective-permute-start.33 = (bf16[1152,384]{1,0:T(8,128)(2,1)S(1)}, bf16[1152,384]{1,0:T(8,128)(2,1)S(1)}, u32[]{:S(2)}, u32[]{:S(2)}) collective-permute-start(bf16[1152,384]{1,0:T(8,128)(2,1)S(1)} %shard_map.283), channel_id=1, source_target_pairs={{0,16},{16,0},{1,17},{17,1},{2,18},{18,2},{3,19},{19,3},{4,20},{20... | collective-permute-start | bytes 2654216 | tf_op jit(solution)/shard_map/ppermute | solution.py:1179
  (2 other events, 3.6 us)

commit v7 on v6

--- a/solution.py
+++ b/solution.py
@@ -320,7 +320,7 @@
 BITS = {"y": 1, "1": 2, "2": 4}
 
 
-COSTS = {"prepare": 2, "load": 4, "attend": 8, "feed_one": 5, "feed_two": 5, "back": 0, "input": 0, "lanes": 0, "rows_u": 4, "rows_q": 0, "rows_o": 0, "result": 0}
+COSTS = {"attend": 8, "feed_one": 5, "feed_two": 5, "back": 0, "input": 0, "lanes": 0, "rows_u": 4, "rows_q": 0, "rows_o": 0, "result": 0}
 AXES = ("src", "dp", "seq")
 SINGLE = jnp.float32
 LOW = jnp.bfloat16

time: 99.7 us -> 99.7 us (level)
  no operation moved by 1% of the time
where the time goes in v7:
time: 99.7 us; the launch traced here: 99.5 us
  starting transfers between devices  41.6 us (42%)
  Pallas kernels  29.5 us (30%)
  waiting for transfers between devices  24.1 us (24%)
  between operations  1.72 us (2%)
  other arithmetic  1.66 us (2%)
    ppermute x16, starting transfers between devices, go(): lax.ppermute(send, AXES, partners(self.name, self.stage, self.groups))  26 us
    pallas_call x11, Pallas kernels, call(): pl.pallas_call(kernel, in_specs=[pl.BlockSpec(memory_space=pl.ANY)] * len...  23.3 us
    ppermute x16, waiting for transfers between devices, go(): lax.ppermute(send, AXES, partners(self.name, self.stage, self.groups))  14 us
    ppermute x4, waiting for transfers between devices, step(): self.flying = lax.ppermute(self.total, 'seq', swap_pairs(2, 1))  7.34 us
    ppermute x11, starting transfers between devices, from_core(): return lax.ppermute(value, 'src', pair)  6.18 us
    ppermute x4, starting transfers between devices, step(): self.flying = lax.ppermute(self.total, 'seq', swap_pairs(2, 1))  4.23 us
    ppermute x1, starting transfers between devices, body_fast(): lax.ppermute(lax.dynamic_index_in_dim(x_both, 1 - place, 0, keepdims=Fals...  3 us
    pallas_call x1, Pallas kernels, prepare(): pl.pallas_call(prepare_kernel, in_specs=[pl.BlockSpec(memory_space=pltpu....  2.82 us
  transfers between devices with their start and end apart: 34, of which 15 were waited for; matrix products, arithmetic and copies ran while one was open for 2% of the time, Pallas kernels for 28%

profile of v7, /device:TPU:0, one launch (start us, length us, event | category | flops | bytes accessed | tf_op | source)
XLA Modules:
  0.0 99.5 jit_solution(6827553846268921434)
XLA Ops:
  1.6 3.0 %collective-permute-start = (bf16[128,768]{1,0:T(8,128)(2,1)S(1)}, bf16[128,768]{1,0:T(8,128)(2,1)S(1)}, u32[]{:S(2)}, u32[]{:S(2)}) collective-permute-start(bf16[128,768]{1,0:T(8,128)(2,1)S(1)} %dynamic-slice_bitcast_fusion), channel_id=1, source_target_pairs={{0,1},{1,0},{2,3},{3,2},{4,5},{5,4},{6,7},{7,6},{8,9},{9,8},{10,11... | collective-permute-start | bytes 589832 | tf_op jit(solution)/shard_map/ppermute | solution.py:1164
  5.3 2.8 %shard_map.271 = (bf16[128,768]{1,0:T(8,128)(2,1)S(1)}, bf16[128,768]{1,0:T(8,128)(2,1)S(1)}, bf16[128,768]{1,0:T(8,128)(2,1)S(1)}, f32[1,128]{1,0:T(1,128)S(1)}...) custom-call(s32[1,1]{1,0:T(1,128)S(6)} %copy.39.refs_0_, s32[2,128]{1,0:T(2,128)} %bitcast.17, ...), custom_call_target="tpu_custom_call" | custom-call | flops 2000000000 | bytes 1 | tf_op jit(solution)/shard_map/pallas_call | solution.py:456
  9.5 4.2 %shard_map.272 = (bf16[768,3072]{1,0:T(8,128)(2,1)S(1)}, bf16[3072,768]{1,0:T(8,128)(2,1)S(1)}, bf16[256,768]{1,0:T(8,128)(2,1)S(1)}, bf16[9,256,256]{2,1,0:T(8,...) custom-call(bf16[768,3072]{1,0:T(8,128)(2,1)} %up_ref.1, ...), custom_call_target="tpu_custom_call" | custom-call | flops 8000000000 | bytes 1 | tf_op jit(solution)/shard_map/pallas_call | solution.py:383
  14.5 2.7 %shard_map.273 = (bf16[2,256,768]{2,1,0:T(8,128)(2,1)S(1)}, bf16[2,256,768]{2,1,0:T(8,128)(2,1)S(1)}, bf16[256,768]{1,0:T(8,128)(2,1)S(1)}, bf16[256,384]{1,0:T(...) custom-call(bf16[256,768]{1,0:T(8,128)(2,1)S(1)} %get-tuple-element.163.n2.left, ...), custom_call_target="tpu_custom_call" | custom-call | flops 5000000000 | bytes 1 | tf_op jit(solution)/shard_map/pallas_call | solution.py:383
  18.1 3.2 %shard_map.274 = (bf16[2,256,768]{2,1,0:T(8,128)(2,1)S(1)}, bf16[2,256,768]{2,1,0:T(8,128)(2,1)S(1)}, f32[256,768]{1,0:T(8,128)S(1)}, bf16[256,768]{1,0:T(8,128)...) custom-call(bf16[256,768]{1,0:T(8,128)(2,1)S(1)} %get-tuple-element.163.n2.left, ...), custom_call_target="tpu_custom_call" | custom-call | flops 5000000000 | bytes 1 | tf_op jit(solution)/shard_map/pallas_call | solution.py:383
  21.7 2.0 %shard_map.275 = (bf16[8,48,1536]{2,1,0:T(8,128)(2,1)S(1)}, bf16[8,48,1536]{2,1,0:T(8,128)(2,1)S(1)}) custom-call(bf16[256,768]{1,0:T(8,128)(2,1)S(1)} %get-tuple-element.163.n2.left, bf16[256,768]{1,0:T(8,128)(2,1)S(1)} %collective-permute-done.1.left_other, bf16[2,256,768]{2,1,0:T(8,128)(2,1)S(1)} %get-tuple-element.165.right, ...), custom_call_target="tpu_custom_call" | custom-call | flops 4000000000 | bytes 1 | tf_op jit(solution)/shard_map/pallas_call | solution.py:383
  23.7 1.7 %collective-permute-start.14 = (bf16[8,48,1536]{2,1,0:T(8,128)(2,1)S(1)}, bf16[8,48,1536]{2,1,0:T(8,128)(2,1)S(1)}, u32[]{:S(2)}, u32[]{:S(2)}) collective-permute-start(bf16[8,48,1536]{2,1,0:T(8,128)(2,1)S(1)} %get-tuple-element.167), channel_id=1, source_target_pairs={{0,2},{1,3},{2,0},{3,1},{4,6},{5,7},{6,4},{7,5},{8,10},{9,11},{10,... | collective-permute-start | bytes 3538952 | tf_op jit(solution)/shard_map/ppermute | solution.py:1112
  25.4 2.3 %shard_map.276 = (bf16[8,192,384]{2,1,0:T(8,128)(2,1)S(1)}, bf16[8,192,384]{2,1,0:T(8,128)(2,1)S(1)}) custom-call(bf16[2,256,768]{2,1,0:T(8,128)(2,1)S(1)} %get-tuple-element.192.g_mine, bf16[2,256,768]{2,1,0:T(8,128)(2,1)S(1)} %get-tuple-element.157.g_theirs, bf16[2,256,768]{2,1,0:T(8,128)(2,1)S(1)} %collective-permute-done.5.other_mine, ...), custom_call_target="tpu_custom_call" | custom-call | flops 1 | bytes 1 | tf_op jit(solution)/shard_map/pallas_call | solution.py:383
  27.7 1.9 %collective-permute-start.13 = (bf16[8,192,384]{2,1,0:T(8,128)(2,1)S(1)}, bf16[8,192,384]{2,1,0:T(8,128)(2,1)S(1)}, u32[]{:S(2)}, u32[]{:S(2)}) collective-permute-start(bf16[8,192,384]{2,1,0:T(8,128)(2,1)S(1)} %get-tuple-element.173), channel_id=1, source_target_pairs={{0,1},{1,0},{2,3},{3,2},{4,5},{5,4},{6,7},{7,6},{8,9},{9,8},{10,11... | collective-permute-start | bytes 3538952 | tf_op jit(solution)/shard_map/ppermute | solution.py:1112
  29.6 3.4 %shard_map.277 = (bf16[256,1152]{1,0:T(8,128)(2,1)S(1)}, bf16[256,1152]{1,0:T(8,128)(2,1)S(1)}, f32[16,768]{1,0:T(8,128)S(1)}) custom-call(bf16[9,256,256]{2,1,0:T(8,128)(2,1)S(1)} %get-tuple-element.174.qkv, bf16[3,1024,256]{2,1,0:T(8,128)(2,1)S(1)} %get-tuple-element.175.probs, bf16[256,768]{1,0:T(8,128)(2,1)S(1)} %get-tuple-element.176.db1.right, ...), custom_call_target="tpu_custom_call" | custom-call | flops 1 | bytes 1 | tf_op jit(solution)/shard_map/pallas_call | solution.py:383
  33.6 1.6 %shard_map.278 = (bf16[128,768]{1,0:T(8,128)(2,1)S(1)}, bf16[128,768]{1,0:T(8,128)(2,1)S(1)}, f32[16,768]{1,0:T(8,128)S(1)}) custom-call(bf16[128,768]{1,0:T(8,128)(2,1)S(1)} %get-tuple-element.180.x_mine, bf16[128,768]{1,0:T(8,128)(2,1)S(1)} %collective-permute-done.x_other, f32[16,768]{1,0:T(8,128)S(1)} %get-tuple-element.134.small, ...), custom_call_target="tpu_custom_call" | custom-call | flops 1 | bytes 1 | tf_op jit(solution)/shard_map/pallas_call | solution.py:383
  40.1 1.8 %shard_map.281 = (bf16[128,768]{1,0:T(8,128)(2,1)S(1)}, bf16[2,128,768]{2,1,0:T(8,128)(2,1)S(1)}) custom-call(bf16[2,256,768]{2,1,0:T(8,128)(2,1)S(1)} %get-tuple-element.192.g_mine, bf16[2,256,768]{2,1,0:T(8,128)(2,1)S(1)} %get-tuple-element.157.g_theirs, f32[256,768]{1,0:T(8,128)S(1)} %get-tuple-element.151.middle, ...), custom_call_target="tpu_custom_call" | custom-call | flops 1 | bytes 1 | tf_op jit(solution)/shard_map/pallas_call | solution.py:383
  42.2 2.0 %collective-permute-start.19 = (bf16[4,48,1536]{2,1,0:T(8,128)(2,1)S(1)}, bf16[4,48,1536]{2,1,0:T(8,128)(2,1)S(1)}, u32[]{:S(2)}, u32[]{:S(2)}) collective-permute-start(bf16[4,48,1536]{2,1,0:T(8,128)(2,1)S(1)} %get-tuple-element.252), channel_id=1, source_target_pairs={{0,1},{1,0},{2,3},{3,2},{4,5},{5,4},{6,7},{7,6},{8,9},{9,8},{10,11... | collective-permute-start | bytes 1769480 | tf_op jit(solution)/shard_map/ppermute | solution.py:1112
  44.5 1.4 %collective-permute-start.18 = (bf16[4,192,384]{2,1,0:T(8,128)(2,1)S(1)}, bf16[4,192,384]{2,1,0:T(8,128)(2,1)S(1)}, u32[]{:S(2)}, u32[]{:S(2)}) collective-permute-start(bf16[4,192,384]{2,1,0:T(8,128)(2,1)S(1)} %get-tuple-element.254), channel_id=1, source_target_pairs={{0,2},{1,3},{2,0},{3,1},{4,6},{5,7},{6,4},{7,5},{8,10},{9,11},{10,... | collective-permute-start | bytes 1769480 | tf_op jit(solution)/shard_map/ppermute | solution.py:1112
  45.9 3.3 %collective-permute-done.12 = bf16[8,64,384]{2,1,0:T(8,128)(2,1)S(1)} collective-permute-done((bf16[8,64,384]{2,1,0:T(8,128)(2,1)S(1)}, bf16[8,64,384]{2,1,0:T(8,128)(2,1)S(1)}, u32[]{:S(2)}, u32[]{:S(2)}) %collective-permute-start.12) | collective-permute-done | bytes 393248 | tf_op jit(solution)/shard_map/ppermute | solution.py:1112
  49.3 3.2 %collective-permute-start.15 = (bf16[4,64,384]{2,1,0:T(8,128)(2,1)S(1)}, bf16[4,64,384]{2,1,0:T(8,128)(2,1)S(1)}, u32[]{:S(2)}, u32[]{:S(2)}) collective-permute-start(bf16[4,64,384]{2,1,0:T(8,128)(2,1)S(1)} %get-tuple-element.263), channel_id=1, source_target_pairs={{0,1},{1,0},{2,3},{3,2},{4,5},{5,4},{6,7},{7,6},{8,9},{9,8},{10,11... | collective-permute-start | bytes 589832 | tf_op jit(solution)/shard_map/ppermute | solution.py:1112
  53.6 1.6 %collective-permute-start.17 = (bf16[4,48,1152]{2,1,0:T(8,128)(2,1)S(1)}, bf16[4,48,1152]{2,1,0:T(8,128)(2,1)S(1)}, u32[]{:S(2)}, u32[]{:S(2)}) collective-permute-start(bf16[4,48,1152]{2,1,0:T(8,128)(2,1)S(1)} %get-tuple-element.255), channel_id=1, source_target_pairs={{0,4},{1,5},{2,6},{3,7},{4,0},{5,1},{6,2},{7,3},{8,12},{9,13},{10,... | collective-permute-start | bytes 1327112 | tf_op jit(solution)/shard_map/ppermute | solution.py:1112
  55.3 4.5 %collective-permute-done.19 = bf16[4,48,1536]{2,1,0:T(8,128)(2,1)S(1)} collective-permute-done((bf16[4,48,1536]{2,1,0:T(8,128)(2,1)S(1)}, bf16[4,48,1536]{2,1,0:T(8,128)(2,1)S(1)}, u32[]{:S(2)}, u32[]{:S(2)}) %collective-permute-start.19) | collective-permute-done | bytes 589856 | tf_op jit(solution)/shard_map/ppermute | solution.py:1112
  59.9 1.6 %collective-permute-start.23 = (bf16[2,48,1536]{2,1,0:T(8,128)(2,1)S(1)}, bf16[2,48,1536]{2,1,0:T(8,128)(2,1)S(1)}, u32[]{:S(2)}, u32[]{:S(2)}) collective-permute-start(bf16[2,48,1536]{2,1,0:T(8,128)(2,1)S(1)} %get-tuple-element.258), channel_id=1, source_target_pairs={{0,4},{1,5},{2,6},{3,7},{4,0},{5,1},{6,2},{7,3},{8,12},{9,13},{10,... | collective-permute-start | bytes 884744 | tf_op jit(solution)/shard_map/ppermute | solution.py:1112
  62.0 1.6 %collective-permute-start.22 = (bf16[2,192,384]{2,1,0:T(8,128)(2,1)S(1)}, bf16[2,192,384]{2,1,0:T(8,128)(2,1)S(1)}, u32[]{:S(2)}, u32[]{:S(2)}) collective-permute-start(bf16[2,192,384]{2,1,0:T(8,128)(2,1)S(1)} %get-tuple-element.260), channel_id=1, source_target_pairs={{0,4},{1,5},{2,6},{3,7},{4,0},{5,1},{6,2},{7,3},{8,12},{9,13},{10,... | collective-permute-start | bytes 884744 | tf_op jit(solution)/shard_map/ppermute | solution.py:1112
  65.0 1.5 %collective-permute-start.21 = (bf16[2,48,1152]{2,1,0:T(8,128)(2,1)S(1)}, bf16[2,48,1152]{2,1,0:T(8,128)(2,1)S(1)}, u32[]{:S(2)}, u32[]{:S(2)}) collective-permute-start(bf16[2,48,1152]{2,1,0:T(8,128)(2,1)S(1)} %get-tuple-element.262), channel_id=1, source_target_pairs={{0,2},{1,3},{2,0},{3,1},{4,6},{5,7},{6,4},{7,5},{8,10},{9,11},{10,... | collective-permute-start | bytes 663560 | tf_op jit(solution)/shard_map/ppermute | solution.py:1112
  66.7 2.7 %collective-permute-start.27 = (bf16[1,48,1536]{2,1,0:T(8,128)(2,1)S(1)}, bf16[1,48,1536]{2,1,0:T(8,128)(2,1)S(1)}, u32[]{:S(2)}, u32[]{:S(2)}) collective-permute-start(bf16[1,48,1536]{2,1,0:T(8,128)(2,1)S(1)} %add_convert_fusion.19), channel_id=1, source_target_pairs={{0,8},{1,9},{2,10},{3,11},{4,12},{5,13},{6,14},{7,15},{8,0},{9,1},... | collective-permute-start | bytes 442376 | tf_op jit(solution)/shard_map/ppermute | solution.py:1112
  69.4 2.1 %collective-permute-start.20 = (bf16[2,128,768]{2,1,0:T(8,128)(2,1)S(1)}, bf16[2,128,768]{2,1,0:T(8,128)(2,1)S(1)}, u32[]{:S(2)}, u32[]{:S(2)}) collective-permute-start(bf16[2,128,768]{2,1,0:T(8,128)(2,1)S(1)} %get-tuple-element.209), channel_id=1, source_target_pairs={{0,1},{1,0},{2,3},{3,2},{4,5},{5,4},{6,7},{7,6},{8,9},{9,8},{10,11... | collective-permute-start | bytes 1179656 | tf_op jit(solution)/shard_map/ppermute | solution.py:1209
  73.4 2.6 %collective-permute-start.24 = (bf16[1,48,1152]{2,1,0:T(8,128)(2,1)S(1)}, bf16[1,48,1152]{2,1,0:T(8,128)(2,1)S(1)}, u32[]{:S(2)}, u32[]{:S(2)}) collective-permute-start(bf16[1,48,1152]{2,1,0:T(8,128)(2,1)S(1)} %add_convert_fusion.21), channel_id=1, source_target_pairs={{0,8},{1,9},{2,10},{3,11},{4,12},{5,13},{6,14},{7,15},{8,0},{9,1},... | collective-permute-start | bytes 331784 | tf_op jit(solution)/shard_map/ppermute | solution.py:1112
  76.5 3.7 %collective-permute-done.28 = bf16[1,192,384]{2,1,0:T(8,128)(2,1)S(1)} collective-permute-done((bf16[1,192,384]{2,1,0:T(8,128)(2,1)S(1)}, bf16[1,192,384]{2,1,0:T(8,128)(2,1)S(1)}, u32[]{:S(2)}, u32[]{:S(2)}) %collective-permute-start.28) | collective-permute-done | bytes 147488 | tf_op jit(solution)/shard_map/ppermute | solution.py:1112
  80.4 2.1 %collective-permute-start.31 = (bf16[48,1536]{1,0:T(8,128)(2,1)S(1)}, bf16[48,1536]{1,0:T(8,128)(2,1)S(1)}, u32[]{:S(2)}, u32[]{:S(2)}) collective-permute-start(bf16[48,1536]{1,0:T(8,128)(2,1)S(1)} %fusion.1.refs_9_.refs_6_), channel_id=1, source_target_pairs={{0,1},{1,0},{2,3},{3,2},{4,5},{5,4},{6,7},{7,6},{8,9},{9,8},{10,11... | collective-permute-start | bytes 442376 | tf_op jit(solution)/shard_map/ppermute | solution.py:1129
  84.8 2.3 %collective-permute-done.29.refs_8_.refs_5_ = bf16[192,384]{1,0:T(8,128)(2,1)S(1)} collective-permute-done((bf16[192,384]{1,0:T(8,128)(2,1)S(1)}, bf16[192,384]{1,0:T(8,128)(2,1)S(1)}, u32[]{:S(2)}, u32[]{:S(2)}) %collective-permute-start.29) | collective-permute-done | bytes 147488 | tf_op jit(solution)/shard_map/ppermute | solution.py:1129
  87.1 2.2 %collective-permute-done.31.refs_10_.refs_7_ = bf16[48,1536]{1,0:T(8,128)(2,1)S(1)} collective-permute-done((bf16[48,1536]{1,0:T(8,128)(2,1)S(1)}, bf16[48,1536]{1,0:T(8,128)(2,1)S(1)}, u32[]{:S(2)}, u32[]{:S(2)}) %collective-permute-start.31) | collective-permute-done | bytes 147488 | tf_op jit(solution)/shard_map/ppermute | solution.py:1129
  89.3 2.9 %collective-permute-done.30.refs_4_.refs_1_ = bf16[64,384]{1,0:T(8,128)(2,1)S(1)} collective-permute-done((bf16[64,384]{1,0:T(8,128)(2,1)S(1)}, bf16[64,384]{1,0:T(8,128)(2,1)S(1)}, u32[]{:S(2)}, u32[]{:S(2)}) %collective-permute-start.30) | collective-permute-done | bytes 49184 | tf_op jit(solution)/shard_map/ppermute | solution.py:1129
  92.3 3.6 %collective-permute-start.33 = (bf16[1152,384]{1,0:T(8,128)(2,1)S(1)}, bf16[1152,384]{1,0:T(8,128)(2,1)S(1)}, u32[]{:S(2)}, u32[]{:S(2)}) collective-permute-start(bf16[1152,384]{1,0:T(8,128)(2,1)S(1)} %shard_map.283), channel_id=1, source_target_pairs={{0,16},{16,0},{1,17},{17,1},{2,18},{18,2},{3,19},{19,3},{4,20},{20... | collective-permute-start | bytes 2654216 | tf_op jit(solution)/shard_map/ppermute | solution.py:1179
  95.9 1.9 %shard_map.282 = (f32[96,768]{1,0:T(8,128)}, f32[96,2304]{1,0:T(8,128)}, f32[384,768]{1,0:T(8,128)}, f32[96,3072]{1,0:T(8,128)}, bf16[2,128,768]{2,1,0:T(8,128)(...) custom-call(bf16[128,768]{1,0:T(8,128)(2,1)S(1)} %get-tuple-element., ...), custom_call_target="tpu_custom_call" | custom-call | flops 40000000000 | bytes 1 | tf_op jit(solution)/shard_map/pallas_call | solution.py:1041
  97.9 1.5 %shard_map.284 = (f32[96,768]{1,0:T(8,128)}, f32[96,2304]{1,0:T(8,128)}, f32[384,768]{1,0:T(8,128)}, f32[96,3072]{1,0:T(8,128)}) custom-call(bf16[1152,384]{1,0:T(8,128)(2,1)S(1)} %collective-permute-done.33.theirs, f32[8,128]{1,0:T(8,128)S(1)} %get-tuple-element.236.share, ...), custom_call_target="tpu_custom_call", output_to_operand_aliasing={{0}: (2, {}), {1}: (3, {}), {2}: (4, {}), {3}: (5, {})} | custom-call | flops 1 | bytes 1 | tf_op jit(solution)/shard_map/pallas_call | solution.py:1057
  (67 shorter events, 19.0 us)
Async XLA Ops:
  1.6 7.9 %collective-permute-start = (bf16[128,768]{1,0:T(8,128)(2,1)S(1)}, bf16[128,768]{1,0:T(8,128)(2,1)S(1)}, u32[]{:S(2)}, u32[]{:S(2)}) collective-permute-start(bf16[128,768]{1,0:T(8,128)(2,1)S(1)} %dynamic-slice_bitcast_fusion), channel_id=1, source_target_pairs={{0,1},{1,0},{2,3},{3,2},{4,5},{5,4},{6,7},{7,6},{8,9},{9,8},{10,11... | collective-permute-start | bytes 589832 | tf_op jit(solution)/shard_map/ppermute | solution.py:1164
  8.1 6.4 %collective-permute-start.4 = (bf16[128,768]{1,0:T(8,128)(2,1)S(1)}, bf16[128,768]{1,0:T(8,128)(2,1)S(1)}, u32[]{:S(2)}, u32[]{:S(2)}) collective-permute-start(bf16[128,768]{1,0:T(8,128)(2,1)S(1)} %get-tuple-element.141), channel_id=1, source_target_pairs={{0,1},{1,0},{2,3},{3,2},{4,5},{5,4},{6,7},{7,6},{8,9},{9,8},{10,11... | collective-permute-start | bytes 589832 | tf_op jit(solution)/shard_map/ppermute | solution.py:1175
  13.7 4.1 %collective-permute-start.2 = (bf16[256,768]{1,0:T(8,128)(2,1)S(1)}, bf16[256,768]{1,0:T(8,128)(2,1)S(1)}, u32[]{:S(2)}, u32[]{:S(2)}) collective-permute-start(bf16[256,768]{1,0:T(8,128)(2,1)S(1)} %get-tuple-element.188.left), channel_id=1, source_target_pairs={{0,16},{16,0},{1,17},{17,1},{2,18},{18,2},{3,19},{19,3},{4,20},{20... | collective-permute-start | bytes 1179656 | tf_op jit(solution)/shard_map/ppermute | solution.py:1179
  13.8 4.3 %collective-permute-start.3 = (bf16[256,768]{1,0:T(8,128)(2,1)S(1)}, bf16[256,768]{1,0:T(8,128)(2,1)S(1)}, u32[]{:S(2)}, u32[]{:S(2)}) collective-permute-start(bf16[256,768]{1,0:T(8,128)(2,1)S(1)} %get-tuple-element.184.left), channel_id=1, source_target_pairs={{0,16},{16,0},{1,17},{17,1},{2,18},{18,2},{3,19},{19,3},{4,20},{20... | collective-permute-start | bytes 1179656 | tf_op jit(solution)/shard_map/ppermute | solution.py:1179
  14.3 3.8 %collective-permute-start.1 = (bf16[256,768]{1,0:T(8,128)(2,1)S(1)}, bf16[256,768]{1,0:T(8,128)(2,1)S(1)}, u32[]{:S(2)}, u32[]{:S(2)}) collective-permute-start(bf16[256,768]{1,0:T(8,128)(2,1)S(1)} %get-tuple-element.163.n2.left), channel_id=1, source_target_pairs={{0,16},{16,0},{1,17},{17,1},{2,18},{18,2},{3,19},{19,3},{4,20},{20... | collective-permute-start | bytes 1179656 | tf_op jit(solution)/shard_map/ppermute | solution.py:1179
  17.2 4.5 %collective-permute-start.6 = (bf16[2,256,768]{2,1,0:T(8,128)(2,1)S(1)}, bf16[2,256,768]{2,1,0:T(8,128)(2,1)S(1)}, u32[]{:S(2)}, u32[]{:S(2)}) collective-permute-start(bf16[2,256,768]{2,1,0:T(8,128)(2,1)S(1)} %get-tuple-element.155), channel_id=1, source_target_pairs={{0,16},{16,0},{1,17},{17,1},{2,18},{18,2},{3,19},{19,3},{4,20},{20... | collective-permute-start | bytes 2359304 | tf_op jit(solution)/shard_map/ppermute | solution.py:1179
  17.5 4.2 %collective-permute-start.8 = (bf16[2,256,768]{2,1,0:T(8,128)(2,1)S(1)}, bf16[2,256,768]{2,1,0:T(8,128)(2,1)S(1)}, u32[]{:S(2)}, u32[]{:S(2)}) collective-permute-start(bf16[2,256,768]{2,1,0:T(8,128)(2,1)S(1)} %get-tuple-element.157.g_theirs), channel_id=1, source_target_pairs={{0,16},{16,0},{1,17},{17,1},{2,18},{18,2},{3,19},{19,3},{4,20},{20... | collective-permute-start | bytes 2359304 | tf_op jit(solution)/shard_map/ppermute | solution.py:1179
  17.8 3.9 %collective-permute-start.7 = (bf16[256,384]{1,0:T(8,128)(2,1)S(1)}, bf16[256,384]{1,0:T(8,128)(2,1)S(1)}, u32[]{:S(2)}, u32[]{:S(2)}) collective-permute-start(bf16[256,384]{1,0:T(8,128)(2,1)S(1)} %get-tuple-element.156), channel_id=1, source_target_pairs={{0,16},{16,0},{1,17},{17,1},{2,18},{18,2},{3,19},{19,3},{4,20},{20... | collective-permute-start | bytes 589832 | tf_op jit(solution)/shard_map/ppermute | solution.py:1179
  21.3 4.1 %collective-permute-start.5 = (bf16[2,256,768]{2,1,0:T(8,128)(2,1)S(1)}, bf16[2,256,768]{2,1,0:T(8,128)(2,1)S(1)}, u32[]{:S(2)}, u32[]{:S(2)}) collective-permute-start(bf16[2,256,768]{2,1,0:T(8,128)(2,1)S(1)} %get-tuple-element.192.g_mine), channel_id=1, source_target_pairs={{0,16},{16,0},{1,17},{17,1},{2,18},{18,2},{3,19},{19,3},{4,20},{20... | collective-permute-start | bytes 2359304 | tf_op jit(solution)/shard_map/ppermute | solution.py:1179
  23.7 18.2 %collective-permute-start.14 = (bf16[8,48,1536]{2,1,0:T(8,128)(2,1)S(1)}, bf16[8,48,1536]{2,1,0:T(8,128)(2,1)S(1)}, u32[]{:S(2)}, u32[]{:S(2)}) collective-permute-start(bf16[8,48,1536]{2,1,0:T(8,128)(2,1)S(1)} %get-tuple-element.167), channel_id=1, source_target_pairs={{0,2},{1,3},{2,0},{3,1},{4,6},{5,7},{6,4},{7,5},{8,10},{9,11},{10,... | collective-permute-start | bytes 3538952 | tf_op jit(solution)/shard_map/ppermute | solution.py:1112
  27.7 16.5 %collective-permute-start.13 = (bf16[8,192,384]{2,1,0:T(8,128)(2,1)S(1)}, bf16[8,192,384]{2,1,0:T(8,128)(2,1)S(1)}, u32[]{:S(2)}, u32[]{:S(2)}) collective-permute-start(bf16[8,192,384]{2,1,0:T(8,128)(2,1)S(1)} %get-tuple-element.173), channel_id=1, source_target_pairs={{0,1},{1,0},{2,3},{3,2},{4,5},{5,4},{6,7},{7,6},{8,9},{9,8},{10,11... | collective-permute-start | bytes 3538952 | tf_op jit(solution)/shard_map/ppermute | solution.py:1112
  33.0 4.9 %collective-permute-start.9 = (bf16[256,1152]{1,0:T(8,128)(2,1)S(1)}, bf16[256,1152]{1,0:T(8,128)(2,1)S(1)}, u32[]{:S(2)}, u32[]{:S(2)}) collective-permute-start(bf16[256,1152]{1,0:T(8,128)(2,1)S(1)} %get-tuple-element.177.dp_theirs), channel_id=1, source_target_pairs={{0,16},{16,0},{1,17},{17,1},{2,18},{18,2},{3,19},{19,3},{4,20},{20... | collective-permute-start | bytes 1769480 | tf_op jit(solution)/shard_map/ppermute | solution.py:1179
  37.2 12.0 %collective-permute-start.12 = (bf16[8,64,384]{2,1,0:T(8,128)(2,1)S(1)}, bf16[8,64,384]{2,1,0:T(8,128)(2,1)S(1)}, u32[]{:S(2)}, u32[]{:S(2)}) collective-permute-start(bf16[8,64,384]{2,1,0:T(8,128)(2,1)S(1)} %get-tuple-element.186), channel_id=1, source_target_pairs={{0,2},{1,3},{2,0},{3,1},{4,6},{5,7},{6,4},{7,5},{8,10},{9,11},{10,... | collective-permute-start | bytes 1179656 | tf_op jit(solution)/shard_map/ppermute | solution.py:1112
  39.3 14.1 %collective-permute-start.16 = (bf16[8,48,1152]{2,1,0:T(8,128)(2,1)S(1)}, bf16[8,48,1152]{2,1,0:T(8,128)(2,1)S(1)}, u32[]{:S(2)}, u32[]{:S(2)}) collective-permute-start(bf16[8,48,1152]{2,1,0:T(8,128)(2,1)S(1)} %get-tuple-element.191), channel_id=1, source_target_pairs={{0,1},{1,0},{2,3},{3,2},{4,5},{5,4},{6,7},{7,6},{8,9},{9,8},{10,11... | collective-permute-start | bytes 2654216 | tf_op jit(solution)/shard_map/ppermute | solution.py:1112
  42.2 17.5 %collective-permute-start.19 = (bf16[4,48,1536]{2,1,0:T(8,128)(2,1)S(1)}, bf16[4,48,1536]{2,1,0:T(8,128)(2,1)S(1)}, u32[]{:S(2)}, u32[]{:S(2)}) collective-permute-start(bf16[4,48,1536]{2,1,0:T(8,128)(2,1)S(1)} %get-tuple-element.252), channel_id=1, source_target_pairs={{0,1},{1,0},{2,3},{3,2},{4,5},{5,4},{6,7},{7,6},{8,9},{9,8},{10,11... | collective-permute-start | bytes 1769480 | tf_op jit(solution)/shard_map/ppermute | solution.py:1112
  44.5 17.3 %collective-permute-start.18 = (bf16[4,192,384]{2,1,0:T(8,128)(2,1)S(1)}, bf16[4,192,384]{2,1,0:T(8,128)(2,1)S(1)}, u32[]{:S(2)}, u32[]{:S(2)}) collective-permute-start(bf16[4,192,384]{2,1,0:T(8,128)(2,1)S(1)} %get-tuple-element.254), channel_id=1, source_target_pairs={{0,2},{1,3},{2,0},{3,1},{4,6},{5,7},{6,4},{7,5},{8,10},{9,11},{10,... | collective-permute-start | bytes 1769480 | tf_op jit(solution)/shard_map/ppermute | solution.py:1112
  49.3 14.5 %collective-permute-start.15 = (bf16[4,64,384]{2,1,0:T(8,128)(2,1)S(1)}, bf16[4,64,384]{2,1,0:T(8,128)(2,1)S(1)}, u32[]{:S(2)}, u32[]{:S(2)}) collective-permute-start(bf16[4,64,384]{2,1,0:T(8,128)(2,1)S(1)} %get-tuple-element.263), channel_id=1, source_target_pairs={{0,1},{1,0},{2,3},{3,2},{4,5},{5,4},{6,7},{7,6},{8,9},{9,8},{10,11... | collective-permute-start | bytes 589832 | tf_op jit(solution)/shard_map/ppermute | solution.py:1112
  53.6 10.0 %collective-permute-start.17 = (bf16[4,48,1152]{2,1,0:T(8,128)(2,1)S(1)}, bf16[4,48,1152]{2,1,0:T(8,128)(2,1)S(1)}, u32[]{:S(2)}, u32[]{:S(2)}) collective-permute-start(bf16[4,48,1152]{2,1,0:T(8,128)(2,1)S(1)} %get-tuple-element.255), channel_id=1, source_target_pairs={{0,4},{1,5},{2,6},{3,7},{4,0},{5,1},{6,2},{7,3},{8,12},{9,13},{10,... | collective-permute-start | bytes 1327112 | tf_op jit(solution)/shard_map/ppermute | solution.py:1112
  59.9 6.8 %collective-permute-start.23 = (bf16[2,48,1536]{2,1,0:T(8,128)(2,1)S(1)}, bf16[2,48,1536]{2,1,0:T(8,128)(2,1)S(1)}, u32[]{:S(2)}, u32[]{:S(2)}) collective-permute-start(bf16[2,48,1536]{2,1,0:T(8,128)(2,1)S(1)} %get-tuple-element.258), channel_id=1, source_target_pairs={{0,4},{1,5},{2,6},{3,7},{4,0},{5,1},{6,2},{7,3},{8,12},{9,13},{10,... | collective-permute-start | bytes 884744 | tf_op jit(solution)/shard_map/ppermute | solution.py:1112
  62.0 9.5 %collective-permute-start.22 = (bf16[2,192,384]{2,1,0:T(8,128)(2,1)S(1)}, bf16[2,192,384]{2,1,0:T(8,128)(2,1)S(1)}, u32[]{:S(2)}, u32[]{:S(2)}) collective-permute-start(bf16[2,192,384]{2,1,0:T(8,128)(2,1)S(1)} %get-tuple-element.260), channel_id=1, source_target_pairs={{0,4},{1,5},{2,6},{3,7},{4,0},{5,1},{6,2},{7,3},{8,12},{9,13},{10,... | collective-permute-start | bytes 884744 | tf_op jit(solution)/shard_map/ppermute | solution.py:1112
  63.8 12.2 %collective-permute-start.25 = (bf16[2,64,384]{2,1,0:T(8,128)(2,1)S(1)}, bf16[2,64,384]{2,1,0:T(8,128)(2,1)S(1)}, u32[]{:S(2)}, u32[]{:S(2)}) collective-permute-start(bf16[2,64,384]{2,1,0:T(8,128)(2,1)S(1)} %get-tuple-element.266), channel_id=1, source_target_pairs={{0,4},{1,5},{2,6},{3,7},{4,0},{5,1},{6,2},{7,3},{8,12},{9,13},{10,... | collective-permute-start | bytes 294920 | tf_op jit(solution)/shard_map/ppermute | solution.py:1112
  65.0 8.4 %collective-permute-start.21 = (bf16[2,48,1152]{2,1,0:T(8,128)(2,1)S(1)}, bf16[2,48,1152]{2,1,0:T(8,128)(2,1)S(1)}, u32[]{:S(2)}, u32[]{:S(2)}) collective-permute-start(bf16[2,48,1152]{2,1,0:T(8,128)(2,1)S(1)} %get-tuple-element.262), channel_id=1, source_target_pairs={{0,2},{1,3},{2,0},{3,1},{4,6},{5,7},{6,4},{7,5},{8,10},{9,11},{10,... | collective-permute-start | bytes 663560 | tf_op jit(solution)/shard_map/ppermute | solution.py:1112
  66.7 13.6 %collective-permute-start.27 = (bf16[1,48,1536]{2,1,0:T(8,128)(2,1)S(1)}, bf16[1,48,1536]{2,1,0:T(8,128)(2,1)S(1)}, u32[]{:S(2)}, u32[]{:S(2)}) collective-permute-start(bf16[1,48,1536]{2,1,0:T(8,128)(2,1)S(1)} %add_convert_fusion.19), channel_id=1, source_target_pairs={{0,8},{1,9},{2,10},{3,11},{4,12},{5,13},{6,14},{7,15},{8,0},{9,1},... | collective-permute-start | bytes 442376 | tf_op jit(solution)/shard_map/ppermute | solution.py:1112
  69.4 15.5 %collective-permute-start.20 = (bf16[2,128,768]{2,1,0:T(8,128)(2,1)S(1)}, bf16[2,128,768]{2,1,0:T(8,128)(2,1)S(1)}, u32[]{:S(2)}, u32[]{:S(2)}) collective-permute-start(bf16[2,128,768]{2,1,0:T(8,128)(2,1)S(1)} %get-tuple-element.209), channel_id=1, source_target_pairs={{0,1},{1,0},{2,3},{3,2},{4,5},{5,4},{6,7},{7,6},{8,9},{9,8},{10,11... | collective-permute-start | bytes 1179656 | tf_op jit(solution)/shard_map/ppermute | solution.py:1209
  71.5 8.7 %collective-permute-start.28 = (bf16[1,192,384]{2,1,0:T(8,128)(2,1)S(1)}, bf16[1,192,384]{2,1,0:T(8,128)(2,1)S(1)}, u32[]{:S(2)}, u32[]{:S(2)}) collective-permute-start(bf16[1,192,384]{2,1,0:T(8,128)(2,1)S(1)} %add_convert_fusion.18), channel_id=1, source_target_pairs={{0,8},{1,9},{2,10},{3,11},{4,12},{5,13},{6,14},{7,15},{8,0},{9,1},... | collective-permute-start | bytes 442376 | tf_op jit(solution)/shard_map/ppermute | solution.py:1112
  73.4 9.3 %collective-permute-start.24 = (bf16[1,48,1152]{2,1,0:T(8,128)(2,1)S(1)}, bf16[1,48,1152]{2,1,0:T(8,128)(2,1)S(1)}, u32[]{:S(2)}, u32[]{:S(2)}) collective-permute-start(bf16[1,48,1152]{2,1,0:T(8,128)(2,1)S(1)} %add_convert_fusion.21), channel_id=1, source_target_pairs={{0,8},{1,9},{2,10},{3,11},{4,12},{5,13},{6,14},{7,15},{8,0},{9,1},... | collective-permute-start | bytes 331784 | tf_op jit(solution)/shard_map/ppermute | solution.py:1112
  76.0 6.6 %collective-permute-start.26 = (bf16[1,64,384]{2,1,0:T(8,128)(2,1)S(1)}, bf16[1,64,384]{2,1,0:T(8,128)(2,1)S(1)}, u32[]{:S(2)}, u32[]{:S(2)}) collective-permute-start(bf16[1,64,384]{2,1,0:T(8,128)(2,1)S(1)} %add_convert_fusion.26), channel_id=1, source_target_pairs={{0,8},{1,9},{2,10},{3,11},{4,12},{5,13},{6,14},{7,15},{8,0},{9,1},... | collective-permute-start | bytes 147464 | tf_op jit(solution)/shard_map/ppermute | solution.py:1112
  80.3 6.8 %collective-permute-start.29 = (bf16[192,384]{1,0:T(8,128)(2,1)S(1)}, bf16[192,384]{1,0:T(8,128)(2,1)S(1)}, u32[]{:S(2)}, u32[]{:S(2)}) collective-permute-start(bf16[192,384]{1,0:T(8,128)(2,1)S(1)} %fusion.refs_7_.refs_4_), channel_id=1, source_target_pairs={{0,1},{1,0},{2,3},{3,2},{4,5},{5,4},{6,7},{7,6},{8,9},{9,8},{10,11... | collective-permute-start | bytes 442376 | tf_op jit(solution)/shard_map/ppermute | solution.py:1129
  80.4 8.9 %collective-permute-start.31 = (bf16[48,1536]{1,0:T(8,128)(2,1)S(1)}, bf16[48,1536]{1,0:T(8,128)(2,1)S(1)}, u32[]{:S(2)}, u32[]{:S(2)}) collective-permute-start(bf16[48,1536]{1,0:T(8,128)(2,1)S(1)} %fusion.1.refs_9_.refs_6_), channel_id=1, source_target_pairs={{0,1},{1,0},{2,3},{3,2},{4,5},{5,4},{6,7},{7,6},{8,9},{9,8},{10,11... | collective-permute-start | bytes 442376 | tf_op jit(solution)/shard_map/ppermute | solution.py:1129
  82.8 9.4 %collective-permute-start.32 = (bf16[48,1152]{1,0:T(8,128)(2,1)S(1)}, bf16[48,1152]{1,0:T(8,128)(2,1)S(1)}, u32[]{:S(2)}, u32[]{:S(2)}) collective-permute-start(bf16[48,1152]{1,0:T(8,128)(2,1)S(1)} %fusion.2.refs_5_.refs_2_), channel_id=1, source_target_pairs={{0,1},{1,0},{2,3},{3,2},{4,5},{5,4},{6,7},{7,6},{8,9},{9,8},{10,11... | collective-permute-start | bytes 331784 | tf_op jit(solution)/shard_map/ppermute | solution.py:1129
  83.8 8.4 %collective-permute-start.30 = (bf16[64,384]{1,0:T(8,128)(2,1)S(1)}, bf16[64,384]{1,0:T(8,128)(2,1)S(1)}, u32[]{:S(2)}, u32[]{:S(2)}) collective-permute-start(bf16[64,384]{1,0:T(8,128)(2,1)S(1)} %fusion.3.refs_3_.refs_0_), channel_id=1, source_target_pairs={{0,1},{1,0},{2,3},{3,2},{4,5},{5,4},{6,7},{7,6},{8,9},{9,8},{10,11... | collective-permute-start | bytes 147464 | tf_op jit(solution)/shard_map/ppermute | solution.py:1129
  92.3 5.6 %collective-permute-start.33 = (bf16[1152,384]{1,0:T(8,128)(2,1)S(1)}, bf16[1152,384]{1,0:T(8,128)(2,1)S(1)}, u32[]{:S(2)}, u32[]{:S(2)}) collective-permute-start(bf16[1152,384]{1,0:T(8,128)(2,1)S(1)} %shard_map.283), channel_id=1, source_target_pairs={{0,16},{16,0},{1,17},{17,1},{2,18},{18,2},{3,19},{19,3},{4,20},{20... | collective-permute-start | bytes 2654216 | tf_op jit(solution)/shard_map/ppermute | solution.py:1179
  (2 other events, 3.6 us)
